TPU v7x, 32 devices: a whole 2x2x4 slice. The times are simulated.
32 devices in a mesh: row: 8 (over y, x, core), col: 4 (over z).
Axes of the slice: x: 2, y: 2, z: 4, core: 2. Of those that a mesh axis runs over, the one named last changes fastest.
Arguments:
- object_field: float32 [2, 2048, 2048], P(None, 'row', 'col'), may hold values from -6 to 6
- probe: float32 [2, 4, 256, 256], replicated, may hold values from -3 to 3
- amplitudes: float32 [8, 4, 6, 256, 256], P('row', 'col'), may hold values from 0.25 to 4
- corners: int32 [8, 4, 6, 2], P('row', 'col'), may hold values from 0 to 1792, as said below
- counts: int32 [8, 4], replicated, may hold values from 1 to 6, as said below
Outputs:
- object_new: float32 [2, 2048, 2048], P(None, 'row', 'col')
- probe_new: float32 [2, 4, 256, 256], replicated
Inputs may be any that keep to these rules, and one draw needn't show every extreme that they name: counts[i, j] live slots on the tile at row i, column j; the later slots of that tile hold unused data; some tile has exactly 6. `corners`: each slot's corner lies inside the tile of the slot; every patch of 256 x 256 cells lies inside the object.
All inputs are finite; a program needn't handle non-finite values.
Results may differ from a plain program's by a relative error of at most 0.0013.
Values sent between devices are 32-bit elements; how exact they have to be, the bound alone decides.
No kernel may reach another device: no remote copies, remote signals or barrier semaphores. Data moves between devices by JAX's collectives and lax.ppermute only.
A program may use at most 64 MiB of HBM per device.

v0:
```python
import math

import jax
import jax.numpy as jnp
from jax import lax
from jax.sharding import PartitionSpec as P


def from_behind(value, axis, steps):
    count = lax.axis_size(axis)
    initial, last = (max(0, -steps), min(count, count - steps))
    return lax.ppermute(value, axis, [(source, source + steps) for source in range(initial, last)])


def tables(pattern_side):
    index = jnp.arange(pattern_side, dtype=jnp.int32)
    product = index[:, None] * index[None, :] % pattern_side
    angle = product.astype(jnp.float32) * (2.0 * math.pi / pattern_side)
    scale = 1.0 / math.sqrt(pattern_side)
    return (
        (jnp.cos(angle) * scale).astype(jnp.bfloat16),
        (-jnp.sin(angle) * scale).astype(jnp.bfloat16),
    )


def left_mul(table, values):
    return jnp.einsum("ab,mbc->mac", table, values, preferred_element_type=jnp.float32)


def right_mul(values, table):
    return jnp.einsum("mab,bc->mac", values, table, preferred_element_type=jnp.float32)


def transform(real_part, imag_part, table_re, table_im):
    rows_re = (left_mul(table_re, real_part) - left_mul(table_im, imag_part)).astype(jnp.bfloat16)
    rows_im = (left_mul(table_re, imag_part) + left_mul(table_im, real_part)).astype(jnp.bfloat16)
    out_re = right_mul(rows_re, table_re) - right_mul(rows_im, table_im)
    out_im = right_mul(rows_im, table_re) + right_mul(rows_re, table_im)
    return (out_re, out_im)


def process(window, amplitude, probe, table_re, table_im):
    probe_re, probe_im = (probe[0], probe[1])
    win_re, win_im = (window[0], window[1])
    psi_re = (probe_re * win_re - probe_im * win_im).astype(jnp.bfloat16)
    psi_im = (probe_re * win_im + probe_im * win_re).astype(jnp.bfloat16)
    wave_re, wave_im = transform(psi_re, psi_im, table_re, table_im)
    model = jnp.sum(wave_re * wave_re + wave_im * wave_im, axis=0)
    factor = amplitude / jnp.sqrt(jnp.maximum(model, 1.0)) - 1.0
    target_re = (wave_re * factor).astype(jnp.bfloat16)
    target_im = (wave_im * factor).astype(jnp.bfloat16)
    chi_re, chi_im = transform(target_re, target_im, table_re, -table_im)
    grad_re = jnp.sum(probe_re * chi_re + probe_im * chi_im, axis=0)
    grad_im = jnp.sum(probe_re * chi_im - probe_im * chi_re, axis=0)
    pgrad_re = win_re * chi_re + win_im * chi_im
    pgrad_im = win_re * chi_im - win_im * chi_re
    return (
        jnp.stack([grad_re, grad_im]),
        jnp.stack([pgrad_re, pgrad_im]),
        win_re * win_re + win_im * win_im,
    )


def add_block(accumulated, added, row_at, col_at):
    zero_index = jnp.zeros((), jnp.int32)
    depth = added.shape[0]
    size = added.shape[1]
    region = lax.dynamic_slice(accumulated, (zero_index, row_at, col_at), (depth, size, size))
    return lax.dynamic_update_slice(accumulated, region + added, (zero_index, row_at, col_at))


def body(object_field, probe, amplitudes, corners, counts):
    tile_rows, tile_cols = (object_field.shape[1], object_field.shape[2])
    pattern_side = probe.shape[-1]
    margin = pattern_side - 1
    table_re, table_im = tables(pattern_side)
    zero_index = jnp.zeros((), jnp.int32)
    my_row = lax.axis_index("row")
    my_col = lax.axis_index("col")
    anchor = jnp.stack([my_row * tile_rows, my_col * tile_cols])
    local = corners[0, 0] - anchor[None, :]
    measured = amplitudes[0, 0]
    my_count = counts[my_row, my_col]
    below = from_behind(object_field[:, :margin, :], "row", -1)
    tall = jnp.concatenate([object_field, below], axis=1)
    beside = from_behind(tall[:, :, :margin], "col", -1)
    extended = jnp.concatenate([tall, beside], axis=2)
    lighting = jnp.sum(probe[0] * probe[0] + probe[1] * probe[1], axis=0)
    accumulated = jnp.zeros((3,) + extended.shape[1:], jnp.float32)
    probe_grad = jnp.zeros(probe.shape, jnp.float32)
    probe_den = jnp.zeros((pattern_side, pattern_side), jnp.float32)

    def with_light(grad):
        return jnp.concatenate([grad, lighting[None]], axis=0)

    def cut_window(slot):
        return lax.dynamic_slice(
            extended, (zero_index, local[slot, 0], local[slot, 1]), (2, pattern_side, pattern_side)
        )

    def own_step(slot, state):
        accumulated, probe_grad, probe_den = state
        grad, pgrad, pden = process(cut_window(slot), measured[slot], probe, table_re, table_im)
        accumulated = add_block(accumulated, with_light(grad), local[slot, 0], local[slot, 1])
        return (accumulated, probe_grad + pgrad, probe_den + pden)

    accumulated, probe_grad, probe_den = lax.fori_loop(
        zero_index, my_count, own_step, (accumulated, probe_grad, probe_den)
    )
    came = from_behind(accumulated[:, :, tile_cols:], "col", 1)
    narrow = accumulated[:, :, :tile_cols]
    narrow = jnp.concatenate([narrow[:, :, :margin] + came, narrow[:, :, margin:]], axis=2)
    came = from_behind(narrow[:, tile_rows:, :], "row", 1)
    short = narrow[:, :tile_rows, :]
    tile_sum = jnp.concatenate([short[:, :margin, :] + came, short[:, margin:, :]], axis=1)
    light = tile_sum[2]
    probe_grad, probe_den = lax.psum((probe_grad, probe_den), ("row", "col"))
    brightest = lax.pmax(jnp.max(light), ("row", "col"))
    object_new = object_field + tile_sum[:2] / (light + 0.1 * brightest)
    probe_new = probe + probe_grad / (probe_den + 0.1 * jnp.max(probe_den))
    return (object_new, probe_new)


def solution(mesh):
    in_specs = (
        P(None, "row", "col"),
        P(),
        P("row", "col", None, None, None),
        P("row", "col", None, None),
        P(),
    )
    out_specs = (P(None, "row", "col"), P())
    return jax.shard_map(body, mesh=mesh, in_specs=in_specs, out_specs=out_specs, check_vma=False)
```

profile of v0, /device:TPU:0, one launch (start us, length us, event | category | flops | bytes accessed | tf_op | source)
XLA Modules:
  0.0 577.1 jit_solution(14386954459421590154)
XLA Ops:
  7.2 3.1 copy.60
  12.2 2.9 collective-permute-done
  15.0 2.1 copy.41
  17.2 2.6 pad_maximum_fusion.1
  21.1 1.4 dynamic_slice.35
  22.8 14.9 %collective-permute-done.1 = f32[2,511,255]{1,0,2:T(2,128)} collective-permute-done((f32[2,511,255]{1,0,2:T(2,128)}, f32[2,511,255]{1,0,2:T(2,128)}, u32[]{:S(2)}, u32[]{:S(2)}) %collective-permute-start.1) | collective-permute-done | bytes 1042472 | tf_op jit(solution)/shard_map/ppermute | solution.py:12
  37.8 8.9 %pad_maximum_fusion = f32[2,511,767]{1,0,2:T(2,128)} fusion(f32[2,511,255]{1,0,2:T(2,128)} %collective-permute-done.1, f32[2,255,512]{1,0,2:T(2,128)S(1)} %copy-done.8, f32[2,256,512]{1,0,2:T(2,128)S(1)} %copy.40), kind=kLoop, calls=%fused_computation.162 | loop fusion | flops 1567748 | bytes 6270992 | tf_op jit(solution)/shard_map/concatenate | solution.py:87
  46.6 1.5 broadcast_in_dim.23
  48.1 2.5 broadcast_in_dim.22
  50.6 224.6 %while.18 = (s32[]{:T(128)}, f32[3,511,767]{2,1,0:T(8,128)}, f32[2,4,256,256]{3,2,1,0:T(8,128)}, f32[256,256]{1,0:T(8,128)S(1)}, s32[]{:T(128)}, /*index=5*/s32[...) while((s32[]{:T(128)}, f32[3,511,767]{2,1,0:T(8,128)}, ...), condition=%wide.region_5.6_spmd.clone.clone, body=%wide.region_1.5_spmd.clone.clone.sunk | while | flops 2179530752 | bytes 58982716 | solution.py:107
  56.2 2.5 constant_dynamic-slice_fusion.6
  79.4 1.9 add_bitcast_fusion.3
  81.3 1.6 maximum_add_fusion.4
  82.9 3.2 maximum_add_fusion.5
  86.2 9.2 %dynamic_update_slice.9 = f32[3,511,767]{2,1,0:T(8,128)} dynamic-update-slice(f32[3,511,767]{2,1,0:T(8,128)} %get-tuple-element.425, f32[3,256,256]{2,1,0:T(8,128)S(1)} %maximum_add_fusion.4, s32[]{:T(128)} %constant.69.clone.1..sunk, s32[]{:T(128)S(6)} %select_n.173, s32[]{:T(128)S(6)} %select_n.174) | dynamic-update-slice | bytes 1572868 | tf_op jit(solution)/shard_map/while/body/dynamic_update_slice | solution.py:69
  100.7 2.5 constant_dynamic-slice_fusion.6
  124.0 1.9 add_bitcast_fusion.3
  125.9 1.6 maximum_add_fusion.4
  127.5 3.2 maximum_add_fusion.5
  130.7 9.1 %dynamic_update_slice.9 = f32[3,511,767]{2,1,0:T(8,128)} dynamic-update-slice(f32[3,511,767]{2,1,0:T(8,128)} %get-tuple-element.425, f32[3,256,256]{2,1,0:T(8,128)S(1)} %maximum_add_fusion.4, s32[]{:T(128)} %constant.69.clone.1..sunk, s32[]{:T(128)S(6)} %select_n.173, s32[]{:T(128)S(6)} %select_n.174) | dynamic-update-slice | bytes 1572868 | tf_op jit(solution)/shard_map/while/body/dynamic_update_slice | solution.py:69
  145.2 2.6 constant_dynamic-slice_fusion.6
  168.5 1.9 add_bitcast_fusion.3
  170.4 1.6 maximum_add_fusion.4
  172.0 3.2 maximum_add_fusion.5
  175.3 9.3 %dynamic_update_slice.9 = f32[3,511,767]{2,1,0:T(8,128)} dynamic-update-slice(f32[3,511,767]{2,1,0:T(8,128)} %get-tuple-element.425, f32[3,256,256]{2,1,0:T(8,128)S(1)} %maximum_add_fusion.4, s32[]{:T(128)} %constant.69.clone.1..sunk, s32[]{:T(128)S(6)} %select_n.173, s32[]{:T(128)S(6)} %select_n.174) | dynamic-update-slice | bytes 1572868 | tf_op jit(solution)/shard_map/while/body/dynamic_update_slice | solution.py:69
  190.0 2.6 constant_dynamic-slice_fusion.6
  213.3 1.9 add_bitcast_fusion.3
  215.2 1.6 maximum_add_fusion.4
  216.8 3.2 maximum_add_fusion.5
  220.1 9.5 %dynamic_update_slice.9 = f32[3,511,767]{2,1,0:T(8,128)} dynamic-update-slice(f32[3,511,767]{2,1,0:T(8,128)} %get-tuple-element.425, f32[3,256,256]{2,1,0:T(8,128)S(1)} %maximum_add_fusion.4, s32[]{:T(128)} %constant.69.clone.1..sunk, s32[]{:T(128)S(6)} %select_n.173, s32[]{:T(128)S(6)} %select_n.174) | dynamic-update-slice | bytes 1572868 | tf_op jit(solution)/shard_map/while/body/dynamic_update_slice | solution.py:69
  234.9 2.7 constant_dynamic-slice_fusion.6
  258.3 1.9 add_bitcast_fusion.3
  260.2 1.6 maximum_add_fusion.4
  261.8 3.2 maximum_add_fusion.5
  265.1 9.3 %dynamic_update_slice.9 = f32[3,511,767]{2,1,0:T(8,128)} dynamic-update-slice(f32[3,511,767]{2,1,0:T(8,128)} %get-tuple-element.425, f32[3,256,256]{2,1,0:T(8,128)S(1)} %maximum_add_fusion.4, s32[]{:T(128)} %constant.69.clone.1..sunk, s32[]{:T(128)S(6)} %select_n.173, s32[]{:T(128)S(6)} %select_n.174) | dynamic-update-slice | bytes 1572868 | tf_op jit(solution)/shard_map/while/body/dynamic_update_slice | solution.py:69
  275.2 1.6 slice.73
  276.9 1.4 collective-permute-start.2
  278.3 2.6 slice.74
  280.8 15.2 %collective-permute-done.2 = f32[3,511,255]{2,1,0:T(8,128)S(1)} collective-permute-done((f32[3,511,255]{2,1,0:T(8,128)S(1)}, f32[3,511,255]{2,1,0:T(8,128)S(1)}, u32[]{:S(2)}, u32[]{:S(2)}) %collective-permute-start.2) | collective-permute-done | bytes 1563692 | tf_op jit(solution)/shard_map/ppermute | solution.py:12
  296.1 1.7 slice_add_fusion
  297.8 1.7 fusion.140
  299.5 2.5 collective-permute-start.3
  302.0 214.4 %all-reduce.3.cloned.1.call-done = (f32[2,4,256,256]{3,2,1,0:T(8,128)}, f32[256,256]{1,0:T(8,128)}) async-done(((f32[2,4,256,256]{3,2,1,0:T(8,128)}, f32[256,256]{1,0:T(8,128)}), (f32[2,4,256,256]{3,2,1,0:T(8,128)}, f32[256,256]{1,0:T(8,128)})) %all-reduce.3.cloned.1.call-update) | async-done | bytes 2359312 | tf_op jit(solution)/shard_map/psum | solution.py:117
  516.4 1.6 reduce_max.19
  519.6 2.5 fusion.142
  525.0 1.7 divide_add_fusion
  526.7 39.3 %pmax.7 = f32[]{:T(128)} all-reduce(f32[]{:T(128)} %slice_reduce_fusion), channel_id=1, replica_groups=mesh['row'=8,'col'=4] {'row','col'}, use_global_device_ids=true, to_apply=%region_7.8 | all-reduce | flops 1 | bytes 8 | tf_op jit(solution)/shard_map/pmax | solution.py:118
  567.8 2.5 fusion.144
  (143 shorter events, 114.8 us)
Async XLA Ops:
  7.2 4.4 copy-start.6
  7.2 509.2 %all-reduce.3.cloned.1.call-start = ((), (), s32[]{:S(2)}) async-start(), calls=%async_computation | async-start | bytes 4718592 | tf_op jit(solution)/shard_map/psum | solution.py:117
  10.3 4.7 collective-permute-start
  17.2 5.4 copy-start
  17.2 5.6 copy-start.11
  19.8 18.0 %collective-permute-start.1 = (f32[2,511,255]{1,0,2:T(2,128)}, f32[2,511,255]{1,0,2:T(2,128)}, u32[]{:S(2)}, u32[]{:S(2)}) collective-permute-start(f32[2,511,255]{1,0,2:T(2,128)} %pad_maximum_fusion.1), channel_id=1, source_target_pairs={{1,0},{2,1},{3,2},{5,4},{6,5},{7,6},{9,8},{10,9},{11,10},{13,12},{... | collective-permute-start | bytes 3127328 | tf_op jit(solution)/shard_map/ppermute | solution.py:12
  21.1 16.7 %copy-start.8 = (f32[2,255,512]{1,0,2:T(2,128)S(1)}, f32[2,255,512]{1,0,2:T(2,128)}, u32[]{:S(2)}) copy-start(f32[2,255,512]{1,0,2:T(2,128)} %copy.41) | copy-start | bytes 3133444
  275.2 5.6 copy-start.5
  276.9 19.2 %collective-permute-start.2 = (f32[3,511,255]{2,1,0:T(8,128)S(1)}, f32[3,511,255]{2,1,0:T(8,128)S(1)}, u32[]{:S(2)}, u32[]{:S(2)}) collective-permute-start(f32[3,511,255]{2,1,0:T(8,128)S(1)} %slice.73), channel_id=1, source_target_pairs={{0,1},{1,2},{2,3},{4,5},{5,6},{6,7},{8,9},{9,10},{10,11},{12,13},{... | collective-permute-start | bytes 4690988 | tf_op jit(solution)/shard_map/ppermute | solution.py:12
  280.8 17.0 %copy-start.1 = (f32[3,511,257]{2,1,0:T(8,128)}, f32[3,511,257]{2,1,0:T(8,128)S(1)}, u32[]{:S(2)}) copy-start(f32[3,511,257]{2,1,0:T(8,128)S(1)} %slice.74) | copy-start | bytes 4727776
  297.8 1.7 copy-start.3
  299.5 220.2 %collective-permute-start.3 = (f32[3,255,512]{2,1,0:T(8,128)}, f32[3,255,512]{2,1,0:T(8,128)}, u32[]{:S(2)}, u32[]{:S(2)}) collective-permute-start(f32[3,255,512]{2,1,0:T(8,128)} %fusion.140), channel_id=1, source_target_pairs={{0,4},{4,8},{8,12},{12,16},{16,20},{20,24},{24,28},{1,5},{5,9},{9,... | collective-permute-start | bytes 4700168 | tf_op jit(solution)/shard_map/ppermute | solution.py:12
  519.6 2.7 copy-start.2
  519.6 3.2 copy-start.4
  522.8 2.2 copy-start.10
  523.0 1.2 copy-start.9
  525.0 42.8 %copy-start.7 = (f32[2,256,512]{2,1,0:T(8,128)S(1)}, f32[2,256,512]{2,1,0:T(8,128)}, u32[]{:S(2)}) copy-start(f32[2,256,512]{2,1,0:T(8,128)} %param.7) | copy-start | bytes 3145732
Sparse Core Ops, SparseCore 0:
  302.1 214.2 all-reduce.2
where the time goes:
time: 575 us; the launch traced here: 577 us
  waiting for transfers between devices  247 us (43%)
  matrix products  104 us (18%)
  local copies, waits for them, and re-layouts  81.4 us (14%)
  other arithmetic  57.5 us (10%)
  blocking collectives  39.3 us (7%)
  loops' own time  25.3 us (4%)
  between operations  15.5 us (3%)
  starting transfers between devices  6.5 us (1%)
    psum x1, waiting for transfers between devices, body(): probe_grad, probe_den = lax.psum((probe_grad, probe_den), ('row', 'col'))  214 us
    dot_general x40, matrix products, right_mul(): jnp.einsum('mab,bc->mac', values, table, preferred_element_type=jnp.float32)  53.7 us
    dot_general x40, matrix products, left_mul(): jnp.einsum('ab,mbc->mac', table, values, preferred_element_type=jnp.float32)  50.5 us
    dynamic_update_slice x5, local copies, waits for them, and re-layouts, add_block(): lax.dynamic_update_slice(accumulated, region + added, (zero_index, row_at...  46.4 us
    pmax x1, blocking collectives, body(): brightest = lax.pmax(jnp.max(light), ('row', 'col'))  39.3 us
    ppermute x4, waiting for transfers between devices, from_behind(): lax.ppermute(value, axis, [(source, source + steps) for source in range(i...  33 us
    another operation x1, loops' own time, body(): lax.fori_loop(zero_index, my_count, own_step, (accumulated, probe_grad, p...  25.3 us
    add x10, other arithmetic, own_step(): return (accumulated, probe_grad + pgrad, probe_den + pden)  16.6 us
  transfers between devices with their start and end apart: 5, of which 4 were waited for; matrix products, arithmetic and copies ran while one was open for 1% of the time, Pallas kernels for 0%

commit v1 on v0

v1 whole, which is shorter than its diff:
```python
import functools
import math

import jax
import jax.numpy as jnp
import numpy as np
from jax import lax
from jax.experimental import pallas as pl
from jax.experimental.pallas import tpu as pltpu
from jax.sharding import PartitionSpec as P

LANES = 128
SUBLANES = 8
VMEM_LIMIT = 56 * 1024 * 1024


def shifted(value, d_row, d_col):
    rows, cols = lax.axis_size("row"), lax.axis_size("col")
    pairs = []
    for r in range(rows):
        for c in range(cols):
            if 0 <= r + d_row < rows and 0 <= c + d_col < cols:
                pairs.append((r * cols + c, (r + d_row) * cols + c + d_col))
    return lax.ppermute(value, ("row", "col"), pairs)


def tables(side):
    index = np.arange(side)
    angle = (index[:, None] * index[None, :] % side) * (2.0 * math.pi / side)
    scale = 1.0 / math.sqrt(side)
    re = (np.cos(angle) * scale).astype(np.float32)
    im = (-np.sin(angle) * scale).astype(np.float32)

    def left(im):
        return np.block([[re, -im], [im, re]])

    def right(im):
        return np.block([[re, im], [-im, re]])

    return [jnp.asarray(t, jnp.bfloat16) for t in (left(im), right(im), left(-im), right(-im))]


def corner_of(row, col):
    row_base = pl.multiple_of(row // SUBLANES * SUBLANES, SUBLANES)
    col_base = pl.multiple_of(col // LANES * LANES, LANES)
    return row_base, row - row_base, col_base, col - col_base


def window_at(ref, part, row, col, side):
    row_base, down, col_base, over = corner_of(row, col)
    groups = side // SUBLANES
    lane = lax.broadcasted_iota(jnp.int32, (side, LANES), 1)
    sub = lax.broadcasted_iota(jnp.int32, (groups, SUBLANES, LANES), 1)
    turned = []
    for j in range(side // LANES + 1):
        block = ref[part, pl.ds(row_base, side + SUBLANES), pl.ds(col_base + j * LANES, LANES)]
        block = block.reshape(groups + 1, SUBLANES, LANES)
        block = pltpu.roll(block, lax.rem(SUBLANES - down, SUBLANES), 1)
        block = jnp.where(sub < SUBLANES - down, block[:groups], block[1:]).reshape(side, LANES)
        turned.append(pltpu.roll(block, lax.rem(LANES - over, LANES), 1))
    parts = [jnp.where(lane < LANES - over, turned[j], turned[j + 1]) for j in range(side // LANES)]
    return jnp.concatenate(parts, axis=1)


def add_at(ref, part, row, col, value, side):
    row_base, down, col_base, over = corner_of(row, col)
    groups = side // SUBLANES
    blocks = side // LANES
    lane = lax.broadcasted_iota(jnp.int32, (side, LANES), 1)
    sub = lax.broadcasted_iota(jnp.int32, (groups + 1, SUBLANES, LANES), 1)
    turned = [pltpu.roll(value[:, j * LANES:(j + 1) * LANES], over, 1) for j in range(blocks)]
    none = jnp.zeros((side, LANES), value.dtype)
    gap = jnp.zeros((1, SUBLANES, LANES), value.dtype)
    for j in range(blocks + 1):
        block = jnp.where(lane >= over, turned[j] if j < blocks else none, turned[j - 1] if j else none)
        block = pltpu.roll(block.reshape(groups, SUBLANES, LANES), down, 1)
        block = jnp.where(
            sub >= down, jnp.concatenate([block, gap], axis=0), jnp.concatenate([gap, block], axis=0)
        )
        place = (part, pl.ds(row_base, side + SUBLANES), pl.ds(col_base + j * LANES, LANES))
        ref[place] += block.reshape(side + SUBLANES, LANES)


def main_kernel(
    count_ref, local_ref, tile_ref, below_ref, right_ref, corner_ref, amp_ref, probe_ref, lf_ref, rf_ref, lg_ref, rg_ref,
    g_tile, g_below, g_right, g_corner, pgrad_ref,
    ext, gacc, stage, turned, wave,
):
    modes, side = probe_ref.shape[1], probe_ref.shape[2]
    rows, cols = tile_ref.shape[1], tile_ref.shape[2]
    ext[:, :rows, :cols] = tile_ref[...]
    ext[:, rows:, :cols] = below_ref[...]
    ext[:, :rows, cols:] = right_ref[...]
    ext[:, rows:, cols:] = corner_ref[...]
    gacc[...] = jnp.zeros_like(gacc)
    pgrad_ref[...] = jnp.zeros_like(pgrad_ref)

    def dot(a, b):
        return jnp.dot(a, b, preferred_element_type=jnp.float32)

    def transform(left_ref, right_ref):
        for k in range(modes):
            got = dot(left_ref[...], stage[:, k * side:(k + 1) * side])
            turned[k * side:(k + 1) * side, :side] = got[:side].astype(jnp.bfloat16)
            turned[k * side:(k + 1) * side, side:] = got[side:].astype(jnp.bfloat16)
        wave[...] = dot(turned[...], right_ref[...])

    def step(p, carry):
        row, col = local_ref[p, 0], local_ref[p, 1]
        win_re = window_at(ext, 0, row, col, side)
        win_im = window_at(ext, 1, row, col, side)
        for k in range(modes):
            pr, pi = probe_ref[0, k], probe_ref[1, k]
            stage[:side, k * side:(k + 1) * side] = (pr * win_re - pi * win_im).astype(jnp.bfloat16)
            stage[side:, k * side:(k + 1) * side] = (pr * win_im + pi * win_re).astype(jnp.bfloat16)
        transform(lf_ref, rf_ref)
        model = jnp.zeros((side, side), jnp.float32)
        for k in range(modes):
            wr, wi = wave[k * side:(k + 1) * side, :side], wave[k * side:(k + 1) * side, side:]
            model += wr * wr + wi * wi
        factor = amp_ref[p] * lax.rsqrt(jnp.maximum(model, 1.0)) - 1.0
        for k in range(modes):
            wr, wi = wave[k * side:(k + 1) * side, :side], wave[k * side:(k + 1) * side, side:]
            stage[:side, k * side:(k + 1) * side] = (wr * factor).astype(jnp.bfloat16)
            stage[side:, k * side:(k + 1) * side] = (wi * factor).astype(jnp.bfloat16)
        transform(lg_ref, rg_ref)
        grad_re = jnp.zeros((side, side), jnp.float32)
        grad_im = jnp.zeros((side, side), jnp.float32)
        win_re = window_at(ext, 0, row, col, side)
        win_im = window_at(ext, 1, row, col, side)
        for k in range(modes):
            cr, ci = wave[k * side:(k + 1) * side, :side], wave[k * side:(k + 1) * side, side:]
            pr, pi = probe_ref[0, k], probe_ref[1, k]
            grad_re += pr * cr + pi * ci
            grad_im += pr * ci - pi * cr
            pgrad_ref[k] += win_re * cr + win_im * ci
            pgrad_ref[modes + k] += win_re * ci - win_im * cr
        pgrad_ref[2 * modes] += win_re * win_re + win_im * win_im
        add_at(gacc, 0, row, col, grad_re, side)
        add_at(gacc, 1, row, col, grad_im, side)
        return carry

    lax.fori_loop(0, count_ref[0], step, 0)
    g_tile[...] = gacc[:, :rows, :cols]
    g_below[...] = gacc[:, rows:, :cols]
    g_right[...] = gacc[:, :rows, cols:]
    g_corner[...] = gacc[:, rows:, cols:]


def light_kernel(total_ref, where_ref, probe_ref, light_ref, top_ref, lit, acc):
    side = probe_ref.shape[2]
    rows, cols = light_ref.shape
    lit[0] = jnp.sum(probe_ref[0] * probe_ref[0] + probe_ref[1] * probe_ref[1], axis=0)
    acc[...] = jnp.zeros_like(acc)

    def step(p, carry):
        add_at(acc, 0, where_ref[p, 0], where_ref[p, 1], lit[0], side)
        return carry

    lax.fori_loop(0, total_ref[0], step, 0)
    light = acc[0, side:side + rows, side:side + cols]
    light_ref[...] = light
    top = jnp.max(light, axis=0, keepdims=True)
    top = jnp.max(top, axis=1, keepdims=True)
    top_ref[...] = jnp.broadcast_to(top, top_ref.shape)


def finish_kernel(top_ref, tile_ref, light_ref, g_tile, g_up, g_left, g_diag, out_ref, total):
    side = g_left.shape[2]
    total[...] = g_tile[...] + g_up[...]
    total[:, :, :side] += g_left[...] + g_diag[...]
    scale = 1.0 / (light_ref[...] + 0.1 * top_ref[0, 0])
    out_ref[0] = tile_ref[0] + total[0] * scale
    out_ref[1] = tile_ref[1] + total[1] * scale


def probe_kernel(probe_ref, sums_ref, out_ref):
    modes = probe_ref.shape[1]
    den = sums_ref[2 * modes]
    top = jnp.max(jnp.max(den, axis=0, keepdims=True), axis=1, keepdims=True)
    scale = 1.0 / (den + 0.1 * top)
    for k in range(modes):
        out_ref[0, k] = probe_ref[0, k] + sums_ref[k] * scale
        out_ref[1, k] = probe_ref[1, k] + sums_ref[modes + k] * scale


def f32(*shape):
    return jax.ShapeDtypeStruct(shape, jnp.float32)


VM = pl.BlockSpec(memory_space=pltpu.VMEM)
SM = pl.BlockSpec(memory_space=pltpu.SMEM)
PARAMS = pltpu.CompilerParams(vmem_limit_bytes=VMEM_LIMIT)


def cost(flops, moved):
    return pl.CostEstimate(flops=flops, bytes_accessed=moved, transcendentals=0)


def body(object_field, probe, amplitudes, corners, counts):
    rows, cols = object_field.shape[1], object_field.shape[2]
    modes, side = probe.shape[1], probe.shape[2]
    slots = amplitudes.shape[2]
    my_row, my_col = lax.axis_index("row"), lax.axis_index("col")
    anchor = jnp.stack([my_row * rows, my_col * cols])
    spots = corners[0, 0]
    local = spots - anchor[None, :]

    from_up = shifted(spots, 1, 0)
    from_left = shifted(spots, 0, 1)
    from_diag = shifted(spots, 1, 1)
    below = shifted(object_field[:, :side, :], -1, 0)
    right = shifted(object_field[:, :, :side], 0, -1)
    corner = shifted(object_field[:, :side, :side], -1, -1)

    def live(d_row, d_col):
        inside = (my_row >= d_row) & (my_col >= d_col)
        number = counts[jnp.maximum(my_row - d_row, 0), jnp.maximum(my_col - d_col, 0)]
        return (jnp.arange(slots) < number) & inside

    where = jnp.concatenate([spots, from_up, from_left, from_diag], axis=0) - anchor[None, :] + side
    flags = jnp.concatenate([live(0, 0), live(1, 0), live(0, 1), live(1, 1)])
    flags = flags & (where[:, 0] > 0) & (where[:, 1] > 0)
    order = jnp.where(flags, jnp.cumsum(flags) - 1, 4 * slots)
    picked = jnp.arange(4 * slots)[:, None] == order[None, :]
    where = jnp.sum(jnp.where(picked[:, :, None], where[None, :, :], 0), axis=1).astype(jnp.int32)
    total = jnp.sum(flags).astype(jnp.int32).reshape(1)
    light, top = pl.pallas_call(
        light_kernel,
        out_shape=(f32(rows, cols), f32(8, LANES)),
        in_specs=[SM, SM, VM],
        out_specs=(VM, VM),
        scratch_shapes=[
            pltpu.VMEM((1, side, side), jnp.float32),
            pltpu.VMEM((1, rows + 2 * side, cols + 2 * side), jnp.float32),
        ],
        compiler_params=PARAMS,
        cost_estimate=cost(10**8, 10**7),
        name="lighting",
    )(total, where, probe)
    top = lax.pmax(top, ("row", "col"))

    count = counts[my_row, my_col].reshape(1)
    g_tile, g_below, g_right, g_corner, sums = pl.pallas_call(
        main_kernel,
        out_shape=(
            f32(2, rows, cols), f32(2, side, cols), f32(2, rows, side), f32(2, side, side),
            f32(2 * modes + 1, side, side),
        ),
        in_specs=[SM, SM] + [VM] * 10,
        out_specs=(VM,) * 5,
        scratch_shapes=[
            pltpu.VMEM((2, rows + side, cols + side), jnp.float32),
            pltpu.VMEM((2, rows + side, cols + side), jnp.float32),
            pltpu.VMEM((2 * side, modes * side), jnp.bfloat16),
            pltpu.VMEM((modes * side, 2 * side), jnp.bfloat16),
            pltpu.VMEM((modes * side, 2 * side), jnp.float32),
        ],
        compiler_params=PARAMS,
        cost_estimate=cost(13 * 10**9, 2 * 10**7),
        name="positions",
    )(count, local, object_field, below, right, corner, amplitudes[0, 0], probe, *tables(side))

    g_up = shifted(g_below, 1, 0)
    g_left = shifted(g_right, 0, 1)
    g_diag = shifted(g_corner, 1, 1)
    sums = lax.psum(sums, ("row", "col"))
    object_new = pl.pallas_call(
        finish_kernel,
        out_shape=f32(2, rows, cols),
        in_specs=[SM] + [VM] * 6,
        out_specs=VM,
        scratch_shapes=[pltpu.VMEM((2, rows, cols), jnp.float32)],
        compiler_params=PARAMS,
        cost_estimate=cost(10**6, 6 * 10**6),
        name="object_update",
    )(top, object_field, light, g_tile, g_up, g_left, g_diag)
    probe_new = pl.pallas_call(
        probe_kernel,
        out_shape=f32(*probe.shape),
        in_specs=[VM] * 2,
        out_specs=VM,
        compiler_params=PARAMS,
        cost_estimate=cost(10**6, 6 * 10**6),
        name="probe_update",
    )(probe, sums)
    return object_new, probe_new


def solution(mesh):
    in_specs = (
        P(None, "row", "col"),
        P(),
        P("row", "col", None, None, None),
        P("row", "col", None, None),
        P(),
    )
    out_specs = (P(None, "row", "col"), P())
    return jax.shard_map(body, mesh=mesh, in_specs=in_specs, out_specs=out_specs, check_vma=False)
```

time: 575 us -> 225 us (0.39)
  waiting for transfers between devices: 247 us -> 83.3 us
  matrix products: 104 us -> 0 us
  local copies, waits for them, and re-layouts: 81.4 us -> 6.59 us
  other arithmetic: 57.5 us -> 6.89 us
  starting transfers between devices: 6.5 us -> 35.6 us
  Pallas kernels: 0 us -> 25.3 us
  loops' own time: 25.3 us -> 0 us
  blocking collectives: 39.3 us -> 52.1 us
    psum x1, waiting for transfers between devices: 214 us -> 74.7 us  [body(): sums = lax.psum(sums, ('row', 'col'))]
    dot_general x80 -> x0, matrix products: 104 us -> none  [the longest x40 53.7 us: right_mul(): jnp.einsum('mab,bc->mac', values, table, preferred_element_type=jnp.float32)]
    dynamic_update_slice x5 -> x0, local copies, waits for them, and re-layouts: 46.4 us -> none  [add_block(): lax.dynamic_update_slice(accumulated, region + added, (zero_index, row_at...]
    add x20 -> x1, other arithmetic: 34 us -> 0.08 us  [body(): jnp.concatenate([spots, from_up, from_left, from_diag], axis=0)]
    ppermute x4 -> x9, starting transfers between devices: 6.46 us -> 35.5 us  [shifted(): return lax.ppermute(value, ('row', 'col'), pairs)]
    pallas_call x0 -> x4, Pallas kernels: none -> 25.3 us  [the longest x1 14 us: body(): pl.pallas_call(main_kernel, out_shape=(f32(2, rows, cols), f32(2, side, c...]
    another operation x1 -> x0, loops' own time: 25.3 us -> none  [body(): lax.fori_loop(zero_index, my_count, own_step, (accumulated, probe_grad, p...]
    ppermute x4 -> x9, waiting for transfers between devices: 33 us -> 8.68 us  [shifted(): return lax.ppermute(value, ('row', 'col'), pairs)]
  transfers between devices with their start and end apart: 5 -> 10, of which waited for: 4 -> 3; matrix products, arithmetic and copies ran while one was open for 1% -> 5% of each run, Pallas kernels for 0% -> 9%
where the time goes in v1:
time: 225 us; the launch traced here: 224 us
  waiting for transfers between devices  83.3 us (37%)
  blocking collectives  52.1 us (23%)
  starting transfers between devices  35.6 us (16%)
  Pallas kernels  25.3 us (11%)
  between operations  14.2 us (6%)
  other arithmetic  6.89 us (3%)
  local copies, waits for them, and re-layouts  6.59 us (3%)
    psum x1, waiting for transfers between devices, body(): sums = lax.psum(sums, ('row', 'col'))  74.7 us
    pmax x1, blocking collectives, body(): top = lax.pmax(top, ('row', 'col'))  52.1 us
    ppermute x9, starting transfers between devices, shifted(): return lax.ppermute(value, ('row', 'col'), pairs)  35.5 us
    pallas_call x1, Pallas kernels, body(): pl.pallas_call(main_kernel, out_shape=(f32(2, rows, cols), f32(2, side, c...  14 us
    ppermute x9, waiting for transfers between devices, shifted(): return lax.ppermute(value, ('row', 'col'), pairs)  8.68 us
    and x4, other arithmetic, live(): return (jnp.arange(slots) < number) & inside  4.99 us
  transfers between devices with their start and end apart: 10, of which 3 were waited for; matrix products, arithmetic and copies ran while one was open for 5% of the time, Pallas kernels for 9%

profile of v1, /device:TPU:0, one launch (start us, length us, event | category | flops | bytes accessed | tf_op | source)
XLA Modules:
  0.0 224.1 jit_solution(10292758003359232035)
XLA Ops:
  7.2 0.0 all-reduce.2.cloned.1.call-start
  7.2 1.3 collective-permute-start.3
  8.5 3.0 %collective-permute-start = (s32[6,2]{0,1:T(2,128)}, s32[6,2]{0,1:T(2,128)S(1)}, u32[]{:S(2)}, u32[]{:S(2)}) collective-permute-start(s32[6,2]{0,1:T(2,128)} %bitcast.16), channel_id=1, source_target_pairs={{0,4},{1,5},{2,6},{3,7},{4,8},{5,9},{6,10},{7,11},{8,12},{9,13},{1... | collective-permute-start | bytes 152 | tf_op jit(solution)/shard_map/ppermute | solution.py:24
  11.6 4.9 %collective-permute-start.1 = (s32[6,2]{0,1:T(2,128)}, s32[6,2]{0,1:T(2,128)S(1)}, u32[]{:S(2)}, u32[]{:S(2)}) collective-permute-start(s32[6,2]{0,1:T(2,128)} %bitcast.17), channel_id=1, source_target_pairs={{0,1},{1,2},{2,3},{4,5},{5,6},{6,7},{8,9},{9,10},{10,11},{12,13},{... | collective-permute-start | bytes 152 | tf_op jit(solution)/shard_map/ppermute | solution.py:24
  16.5 1.1 slice.12
  17.6 1.3 collective-permute-start.4
  18.9 1.3 collective-permute-start.5
  20.2 0.8 copy.19
  21.0 1.5 fusion.5
  22.5 1.3 compare_and_fusion.2
  23.8 1.3 compare_and_fusion.6
  25.0 0.1 pad_add_fusion
  25.1 1.2 compare_and_fusion
  26.3 1.2 compare_and_fusion.4
  27.6 0.6 broadcast_subtract_fusion.local_ref
  28.2 6.1 %collective-permute-done.4.right_ref = f32[2,256,256]{2,1,0:T(8,128)S(1)} collective-permute-done((f32[2,256,256]{2,1,0:T(8,128)S(1)}, f32[2,256,256]{2,1,0:T(8,128)S(1)}, u32[]{:S(2)}, u32[]{:S(2)}) %collective-permute-start.4) | collective-permute-done | bytes 524320 | tf_op jit(solution)/shard_map/ppermute | solution.py:24
  34.3 2.9 %collective-permute-start.2 = (s32[6,2]{0,1:T(2,128)}, s32[6,2]{0,1:T(2,128)S(1)}, u32[]{:S(2)}, u32[]{:S(2)}) collective-permute-start(s32[6,2]{0,1:T(2,128)} %bitcast.19), channel_id=1, source_target_pairs={{0,5},{1,6},{2,7},{4,9},{5,10},{6,11},{8,13},{9,14},{10,15},{12,17... | collective-permute-start | bytes 152 | tf_op jit(solution)/shard_map/ppermute | solution.py:24
  37.2 2.6 %collective-permute-done.5.corner_ref = f32[2,256,256]{2,1,0:T(8,128)S(1)} collective-permute-done((f32[2,256,256]{2,1,0:T(8,128)S(1)}, f32[2,256,256]{2,1,0:T(8,128)S(1)}, u32[]{:S(2)}, u32[]{:S(2)}) %collective-permute-start.5) | collective-permute-done | bytes 524320 | tf_op jit(solution)/shard_map/ppermute | solution.py:24
  39.7 0.0 collective-permute-done.3.below_ref
  39.8 0.8 copy-done.6
  40.5 0.3 copy-done.4
  40.9 14.0 %positions.1 = (f32[2,256,512]{2,1,0:T(8,128)}, f32[2,256,512]{2,1,0:T(8,128)}, f32[2,256,256]{2,1,0:T(8,128)}, f32[2,256,256]{2,1,0:T(8,128)}, f32[9,256,256]{2,1,0:T(8,128)}) custom-call(s32[1]{0:T(128)} %bitcast.10.count_ref, s32[6,2]{1,0:T(8,128)} %broadcast_subtract_fusion.local_ref, f32[2,256,512]{2,1,0:T(8,128)} %tile_ref.3, ...), custom_call_target="tpu_custom_call" | custom-call | flops 12999999488 | bytes 20000000 | tf_op jit(solution)/shard_map/positions/pallas_call | solution.py:244
  54.9 18.1 %collective-permute-start.6 = (f32[2,256,512]{2,1,0:T(8,128)}, f32[2,256,512]{2,1,0:T(8,128)S(1)}, u32[]{:S(2)}, u32[]{:S(2)}) collective-permute-start(f32[2,256,512]{2,1,0:T(8,128)} %get-tuple-element.12), channel_id=1, source_target_pairs={{0,4},{1,5},{2,6},{3,7},{4,8},{5,9},{6,10},{7,11},{8,12},{9,13},{1... | collective-permute-start | bytes 3145736 | tf_op jit(solution)/shard_map/ppermute | solution.py:24
  73.0 0.0 all-reduce.2.cloned.1.call-update
  73.0 0.0 collective-permute-done
  73.1 0.0 collective-permute-done.1
  73.1 0.0 collective-permute-done.2
  73.1 0.1 fusion.3
  73.2 0.1 fusion.2
  73.2 0.1 copy.17
  73.4 0.1 add_reduce_fusion
  73.5 1.3 collective-permute-start.7
  74.8 1.3 collective-permute-start.8
  76.2 0.1 broadcast_select_fusion
  76.3 0.1 select_reduce_fusion
  76.4 0.7 copy.18.where_ref
  77.1 0.7 convert_reduce_fusion
  77.8 3.8 %lighting.1 = (f32[256,512]{1,0:T(8,128)}, f32[8,128]{1,0:T(8,128)}) custom-call(s32[1]{0:T(128)} %bitcast.9.total_ref, s32[24,2]{1,0:T(8,128)} %copy.18.where_ref, f32[2,4,256,256]{3,2,1,0:T(8,128)} %probe_ref.5), custom_call_target="tpu_custom_call" | custom-call | flops 100000000 | bytes 10000000 | tf_op jit(solution)/shard_map/lighting/pallas_call | solution.py:228
  81.5 52.1 %pmax.7.top_ref = f32[8,128]{1,0:T(8,128)} all-reduce(f32[8,128]{1,0:T(8,128)} %get-tuple-element.9), channel_id=1, replica_groups=mesh['row'=8,'col'=4] {'row','col'}, use_global_device_ids=true, to_apply=%region_3.4 | all-reduce | flops 1024 | bytes 8192 | tf_op jit(solution)/shard_map/pmax | solution.py:241
  133.6 0.0 collective-permute-done.7.g_left
  133.6 0.0 collective-permute-done.8.g_diag
  133.6 0.0 collective-permute-done.6.g_up
  133.7 0.8 copy-done.1
  134.4 0.2 copy-done.2
  134.6 0.3 copy-done
  134.9 3.5 %object_update.1 = f32[2,256,512]{2,1,0:T(8,128)} custom-call(f32[8,128]{1,0:T(8,128)} %pmax.7.top_ref, f32[2,256,512]{2,1,0:T(8,128)} %tile_ref.3, f32[256,512]{1,0:T(8,128)} %get-tuple-element.10.light_ref, f32[2,256,512]{2,1,0:T(8,128)} %get-tuple-element.11.g_tile, f32[2,256,512]{2,1,0:T(8,128)} %copy-done, f32[2,256,256]{2,1,0:T(8,128)} %copy-done.1, ...), custom_call_target="tpu_custom_call" | custom-call | flops 1000000 | bytes 6000000 | tf_op jit(solution)/shard_map/object_update/pallas_call | solution.py:268
  138.5 74.7 %all-reduce.2.cloned.1.call-done.sums_ref = f32[9,256,256]{2,1,0:T(8,128)} async-done(((f32[9,256,256]{2,1,0:T(8,128)}), f32[9,256,256]{2,1,0:T(8,128)}) %all-reduce.2.cloned.1.call-update) | async-done | bytes 2359312 | tf_op jit(solution)/shard_map/psum | solution.py:267
  213.1 4.1 %probe_update.1 = f32[2,4,256,256]{3,2,1,0:T(8,128)} custom-call(f32[2,4,256,256]{3,2,1,0:T(8,128)} %probe_ref.5, f32[9,256,256]{2,1,0:T(8,128)} %all-reduce.2.cloned.1.call-done.sums_ref), custom_call_target="tpu_custom_call" | custom-call | flops 1000000 | bytes 6000000 | tf_op jit(solution)/shard_map/probe_update/pallas_call | solution.py:278
  (15 shorter events, 0.1 us)
Async XLA Ops:
  7.2 206.0 %all-reduce.2.cloned.1.call-start = ((), (), s32[]{:S(2)}) async-start(), calls=%async_computation | async-start | bytes 4718592 | tf_op jit(solution)/shard_map/psum | solution.py:267
  7.2 32.5 %collective-permute-start.3 = (f32[2,256,512]{2,1,0:T(8,128)}, f32[2,256,512]{2,1,0:T(8,128)S(1)}, u32[]{:S(2)}, u32[]{:S(2)}) collective-permute-start(f32[2,256,512]{2,1,0:T(8,128)} %tile_ref.3), channel_id=1, source_target_pairs={{4,0},{5,1},{6,2},{7,3},{8,4},{9,5},{10,6},{11,7},{12,8},{13,9},{1... | collective-permute-start | bytes 3145736 | tf_op jit(solution)/shard_map/ppermute | solution.py:24
  8.5 64.5 %collective-permute-start = (s32[6,2]{0,1:T(2,128)}, s32[6,2]{0,1:T(2,128)S(1)}, u32[]{:S(2)}, u32[]{:S(2)}) collective-permute-start(s32[6,2]{0,1:T(2,128)} %bitcast.16), channel_id=1, source_target_pairs={{0,4},{1,5},{2,6},{3,7},{4,8},{5,9},{6,10},{7,11},{8,12},{9,13},{1... | collective-permute-start | bytes 152 | tf_op jit(solution)/shard_map/ppermute | solution.py:24
  11.6 61.5 %collective-permute-start.1 = (s32[6,2]{0,1:T(2,128)}, s32[6,2]{0,1:T(2,128)S(1)}, u32[]{:S(2)}, u32[]{:S(2)}) collective-permute-start(s32[6,2]{0,1:T(2,128)} %bitcast.17), channel_id=1, source_target_pairs={{0,1},{1,2},{2,3},{4,5},{5,6},{6,7},{8,9},{9,10},{10,11},{12,13},{... | collective-permute-start | bytes 152 | tf_op jit(solution)/shard_map/ppermute | solution.py:24
  17.6 16.7 %collective-permute-start.4 = (f32[2,256,256]{2,1,0:T(8,128)S(1)}, f32[2,256,256]{2,1,0:T(8,128)S(1)}, u32[]{:S(2)}, u32[]{:S(2)}) collective-permute-start(f32[2,256,256]{2,1,0:T(8,128)S(1)} %slice.12), channel_id=1, source_target_pairs={{1,0},{2,1},{3,2},{5,4},{6,5},{7,6},{9,8},{10,9},{11,10},{13,12},{... | collective-permute-start | bytes 1572872 | tf_op jit(solution)/shard_map/ppermute | solution.py:24
  18.9 20.9 %collective-permute-start.5 = (f32[2,256,256]{2,1,0:T(8,128)S(1)}, f32[2,256,256]{2,1,0:T(8,128)S(1)}, u32[]{:S(2)}, u32[]{:S(2)}) collective-permute-start(f32[2,256,256]{2,1,0:T(8,128)S(1)} %slice.12), channel_id=1, source_target_pairs={{5,0},{6,1},{7,2},{9,4},{10,5},{11,6},{13,8},{14,9},{15,10},{17,12... | collective-permute-start | bytes 1572872 | tf_op jit(solution)/shard_map/ppermute | solution.py:24
  34.3 5.5 %copy-start.5 = (f32[2,256,256]{2,1,0:T(8,128)}, f32[2,256,256]{2,1,0:T(8,128)S(1)}, u32[]{:S(2)}) copy-start(f32[2,256,256]{2,1,0:T(8,128)S(1)} %collective-permute-done.4.right_ref) | copy-start | bytes 1572868
  34.3 38.8 %collective-permute-start.2 = (s32[6,2]{0,1:T(2,128)}, s32[6,2]{0,1:T(2,128)S(1)}, u32[]{:S(2)}, u32[]{:S(2)}) collective-permute-start(s32[6,2]{0,1:T(2,128)} %bitcast.19), channel_id=1, source_target_pairs={{0,5},{1,6},{2,7},{4,9},{5,10},{6,11},{8,13},{9,14},{10,15},{12,17... | collective-permute-start | bytes 152 | tf_op jit(solution)/shard_map/ppermute | solution.py:24
  39.7 0.8 copy-start.6
  39.7 1.1 copy-start.4
  54.8 18.2 %copy-start.3 = (s32[1,1,6,2]{2,3,1,0:T(2,128)S(1)}, s32[1,1,6,2]{2,3,1,0:T(2,128)}, u32[]{:S(2)}) copy-start(s32[1,1,6,2]{2,3,1,0:T(2,128)} %param.12) | copy-start | bytes 148
  54.9 18.6 %copy-start.8 = (f32[2,256,256]{2,1,0:T(8,128)S(1)}, f32[2,256,256]{2,1,0:T(8,128)}, u32[]{:S(2)}) copy-start(f32[2,256,256]{2,1,0:T(8,128)} %get-tuple-element.13) | copy-start | bytes 1572868
  54.9 20.0 %copy-start.7 = (f32[2,256,256]{2,1,0:T(8,128)S(1)}, f32[2,256,256]{2,1,0:T(8,128)}, u32[]{:S(2)}) copy-start(f32[2,256,256]{2,1,0:T(8,128)} %get-tuple-element.14) | copy-start | bytes 1572868
  54.9 78.8 %collective-permute-start.6 = (f32[2,256,512]{2,1,0:T(8,128)}, f32[2,256,512]{2,1,0:T(8,128)S(1)}, u32[]{:S(2)}, u32[]{:S(2)}) collective-permute-start(f32[2,256,512]{2,1,0:T(8,128)} %get-tuple-element.12), channel_id=1, source_target_pairs={{0,4},{1,5},{2,6},{3,7},{4,8},{5,9},{6,10},{7,11},{8,12},{9,13},{1... | collective-permute-start | bytes 3145736 | tf_op jit(solution)/shard_map/ppermute | solution.py:24
  73.5 60.1 %collective-permute-start.7 = (f32[2,256,256]{2,1,0:T(8,128)S(1)}, f32[2,256,256]{2,1,0:T(8,128)S(1)}, u32[]{:S(2)}, u32[]{:S(2)}) collective-permute-start(f32[2,256,256]{2,1,0:T(8,128)S(1)} %copy-done.8), channel_id=1, source_target_pairs={{0,1},{1,2},{2,3},{4,5},{5,6},{6,7},{8,9},{9,10},{10,11},{12,13},{... | collective-permute-start | bytes 1572872 | tf_op jit(solution)/shard_map/ppermute | solution.py:24
  74.8 58.8 %collective-permute-start.8 = (f32[2,256,256]{2,1,0:T(8,128)S(1)}, f32[2,256,256]{2,1,0:T(8,128)S(1)}, u32[]{:S(2)}, u32[]{:S(2)}) collective-permute-start(f32[2,256,256]{2,1,0:T(8,128)S(1)} %copy-done.7), channel_id=1, source_target_pairs={{0,5},{1,6},{2,7},{4,9},{5,10},{6,11},{8,13},{9,14},{10,15},{12,17... | collective-permute-start | bytes 1572872 | tf_op jit(solution)/shard_map/ppermute | solution.py:24
  133.6 0.8 copy-start.1
  133.6 1.0 copy-start.2
  133.6 1.3 copy-start
Sparse Core Ops, SparseCore 0:
  73.2 139.9 all-reduce.1

commit v2 on v1

--- a/solution.py
+++ b/solution.py
@@ -21,6 +21,12 @@
         for c in range(cols):
             if 0 <= r + d_row < rows and 0 <= c + d_col < cols:
                 pairs.append((r * cols + c, (r + d_row) * cols + c + d_col))
+    return lax.ppermute(value, ("row", "col"), pairs)
+
+
+def swapped(value, flip_row, flip_col):
+    rows, cols = lax.axis_size("row"), lax.axis_size("col")
+    pairs = [(r * cols + c, (r ^ flip_row) * cols + (c ^ flip_col)) for r in range(rows) for c in range(cols)]
     return lax.ppermute(value, ("row", "col"), pairs)
 
 
@@ -82,18 +88,20 @@
 
 
 def main_kernel(
-    count_ref, local_ref, tile_ref, below_ref, right_ref, corner_ref, amp_ref, probe_ref, lf_ref, rf_ref, lg_ref, rg_ref,
-    g_tile, g_below, g_right, g_corner, pgrad_ref,
-    ext, gacc, stage, turned, wave,
+    counts_ref, spots_ref, tile_ref, below_ref, right_ref, corner_ref, amp_ref, probe_ref, top_ref,
+    lf_ref, rf_ref, lg_ref, rg_ref,
+    g_tile, g_below, g_right, g_corner, mine_ref, other_ref,
+    ext, gacc, stage, turned, wave, wins, sums,
 ):
     modes, side = probe_ref.shape[1], probe_ref.shape[2]
     rows, cols = tile_ref.shape[1], tile_ref.shape[2]
+    my_row, my_col = lax.axis_index("row"), lax.axis_index("col")
     ext[:, :rows, :cols] = tile_ref[...]
     ext[:, rows:, :cols] = below_ref[...]
     ext[:, :rows, cols:] = right_ref[...]
     ext[:, rows:, cols:] = corner_ref[...]
     gacc[...] = jnp.zeros_like(gacc)
-    pgrad_ref[...] = jnp.zeros_like(pgrad_ref)
+    sums[...] = jnp.zeros_like(sums)
 
     def dot(a, b):
         return jnp.dot(a, b, preferred_element_type=jnp.float32)
@@ -105,64 +113,146 @@
             turned[k * side:(k + 1) * side, side:] = got[side:].astype(jnp.bfloat16)
         wave[...] = dot(turned[...], right_ref[...])
 
+    def plane(index):
+        return slice(index * side, (index + 1) * side)
+
     def step(p, carry):
-        row, col = local_ref[p, 0], local_ref[p, 1]
+        row, col = spots_ref[p, 0] - my_row * rows, spots_ref[p, 1] - my_col * cols
         win_re = window_at(ext, 0, row, col, side)
         win_im = window_at(ext, 1, row, col, side)
+        wins[0], wins[1] = win_re, win_im
+        sums[plane(2 * modes)] += win_re * win_re + win_im * win_im
         for k in range(modes):
             pr, pi = probe_ref[0, k], probe_ref[1, k]
-            stage[:side, k * side:(k + 1) * side] = (pr * win_re - pi * win_im).astype(jnp.bfloat16)
-            stage[side:, k * side:(k + 1) * side] = (pr * win_im + pi * win_re).astype(jnp.bfloat16)
+            stage[:side, plane(k)] = (pr * win_re - pi * win_im).astype(jnp.bfloat16)
+            stage[side:, plane(k)] = (pr * win_im + pi * win_re).astype(jnp.bfloat16)
         transform(lf_ref, rf_ref)
         model = jnp.zeros((side, side), jnp.float32)
         for k in range(modes):
-            wr, wi = wave[k * side:(k + 1) * side, :side], wave[k * side:(k + 1) * side, side:]
+            wr, wi = wave[plane(k), :side], wave[plane(k), side:]
             model += wr * wr + wi * wi
         factor = amp_ref[p] * lax.rsqrt(jnp.maximum(model, 1.0)) - 1.0
         for k in range(modes):
-            wr, wi = wave[k * side:(k + 1) * side, :side], wave[k * side:(k + 1) * side, side:]
-            stage[:side, k * side:(k + 1) * side] = (wr * factor).astype(jnp.bfloat16)
-            stage[side:, k * side:(k + 1) * side] = (wi * factor).astype(jnp.bfloat16)
+            wr, wi = wave[plane(k), :side], wave[plane(k), side:]
+            stage[:side, plane(k)] = (wr * factor).astype(jnp.bfloat16)
+            stage[side:, plane(k)] = (wi * factor).astype(jnp.bfloat16)
         transform(lg_ref, rg_ref)
         grad_re = jnp.zeros((side, side), jnp.float32)
         grad_im = jnp.zeros((side, side), jnp.float32)
-        win_re = window_at(ext, 0, row, col, side)
-        win_im = window_at(ext, 1, row, col, side)
-        for k in range(modes):
-            cr, ci = wave[k * side:(k + 1) * side, :side], wave[k * side:(k + 1) * side, side:]
+        for k in range(modes):
+            cr, ci = wave[plane(k), :side], wave[plane(k), side:]
             pr, pi = probe_ref[0, k], probe_ref[1, k]
             grad_re += pr * cr + pi * ci
             grad_im += pr * ci - pi * cr
-            pgrad_ref[k] += win_re * cr + win_im * ci
-            pgrad_ref[modes + k] += win_re * ci - win_im * cr
-        pgrad_ref[2 * modes] += win_re * win_re + win_im * win_im
+            sums[plane(k)] += wins[0] * cr + wins[1] * ci
+            sums[plane(modes + k)] += wins[0] * ci - wins[1] * cr
         add_at(gacc, 0, row, col, grad_re, side)
         add_at(gacc, 1, row, col, grad_im, side)
         return carry
 
-    lax.fori_loop(0, count_ref[0], step, 0)
+    lax.fori_loop(0, counts_ref[my_row, my_col], step, 0)
     g_tile[...] = gacc[:, :rows, :cols]
     g_below[...] = gacc[:, rows:, :cols]
     g_right[...] = gacc[:, :rows, cols:]
     g_corner[...] = gacc[:, rows:, cols:]
-
-
-def light_kernel(total_ref, where_ref, probe_ref, light_ref, top_ref, lit, acc):
+    half = mine_ref.shape[0]
+    core = lax.rem(my_row, 2)
+    mine_ref[...] = sums[pl.ds(pl.multiple_of(core * half, SUBLANES), half)]
+    other_ref[:half] = sums[pl.ds(pl.multiple_of((1 - core) * half, SUBLANES), half)]
+    other_ref[half:] = top_ref[...]
+
+
+def light_kernel(counts_ref, spots_ref, up_ref, left_ref, diag_ref, probe_ref, light_ref, top_ref, lit, acc):
     side = probe_ref.shape[2]
     rows, cols = light_ref.shape
-    lit[0] = jnp.sum(probe_ref[0] * probe_ref[0] + probe_ref[1] * probe_ref[1], axis=0)
+    my_row, my_col = lax.axis_index("row"), lax.axis_index("col")
+    lit[...] = jnp.sum(probe_ref[0] * probe_ref[0] + probe_ref[1] * probe_ref[1], axis=0)
     acc[...] = jnp.zeros_like(acc)
-
-    def step(p, carry):
-        add_at(acc, 0, where_ref[p, 0], where_ref[p, 1], lit[0], side)
-        return carry
-
-    lax.fori_loop(0, total_ref[0], step, 0)
+    for ref, d_row, d_col in ((spots_ref, 0, 0), (up_ref, 1, 0), (left_ref, 0, 1), (diag_ref, 1, 1)):
+        inside = (my_row >= d_row) & (my_col >= d_col)
+        number = counts_ref[jnp.maximum(my_row - d_row, 0), jnp.maximum(my_col - d_col, 0)]
+
+        def step(p, carry, ref=ref):
+            row, col = ref[p, 0] - my_row * rows + side, ref[p, 1] - my_col * cols + side
+
+            @pl.when((row > 0) & (col > 0))
+            def _():
+                add_at(acc, 0, row, col, lit[...], side)
+
+            return carry
+
+        lax.fori_loop(0, jnp.where(inside, number, 0), step, 0)
     light = acc[0, side:side + rows, side:side + cols]
     light_ref[...] = light
     top = jnp.max(light, axis=0, keepdims=True)
     top = jnp.max(top, axis=1, keepdims=True)
     top_ref[...] = jnp.broadcast_to(top, top_ref.shape)
+
+
+def fold_kernel(group, rank_of, *refs):
+    received, rest = refs[2:2 + group[0] - 1], refs[2 + group[0] - 1:]
+    own_ref, top_ref = refs[:2]
+    parts = group[1]
+    out_own, out_top, out_other, total = rest[0], rest[1], rest[2:2 + parts - 1], rest[-1]
+    rows = own_ref.shape[0]
+    value, top = own_ref[...], top_ref[...]
+    for ref in received:
+        value += ref[:rows]
+        top = jnp.maximum(top, ref[rows:])
+    out_top[...] = top
+    if parts == 1:
+        out_own[...] = value
+        return
+    total[...] = value
+    rank, share = rank_of(), rows // parts
+    out_own[...] = total[pl.ds(pl.multiple_of(rank * share, SUBLANES), share)]
+    for d, ref in enumerate(out_other, 1):
+        ref[:share] = total[pl.ds(pl.multiple_of((rank ^ d) * share, SUBLANES), share)]
+        ref[share:] = top
+
+
+def fold(own, top, received, parts, rank_of, name):
+    rows, width = own.shape
+    share = rows // parts
+    got = pl.pallas_call(
+        functools.partial(fold_kernel, (len(received) + 1, parts), rank_of),
+        out_shape=(f32(share, width), f32(*top.shape)) + (f32(share + SUBLANES, width),) * (parts - 1),
+        in_specs=[VM] * (2 + len(received)),
+        out_specs=(VM,) * (parts + 1),
+        scratch_shapes=[pltpu.VMEM((rows, width), jnp.float32)],
+        compiler_params=PARAMS,
+        cost_estimate=cost(10**6, 4 * rows * width * (len(received) + 2)),
+        name=name,
+    )(own, top, *received)
+    return got[0], got[1], got[2:]
+
+
+def unfold_kernel(rank_of, *refs):
+    out_ref = refs[-1]
+    share, rank = refs[0].shape[0], rank_of()
+    for d, ref in enumerate(refs[:-1]):
+        out_ref[pl.ds(pl.multiple_of((rank ^ d) * share, SUBLANES), share)] = ref[...]
+
+
+def unfold(parts, rank_of, name):
+    share, width = parts[0].shape
+    return pl.pallas_call(
+        functools.partial(unfold_kernel, rank_of),
+        out_shape=f32(share * len(parts), width),
+        in_specs=[VM] * len(parts),
+        out_specs=VM,
+        compiler_params=PARAMS,
+        cost_estimate=cost(10**6, 8 * share * width * len(parts)),
+        name=name,
+    )(*parts)
+
+
+def pair_rank():
+    return lax.axis_index("row") // 2
+
+
+def col_rank():
+    return lax.axis_index("col")
 
 
 def finish_kernel(top_ref, tile_ref, light_ref, g_tile, g_up, g_left, g_diag, out_ref, total):
@@ -174,14 +264,18 @@
     out_ref[1] = tile_ref[1] + total[1] * scale
 
 
-def probe_kernel(probe_ref, sums_ref, out_ref):
-    modes = probe_ref.shape[1]
-    den = sums_ref[2 * modes]
+def probe_kernel(probe_ref, mine_ref, other_ref, out_ref, sums):
+    modes, side = probe_ref.shape[1], probe_ref.shape[2]
+    half = mine_ref.shape[0]
+    core = lax.rem(lax.axis_index("row"), 2)
+    sums[pl.ds(pl.multiple_of(core * half, SUBLANES), half)] = mine_ref[...]
+    sums[pl.ds(pl.multiple_of((1 - core) * half, SUBLANES), half)] = other_ref[...]
+    den = sums[2 * modes * side:(2 * modes + 1) * side]
     top = jnp.max(jnp.max(den, axis=0, keepdims=True), axis=1, keepdims=True)
     scale = 1.0 / (den + 0.1 * top)
     for k in range(modes):
-        out_ref[0, k] = probe_ref[0, k] + sums_ref[k] * scale
-        out_ref[1, k] = probe_ref[1, k] + sums_ref[modes + k] * scale
+        out_ref[0, k] = probe_ref[0, k] + sums[k * side:(k + 1) * side] * scale
+        out_ref[1, k] = probe_ref[1, k] + sums[(modes + k) * side:(modes + k + 1) * side] * scale
 
 
 def f32(*shape):
@@ -200,11 +294,11 @@
 def body(object_field, probe, amplitudes, corners, counts):
     rows, cols = object_field.shape[1], object_field.shape[2]
     modes, side = probe.shape[1], probe.shape[2]
-    slots = amplitudes.shape[2]
-    my_row, my_col = lax.axis_index("row"), lax.axis_index("col")
-    anchor = jnp.stack([my_row * rows, my_col * cols])
+    pairs, n_col = lax.axis_size("row") // 2, lax.axis_size("col")
+    step = SUBLANES * 2 * pairs * n_col
+    total_rows = -(-(2 * modes + 1) * side // step) * step
+    half = total_rows // 2
     spots = corners[0, 0]
-    local = spots - anchor[None, :]
 
     from_up = shifted(spots, 1, 0)
     from_left = shifted(spots, 0, 1)
@@ -213,58 +307,55 @@
     right = shifted(object_field[:, :, :side], 0, -1)
     corner = shifted(object_field[:, :side, :side], -1, -1)
 
-    def live(d_row, d_col):
-        inside = (my_row >= d_row) & (my_col >= d_col)
-        number = counts[jnp.maximum(my_row - d_row, 0), jnp.maximum(my_col - d_col, 0)]
-        return (jnp.arange(slots) < number) & inside
-
-    where = jnp.concatenate([spots, from_up, from_left, from_diag], axis=0) - anchor[None, :] + side
-    flags = jnp.concatenate([live(0, 0), live(1, 0), live(0, 1), live(1, 1)])
-    flags = flags & (where[:, 0] > 0) & (where[:, 1] > 0)
-    order = jnp.where(flags, jnp.cumsum(flags) - 1, 4 * slots)
-    picked = jnp.arange(4 * slots)[:, None] == order[None, :]
-    where = jnp.sum(jnp.where(picked[:, :, None], where[None, :, :], 0), axis=1).astype(jnp.int32)
-    total = jnp.sum(flags).astype(jnp.int32).reshape(1)
     light, top = pl.pallas_call(
         light_kernel,
-        out_shape=(f32(rows, cols), f32(8, LANES)),
-        in_specs=[SM, SM, VM],
+        out_shape=(f32(rows, cols), f32(SUBLANES, side)),
+        in_specs=[SM] * 5 + [VM],
         out_specs=(VM, VM),
         scratch_shapes=[
-            pltpu.VMEM((1, side, side), jnp.float32),
+            pltpu.VMEM((side, side), jnp.float32),
             pltpu.VMEM((1, rows + 2 * side, cols + 2 * side), jnp.float32),
         ],
         compiler_params=PARAMS,
         cost_estimate=cost(10**8, 10**7),
         name="lighting",
-    )(total, where, probe)
-    top = lax.pmax(top, ("row", "col"))
-
-    count = counts[my_row, my_col].reshape(1)
-    g_tile, g_below, g_right, g_corner, sums = pl.pallas_call(
+    )(counts, spots, from_up, from_left, from_diag, probe)
+
+    g_tile, g_below, g_right, g_corner, mine, other = pl.pallas_call(
         main_kernel,
         out_shape=(
             f32(2, rows, cols), f32(2, side, cols), f32(2, rows, side), f32(2, side, side),
-            f32(2 * modes + 1, side, side),
+            f32(half, side), f32(half + SUBLANES, side),
         ),
-        in_specs=[SM, SM] + [VM] * 10,
-        out_specs=(VM,) * 5,
+        in_specs=[SM] * 2 + [VM] * 11,
+        out_specs=(VM,) * 6,
         scratch_shapes=[
             pltpu.VMEM((2, rows + side, cols + side), jnp.float32),
             pltpu.VMEM((2, rows + side, cols + side), jnp.float32),
             pltpu.VMEM((2 * side, modes * side), jnp.bfloat16),
             pltpu.VMEM((modes * side, 2 * side), jnp.bfloat16),
             pltpu.VMEM((modes * side, 2 * side), jnp.float32),
+            pltpu.VMEM((2, side, side), jnp.float32),
+            pltpu.VMEM((total_rows, side), jnp.float32),
         ],
         compiler_params=PARAMS,
         cost_estimate=cost(13 * 10**9, 2 * 10**7),
         name="positions",
-    )(count, local, object_field, below, right, corner, amplitudes[0, 0], probe, *tables(side))
-
+    )(counts, spots, object_field, below, right, corner, amplitudes[0, 0], probe, top, *tables(side))
+
+    received = [swapped(other, 1, 0)]
     g_up = shifted(g_below, 1, 0)
     g_left = shifted(g_right, 0, 1)
     g_diag = shifted(g_corner, 1, 1)
-    sums = lax.psum(sums, ("row", "col"))
+    own, top, others = fold(mine, top, received, pairs, pair_rank, "fold_chip")
+    received = [swapped(value, 2 * d, 0) for d, value in enumerate(others, 1)]
+    own, top, others = fold(own, top, received, n_col, col_rank, "fold_plane")
+    received = [swapped(value, 0, d) for d, value in enumerate(others, 1)]
+    own, top, _ = fold(own, top, received, 1, None, "fold_all")
+    own = unfold([own] + [swapped(own, 0, d) for d in range(1, n_col)], col_rank, "unfold_col")
+    own = unfold([own] + [swapped(own, 2 * d, 0) for d in range(1, pairs)], pair_rank, "unfold_pairs")
+    other = swapped(own, 1, 0)
+
     object_new = pl.pallas_call(
         finish_kernel,
         out_shape=f32(2, rows, cols),
@@ -278,12 +369,13 @@
     probe_new = pl.pallas_call(
         probe_kernel,
         out_shape=f32(*probe.shape),
-        in_specs=[VM] * 2,
+        in_specs=[VM] * 3,
         out_specs=VM,
+        scratch_shapes=[pltpu.VMEM((total_rows, side), jnp.float32)],
         compiler_params=PARAMS,
         cost_estimate=cost(10**6, 6 * 10**6),
         name="probe_update",
-    )(probe, sums)
+    )(probe, own, other)
     return object_new, probe_new
 
 

time: 225 us -> 169 us (0.75)
  blocking collectives: 52.1 us -> 0 us
  starting transfers between devices: 35.6 us -> 63.5 us
  waiting for transfers between devices: 83.3 us -> 61.5 us
  between operations: 14.2 us -> 0.84 us
  other arithmetic: 6.89 us -> 0 us
  Pallas kernels: 25.3 us -> 31.4 us
  local copies, waits for them, and re-layouts: 6.59 us -> 12.4 us
    psum x1 -> x0, waiting for transfers between devices: 74.7 us -> none  [body(): sums = lax.psum(sums, ('row', 'col'))]
    pmax x1 -> x0, blocking collectives: 52.1 us -> none  [body(): top = lax.pmax(top, ('row', 'col'))]
    ppermute x0 -> x14, waiting for transfers between devices: none -> 40.4 us  [swapped(): return lax.ppermute(value, ('row', 'col'), pairs)]
    ppermute x0 -> x14, starting transfers between devices: none -> 39.4 us  [swapped(): return lax.ppermute(value, ('row', 'col'), pairs)]
    ppermute x9, waiting for transfers between devices: 8.68 us -> 21 us  [shifted(): return lax.ppermute(value, ('row', 'col'), pairs)]
    ppermute x9, starting transfers between devices: 35.5 us -> 24.1 us  [shifted(): return lax.ppermute(value, ('row', 'col'), pairs)]
    pallas_call x1 -> x6, Pallas kernels: 3.77 us -> 13.7 us  [the longest x3 6.55 us: fold(): pl.pallas_call(functools.partial(fold_kernel, (len(received) + 1, parts),...]
    unnamed x18 -> x55, local copies, waits for them, and re-layouts: 2.45 us -> 10.6 us
  transfers between devices with their start and end apart: 10 -> 23, of which waited for: 3 -> 12; matrix products, arithmetic and copies ran while one was open for 5% -> 2% of each run, Pallas kernels for 9% -> 4%
where the time goes in v2:
time: 169 us; the launch traced here: 170 us
  starting transfers between devices  63.5 us (38%)
  waiting for transfers between devices  61.5 us (36%)
  Pallas kernels  31.4 us (19%)
  local copies, waits for them, and re-layouts  12.4 us (7%)
    ppermute x14, waiting for transfers between devices, swapped(): return lax.ppermute(value, ('row', 'col'), pairs)  40.4 us
    ppermute x14, starting transfers between devices, swapped(): return lax.ppermute(value, ('row', 'col'), pairs)  39.4 us
    ppermute x9, starting transfers between devices, shifted(): return lax.ppermute(value, ('row', 'col'), pairs)  24.1 us
    ppermute x9, waiting for transfers between devices, shifted(): return lax.ppermute(value, ('row', 'col'), pairs)  21 us
    unnamed x55, local copies, waits for them, and re-layouts  10.6 us
    pallas_call x1, Pallas kernels, body(): pl.pallas_call(main_kernel, out_shape=(f32(2, rows, cols), f32(2, side, c...  9.99 us
    pallas_call x3, Pallas kernels, fold(): pl.pallas_call(functools.partial(fold_kernel, (len(received) + 1, parts),...  6.55 us
    pallas_call x1, Pallas kernels, body(): pl.pallas_call(probe_kernel, out_shape=f32(*probe.shape), in_specs=[VM] *...  4.2 us
  transfers between devices with their start and end apart: 23, of which 12 were waited for; matrix products, arithmetic and copies ran while one was open for 2% of the time, Pallas kernels for 4%

profile of v2, /device:TPU:0, one launch (start us, length us, event | category | flops | bytes accessed | tf_op | source)
XLA Modules:
  0.0 169.6 jit_solution(2440346899080313969)
XLA Ops:
  0.6 1.3 collective-permute-start
  1.9 1.1 slice.4
  3.0 1.3 collective-permute-start.2
  4.3 1.3 collective-permute-start.1
  5.6 0.8 copy.17.spots_ref
  6.4 6.9 %collective-permute-start.5 = (s32[6,2]{1,0:T(8,128)S(1)}, s32[6,2]{1,0:T(8,128)S(1)}, u32[]{:S(2)}, u32[]{:S(2)}) collective-permute-start(s32[6,2]{1,0:T(8,128)S(1)} %copy.17.spots_ref), channel_id=1, source_target_pairs={{0,5},{1,6},{2,7},{4,9},{5,10},{6,11},{8,13},{9,14},{10,15},{12,17... | collective-permute-start | bytes 152 | tf_op jit(solution)/shard_map/ppermute | solution.py:24
  13.3 3.6 %collective-permute-start.4 = (s32[6,2]{1,0:T(8,128)S(1)}, s32[6,2]{1,0:T(8,128)S(1)}, u32[]{:S(2)}, u32[]{:S(2)}) collective-permute-start(s32[6,2]{1,0:T(8,128)S(1)} %copy.17.spots_ref), channel_id=1, source_target_pairs={{0,1},{1,2},{2,3},{4,5},{5,6},{6,7},{8,9},{9,10},{10,11},{12,13},{... | collective-permute-start | bytes 152 | tf_op jit(solution)/shard_map/ppermute | solution.py:24
  16.9 1.3 copy.16.counts_ref
  18.3 2.9 %collective-permute-start.3 = (s32[6,2]{1,0:T(8,128)S(1)}, s32[6,2]{1,0:T(8,128)S(1)}, u32[]{:S(2)}, u32[]{:S(2)}) collective-permute-start(s32[6,2]{1,0:T(8,128)S(1)} %copy.17.spots_ref), channel_id=1, source_target_pairs={{0,4},{1,5},{2,6},{3,7},{4,8},{5,9},{6,10},{7,11},{8,12},{9,13},{1... | collective-permute-start | bytes 152 | tf_op jit(solution)/shard_map/ppermute | solution.py:24
  21.2 0.8 collective-permute-done.3.up_ref
  22.6 3.0 %lighting.1 = (f32[256,512]{1,0:T(8,128)}, f32[8,256]{1,0:T(8,128)}) custom-call(s32[8,4]{1,0:T(8,128)} %copy.16.counts_ref, s32[6,2]{1,0:T(8,128)} %copy-done.17, s32[6,2]{1,0:T(8,128)} %copy-done.20, s32[6,2]{1,0:T(8,128)} %copy-done.19, s32[6,2]{1,0:T(8,128)} %copy-done.18, f32[2,4,256,256]{3,2,1,0:T(8,128)} %probe_ref.5), custom_call_target="tpu_custom_call" | custom-call | flops 100000000 | bytes 10000000 | tf_op jit(solution)/shard_map/lighting/pallas_call | solution.py:310
  25.7 0.8 copy-done.25
  26.9 10.0 %positions.1 = (f32[2,256,512]{2,1,0:T(8,128)}, f32[2,256,512]{2,1,0:T(8,128)}, f32[2,256,256]{2,1,0:T(8,128)}, f32[2,256,256]{2,1,0:T(8,128)}, f32[1152,256]{1,0:T(8,128)}, /*index=5*/f32[1160,256]{1,0:T(8,128)}) custom-call(s32[8,4]{1,0:T(8,128)} %copy.16.counts_ref, s32[6,2]{1,0:T(8,128)} %copy-done.17, f32[2,256,512]{2,1,0:T(8,128)} %tile_ref.3, ...), custom_call_target="tpu_custom_call" | custom-call | flops 12999999488 | bytes 20000000 | tf_op jit(solution)/shard_map/positions/pallas_call | solution.py:324
  36.9 7.9 %collective-permute-start.6 = (f32[1160,256]{1,0:T(8,128)}, f32[1160,256]{1,0:T(8,128)S(1)}, u32[]{:S(2)}, u32[]{:S(2)}) collective-permute-start(f32[1160,256]{1,0:T(8,128)} %get-tuple-element.24), channel_id=1, source_target_pairs={{0,4},{1,5},{2,6},{3,7},{4,0},{5,1},{6,2},{7,3},{8,12},{9,13},{10,... | collective-permute-start | bytes 3563528 | tf_op jit(solution)/shard_map/ppermute | solution.py:30
  44.9 2.7 %collective-permute-done.6.refs_2_ = f32[1160,256]{1,0:T(8,128)S(1)} collective-permute-done((f32[1160,256]{1,0:T(8,128)}, f32[1160,256]{1,0:T(8,128)S(1)}, u32[]{:S(2)}, u32[]{:S(2)}) %collective-permute-start.6) | collective-permute-done | bytes 1187872 | tf_op jit(solution)/shard_map/ppermute | solution.py:30
  47.6 1.0 copy-done
  48.6 2.8 %fold_chip.1 = (f32[288,256]{1,0:T(8,128)}, f32[8,256]{1,0:T(8,128)}, f32[296,256]{1,0:T(8,128)}, f32[296,256]{1,0:T(8,128)}, f32[296,256]{1,0:T(8,128)}) custom-call(f32[1152,256]{1,0:T(8,128)} %get-tuple-element.23.refs_0_, f32[8,256]{1,0:T(8,128)} %get-tuple-element.22.top_ref.refs_1_, f32[1160,256]{1,0:T(8,128)} %copy-done), custom_call_target="tpu_custom_call" | custom-call | flops 1000000 | bytes 3538944 | tf_op jit(solution)/shard_map/fold_chip/pallas_call | solution.py:217
  51.4 10.8 %collective-permute-start.7 = (f32[296,256]{1,0:T(8,128)}, f32[296,256]{1,0:T(8,128)S(1)}, u32[]{:S(2)}, u32[]{:S(2)}) collective-permute-start(f32[296,256]{1,0:T(8,128)} %get-tuple-element.27), channel_id=1, source_target_pairs={{0,8},{1,9},{2,10},{3,11},{4,12},{5,13},{6,14},{7,15},{8,0},{9,1},... | collective-permute-start | bytes 909320 | tf_op jit(solution)/shard_map/ppermute | solution.py:30
  62.1 4.1 %collective-permute-start.8 = (f32[296,256]{1,0:T(8,128)}, f32[296,256]{1,0:T(8,128)S(1)}, u32[]{:S(2)}, u32[]{:S(2)}) collective-permute-start(f32[296,256]{1,0:T(8,128)} %get-tuple-element.28), channel_id=1, source_target_pairs={{0,16},{1,17},{2,18},{3,19},{4,20},{5,21},{6,22},{7,23},{8,24},{9,... | collective-permute-start | bytes 909320 | tf_op jit(solution)/shard_map/ppermute | solution.py:30
  66.3 4.0 %collective-permute-done.7.refs_2_ = f32[296,256]{1,0:T(8,128)S(1)} collective-permute-done((f32[296,256]{1,0:T(8,128)}, f32[296,256]{1,0:T(8,128)S(1)}, u32[]{:S(2)}, u32[]{:S(2)}) %collective-permute-start.7) | collective-permute-done | bytes 303136 | tf_op jit(solution)/shard_map/ppermute | solution.py:30
  70.3 10.1 %collective-permute-done.8.refs_3_ = f32[296,256]{1,0:T(8,128)S(1)} collective-permute-done((f32[296,256]{1,0:T(8,128)}, f32[296,256]{1,0:T(8,128)S(1)}, u32[]{:S(2)}, u32[]{:S(2)}) %collective-permute-start.8) | collective-permute-done | bytes 303136 | tf_op jit(solution)/shard_map/ppermute | solution.py:30
  81.2 2.1 %fold_plane.1 = (f32[72,256]{1,0:T(8,128)}, f32[8,256]{1,0:T(8,128)}, f32[80,256]{1,0:T(8,128)}, f32[80,256]{1,0:T(8,128)}, f32[80,256]{1,0:T(8,128)}) custom-call(f32[288,256]{1,0:T(8,128)} %get-tuple-element.25.refs_0_, f32[8,256]{1,0:T(8,128)} %get-tuple-element.26.refs_1_, f32[296,256]{1,0:T(8,128)} %copy-done.5, f32[296,256]{1,0:T(8,128)} %copy-done.6, ...), custom_call_target="tpu_custom_call" | custom-call | flops 1000000 | bytes 1474560 | tf_op jit(solution)/shard_map/fold_plane/pallas_call | solution.py:217
  83.3 6.3 %collective-permute-start.10 = (f32[80,256]{1,0:T(8,128)}, f32[80,256]{1,0:T(8,128)S(1)}, u32[]{:S(2)}, u32[]{:S(2)}) collective-permute-start(f32[80,256]{1,0:T(8,128)} %get-tuple-element.32), channel_id=1, source_target_pairs={{0,1},{1,0},{2,3},{3,2},{4,5},{5,4},{6,7},{7,6},{8,9},{9,8},{10,11... | collective-permute-start | bytes 245768 | tf_op jit(solution)/shard_map/ppermute | solution.py:30
  89.6 2.3 %collective-permute-start.12 = (f32[80,256]{1,0:T(8,128)}, f32[80,256]{1,0:T(8,128)S(1)}, u32[]{:S(2)}, u32[]{:S(2)}) collective-permute-start(f32[80,256]{1,0:T(8,128)} %get-tuple-element.34), channel_id=1, source_target_pairs={{0,3},{1,2},{2,1},{3,0},{4,7},{5,6},{6,5},{7,4},{8,11},{9,10},{10,... | collective-permute-start | bytes 245768 | tf_op jit(solution)/shard_map/ppermute | solution.py:30
  92.5 5.1 %collective-permute-done.11.refs_3_ = f32[80,256]{1,0:T(8,128)S(1)} collective-permute-done((f32[80,256]{1,0:T(8,128)}, f32[80,256]{1,0:T(8,128)S(1)}, u32[]{:S(2)}, u32[]{:S(2)}) %collective-permute-start.11) | collective-permute-done | bytes 81952 | tf_op jit(solution)/shard_map/ppermute | solution.py:30
  98.2 1.7 fold_all.1
  99.9 1.2 collective-permute-start.18
  101.1 2.3 %collective-permute-start.17 = (f32[72,256]{1,0:T(8,128)}, f32[72,256]{1,0:T(8,128)S(1)}, u32[]{:S(2)}, u32[]{:S(2)}) collective-permute-start(f32[72,256]{1,0:T(8,128)} %get-tuple-element.41.refs_0_), channel_id=1, source_target_pairs={{0,2},{1,3},{2,0},{3,1},{4,6},{5,7},{6,4},{7,5},{8,10},{9,11},{10,... | collective-permute-start | bytes 221192 | tf_op jit(solution)/shard_map/ppermute | solution.py:30
  103.4 0.9 collective-permute-start.16
  104.3 2.7 %collective-permute-done.18.refs_3_ = f32[72,256]{1,0:T(8,128)S(1)} collective-permute-done((f32[72,256]{1,0:T(8,128)}, f32[72,256]{1,0:T(8,128)S(1)}, u32[]{:S(2)}, u32[]{:S(2)}) %collective-permute-start.18) | collective-permute-done | bytes 73760 | tf_op jit(solution)/shard_map/ppermute | solution.py:30
  107.0 3.3 %collective-permute-done.17.refs_2_ = f32[72,256]{1,0:T(8,128)S(1)} collective-permute-done((f32[72,256]{1,0:T(8,128)}, f32[72,256]{1,0:T(8,128)S(1)}, u32[]{:S(2)}, u32[]{:S(2)}) %collective-permute-start.17) | collective-permute-done | bytes 73760 | tf_op jit(solution)/shard_map/ppermute | solution.py:30
  111.5 1.7 %unfold_col.1.refs_0_ = f32[288,256]{1,0:T(8,128)} custom-call(f32[72,256]{1,0:T(8,128)} %get-tuple-element.41.refs_0_, f32[72,256]{1,0:T(8,128)} %copy-done.16, f32[72,256]{1,0:T(8,128)} %copy-done.15, f32[72,256]{1,0:T(8,128)} %copy-done.14), custom_call_target="tpu_custom_call" | custom-call | flops 1000000 | bytes 589824 | tf_op jit(solution)/shard_map/unfold_col/pallas_call | solution.py:239
  113.3 2.0 %collective-permute-start.20 = (f32[288,256]{1,0:T(8,128)}, f32[288,256]{1,0:T(8,128)S(1)}, u32[]{:S(2)}, u32[]{:S(2)}) collective-permute-start(f32[288,256]{1,0:T(8,128)} %unfold_col.1.refs_0_), channel_id=1, source_target_pairs={{0,16},{1,17},{2,18},{3,19},{4,20},{5,21},{6,22},{7,23},{8,24},{9,... | collective-permute-start | bytes 884744 | tf_op jit(solution)/shard_map/ppermute | solution.py:30
  115.3 1.5 collective-permute-start.19
  116.8 7.5 %collective-permute-done.21.refs_3_ = f32[288,256]{1,0:T(8,128)S(1)} collective-permute-done((f32[288,256]{1,0:T(8,128)}, f32[288,256]{1,0:T(8,128)S(1)}, u32[]{:S(2)}, u32[]{:S(2)}) %collective-permute-start.21) | collective-permute-done | bytes 294944 | tf_op jit(solution)/shard_map/ppermute | solution.py:30
  124.3 4.5 %collective-permute-done.20.refs_2_ = f32[288,256]{1,0:T(8,128)S(1)} collective-permute-done((f32[288,256]{1,0:T(8,128)}, f32[288,256]{1,0:T(8,128)S(1)}, u32[]{:S(2)}, u32[]{:S(2)}) %collective-permute-start.20) | collective-permute-done | bytes 294944 | tf_op jit(solution)/shard_map/ppermute | solution.py:30
  128.8 0.7 copy-done.9
  129.5 0.7 copy-done.10
  130.2 2.4 %unfold_pairs.1.mine_ref = f32[1152,256]{1,0:T(8,128)} custom-call(f32[288,256]{1,0:T(8,128)} %unfold_col.1.refs_0_, f32[288,256]{1,0:T(8,128)} %copy-done.10, f32[288,256]{1,0:T(8,128)} %copy-done.9, f32[288,256]{1,0:T(8,128)} %copy-done.8), custom_call_target="tpu_custom_call" | custom-call | flops 1000000 | bytes 2359296 | tf_op jit(solution)/shard_map/unfold_pairs/pallas_call | solution.py:239
  132.7 2.5 %collective-permute-start.13 = (f32[2,256,512]{2,1,0:T(8,128)S(1)}, f32[2,256,512]{2,1,0:T(8,128)S(1)}, u32[]{:S(2)}, u32[]{:S(2)}) collective-permute-start(f32[2,256,512]{2,1,0:T(8,128)S(1)} %copy-done.21), channel_id=1, source_target_pairs={{0,4},{1,5},{2,6},{3,7},{4,8},{5,9},{6,10},{7,11},{8,12},{9,13},{1... | collective-permute-start | bytes 3145736 | tf_op jit(solution)/shard_map/ppermute | solution.py:24
  135.1 1.3 collective-permute-start.14
  136.5 3.0 %collective-permute-start.15 = (f32[2,256,256]{2,1,0:T(8,128)S(1)}, f32[2,256,256]{2,1,0:T(8,128)S(1)}, u32[]{:S(2)}, u32[]{:S(2)}) collective-permute-start(f32[2,256,256]{2,1,0:T(8,128)S(1)} %copy-done.23), channel_id=1, source_target_pairs={{0,5},{1,6},{2,7},{4,9},{5,10},{6,11},{8,13},{9,14},{10,15},{12,17... | collective-permute-start | bytes 1572872 | tf_op jit(solution)/shard_map/ppermute | solution.py:24
  139.5 9.0 %collective-permute-done.14.g_left = f32[2,256,256]{2,1,0:T(8,128)S(1)} collective-permute-done((f32[2,256,256]{2,1,0:T(8,128)S(1)}, f32[2,256,256]{2,1,0:T(8,128)S(1)}, u32[]{:S(2)}, u32[]{:S(2)}) %collective-permute-start.14) | collective-permute-done | bytes 524320 | tf_op jit(solution)/shard_map/ppermute | solution.py:24
  148.5 11.2 %collective-permute-done.15.g_diag = f32[2,256,256]{2,1,0:T(8,128)S(1)} collective-permute-done((f32[2,256,256]{2,1,0:T(8,128)S(1)}, f32[2,256,256]{2,1,0:T(8,128)S(1)}, u32[]{:S(2)}, u32[]{:S(2)}) %collective-permute-start.15) | collective-permute-done | bytes 524320 | tf_op jit(solution)/shard_map/ppermute | solution.py:24
  159.7 0.8 copy-done.4
  160.9 3.5 %object_update.1 = f32[2,256,512]{2,1,0:T(8,128)} custom-call(f32[8,256]{1,0:T(8,128)} %get-tuple-element.35.top_ref, f32[2,256,512]{2,1,0:T(8,128)} %tile_ref.3, f32[256,512]{1,0:T(8,128)} %get-tuple-element.36.light_ref, f32[2,256,512]{2,1,0:T(8,128)} %get-tuple-element.37.g_tile, f32[2,256,512]{2,1,0:T(8,128)} %copy-done.2, f32[2,256,256]{2,1,0:T(8,128)} %copy-done.3, ...), custom_call_target="tpu_custom_call" | custom-call | flops 1000000 | bytes 6000000 | tf_op jit(solution)/shard_map/object_update/pallas_call | solution.py:359
  164.4 1.0 copy-done.1
  165.4 4.2 %probe_update.1 = f32[2,4,256,256]{3,2,1,0:T(8,128)} custom-call(f32[2,4,256,256]{3,2,1,0:T(8,128)} %probe_ref.5, f32[1152,256]{1,0:T(8,128)} %unfold_pairs.1.mine_ref, f32[1152,256]{1,0:T(8,128)} %copy-done.1), custom_call_target="tpu_custom_call" | custom-call | flops 1000000 | bytes 6000000 | tf_op jit(solution)/shard_map/probe_update/pallas_call | solution.py:369
  (64 shorter events, 4.9 us)
Async XLA Ops:
  0.6 25.0 %collective-permute-start = (f32[2,256,512]{2,1,0:T(8,128)}, f32[2,256,512]{2,1,0:T(8,128)S(1)}, u32[]{:S(2)}, u32[]{:S(2)}) collective-permute-start(f32[2,256,512]{2,1,0:T(8,128)} %tile_ref.3), channel_id=1, source_target_pairs={{4,0},{5,1},{6,2},{7,3},{8,4},{9,5},{10,6},{11,7},{12,8},{13,9},{1... | collective-permute-start | bytes 3145736 | tf_op jit(solution)/shard_map/ppermute | solution.py:24
  3.0 22.6 %collective-permute-start.2 = (f32[2,256,256]{2,1,0:T(8,128)S(1)}, f32[2,256,256]{2,1,0:T(8,128)S(1)}, u32[]{:S(2)}, u32[]{:S(2)}) collective-permute-start(f32[2,256,256]{2,1,0:T(8,128)S(1)} %slice.4), channel_id=1, source_target_pairs={{5,0},{6,1},{7,2},{9,4},{10,5},{11,6},{13,8},{14,9},{15,10},{17,12... | collective-permute-start | bytes 1572872 | tf_op jit(solution)/shard_map/ppermute | solution.py:24
  4.3 21.3 %collective-permute-start.1 = (f32[2,256,256]{2,1,0:T(8,128)S(1)}, f32[2,256,256]{2,1,0:T(8,128)S(1)}, u32[]{:S(2)}, u32[]{:S(2)}) collective-permute-start(f32[2,256,256]{2,1,0:T(8,128)S(1)} %slice.4), channel_id=1, source_target_pairs={{1,0},{2,1},{3,2},{5,4},{6,5},{7,6},{9,8},{10,9},{11,10},{13,12},{... | collective-permute-start | bytes 1572872 | tf_op jit(solution)/shard_map/ppermute | solution.py:24
  6.4 15.6 %copy-start.17 = (s32[6,2]{1,0:T(8,128)}, s32[6,2]{1,0:T(8,128)S(1)}, u32[]{:S(2)}) copy-start(s32[6,2]{1,0:T(8,128)S(1)} %copy.17.spots_ref) | copy-start | bytes 148
  6.4 11.9 %collective-permute-start.5 = (s32[6,2]{1,0:T(8,128)S(1)}, s32[6,2]{1,0:T(8,128)S(1)}, u32[]{:S(2)}, u32[]{:S(2)}) collective-permute-start(s32[6,2]{1,0:T(8,128)S(1)} %copy.17.spots_ref), channel_id=1, source_target_pairs={{0,5},{1,6},{2,7},{4,9},{5,10},{6,11},{8,13},{9,14},{10,15},{12,17... | collective-permute-start | bytes 152 | tf_op jit(solution)/shard_map/ppermute | solution.py:24
  13.3 7.9 %collective-permute-start.4 = (s32[6,2]{1,0:T(8,128)S(1)}, s32[6,2]{1,0:T(8,128)S(1)}, u32[]{:S(2)}, u32[]{:S(2)}) collective-permute-start(s32[6,2]{1,0:T(8,128)S(1)} %copy.17.spots_ref), channel_id=1, source_target_pairs={{0,1},{1,2},{2,3},{4,5},{5,6},{6,7},{8,9},{9,10},{10,11},{12,13},{... | collective-permute-start | bytes 152 | tf_op jit(solution)/shard_map/ppermute | solution.py:24
  18.3 3.7 %copy-start.18 = (s32[6,2]{1,0:T(8,128)}, s32[6,2]{1,0:T(8,128)S(1)}, u32[]{:S(2)}) copy-start(s32[6,2]{1,0:T(8,128)S(1)} %collective-permute-done.5.diag_ref) | copy-start | bytes 148
  18.3 3.7 %collective-permute-start.3 = (s32[6,2]{1,0:T(8,128)S(1)}, s32[6,2]{1,0:T(8,128)S(1)}, u32[]{:S(2)}, u32[]{:S(2)}) collective-permute-start(s32[6,2]{1,0:T(8,128)S(1)} %copy.17.spots_ref), channel_id=1, source_target_pairs={{0,4},{1,5},{2,6},{3,7},{4,8},{5,9},{6,10},{7,11},{8,12},{9,13},{1... | collective-permute-start | bytes 152 | tf_op jit(solution)/shard_map/ppermute | solution.py:24
  21.2 0.8 copy-start.19
  25.6 0.8 copy-start.25
  25.6 1.0 copy-start.26
  25.6 1.3 copy-start.22
  36.9 10.6 %collective-permute-start.6 = (f32[1160,256]{1,0:T(8,128)}, f32[1160,256]{1,0:T(8,128)S(1)}, u32[]{:S(2)}, u32[]{:S(2)}) collective-permute-start(f32[1160,256]{1,0:T(8,128)} %get-tuple-element.24), channel_id=1, source_target_pairs={{0,4},{1,5},{2,6},{3,7},{4,0},{5,1},{6,2},{7,3},{8,12},{9,13},{10,... | collective-permute-start | bytes 3563528 | tf_op jit(solution)/shard_map/ppermute | solution.py:30
  47.6 1.0 copy-start
  51.4 18.9 %collective-permute-start.7 = (f32[296,256]{1,0:T(8,128)}, f32[296,256]{1,0:T(8,128)S(1)}, u32[]{:S(2)}, u32[]{:S(2)}) collective-permute-start(f32[296,256]{1,0:T(8,128)} %get-tuple-element.27), channel_id=1, source_target_pairs={{0,8},{1,9},{2,10},{3,11},{4,12},{5,13},{6,14},{7,15},{8,0},{9,1},... | collective-permute-start | bytes 909320 | tf_op jit(solution)/shard_map/ppermute | solution.py:30
  62.1 18.3 %collective-permute-start.8 = (f32[296,256]{1,0:T(8,128)}, f32[296,256]{1,0:T(8,128)S(1)}, u32[]{:S(2)}, u32[]{:S(2)}) collective-permute-start(f32[296,256]{1,0:T(8,128)} %get-tuple-element.28), channel_id=1, source_target_pairs={{0,16},{1,17},{2,18},{3,19},{4,20},{5,21},{6,22},{7,23},{8,24},{9,... | collective-permute-start | bytes 909320 | tf_op jit(solution)/shard_map/ppermute | solution.py:30
  66.3 14.1 %collective-permute-start.9 = (f32[296,256]{1,0:T(8,128)}, f32[296,256]{1,0:T(8,128)S(1)}, u32[]{:S(2)}, u32[]{:S(2)}) collective-permute-start(f32[296,256]{1,0:T(8,128)} %get-tuple-element.29), channel_id=1, source_target_pairs={{0,24},{1,25},{2,26},{3,27},{4,28},{5,29},{6,30},{7,31},{8,16},{9,... | collective-permute-start | bytes 909320 | tf_op jit(solution)/shard_map/ppermute | solution.py:30
  70.3 10.1 %copy-start.5 = (f32[296,256]{1,0:T(8,128)}, f32[296,256]{1,0:T(8,128)S(1)}, u32[]{:S(2)}) copy-start(f32[296,256]{1,0:T(8,128)S(1)} %collective-permute-done.7.refs_2_) | copy-start | bytes 909316
  80.4 0.7 copy-start.6
  80.4 0.8 copy-start.7
  83.3 9.2 %collective-permute-start.10 = (f32[80,256]{1,0:T(8,128)}, f32[80,256]{1,0:T(8,128)S(1)}, u32[]{:S(2)}, u32[]{:S(2)}) collective-permute-start(f32[80,256]{1,0:T(8,128)} %get-tuple-element.32), channel_id=1, source_target_pairs={{0,1},{1,0},{2,3},{3,2},{4,5},{5,4},{6,7},{7,6},{8,9},{9,8},{10,11... | collective-permute-start | bytes 245768 | tf_op jit(solution)/shard_map/ppermute | solution.py:30
  89.6 8.0 %collective-permute-start.11 = (f32[80,256]{1,0:T(8,128)}, f32[80,256]{1,0:T(8,128)S(1)}, u32[]{:S(2)}, u32[]{:S(2)}) collective-permute-start(f32[80,256]{1,0:T(8,128)} %get-tuple-element.33), channel_id=1, source_target_pairs={{0,2},{1,3},{2,0},{3,1},{4,6},{5,7},{6,4},{7,5},{8,10},{9,11},{10,... | collective-permute-start | bytes 245768 | tf_op jit(solution)/shard_map/ppermute | solution.py:30
  89.6 8.0 %collective-permute-start.12 = (f32[80,256]{1,0:T(8,128)}, f32[80,256]{1,0:T(8,128)S(1)}, u32[]{:S(2)}, u32[]{:S(2)}) collective-permute-start(f32[80,256]{1,0:T(8,128)} %get-tuple-element.34), channel_id=1, source_target_pairs={{0,3},{1,2},{2,1},{3,0},{4,7},{5,6},{6,5},{7,4},{8,11},{9,10},{10,... | collective-permute-start | bytes 245768 | tf_op jit(solution)/shard_map/ppermute | solution.py:30
  92.5 5.1 %copy-start.11 = (f32[80,256]{1,0:T(8,128)}, f32[80,256]{1,0:T(8,128)S(1)}, u32[]{:S(2)}) copy-start(f32[80,256]{1,0:T(8,128)S(1)} %collective-permute-done.10.refs_2_) | copy-start | bytes 245764
  97.6 0.6 copy-start.12
  97.6 0.6 copy-start.13
  99.9 7.1 %collective-permute-start.18 = (f32[72,256]{1,0:T(8,128)}, f32[72,256]{1,0:T(8,128)S(1)}, u32[]{:S(2)}, u32[]{:S(2)}) collective-permute-start(f32[72,256]{1,0:T(8,128)} %get-tuple-element.41.refs_0_), channel_id=1, source_target_pairs={{0,3},{1,2},{2,1},{3,0},{4,7},{5,6},{6,5},{7,4},{8,11},{9,10},{10,... | collective-permute-start | bytes 221192 | tf_op jit(solution)/shard_map/ppermute | solution.py:30
  101.1 9.2 %collective-permute-start.17 = (f32[72,256]{1,0:T(8,128)}, f32[72,256]{1,0:T(8,128)S(1)}, u32[]{:S(2)}, u32[]{:S(2)}) collective-permute-start(f32[72,256]{1,0:T(8,128)} %get-tuple-element.41.refs_0_), channel_id=1, source_target_pairs={{0,2},{1,3},{2,0},{3,1},{4,6},{5,7},{6,4},{7,5},{8,10},{9,11},{10,... | collective-permute-start | bytes 221192 | tf_op jit(solution)/shard_map/ppermute | solution.py:30
  103.4 6.9 %collective-permute-start.16 = (f32[72,256]{1,0:T(8,128)}, f32[72,256]{1,0:T(8,128)S(1)}, u32[]{:S(2)}, u32[]{:S(2)}) collective-permute-start(f32[72,256]{1,0:T(8,128)} %get-tuple-element.41.refs_0_), channel_id=1, source_target_pairs={{0,1},{1,0},{2,3},{3,2},{4,5},{5,4},{6,7},{7,6},{8,9},{9,8},{10,11... | collective-permute-start | bytes 221192 | tf_op jit(solution)/shard_map/ppermute | solution.py:30
  107.0 3.3 %copy-start.14 = (f32[72,256]{1,0:T(8,128)}, f32[72,256]{1,0:T(8,128)S(1)}, u32[]{:S(2)}) copy-start(f32[72,256]{1,0:T(8,128)S(1)} %collective-permute-done.18.refs_3_) | copy-start | bytes 221188
  110.9 0.6 copy-start.16
  113.3 19.4 %copy-start.21 = (f32[2,256,512]{2,1,0:T(8,128)S(1)}, f32[2,256,512]{2,1,0:T(8,128)}, u32[]{:S(2)}) copy-start(f32[2,256,512]{2,1,0:T(8,128)} %get-tuple-element.38) | copy-start | bytes 3145732
  113.3 21.9 %copy-start.24 = (f32[2,256,256]{2,1,0:T(8,128)S(1)}, f32[2,256,256]{2,1,0:T(8,128)}, u32[]{:S(2)}) copy-start(f32[2,256,256]{2,1,0:T(8,128)} %get-tuple-element.39) | copy-start | bytes 1572868
  113.3 23.2 %copy-start.23 = (f32[2,256,256]{2,1,0:T(8,128)S(1)}, f32[2,256,256]{2,1,0:T(8,128)}, u32[]{:S(2)}) copy-start(f32[2,256,256]{2,1,0:T(8,128)} %get-tuple-element.40) | copy-start | bytes 1572868
  113.3 11.1 %collective-permute-start.21 = (f32[288,256]{1,0:T(8,128)}, f32[288,256]{1,0:T(8,128)S(1)}, u32[]{:S(2)}, u32[]{:S(2)}) collective-permute-start(f32[288,256]{1,0:T(8,128)} %unfold_col.1.refs_0_), channel_id=1, source_target_pairs={{0,24},{1,25},{2,26},{3,27},{4,28},{5,29},{6,30},{7,31},{8,16},{9,... | collective-permute-start | bytes 884744 | tf_op jit(solution)/shard_map/ppermute | solution.py:30
  113.3 15.5 %collective-permute-start.20 = (f32[288,256]{1,0:T(8,128)}, f32[288,256]{1,0:T(8,128)S(1)}, u32[]{:S(2)}, u32[]{:S(2)}) collective-permute-start(f32[288,256]{1,0:T(8,128)} %unfold_col.1.refs_0_), channel_id=1, source_target_pairs={{0,16},{1,17},{2,18},{3,19},{4,20},{5,21},{6,22},{7,23},{8,24},{9,... | collective-permute-start | bytes 884744 | tf_op jit(solution)/shard_map/ppermute | solution.py:30
  115.3 13.5 %collective-permute-start.19 = (f32[288,256]{1,0:T(8,128)}, f32[288,256]{1,0:T(8,128)S(1)}, u32[]{:S(2)}, u32[]{:S(2)}) collective-permute-start(f32[288,256]{1,0:T(8,128)} %unfold_col.1.refs_0_), channel_id=1, source_target_pairs={{0,8},{1,9},{2,10},{3,11},{4,12},{5,13},{6,14},{7,15},{8,0},{9,1},... | collective-permute-start | bytes 884744 | tf_op jit(solution)/shard_map/ppermute | solution.py:30
  124.3 4.5 %copy-start.8 = (f32[288,256]{1,0:T(8,128)}, f32[288,256]{1,0:T(8,128)S(1)}, u32[]{:S(2)}) copy-start(f32[288,256]{1,0:T(8,128)S(1)} %collective-permute-done.21.refs_3_) | copy-start | bytes 884740
  128.8 0.7 copy-start.9
  129.5 0.7 copy-start.10
  132.6 31.7 %collective-permute-start.22 = (f32[1152,256]{1,0:T(8,128)}, f32[1152,256]{1,0:T(8,128)S(1)}, u32[]{:S(2)}, u32[]{:S(2)}) collective-permute-start(f32[1152,256]{1,0:T(8,128)} %unfold_pairs.1.mine_ref), channel_id=1, source_target_pairs={{0,4},{1,5},{2,6},{3,7},{4,0},{5,1},{6,2},{7,3},{8,12},{9,13},{10,... | collective-permute-start | bytes 3538952 | tf_op jit(solution)/shard_map/ppermute | solution.py:30
  132.7 27.1 %collective-permute-start.13 = (f32[2,256,512]{2,1,0:T(8,128)S(1)}, f32[2,256,512]{2,1,0:T(8,128)S(1)}, u32[]{:S(2)}, u32[]{:S(2)}) collective-permute-start(f32[2,256,512]{2,1,0:T(8,128)S(1)} %copy-done.21), channel_id=1, source_target_pairs={{0,4},{1,5},{2,6},{3,7},{4,8},{5,9},{6,10},{7,11},{8,12},{9,13},{1... | collective-permute-start | bytes 3145736 | tf_op jit(solution)/shard_map/ppermute | solution.py:24
  135.1 13.4 %collective-permute-start.14 = (f32[2,256,256]{2,1,0:T(8,128)S(1)}, f32[2,256,256]{2,1,0:T(8,128)S(1)}, u32[]{:S(2)}, u32[]{:S(2)}) collective-permute-start(f32[2,256,256]{2,1,0:T(8,128)S(1)} %copy-done.24), channel_id=1, source_target_pairs={{0,1},{1,2},{2,3},{4,5},{5,6},{6,7},{8,9},{9,10},{10,11},{12,13},{... | collective-permute-start | bytes 1572872 | tf_op jit(solution)/shard_map/ppermute | solution.py:24
  136.5 23.2 %collective-permute-start.15 = (f32[2,256,256]{2,1,0:T(8,128)S(1)}, f32[2,256,256]{2,1,0:T(8,128)S(1)}, u32[]{:S(2)}, u32[]{:S(2)}) collective-permute-start(f32[2,256,256]{2,1,0:T(8,128)S(1)} %copy-done.23), channel_id=1, source_target_pairs={{0,5},{1,6},{2,7},{4,9},{5,10},{6,11},{8,13},{9,14},{10,15},{12,17... | collective-permute-start | bytes 1572872 | tf_op jit(solution)/shard_map/ppermute | solution.py:24
  148.5 11.2 %copy-start.3 = (f32[2,256,256]{2,1,0:T(8,128)}, f32[2,256,256]{2,1,0:T(8,128)S(1)}, u32[]{:S(2)}) copy-start(f32[2,256,256]{2,1,0:T(8,128)S(1)} %collective-permute-done.14.g_left) | copy-start | bytes 1572868
  159.7 0.8 copy-start.4
  159.7 1.1 copy-start.2
  164.4 1.0 copy-start.1
  (2 other events, 1.2 us)

commit v3 on v2

--- a/solution.py
+++ b/solution.py
@@ -90,7 +90,7 @@
 def main_kernel(
     counts_ref, spots_ref, tile_ref, below_ref, right_ref, corner_ref, amp_ref, probe_ref, top_ref,
     lf_ref, rf_ref, lg_ref, rg_ref,
-    g_tile, g_below, g_right, g_corner, mine_ref, other_ref,
+    g_tile, g_below, g_side, mine_ref, other_ref,
     ext, gacc, stage, turned, wave, wins, sums,
 ):
     modes, side = probe_ref.shape[1], probe_ref.shape[2]
@@ -153,13 +153,17 @@
     lax.fori_loop(0, counts_ref[my_row, my_col], step, 0)
     g_tile[...] = gacc[:, :rows, :cols]
     g_below[...] = gacc[:, rows:, :cols]
-    g_right[...] = gacc[:, :rows, cols:]
-    g_corner[...] = gacc[:, rows:, cols:]
-    half = mine_ref.shape[0]
+    g_side[...] = gacc[:, :, cols:]
+    pairs = lax.axis_size("row") // 2
+    share = mine_ref.shape[0] // pairs - SUBLANES
+    half = share * pairs
     core = lax.rem(my_row, 2)
-    mine_ref[...] = sums[pl.ds(pl.multiple_of(core * half, SUBLANES), half)]
-    other_ref[:half] = sums[pl.ds(pl.multiple_of((1 - core) * half, SUBLANES), half)]
-    other_ref[half:] = top_ref[...]
+    for ref, base in ((mine_ref, core * half), (other_ref, (1 - core) * half)):
+        base = pl.multiple_of(base, SUBLANES)
+        for j in range(pairs):
+            at = j * (share + SUBLANES)
+            ref[at:at + share] = sums[pl.ds(base + j * share, share)]
+            ref[at + share:at + share + SUBLANES] = top_ref[...]
 
 
 def light_kernel(counts_ref, spots_ref, up_ref, left_ref, diag_ref, probe_ref, light_ref, top_ref, lit, acc):
@@ -189,87 +193,39 @@
     top_ref[...] = jnp.broadcast_to(top, top_ref.shape)
 
 
-def fold_kernel(group, rank_of, *refs):
-    received, rest = refs[2:2 + group[0] - 1], refs[2 + group[0] - 1:]
-    own_ref, top_ref = refs[:2]
-    parts = group[1]
-    out_own, out_top, out_other, total = rest[0], rest[1], rest[2:2 + parts - 1], rest[-1]
-    rows = own_ref.shape[0]
-    value, top = own_ref[...], top_ref[...]
-    for ref in received:
-        value += ref[:rows]
-        top = jnp.maximum(top, ref[rows:])
-    out_top[...] = top
-    if parts == 1:
-        out_own[...] = value
-        return
-    total[...] = value
-    rank, share = rank_of(), rows // parts
-    out_own[...] = total[pl.ds(pl.multiple_of(rank * share, SUBLANES), share)]
-    for d, ref in enumerate(out_other, 1):
-        ref[:share] = total[pl.ds(pl.multiple_of((rank ^ d) * share, SUBLANES), share)]
-        ref[share:] = top
-
-
-def fold(own, top, received, parts, rank_of, name):
-    rows, width = own.shape
-    share = rows // parts
-    got = pl.pallas_call(
-        functools.partial(fold_kernel, (len(received) + 1, parts), rank_of),
-        out_shape=(f32(share, width), f32(*top.shape)) + (f32(share + SUBLANES, width),) * (parts - 1),
-        in_specs=[VM] * (2 + len(received)),
-        out_specs=(VM,) * (parts + 1),
-        scratch_shapes=[pltpu.VMEM((rows, width), jnp.float32)],
-        compiler_params=PARAMS,
-        cost_estimate=cost(10**6, 4 * rows * width * (len(received) + 2)),
-        name=name,
-    )(own, top, *received)
-    return got[0], got[1], got[2:]
-
-
-def unfold_kernel(rank_of, *refs):
-    out_ref = refs[-1]
-    share, rank = refs[0].shape[0], rank_of()
-    for d, ref in enumerate(refs[:-1]):
-        out_ref[pl.ds(pl.multiple_of((rank ^ d) * share, SUBLANES), share)] = ref[...]
-
-
-def unfold(parts, rank_of, name):
-    share, width = parts[0].shape
-    return pl.pallas_call(
-        functools.partial(unfold_kernel, rank_of),
-        out_shape=f32(share * len(parts), width),
-        in_specs=[VM] * len(parts),
-        out_specs=VM,
-        compiler_params=PARAMS,
-        cost_estimate=cost(10**6, 8 * share * width * len(parts)),
-        name=name,
-    )(*parts)
-
-
-def pair_rank():
-    return lax.axis_index("row") // 2
-
-
-def col_rank():
-    return lax.axis_index("col")
-
-
-def finish_kernel(top_ref, tile_ref, light_ref, g_tile, g_up, g_left, g_diag, out_ref, total):
+def merge(share, values):
+    summed = jnp.arange(values[0].shape[0])[:, None] < share
+    return functools.reduce(lambda a, b: jnp.where(summed, a + b, jnp.maximum(a, b)), values)
+
+
+def finish_kernel(tile_ref, light_ref, top_ref, g_tile, g_left, g_up, out_ref):
     side = g_left.shape[2]
-    total[...] = g_tile[...] + g_up[...]
-    total[:, :, :side] += g_left[...] + g_diag[...]
-    scale = 1.0 / (light_ref[...] + 0.1 * top_ref[0, 0])
-    out_ref[0] = tile_ref[0] + total[0] * scale
-    out_ref[1] = tile_ref[1] + total[1] * scale
-
-
-def probe_kernel(probe_ref, mine_ref, other_ref, out_ref, sums):
+    rows, cols = light_ref.shape
+    top = top_ref[0:1, 0:1]
+    for at in range(0, cols, side):
+        part = slice(at, at + side)
+        scale = 1.0 / (light_ref[:, part] + 0.1 * top)
+        for i in range(2):
+            total = g_tile[i, :, part] + g_up[i, :, part]
+            if at == 0:
+                total += g_left[i, :rows]
+            out_ref[i, :, part] = tile_ref[i, :, part] + total * scale
+
+
+def probe_kernel(parts, probe_ref, *refs):
+    pairs, n_col = parts
+    block_refs, out_ref, sums = refs[:-2], refs[-2], refs[-1]
     modes, side = probe_ref.shape[1], probe_ref.shape[2]
-    half = mine_ref.shape[0]
-    core = lax.rem(lax.axis_index("row"), 2)
-    sums[pl.ds(pl.multiple_of(core * half, SUBLANES), half)] = mine_ref[...]
-    sums[pl.ds(pl.multiple_of((1 - core) * half, SUBLANES), half)] = other_ref[...]
+    share = block_refs[0].shape[0]
+    piece = share // n_col
+    my_row, my_col = lax.axis_index("row"), lax.axis_index("col")
+    core, pair = lax.rem(my_row, 2), my_row // 2
+    for i, ref in enumerate(block_refs):
+        flip, d = i // pairs, i % pairs
+        base = ((core ^ flip) * pairs + (pair ^ d)) * share
+        for e in range(n_col):
+            to = pl.multiple_of(base + (my_col ^ e) * piece, SUBLANES)
+            sums[pl.ds(to, piece)] = ref[e * piece:(e + 1) * piece]
     den = sums[2 * modes * side:(2 * modes + 1) * side]
     top = jnp.max(jnp.max(den, axis=0, keepdims=True), axis=1, keepdims=True)
     scale = 1.0 / (den + 0.1 * top)
@@ -297,15 +253,17 @@
     pairs, n_col = lax.axis_size("row") // 2, lax.axis_size("col")
     step = SUBLANES * 2 * pairs * n_col
     total_rows = -(-(2 * modes + 1) * side // step) * step
-    half = total_rows // 2
+    share = total_rows // (2 * pairs)
+    piece = share // n_col
+    pair, my_col = lax.axis_index("row") // 2, lax.axis_index("col")
     spots = corners[0, 0]
 
+    right = shifted(object_field[:, :, :side], 0, -1)
     from_up = shifted(spots, 1, 0)
     from_left = shifted(spots, 0, 1)
     from_diag = shifted(spots, 1, 1)
     below = shifted(object_field[:, :side, :], -1, 0)
-    right = shifted(object_field[:, :, :side], 0, -1)
-    corner = shifted(object_field[:, :side, :side], -1, -1)
+    corner = shifted(right[:, :side, :], -1, 0)
 
     light, top = pl.pallas_call(
         light_kernel,
@@ -321,14 +279,14 @@
         name="lighting",
     )(counts, spots, from_up, from_left, from_diag, probe)
 
-    g_tile, g_below, g_right, g_corner, mine, other = pl.pallas_call(
+    g_tile, g_below, g_side, mine, other = pl.pallas_call(
         main_kernel,
         out_shape=(
-            f32(2, rows, cols), f32(2, side, cols), f32(2, rows, side), f32(2, side, side),
-            f32(half, side), f32(half + SUBLANES, side),
+            f32(2, rows, cols), f32(2, side, cols), f32(2, rows + side, side),
+            f32(pairs * (share + SUBLANES), side), f32(pairs * (share + SUBLANES), side),
         ),
         in_specs=[SM] * 2 + [VM] * 11,
-        out_specs=(VM,) * 6,
+        out_specs=(VM,) * 5,
         scratch_shapes=[
             pltpu.VMEM((2, rows + side, cols + side), jnp.float32),
             pltpu.VMEM((2, rows + side, cols + side), jnp.float32),
@@ -343,39 +301,50 @@
         name="positions",
     )(counts, spots, object_field, below, right, corner, amplitudes[0, 0], probe, top, *tables(side))
 
-    received = [swapped(other, 1, 0)]
-    g_up = shifted(g_below, 1, 0)
-    g_left = shifted(g_right, 0, 1)
-    g_diag = shifted(g_corner, 1, 1)
-    own, top, others = fold(mine, top, received, pairs, pair_rank, "fold_chip")
-    received = [swapped(value, 2 * d, 0) for d, value in enumerate(others, 1)]
-    own, top, others = fold(own, top, received, n_col, col_rank, "fold_plane")
-    received = [swapped(value, 0, d) for d, value in enumerate(others, 1)]
-    own, top, _ = fold(own, top, received, 1, None, "fold_all")
-    own = unfold([own] + [swapped(own, 0, d) for d in range(1, n_col)], col_rank, "unfold_col")
-    own = unfold([own] + [swapped(own, 2 * d, 0) for d in range(1, pairs)], pair_rank, "unfold_pairs")
-    other = swapped(own, 1, 0)
-
+    g_left = shifted(g_side, 0, 1)
+    arrived = swapped(other, 1, 0)
+
+    def cut(value, start, size):
+        return lax.dynamic_slice_in_dim(value, start, size, 0)
+
+    def chip_sum(d):
+        start = (pair ^ d) * (share + SUBLANES)
+        return merge(share, [cut(mine, start, share + SUBLANES), cut(arrived, start, share + SUBLANES)])
+
+    plane_sum = merge(share, [chip_sum(0)] + [swapped(chip_sum(d), 2 * d, 0) for d in range(1, pairs)])
+    lower = jnp.concatenate([g_below[:, :, :side] + g_left[:, rows:], g_below[:, :, side:]], axis=2)
+    plane_sum, lower = lax.optimization_barrier((plane_sum, lower))
+    g_up = shifted(lower, 1, 0)
+
+    def col_part(e):
+        return jnp.concatenate([cut(plane_sum, (my_col ^ e) * piece, piece), plane_sum[share:]], axis=0)
+
+    own = merge(piece, [col_part(0)] + [swapped(col_part(e), 0, e) for e in range(1, n_col)])
+    top = own[piece:]
+    own = own[:piece]
+    own = jnp.concatenate([own] + [swapped(own, 0, e) for e in range(1, n_col)], axis=0)
     object_new = pl.pallas_call(
         finish_kernel,
         out_shape=f32(2, rows, cols),
-        in_specs=[SM] + [VM] * 6,
+        in_specs=[VM] * 6,
         out_specs=VM,
-        scratch_shapes=[pltpu.VMEM((2, rows, cols), jnp.float32)],
         compiler_params=PARAMS,
         cost_estimate=cost(10**6, 6 * 10**6),
         name="object_update",
-    )(top, object_field, light, g_tile, g_up, g_left, g_diag)
+    )(object_field, light, top, g_tile, g_left, g_up)
+    own, object_new = lax.optimization_barrier((own, object_new))
+    blocks = [own] + [swapped(own, 2 * d, 0) for d in range(1, pairs)]
+    blocks = blocks + [swapped(block, 1, 0) for block in blocks]
     probe_new = pl.pallas_call(
-        probe_kernel,
+        functools.partial(probe_kernel, (pairs, n_col)),
         out_shape=f32(*probe.shape),
-        in_specs=[VM] * 3,
+        in_specs=[VM] * (1 + len(blocks)),
         out_specs=VM,
         scratch_shapes=[pltpu.VMEM((total_rows, side), jnp.float32)],
         compiler_params=PARAMS,
         cost_estimate=cost(10**6, 6 * 10**6),
         name="probe_update",
-    )(probe, own, other)
+    )(probe, *blocks)
     return object_new, probe_new
 
 

time: 169 us -> 147 us (0.87)
  Pallas kernels: 31.4 us -> 21 us
  starting transfers between devices: 63.5 us -> 55.8 us
  waiting for transfers between devices: 61.5 us -> 57.1 us
  local copies, waits for them, and re-layouts: 12.4 us -> 8.78 us
  other arithmetic: 0 us -> 3.14 us
    ppermute x14 -> x17, waiting for transfers between devices: 40.4 us -> 23.5 us  [swapped(): return lax.ppermute(value, ('row', 'col'), pairs)]
    ppermute x9 -> x8, waiting for transfers between devices: 21 us -> 33.7 us  [shifted(): return lax.ppermute(value, ('row', 'col'), pairs)]
    pallas_call x7 -> x2, Pallas kernels: 18.4 us -> 7.83 us  [the longest x1 4.15 us: body(): pl.pallas_call(functools.partial(probe_kernel, (pairs, n_col)), out_shape...]
    ppermute x14 -> x17, starting transfers between devices: 39.4 us -> 31.5 us  [swapped(): return lax.ppermute(value, ('row', 'col'), pairs)]
    unnamed x55 -> x37, local copies, waits for them, and re-layouts: 10.6 us -> 6.29 us
    select_n x0 -> x3, other arithmetic: none -> 2.84 us  [merge(): jnp.where(summed, a + b, jnp.maximum(a, b))]
    ppermute x9 -> x8, starting transfers between devices: 24.1 us -> 24.3 us  [shifted(): return lax.ppermute(value, ('row', 'col'), pairs)]
  transfers between devices with their start and end apart: 23 -> 25, of which waited for: 12 -> 9; matrix products, arithmetic and copies ran while one was open for 2% -> 4% of each run, Pallas kernels for 4% -> 2%
where the time goes in v3:
time: 147 us
  waiting for transfers between devices  57.1 us (39%)
  starting transfers between devices  55.8 us (38%)
  Pallas kernels  21 us (14%)
  local copies, waits for them, and re-layouts  8.78 us (6%)
  other arithmetic  3.14 us (2%)
    ppermute x8, waiting for transfers between devices, shifted(): return lax.ppermute(value, ('row', 'col'), pairs)  33.7 us
    ppermute x17, starting transfers between devices, swapped(): return lax.ppermute(value, ('row', 'col'), pairs)  31.5 us
    ppermute x8, starting transfers between devices, shifted(): return lax.ppermute(value, ('row', 'col'), pairs)  24.3 us
    ppermute x17, waiting for transfers between devices, swapped(): return lax.ppermute(value, ('row', 'col'), pairs)  23.5 us
    pallas_call x1, Pallas kernels, body(): pl.pallas_call(main_kernel, out_shape=(f32(2, rows, cols), f32(2, side, c...  10.2 us
    unnamed x37, local copies, waits for them, and re-layouts  6.29 us
    pallas_call x1, Pallas kernels, body(): pl.pallas_call(functools.partial(probe_kernel, (pairs, n_col)), out_shape...  4.15 us
    pallas_call x1, Pallas kernels, body(): pl.pallas_call(finish_kernel, out_shape=f32(2, rows, cols), in_specs=[VM]...  3.68 us
  transfers between devices with their start and end apart: 25, of which 9 were waited for; matrix products, arithmetic and copies ran while one was open for 4% of the time, Pallas kernels for 2%

profile of v3, /device:TPU:0, one launch (start us, length us, event | category | flops | bytes accessed | tf_op | source)
XLA Modules:
  0.0 146.9 jit_solution(3873551170388083412)
XLA Ops:
  0.6 1.3 collective-permute-start
  1.9 1.1 slice.24
  3.0 1.3 collective-permute-start.1
  4.3 16.0 %collective-permute-done.1.right_ref = f32[2,256,256]{2,1,0:T(8,128)S(1)} collective-permute-done((f32[2,256,256]{2,1,0:T(8,128)S(1)}, f32[2,256,256]{2,1,0:T(8,128)S(1)}, u32[]{:S(2)}, u32[]{:S(2)}) %collective-permute-start.1) | collective-permute-done | bytes 524320 | tf_op jit(solution)/shard_map/ppermute | solution.py:24
  20.4 1.3 collective-permute-start.2
  21.6 0.8 copy.17.spots_ref
  22.4 3.0 %collective-permute-start.3 = (s32[6,2]{1,0:T(8,128)S(1)}, s32[6,2]{1,0:T(8,128)S(1)}, u32[]{:S(2)}, u32[]{:S(2)}) collective-permute-start(s32[6,2]{1,0:T(8,128)S(1)} %copy.17.spots_ref), channel_id=1, source_target_pairs={{0,4},{1,5},{2,6},{3,7},{4,8},{5,9},{6,10},{7,11},{8,12},{9,13},{1... | collective-permute-start | bytes 152 | tf_op jit(solution)/shard_map/ppermute | solution.py:24
  25.4 4.1 %collective-permute-start.4 = (s32[6,2]{1,0:T(8,128)S(1)}, s32[6,2]{1,0:T(8,128)S(1)}, u32[]{:S(2)}, u32[]{:S(2)}) collective-permute-start(s32[6,2]{1,0:T(8,128)S(1)} %copy.17.spots_ref), channel_id=1, source_target_pairs={{0,1},{1,2},{2,3},{4,5},{5,6},{6,7},{8,9},{9,10},{10,11},{12,13},{... | collective-permute-start | bytes 152 | tf_op jit(solution)/shard_map/ppermute | solution.py:24
  29.6 4.2 %collective-permute-start.5 = (s32[6,2]{1,0:T(8,128)S(1)}, s32[6,2]{1,0:T(8,128)S(1)}, u32[]{:S(2)}, u32[]{:S(2)}) collective-permute-start(s32[6,2]{1,0:T(8,128)S(1)} %copy.17.spots_ref), channel_id=1, source_target_pairs={{0,5},{1,6},{2,7},{4,9},{5,10},{6,11},{8,13},{9,14},{10,15},{12,17... | collective-permute-start | bytes 152 | tf_op jit(solution)/shard_map/ppermute | solution.py:24
  33.8 1.3 copy.16.counts_ref
  35.2 0.6 copy-done.12
  35.8 0.6 copy-done.14
  36.4 3.0 %lighting.1 = (f32[256,512]{1,0:T(8,128)}, f32[8,256]{1,0:T(8,128)}) custom-call(s32[8,4]{1,0:T(8,128)} %copy.16.counts_ref, s32[6,2]{1,0:T(8,128)} %copy-done.11, s32[6,2]{1,0:T(8,128)} %copy-done.12, s32[6,2]{1,0:T(8,128)} %copy-done.13, s32[6,2]{1,0:T(8,128)} %copy-done.14, f32[2,4,256,256]{3,2,1,0:T(8,128)} %probe_ref.5), custom_call_target="tpu_custom_call" | custom-call | flops 100000000 | bytes 10000000 | tf_op jit(solution)/shard_map/lighting/pallas_call | solution.py:268
  39.4 0.9 copy-done.15
  40.3 0.2 copy-done.17
  40.5 10.2 %positions.1 = (f32[2,256,512]{2,1,0:T(8,128)}, f32[2,256,512]{2,1,0:T(8,128)}, f32[2,512,256]{2,1,0:T(8,128)}, f32[1184,256]{1,0:T(8,128)}, f32[1184,256]{1,0:T(8,128)}) custom-call(s32[8,4]{1,0:T(8,128)} %copy.16.counts_ref, s32[6,2]{1,0:T(8,128)} %copy-done.11, f32[2,256,512]{2,1,0:T(8,128)} %tile_ref.3, f32[2,256,512]{2,1,0:T(8,128)} %copy-done.15, ...), custom_call_target="tpu_custom_call" | custom-call | flops 12999999488 | bytes 20000000 | tf_op jit(solution)/shard_map/positions/pallas_call | solution.py:282
  50.7 15.1 %collective-permute-start.6 = (f32[1184,256]{1,0:T(8,128)}, f32[1184,256]{1,0:T(8,128)S(1)}, u32[]{:S(2)}, u32[]{:S(2)}) collective-permute-start(f32[1184,256]{1,0:T(8,128)} %get-tuple-element.15), channel_id=1, source_target_pairs={{0,4},{1,5},{2,6},{3,7},{4,0},{5,1},{6,2},{7,3},{8,12},{9,13},{10,... | collective-permute-start | bytes 3637256 | tf_op jit(solution)/shard_map/ppermute | solution.py:30
  65.8 7.7 %collective-permute-start.10 = (f32[2,512,256]{2,1,0:T(8,128)}, f32[2,512,256]{2,1,0:T(8,128)S(1)}, u32[]{:S(2)}, u32[]{:S(2)}) collective-permute-start(f32[2,512,256]{2,1,0:T(8,128)} %get-tuple-element.17), channel_id=1, source_target_pairs={{0,1},{1,2},{2,3},{4,5},{5,6},{6,7},{8,9},{9,10},{10,11},{12,13},{... | collective-permute-start | bytes 3145736 | tf_op jit(solution)/shard_map/ppermute | solution.py:24
  73.5 1.6 %maximum_select_fusion.3 = (f32[296,256]{1,0:T(8,128)S(1)}, f32[296,256]{1,0:T(8,128)S(1)}, f32[296,256]{1,0:T(8,128)S(1)}) fusion(f32[1184,256]{1,0:T(8,128)S(1)} %collective-permute-done.6, s32[]{:T(128)S(6)} %select_n.68, f32[1184,256]{1,0:T(8,128)} %get-tuple-element.14, pred[296]{0:T(512)(128)(4,1)S(1)} %iota_compare_fusion, s32[]{:T(128)S(6)} %select_n.74, ...), kind=kLoop, calls=%fused_computation.5 | loop fusion | flops 681984 | bytes 2728244 | tf_op jit(solution)/shard_map/jit(_where)/select_n | solution.py:198
  75.1 2.1 %collective-permute-start.9 = (f32[296,256]{1,0:T(8,128)S(1)}, f32[296,256]{1,0:T(8,128)S(1)}, u32[]{:S(2)}, u32[]{:S(2)}) collective-permute-start(f32[296,256]{1,0:T(8,128)S(1)} %get-tuple-element.25), channel_id=1, source_target_pairs={{0,24},{1,25},{2,26},{3,27},{4,28},{5,29},{6,30},{7,31},{8,16},{9,... | collective-permute-start | bytes 909320 | tf_op jit(solution)/shard_map/ppermute | solution.py:30
  77.3 1.4 collective-permute-start.7
  78.7 17.6 %collective-permute-done.10.g_left = f32[2,512,256]{2,1,0:T(8,128)S(1)} collective-permute-done((f32[2,512,256]{2,1,0:T(8,128)}, f32[2,512,256]{2,1,0:T(8,128)S(1)}, u32[]{:S(2)}, u32[]{:S(2)}) %collective-permute-start.10) | collective-permute-done | bytes 1048608 | tf_op jit(solution)/shard_map/ppermute | solution.py:24
  96.3 0.1 slice_add_fusion
  96.4 0.9 copy-done
  97.3 0.1 pad_maximum_fusion
  97.5 1.2 maximum_select_fusion
  98.6 1.4 collective-permute-start.17
  100.1 0.1 collective-permute-start.13
  100.2 3.8 %collective-permute-start.12 = (f32[80,256]{1,0:T(8,128)S(1)}, f32[80,256]{1,0:T(8,128)S(1)}, u32[]{:S(2)}, u32[]{:S(2)}) collective-permute-start(f32[80,256]{1,0:T(8,128)S(1)} %get-tuple-element.34), channel_id=1, source_target_pairs={{0,2},{1,3},{2,0},{3,1},{4,6},{5,7},{6,4},{7,5},{8,10},{9,11},{10,... | collective-permute-start | bytes 245768 | tf_op jit(solution)/shard_map/ppermute | solution.py:30
  104.0 0.5 collective-permute-start.11
  104.6 2.8 %collective-permute-done.13 = f32[80,256]{1,0:T(8,128)S(1)} collective-permute-done((f32[80,256]{1,0:T(8,128)S(1)}, f32[80,256]{1,0:T(8,128)S(1)}, u32[]{:S(2)}, u32[]{:S(2)}) %collective-permute-start.13) | collective-permute-done | bytes 81952 | tf_op jit(solution)/shard_map/ppermute | solution.py:30
  107.3 4.0 %collective-permute-done.12 = f32[80,256]{1,0:T(8,128)S(1)} collective-permute-done((f32[80,256]{1,0:T(8,128)S(1)}, f32[80,256]{1,0:T(8,128)S(1)}, u32[]{:S(2)}, u32[]{:S(2)}) %collective-permute-start.12) | collective-permute-done | bytes 81952 | tf_op jit(solution)/shard_map/ppermute | solution.py:30
  111.3 0.1 maximum_select_fusion.4
  111.5 1.3 collective-permute-start.16
  112.8 3.2 %collective-permute-start.14 = (f32[72,256]{1,0:T(8,128)S(1)}, f32[72,256]{1,0:T(8,128)S(1)}, u32[]{:S(2)}, u32[]{:S(2)}) collective-permute-start(f32[72,256]{1,0:T(8,128)S(1)} %slice.32), channel_id=1, source_target_pairs={{0,1},{1,0},{2,3},{3,2},{4,5},{5,4},{6,7},{7,6},{8,9},{9,8},{10,11... | collective-permute-start | bytes 221192 | tf_op jit(solution)/shard_map/ppermute | solution.py:30
  115.9 0.6 slice.33.top_ref
  116.5 2.0 %collective-permute-done.16 = f32[72,256]{1,0:T(8,128)S(1)} collective-permute-done((f32[72,256]{1,0:T(8,128)S(1)}, f32[72,256]{1,0:T(8,128)S(1)}, u32[]{:S(2)}, u32[]{:S(2)}) %collective-permute-start.16) | collective-permute-done | bytes 73760 | tf_op jit(solution)/shard_map/ppermute | solution.py:30
  118.5 1.8 %collective-permute-done.15 = f32[72,256]{1,0:T(8,128)S(1)} collective-permute-done((f32[72,256]{1,0:T(8,128)S(1)}, f32[72,256]{1,0:T(8,128)S(1)}, u32[]{:S(2)}, u32[]{:S(2)}) %collective-permute-start.15) | collective-permute-done | bytes 73760 | tf_op jit(solution)/shard_map/ppermute | solution.py:30
  120.5 1.0 copy-done.3
  121.5 3.7 %object_update.1 = f32[2,256,512]{2,1,0:T(8,128)} custom-call(f32[2,256,512]{2,1,0:T(8,128)} %tile_ref.3, f32[256,512]{1,0:T(8,128)} %get-tuple-element.19.light_ref, f32[8,256]{1,0:T(8,128)} %slice.33.top_ref, f32[2,256,512]{2,1,0:T(8,128)} %get-tuple-element.20.g_tile, f32[2,512,256]{2,1,0:T(8,128)} %copy-done, f32[2,256,512]{2,1,0:T(8,128)} %copy-done.3), custom_call_target="tpu_custom_call" | custom-call | flops 1000000 | bytes 6000000 | tf_op jit(solution)/shard_map/object_update/pallas_call | solution.py:326
  125.2 2.3 %collective-permute-start.19 = (f32[288,256]{1,0:T(8,128)S(1)}, f32[288,256]{1,0:T(8,128)S(1)}, u32[]{:S(2)}, u32[]{:S(2)}) collective-permute-start(f32[288,256]{1,0:T(8,128)S(1)} %pad_maximum_fusion.1.refs_0_), channel_id=1, source_target_pairs={{0,16},{1,17},{2,18},{3,19},{4,20},{5,21},{6,22},{7,23},{8,24},{9,... | collective-permute-start | bytes 884744 | tf_op jit(solution)/shard_map/ppermute | solution.py:30
  127.5 1.2 collective-permute-start.20
  128.7 6.4 %collective-permute-done.18.refs_1_ = f32[288,256]{1,0:T(8,128)S(1)} collective-permute-done((f32[288,256]{1,0:T(8,128)S(1)}, f32[288,256]{1,0:T(8,128)S(1)}, u32[]{:S(2)}, u32[]{:S(2)}) %collective-permute-start.18) | collective-permute-done | bytes 294944 | tf_op jit(solution)/shard_map/ppermute | solution.py:30
  135.1 0.5 collective-permute-start.23
  135.6 4.9 %collective-permute-done.20.refs_3_ = f32[288,256]{1,0:T(8,128)S(1)} collective-permute-done((f32[288,256]{1,0:T(8,128)S(1)}, f32[288,256]{1,0:T(8,128)S(1)}, u32[]{:S(2)}, u32[]{:S(2)}) %collective-permute-start.20) | collective-permute-done | bytes 294944 | tf_op jit(solution)/shard_map/ppermute | solution.py:30
  140.5 1.5 %collective-permute-done.24.refs_7_ = f32[288,256]{1,0:T(8,128)S(1)} collective-permute-done((f32[288,256]{1,0:T(8,128)S(1)}, f32[288,256]{1,0:T(8,128)S(1)}, u32[]{:S(2)}, u32[]{:S(2)}) %collective-permute-start.24) | collective-permute-done | bytes 294944 | tf_op jit(solution)/shard_map/ppermute | solution.py:30
  142.1 0.7 copy-done.10
  142.8 4.2 %probe_update.1 = f32[2,4,256,256]{3,2,1,0:T(8,128)} custom-call(f32[2,4,256,256]{3,2,1,0:T(8,128)} %probe_ref.5, f32[288,256]{1,0:T(8,128)} %copy-done.1, f32[288,256]{1,0:T(8,128)} %copy-done.4, f32[288,256]{1,0:T(8,128)} %copy-done.5, f32[288,256]{1,0:T(8,128)} %copy-done.6, f32[288,256]{1,0:T(8,128)} %copy-done.7, f32[288,256]{1,0:T(8,128)} %copy-done.8, ...), custom_call_target="tpu_custom_call" | custom-call | flops 1000000 | bytes 6000000 | tf_op jit(solution)/shard_map/probe_update/pallas_call | solution.py:338
  (58 shorter events, 0.2 us)
Async XLA Ops:
  0.6 38.7 %collective-permute-start = (f32[2,256,512]{2,1,0:T(8,128)}, f32[2,256,512]{2,1,0:T(8,128)S(1)}, u32[]{:S(2)}, u32[]{:S(2)}) collective-permute-start(f32[2,256,512]{2,1,0:T(8,128)} %tile_ref.3), channel_id=1, source_target_pairs={{4,0},{5,1},{6,2},{7,3},{8,4},{9,5},{10,6},{11,7},{12,8},{13,9},{1... | collective-permute-start | bytes 3145736 | tf_op jit(solution)/shard_map/ppermute | solution.py:24
  3.0 17.3 %collective-permute-start.1 = (f32[2,256,256]{2,1,0:T(8,128)S(1)}, f32[2,256,256]{2,1,0:T(8,128)S(1)}, u32[]{:S(2)}, u32[]{:S(2)}) collective-permute-start(f32[2,256,256]{2,1,0:T(8,128)S(1)} %slice.24), channel_id=1, source_target_pairs={{1,0},{2,1},{3,2},{5,4},{6,5},{7,6},{9,8},{10,9},{11,10},{13,12},{... | collective-permute-start | bytes 1572872 | tf_op jit(solution)/shard_map/ppermute | solution.py:24
  20.4 19.0 %copy-start.16 = (f32[2,256,256]{2,1,0:T(8,128)}, f32[2,256,256]{2,1,0:T(8,128)S(1)}, u32[]{:S(2)}) copy-start(f32[2,256,256]{2,1,0:T(8,128)S(1)} %collective-permute-done.1.right_ref) | copy-start | bytes 1572868
  20.4 19.0 %collective-permute-start.2 = (f32[2,256,256]{2,1,0:T(8,128)S(1)}, f32[2,256,256]{2,1,0:T(8,128)S(1)}, u32[]{:S(2)}, u32[]{:S(2)}) collective-permute-start(f32[2,256,256]{2,1,0:T(8,128)S(1)} %collective-permute-done.1.right_ref), channel_id=1, source_target_pairs={{4,0},{5,1},{6,2},{7,3},{8,4},{9,5},{10,6},{11,7},{12,8},{13,9},{1... | collective-permute-start | bytes 1572872 | tf_op jit(solution)/shard_map/ppermute | solution.py:24
  22.4 12.8 %copy-start.11 = (s32[6,2]{1,0:T(8,128)}, s32[6,2]{1,0:T(8,128)S(1)}, u32[]{:S(2)}) copy-start(s32[6,2]{1,0:T(8,128)S(1)} %copy.17.spots_ref) | copy-start | bytes 148
  22.4 12.7 %collective-permute-start.3 = (s32[6,2]{1,0:T(8,128)S(1)}, s32[6,2]{1,0:T(8,128)S(1)}, u32[]{:S(2)}, u32[]{:S(2)}) collective-permute-start(s32[6,2]{1,0:T(8,128)S(1)} %copy.17.spots_ref), channel_id=1, source_target_pairs={{0,4},{1,5},{2,6},{3,7},{4,8},{5,9},{6,10},{7,11},{8,12},{9,13},{1... | collective-permute-start | bytes 152 | tf_op jit(solution)/shard_map/ppermute | solution.py:24
  25.4 9.7 %collective-permute-start.4 = (s32[6,2]{1,0:T(8,128)S(1)}, s32[6,2]{1,0:T(8,128)S(1)}, u32[]{:S(2)}, u32[]{:S(2)}) collective-permute-start(s32[6,2]{1,0:T(8,128)S(1)} %copy.17.spots_ref), channel_id=1, source_target_pairs={{0,1},{1,2},{2,3},{4,5},{5,6},{6,7},{8,9},{9,10},{10,11},{12,13},{... | collective-permute-start | bytes 152 | tf_op jit(solution)/shard_map/ppermute | solution.py:24
  29.6 5.6 %collective-permute-start.5 = (s32[6,2]{1,0:T(8,128)S(1)}, s32[6,2]{1,0:T(8,128)S(1)}, u32[]{:S(2)}, u32[]{:S(2)}) collective-permute-start(s32[6,2]{1,0:T(8,128)S(1)} %copy.17.spots_ref), channel_id=1, source_target_pairs={{0,5},{1,6},{2,7},{4,9},{5,10},{6,11},{8,13},{9,14},{10,15},{12,17... | collective-permute-start | bytes 152 | tf_op jit(solution)/shard_map/ppermute | solution.py:24
  35.2 0.6 copy-start.12
  35.2 0.6 copy-start.13
  35.8 0.6 copy-start.14
  39.4 1.0 copy-start.15
  39.4 1.1 copy-start.17
  50.7 22.9 %collective-permute-start.6 = (f32[1184,256]{1,0:T(8,128)}, f32[1184,256]{1,0:T(8,128)S(1)}, u32[]{:S(2)}, u32[]{:S(2)}) collective-permute-start(f32[1184,256]{1,0:T(8,128)} %get-tuple-element.15), channel_id=1, source_target_pairs={{0,4},{1,5},{2,6},{3,7},{4,0},{5,1},{6,2},{7,3},{8,12},{9,13},{10,... | collective-permute-start | bytes 3637256 | tf_op jit(solution)/shard_map/ppermute | solution.py:30
  65.8 30.5 %collective-permute-start.10 = (f32[2,512,256]{2,1,0:T(8,128)}, f32[2,512,256]{2,1,0:T(8,128)S(1)}, u32[]{:S(2)}, u32[]{:S(2)}) collective-permute-start(f32[2,512,256]{2,1,0:T(8,128)} %get-tuple-element.17), channel_id=1, source_target_pairs={{0,1},{1,2},{2,3},{4,5},{5,6},{6,7},{8,9},{9,10},{10,11},{12,13},{... | collective-permute-start | bytes 3145736 | tf_op jit(solution)/shard_map/ppermute | solution.py:24
  73.5 22.8 %copy-start.2 = (f32[2,256,512]{2,1,0:T(8,128)S(1)}, f32[2,256,512]{2,1,0:T(8,128)}, u32[]{:S(2)}) copy-start(f32[2,256,512]{2,1,0:T(8,128)} %get-tuple-element.16) | copy-start | bytes 3145732
  75.1 22.3 %collective-permute-start.9 = (f32[296,256]{1,0:T(8,128)S(1)}, f32[296,256]{1,0:T(8,128)S(1)}, u32[]{:S(2)}, u32[]{:S(2)}) collective-permute-start(f32[296,256]{1,0:T(8,128)S(1)} %get-tuple-element.25), channel_id=1, source_target_pairs={{0,24},{1,25},{2,26},{3,27},{4,28},{5,29},{6,30},{7,31},{8,16},{9,... | collective-permute-start | bytes 909320 | tf_op jit(solution)/shard_map/ppermute | solution.py:30
  77.3 20.2 %collective-permute-start.8 = (f32[296,256]{1,0:T(8,128)S(1)}, f32[296,256]{1,0:T(8,128)S(1)}, u32[]{:S(2)}, u32[]{:S(2)}) collective-permute-start(f32[296,256]{1,0:T(8,128)S(1)} %get-tuple-element.26), channel_id=1, source_target_pairs={{0,16},{1,17},{2,18},{3,19},{4,20},{5,21},{6,22},{7,23},{8,24},{9,... | collective-permute-start | bytes 909320 | tf_op jit(solution)/shard_map/ppermute | solution.py:30
  77.3 20.2 %collective-permute-start.7 = (f32[296,256]{1,0:T(8,128)S(1)}, f32[296,256]{1,0:T(8,128)S(1)}, u32[]{:S(2)}, u32[]{:S(2)}) collective-permute-start(f32[296,256]{1,0:T(8,128)S(1)} %get-tuple-element.24), channel_id=1, source_target_pairs={{0,8},{1,9},{2,10},{3,11},{4,12},{5,13},{6,14},{7,15},{8,0},{9,1},... | collective-permute-start | bytes 909320 | tf_op jit(solution)/shard_map/ppermute | solution.py:30
  96.3 1.0 copy-start
  98.6 21.8 %collective-permute-start.17 = (f32[2,256,512]{2,1,0:T(8,128)S(1)}, f32[2,256,512]{2,1,0:T(8,128)S(1)}, u32[]{:S(2)}, u32[]{:S(2)}) collective-permute-start(f32[2,256,512]{2,1,0:T(8,128)S(1)} %pad_maximum_fusion), channel_id=1, source_target_pairs={{0,4},{1,5},{2,6},{3,7},{4,8},{5,9},{6,10},{7,11},{8,12},{9,13},{1... | collective-permute-start | bytes 3145736 | tf_op jit(solution)/shard_map/ppermute | solution.py:24
  100.1 7.2 %collective-permute-start.13 = (f32[80,256]{1,0:T(8,128)S(1)}, f32[80,256]{1,0:T(8,128)S(1)}, u32[]{:S(2)}, u32[]{:S(2)}) collective-permute-start(f32[80,256]{1,0:T(8,128)S(1)} %get-tuple-element.35), channel_id=1, source_target_pairs={{0,3},{1,2},{2,1},{3,0},{4,7},{5,6},{6,5},{7,4},{8,11},{9,10},{10,... | collective-permute-start | bytes 245768 | tf_op jit(solution)/shard_map/ppermute | solution.py:30
  100.2 11.2 %collective-permute-start.12 = (f32[80,256]{1,0:T(8,128)S(1)}, f32[80,256]{1,0:T(8,128)S(1)}, u32[]{:S(2)}, u32[]{:S(2)}) collective-permute-start(f32[80,256]{1,0:T(8,128)S(1)} %get-tuple-element.34), channel_id=1, source_target_pairs={{0,2},{1,3},{2,0},{3,1},{4,6},{5,7},{6,4},{7,5},{8,10},{9,11},{10,... | collective-permute-start | bytes 245768 | tf_op jit(solution)/shard_map/ppermute | solution.py:30
  104.0 7.3 %collective-permute-start.11 = (f32[80,256]{1,0:T(8,128)S(1)}, f32[80,256]{1,0:T(8,128)S(1)}, u32[]{:S(2)}, u32[]{:S(2)}) collective-permute-start(f32[80,256]{1,0:T(8,128)S(1)} %get-tuple-element.33), channel_id=1, source_target_pairs={{0,1},{1,0},{2,3},{3,2},{4,5},{5,4},{6,7},{7,6},{8,9},{9,8},{10,11... | collective-permute-start | bytes 245768 | tf_op jit(solution)/shard_map/ppermute | solution.py:30
  111.5 7.1 %collective-permute-start.16 = (f32[72,256]{1,0:T(8,128)S(1)}, f32[72,256]{1,0:T(8,128)S(1)}, u32[]{:S(2)}, u32[]{:S(2)}) collective-permute-start(f32[72,256]{1,0:T(8,128)S(1)} %slice.32), channel_id=1, source_target_pairs={{0,3},{1,2},{2,1},{3,0},{4,7},{5,6},{6,5},{7,4},{8,11},{9,10},{10,... | collective-permute-start | bytes 221192 | tf_op jit(solution)/shard_map/ppermute | solution.py:30
  112.8 7.6 %collective-permute-start.15 = (f32[72,256]{1,0:T(8,128)S(1)}, f32[72,256]{1,0:T(8,128)S(1)}, u32[]{:S(2)}, u32[]{:S(2)}) collective-permute-start(f32[72,256]{1,0:T(8,128)S(1)} %slice.32), channel_id=1, source_target_pairs={{0,2},{1,3},{2,0},{3,1},{4,6},{5,7},{6,4},{7,5},{8,10},{9,11},{10,... | collective-permute-start | bytes 221192 | tf_op jit(solution)/shard_map/ppermute | solution.py:30
  112.8 7.6 %collective-permute-start.14 = (f32[72,256]{1,0:T(8,128)S(1)}, f32[72,256]{1,0:T(8,128)S(1)}, u32[]{:S(2)}, u32[]{:S(2)}) collective-permute-start(f32[72,256]{1,0:T(8,128)S(1)} %slice.32), channel_id=1, source_target_pairs={{0,1},{1,0},{2,3},{3,2},{4,5},{5,4},{6,7},{7,6},{8,9},{9,8},{10,11... | collective-permute-start | bytes 221192 | tf_op jit(solution)/shard_map/ppermute | solution.py:30
  120.4 8.2 %copy-start.1 = (f32[288,256]{1,0:T(8,128)}, f32[288,256]{1,0:T(8,128)S(1)}, u32[]{:S(2)}) copy-start(f32[288,256]{1,0:T(8,128)S(1)} %pad_maximum_fusion.1.refs_0_) | copy-start | bytes 884740
  120.4 1.0 copy-start.3
  125.2 9.9 %collective-permute-start.18 = (f32[288,256]{1,0:T(8,128)S(1)}, f32[288,256]{1,0:T(8,128)S(1)}, u32[]{:S(2)}, u32[]{:S(2)}) collective-permute-start(f32[288,256]{1,0:T(8,128)S(1)} %pad_maximum_fusion.1.refs_0_), channel_id=1, source_target_pairs={{0,8},{1,9},{2,10},{3,11},{4,12},{5,13},{6,14},{7,15},{8,0},{9,1},... | collective-permute-start | bytes 884744 | tf_op jit(solution)/shard_map/ppermute | solution.py:30
  125.2 9.9 %collective-permute-start.19 = (f32[288,256]{1,0:T(8,128)S(1)}, f32[288,256]{1,0:T(8,128)S(1)}, u32[]{:S(2)}, u32[]{:S(2)}) collective-permute-start(f32[288,256]{1,0:T(8,128)S(1)} %pad_maximum_fusion.1.refs_0_), channel_id=1, source_target_pairs={{0,16},{1,17},{2,18},{3,19},{4,20},{5,21},{6,22},{7,23},{8,24},{9,... | collective-permute-start | bytes 884744 | tf_op jit(solution)/shard_map/ppermute | solution.py:30
  127.5 13.0 %collective-permute-start.20 = (f32[288,256]{1,0:T(8,128)S(1)}, f32[288,256]{1,0:T(8,128)S(1)}, u32[]{:S(2)}, u32[]{:S(2)}) collective-permute-start(f32[288,256]{1,0:T(8,128)S(1)} %pad_maximum_fusion.1.refs_0_), channel_id=1, source_target_pairs={{0,24},{1,25},{2,26},{3,27},{4,28},{5,29},{6,30},{7,31},{8,16},{9,... | collective-permute-start | bytes 884744 | tf_op jit(solution)/shard_map/ppermute | solution.py:30
  128.7 11.8 %collective-permute-start.21 = (f32[288,256]{1,0:T(8,128)S(1)}, f32[288,256]{1,0:T(8,128)S(1)}, u32[]{:S(2)}, u32[]{:S(2)}) collective-permute-start(f32[288,256]{1,0:T(8,128)S(1)} %pad_maximum_fusion.1.refs_0_), channel_id=1, source_target_pairs={{0,4},{1,5},{2,6},{3,7},{4,0},{5,1},{6,2},{7,3},{8,12},{9,13},{10,... | collective-permute-start | bytes 884744 | tf_op jit(solution)/shard_map/ppermute | solution.py:30
  135.0 7.0 %copy-start.4 = (f32[288,256]{1,0:T(8,128)}, f32[288,256]{1,0:T(8,128)S(1)}, u32[]{:S(2)}) copy-start(f32[288,256]{1,0:T(8,128)S(1)} %collective-permute-done.18.refs_1_) | copy-start | bytes 884740
  135.0 5.4 %collective-permute-start.22 = (f32[288,256]{1,0:T(8,128)S(1)}, f32[288,256]{1,0:T(8,128)S(1)}, u32[]{:S(2)}, u32[]{:S(2)}) collective-permute-start(f32[288,256]{1,0:T(8,128)S(1)} %collective-permute-done.18.refs_1_), channel_id=1, source_target_pairs={{0,4},{1,5},{2,6},{3,7},{4,0},{5,1},{6,2},{7,3},{8,12},{9,13},{10,... | collective-permute-start | bytes 884744 | tf_op jit(solution)/shard_map/ppermute | solution.py:30
  135.0 7.0 %copy-start.5 = (f32[288,256]{1,0:T(8,128)}, f32[288,256]{1,0:T(8,128)S(1)}, u32[]{:S(2)}) copy-start(f32[288,256]{1,0:T(8,128)S(1)} %collective-permute-done.19.refs_2_) | copy-start | bytes 884740
  135.1 5.4 %collective-permute-start.23 = (f32[288,256]{1,0:T(8,128)S(1)}, f32[288,256]{1,0:T(8,128)S(1)}, u32[]{:S(2)}, u32[]{:S(2)}) collective-permute-start(f32[288,256]{1,0:T(8,128)S(1)} %collective-permute-done.19.refs_2_), channel_id=1, source_target_pairs={{0,4},{1,5},{2,6},{3,7},{4,0},{5,1},{6,2},{7,3},{8,12},{9,13},{10,... | collective-permute-start | bytes 884744 | tf_op jit(solution)/shard_map/ppermute | solution.py:30
  140.4 1.6 %copy-start.6 = (f32[288,256]{1,0:T(8,128)}, f32[288,256]{1,0:T(8,128)S(1)}, u32[]{:S(2)}) copy-start(f32[288,256]{1,0:T(8,128)S(1)} %collective-permute-done.20.refs_3_) | copy-start | bytes 884740
  140.4 1.6 %collective-permute-start.24 = (f32[288,256]{1,0:T(8,128)S(1)}, f32[288,256]{1,0:T(8,128)S(1)}, u32[]{:S(2)}, u32[]{:S(2)}) collective-permute-start(f32[288,256]{1,0:T(8,128)S(1)} %collective-permute-done.20.refs_3_), channel_id=1, source_target_pairs={{0,4},{1,5},{2,6},{3,7},{4,0},{5,1},{6,2},{7,3},{8,12},{9,13},{10,... | collective-permute-start | bytes 884744 | tf_op jit(solution)/shard_map/ppermute | solution.py:30
  140.5 1.6 %copy-start.7 = (f32[288,256]{1,0:T(8,128)}, f32[288,256]{1,0:T(8,128)S(1)}, u32[]{:S(2)}) copy-start(f32[288,256]{1,0:T(8,128)S(1)} %collective-permute-done.21.refs_4_) | copy-start | bytes 884740
  140.5 1.6 %copy-start.8 = (f32[288,256]{1,0:T(8,128)}, f32[288,256]{1,0:T(8,128)S(1)}, u32[]{:S(2)}) copy-start(f32[288,256]{1,0:T(8,128)S(1)} %collective-permute-done.22.refs_5_) | copy-start | bytes 884740
  140.5 1.6 %copy-start.9 = (f32[288,256]{1,0:T(8,128)}, f32[288,256]{1,0:T(8,128)S(1)}, u32[]{:S(2)}) copy-start(f32[288,256]{1,0:T(8,128)S(1)} %collective-permute-done.23.refs_6_) | copy-start | bytes 884740
  142.1 0.7 copy-start.10

commit v4 on v3

--- a/solution.py
+++ b/solution.py
@@ -11,7 +11,7 @@
 
 LANES = 128
 SUBLANES = 8
-VMEM_LIMIT = 56 * 1024 * 1024
+MIB = 1024 * 1024
 
 
 def shifted(value, d_row, d_col):
@@ -36,14 +36,19 @@
     scale = 1.0 / math.sqrt(side)
     re = (np.cos(angle) * scale).astype(np.float32)
     im = (-np.sin(angle) * scale).astype(np.float32)
-
-    def left(im):
-        return np.block([[re, -im], [im, re]])
-
-    def right(im):
-        return np.block([[re, im], [-im, re]])
-
-    return [jnp.asarray(t, jnp.bfloat16) for t in (left(im), right(im), left(-im), right(-im))]
+    blocks = []
+    for first in (0, 1):
+        a, b = re[first::2, :side // 2], im[first::2, :side // 2]
+        blocks.append(np.block([[a, -b], [b, a]]))
+    return jnp.asarray(np.stack(blocks + [block.T for block in blocks]), jnp.bfloat16)
+
+
+def evens_first(amplitudes):
+    side = amplitudes.shape[-1]
+    order = np.concatenate([np.arange(0, side, 2), np.arange(1, side, 2)])
+    pick = jnp.asarray(np.eye(side)[order], jnp.float32)
+    rows = jnp.einsum("ab,sbc->sac", pick, amplitudes, precision=lax.Precision.HIGHEST)
+    return jnp.einsum("sac,dc->sad", rows, pick, precision=lax.Precision.HIGHEST)
 
 
 def corner_of(row, col):
@@ -88,33 +93,35 @@
 
 
 def main_kernel(
-    counts_ref, spots_ref, tile_ref, below_ref, right_ref, corner_ref, amp_ref, probe_ref, top_ref,
-    lf_ref, rf_ref, lg_ref, rg_ref,
+    counts_ref, spots_ref, tile_ref, below_ref, right_ref, corner_ref, amp_ref, probe_ref, top_ref, table_ref,
     g_tile, g_below, g_side, mine_ref, other_ref,
-    ext, gacc, stage, turned, wave, wins, sums,
+    ext, gacc, stage, turned, wave, wins, sums, in_sem, out_sem,
 ):
     modes, side = probe_ref.shape[1], probe_ref.shape[2]
     rows, cols = tile_ref.shape[1], tile_ref.shape[2]
+    low = side // 2
     my_row, my_col = lax.axis_index("row"), lax.axis_index("col")
-    ext[:, :rows, :cols] = tile_ref[...]
-    ext[:, rows:, :cols] = below_ref[...]
-    ext[:, :rows, cols:] = right_ref[...]
-    ext[:, rows:, cols:] = corner_ref[...]
+    loads = [
+        pltpu.make_async_copy(ref, ext.at[:, pl.ds(r, ref.shape[1]), pl.ds(c, ref.shape[2])], in_sem.at[i])
+        for i, (ref, r, c) in enumerate(
+            ((tile_ref, 0, 0), (below_ref, rows, 0), (right_ref, 0, cols), (corner_ref, rows, cols))
+        )
+    ]
+    for load in loads:
+        load.start()
     gacc[...] = jnp.zeros_like(gacc)
     sums[...] = jnp.zeros_like(sums)
+    for load in loads:
+        load.wait()
 
     def dot(a, b):
         return jnp.dot(a, b, preferred_element_type=jnp.float32)
 
-    def transform(left_ref, right_ref):
-        for k in range(modes):
-            got = dot(left_ref[...], stage[:, k * side:(k + 1) * side])
-            turned[k * side:(k + 1) * side, :side] = got[:side].astype(jnp.bfloat16)
-            turned[k * side:(k + 1) * side, side:] = got[side:].astype(jnp.bfloat16)
-        wave[...] = dot(turned[...], right_ref[...])
-
     def plane(index):
         return slice(index * side, (index + 1) * side)
+
+    def bf16(value):
+        return value.astype(jnp.bfloat16)
 
     def step(p, carry):
         row, col = spots_ref[p, 0] - my_row * rows, spots_ref[p, 1] - my_col * cols
@@ -124,46 +131,86 @@
         sums[plane(2 * modes)] += win_re * win_re + win_im * win_im
         for k in range(modes):
             pr, pi = probe_ref[0, k], probe_ref[1, k]
-            stage[:side, plane(k)] = (pr * win_re - pi * win_im).astype(jnp.bfloat16)
-            stage[side:, plane(k)] = (pr * win_im + pi * win_re).astype(jnp.bfloat16)
-        transform(lf_ref, rf_ref)
-        model = jnp.zeros((side, side), jnp.float32)
+            for i, psi in enumerate((pr * win_re - pi * win_im, pr * win_im + pi * win_re)):
+                stage[0, i * low:(i + 1) * low, plane(k)] = bf16(psi[:low] + psi[low:])
+                stage[1, i * low:(i + 1) * low, plane(k)] = bf16(psi[:low] - psi[low:])
         for k in range(modes):
-            wr, wi = wave[plane(k), :side], wave[plane(k), side:]
-            model += wr * wr + wi * wi
-        factor = amp_ref[p] * lax.rsqrt(jnp.maximum(model, 1.0)) - 1.0
+            for parity in range(2):
+                half = dot(table_ref[parity], stage[parity, :, plane(k)])
+                at = k * side + parity * low
+                for i in range(2):
+                    left, right = half[i * low:(i + 1) * low, :low], half[i * low:(i + 1) * low, low:]
+                    turned[0, at:at + low, i * low:(i + 1) * low] = bf16(left + right)
+                    turned[1, at:at + low, i * low:(i + 1) * low] = bf16(left - right)
+        for parity in range(2):
+            wave[parity] = dot(turned[parity], table_ref[2 + parity])
+        for parity in range(2):
+            model = jnp.zeros((side, low), jnp.float32)
+            for k in range(modes):
+                wr, wi = wave[parity, plane(k), :low], wave[parity, plane(k), low:]
+                model += wr * wr + wi * wi
+            factor = amp_ref[p, :, parity * low:(parity + 1) * low] * lax.rsqrt(jnp.maximum(model, 1.0)) - 1.0
+            for k in range(modes):
+                at = k * side + parity * low
+                for i in range(2):
+                    target = bf16(wave[parity, plane(k), i * low:(i + 1) * low] * factor)
+                    stage[0, i * low:(i + 1) * low, at:at + low] = target[:low]
+                    stage[1, i * low:(i + 1) * low, at:at + low] = target[low:]
         for k in range(modes):
-            wr, wi = wave[plane(k), :side], wave[plane(k), side:]
-            stage[:side, plane(k)] = (wr * factor).astype(jnp.bfloat16)
-            stage[side:, plane(k)] = (wi * factor).astype(jnp.bfloat16)
-        transform(lg_ref, rg_ref)
-        grad_re = jnp.zeros((side, side), jnp.float32)
-        grad_im = jnp.zeros((side, side), jnp.float32)
-        for k in range(modes):
-            cr, ci = wave[plane(k), :side], wave[plane(k), side:]
-            pr, pi = probe_ref[0, k], probe_ref[1, k]
-            grad_re += pr * cr + pi * ci
-            grad_im += pr * ci - pi * cr
-            sums[plane(k)] += wins[0] * cr + wins[1] * ci
-            sums[plane(modes + k)] += wins[0] * ci - wins[1] * cr
-        add_at(gacc, 0, row, col, grad_re, side)
-        add_at(gacc, 1, row, col, grad_im, side)
+            even = dot(table_ref[2], stage[0, :, plane(k)])
+            odd = dot(table_ref[3], stage[1, :, plane(k)])
+            for lower, back in enumerate((bf16(even + odd), bf16(even - odd))):
+                at = k * side + lower * low
+                for i in range(2):
+                    for parity in range(2):
+                        turned[parity, at:at + low, i * low:(i + 1) * low] = (
+                            back[i * low:(i + 1) * low, parity * low:(parity + 1) * low]
+                        )
+        for parity in range(2):
+            wave[parity] = dot(turned[parity], table_ref[parity])
+        grads = []
+        for lower in range(2):
+            part = slice(lower * low, (lower + 1) * low)
+            grad_re = jnp.zeros((side, low), jnp.float32)
+            grad_im = jnp.zeros((side, low), jnp.float32)
+            win_re, win_im = wins[0, :, part], wins[1, :, part]
+            for k in range(modes):
+                even_re, even_im = wave[0, plane(k), :low], wave[0, plane(k), low:]
+                odd_re, odd_im = wave[1, plane(k), :low], wave[1, plane(k), low:]
+                if lower:
+                    cr, ci = even_re - odd_re, even_im - odd_im
+                else:
+                    cr, ci = even_re + odd_re, even_im + odd_im
+                pr, pi = probe_ref[0, k, :, part], probe_ref[1, k, :, part]
+                grad_re += pr * cr + pi * ci
+                grad_im += pr * ci - pi * cr
+                sums[plane(k), part] += win_re * cr + win_im * ci
+                sums[plane(modes + k), part] += win_re * ci - win_im * cr
+            grads.append((grad_re, grad_im))
+        for i in range(2):
+            add_at(gacc, i, row, col, jnp.concatenate([grads[0][i], grads[1][i]], axis=1), side)
         return carry
 
     lax.fori_loop(0, counts_ref[my_row, my_col], step, 0)
-    g_tile[...] = gacc[:, :rows, :cols]
-    g_below[...] = gacc[:, rows:, :cols]
-    g_side[...] = gacc[:, :, cols:]
+
     pairs = lax.axis_size("row") // 2
     share = mine_ref.shape[0] // pairs - SUBLANES
-    half = share * pairs
     core = lax.rem(my_row, 2)
-    for ref, base in ((mine_ref, core * half), (other_ref, (1 - core) * half)):
+    stores = []
+    for ref, base in ((other_ref, (1 - core) * (share * pairs)), (mine_ref, core * (share * pairs))):
         base = pl.multiple_of(base, SUBLANES)
         for j in range(pairs):
             at = j * (share + SUBLANES)
-            ref[at:at + share] = sums[pl.ds(base + j * share, share)]
-            ref[at + share:at + share + SUBLANES] = top_ref[...]
+            stores.append((sums.at[pl.ds(base + j * share, share)], ref.at[pl.ds(at, share)]))
+            stores.append((top_ref, ref.at[pl.ds(at + share, SUBLANES)]))
+    stores.append((gacc.at[:, :, pl.ds(cols, side)], g_side))
+    stores.append((gacc.at[:, pl.ds(0, rows), pl.ds(0, cols)], g_tile))
+    stores.append((gacc.at[:, pl.ds(rows, side), pl.ds(0, cols)], g_below))
+    stores = [pltpu.make_async_copy(a, b, out_sem.at[i]) for i, (a, b) in enumerate(stores)]
+    for store in stores:
+        store.start()
+    for store in stores:
+        store.wait()
 
 
 def light_kernel(counts_ref, spots_ref, up_ref, left_ref, diag_ref, probe_ref, light_ref, top_ref, lit, acc):
@@ -240,7 +287,11 @@
 
 VM = pl.BlockSpec(memory_space=pltpu.VMEM)
 SM = pl.BlockSpec(memory_space=pltpu.SMEM)
-PARAMS = pltpu.CompilerParams(vmem_limit_bytes=VMEM_LIMIT)
+ANY = pl.BlockSpec(memory_space=pl.ANY)
+
+
+def params(mib):
+    return pltpu.CompilerParams(vmem_limit_bytes=mib * MIB)
 
 
 def cost(flops, moved):
@@ -263,8 +314,6 @@
     from_left = shifted(spots, 0, 1)
     from_diag = shifted(spots, 1, 1)
     below = shifted(object_field[:, :side, :], -1, 0)
-    corner = shifted(right[:, :side, :], -1, 0)
-
     light, top = pl.pallas_call(
         light_kernel,
         out_shape=(f32(rows, cols), f32(SUBLANES, side)),
@@ -274,32 +323,36 @@
             pltpu.VMEM((side, side), jnp.float32),
             pltpu.VMEM((1, rows + 2 * side, cols + 2 * side), jnp.float32),
         ],
-        compiler_params=PARAMS,
+        compiler_params=params(12),
         cost_estimate=cost(10**8, 10**7),
         name="lighting",
     )(counts, spots, from_up, from_left, from_diag, probe)
 
+    right, light = lax.optimization_barrier((right, light))
+    corner = shifted(right[:, :side, :], -1, 0)
     g_tile, g_below, g_side, mine, other = pl.pallas_call(
         main_kernel,
         out_shape=(
             f32(2, rows, cols), f32(2, side, cols), f32(2, rows + side, side),
             f32(pairs * (share + SUBLANES), side), f32(pairs * (share + SUBLANES), side),
         ),
-        in_specs=[SM] * 2 + [VM] * 11,
-        out_specs=(VM,) * 5,
+        in_specs=[SM] * 2 + [ANY] * 4 + [VM] * 4,
+        out_specs=(ANY,) * 5,
         scratch_shapes=[
             pltpu.VMEM((2, rows + side, cols + side), jnp.float32),
             pltpu.VMEM((2, rows + side, cols + side), jnp.float32),
-            pltpu.VMEM((2 * side, modes * side), jnp.bfloat16),
-            pltpu.VMEM((modes * side, 2 * side), jnp.bfloat16),
-            pltpu.VMEM((modes * side, 2 * side), jnp.float32),
+            pltpu.VMEM((2, side, modes * side), jnp.bfloat16),
+            pltpu.VMEM((2, modes * side, side), jnp.bfloat16),
+            pltpu.VMEM((2, modes * side, side), jnp.float32),
             pltpu.VMEM((2, side, side), jnp.float32),
             pltpu.VMEM((total_rows, side), jnp.float32),
+            pltpu.SemaphoreType.DMA((4,)),
+            pltpu.SemaphoreType.DMA((4 * pairs + 3,)),
         ],
-        compiler_params=PARAMS,
-        cost_estimate=cost(13 * 10**9, 2 * 10**7),
+        compiler_params=params(28),
+        cost_estimate=cost(7 * 10**9, 2 * 10**7),
         name="positions",
-    )(counts, spots, object_field, below, right, corner, amplitudes[0, 0], probe, top, *tables(side))
+    )(counts, spots, object_field, below, right, corner, evens_first(amplitudes[0, 0]), probe, top, tables(side))
 
     g_left = shifted(g_side, 0, 1)
     arrived = swapped(other, 1, 0)
@@ -328,7 +381,7 @@
         out_shape=f32(2, rows, cols),
         in_specs=[VM] * 6,
         out_specs=VM,
-        compiler_params=PARAMS,
+        compiler_params=params(10),
         cost_estimate=cost(10**6, 6 * 10**6),
         name="object_update",
     )(object_field, light, top, g_tile, g_left, g_up)
@@ -341,7 +394,7 @@
         in_specs=[VM] * (1 + len(blocks)),
         out_specs=VM,
         scratch_shapes=[pltpu.VMEM((total_rows, side), jnp.float32)],
-        compiler_params=PARAMS,
+        compiler_params=params(14),
         cost_estimate=cost(10**6, 6 * 10**6),
         name="probe_update",
     )(probe, *blocks)

time: 147 us -> 137 us (0.932)
  waiting for transfers between devices: 57.1 us -> 42.4 us
  Pallas kernels: 21 us -> 24.1 us
  matrix products: 0 us -> 2.87 us
  starting transfers between devices: 55.8 us -> 53.2 us
    ppermute x8, waiting for transfers between devices: 33.7 us -> 17.6 us  [shifted(): return lax.ppermute(value, ('row', 'col'), pairs)]
    ppermute x17, starting transfers between devices: 31.5 us -> 20.2 us  [swapped(): return lax.ppermute(value, ('row', 'col'), pairs)]
    ppermute x8, starting transfers between devices: 24.3 us -> 33 us  [shifted(): return lax.ppermute(value, ('row', 'col'), pairs)]
    pallas_call x1, Pallas kernels: 10.2 us -> 17.1 us  [body(): pl.pallas_call(main_kernel, out_shape=(f32(2, rows, cols), f32(2, side, c...]
    dot_general x0 -> x2, matrix products: none -> 2.87 us  [the longest x1 1.45 us: evens_first(): jnp.einsum('ab,sbc->sac', pick, amplitudes, precision=lax.Precision.HIGHEST)]
    pallas_call x1, Pallas kernels: 4.15 us -> 1.93 us  [body(): pl.pallas_call(functools.partial(probe_kernel, (pairs, n_col)), out_shape...]
    unnamed x37 -> x27, local copies, waits for them, and re-layouts: 6.29 us -> 5.76 us
  transfers between devices with their start and end apart: 25 -> 25, of which waited for: 9 -> 11; matrix products, arithmetic and copies ran while one was open for 4% -> 6% of each run, Pallas kernels for 2% -> 2%
where the time goes in v4:
time: 137 us; the launch traced here: 136 us
  starting transfers between devices  53.2 us (39%)
  waiting for transfers between devices  42.4 us (31%)
  Pallas kernels  24.1 us (18%)
  local copies, waits for them, and re-layouts  7.77 us (6%)
  other arithmetic  4.47 us (3%)
  matrix products  2.87 us (2%)
    ppermute x8, starting transfers between devices, shifted(): return lax.ppermute(value, ('row', 'col'), pairs)  33 us
    ppermute x17, waiting for transfers between devices, swapped(): return lax.ppermute(value, ('row', 'col'), pairs)  24.8 us
    ppermute x17, starting transfers between devices, swapped(): return lax.ppermute(value, ('row', 'col'), pairs)  20.2 us
    ppermute x8, waiting for transfers between devices, shifted(): return lax.ppermute(value, ('row', 'col'), pairs)  17.6 us
    pallas_call x1, Pallas kernels, body(): pl.pallas_call(main_kernel, out_shape=(f32(2, rows, cols), f32(2, side, c...  17.1 us
    unnamed x27, local copies, waits for them, and re-layouts  5.76 us
    select_n x3, other arithmetic, merge(): jnp.where(summed, a + b, jnp.maximum(a, b))  3.18 us
    pallas_call x1, Pallas kernels, body(): pl.pallas_call(finish_kernel, out_shape=f32(2, rows, cols), in_specs=[VM]...  2.74 us
  transfers between devices with their start and end apart: 25, of which 11 were waited for; matrix products, arithmetic and copies ran while one was open for 6% of the time, Pallas kernels for 2%

profile of v4, /device:TPU:0, one launch (start us, length us, event | category | flops | bytes accessed | tf_op | source)
XLA Modules:
  0.0 135.7 jit_solution(2035066076379341737)
XLA Ops:
  0.7 1.2 slice.24
  1.9 1.3 collective-permute-start.1
  3.2 1.3 collective-permute-start
  4.5 0.8 copy.15.spots_ref
  5.2 3.0 %collective-permute-start.2 = (s32[6,2]{1,0:T(8,128)S(1)}, s32[6,2]{1,0:T(8,128)S(1)}, u32[]{:S(2)}, u32[]{:S(2)}) collective-permute-start(s32[6,2]{1,0:T(8,128)S(1)} %copy.15.spots_ref), channel_id=1, source_target_pairs={{0,4},{1,5},{2,6},{3,7},{4,8},{5,9},{6,10},{7,11},{8,12},{9,13},{1... | collective-permute-start | bytes 152 | tf_op jit(solution)/shard_map/ppermute | solution.py:24
  8.3 5.6 %collective-permute-start.3 = (s32[6,2]{1,0:T(8,128)S(1)}, s32[6,2]{1,0:T(8,128)S(1)}, u32[]{:S(2)}, u32[]{:S(2)}) collective-permute-start(s32[6,2]{1,0:T(8,128)S(1)} %copy.15.spots_ref), channel_id=1, source_target_pairs={{0,1},{1,2},{2,3},{4,5},{5,6},{6,7},{8,9},{9,10},{10,11},{12,13},{... | collective-permute-start | bytes 152 | tf_op jit(solution)/shard_map/ppermute | solution.py:24
  13.8 4.4 %collective-permute-start.4 = (s32[6,2]{1,0:T(8,128)S(1)}, s32[6,2]{1,0:T(8,128)S(1)}, u32[]{:S(2)}, u32[]{:S(2)}) collective-permute-start(s32[6,2]{1,0:T(8,128)S(1)} %copy.15.spots_ref), channel_id=1, source_target_pairs={{0,5},{1,6},{2,7},{4,9},{5,10},{6,11},{8,13},{9,14},{10,15},{12,17... | collective-permute-start | bytes 152 | tf_op jit(solution)/shard_map/ppermute | solution.py:24
  18.2 0.8 copy.14.counts_ref
  19.0 0.5 collective-permute-done.4.diag_ref
  19.5 1.6 %copy-done.1 = f32[2,4,256,256]{3,2,1,0:T(8,128)S(1)} copy-done((f32[2,4,256,256]{3,2,1,0:T(8,128)S(1)}, f32[2,4,256,256]{3,2,1,0:T(8,128)}, u32[]{:S(2)}) %copy-start.1) | copy-done | bytes 2097176
  21.1 2.3 %lighting.1 = (f32[256,512]{1,0:T(8,128)S(1)}, f32[8,256]{1,0:T(8,128)S(1)}) custom-call(s32[8,4]{1,0:T(8,128)S(1)} %copy.14.counts_ref, s32[6,2]{1,0:T(8,128)S(1)} %copy.15.spots_ref, s32[6,2]{1,0:T(8,128)S(1)} %collective-permute-done.2.up_ref, s32[6,2]{1,0:T(8,128)S(1)} %collective-permute-done.3.left_ref, s32[6,2]{1,0:T(8,128)S(1)} %collective-permute-done.4.diag_ref, ...), custom_call_target="tpu_custom_call" | custom-call | flops 100000000 | bytes 10000000 | tf_op jit(solution)/shard_map/lighting/pallas_call | solution.py:317
  23.4 1.3 collective-permute-start.5
  24.7 1.4 %fusion.2 = f32[256,6,256]{2,0,1:T(8,128)S(1)} fusion(f32[256,256,1]{1,0,2:T(8,128)S(1)} %copy-done.12, f32[1,1,6,256,256]{4,3,2,1,0:T(8,128)S(1)} %copy-done), kind=kOutput, calls=%fused_computation.2 | convolution fusion | flops 1207959552 | bytes 3407872 | tf_op jit(solution)/shard_map/ab,sbc->sac/dot_general | solution.py:50
  26.2 1.4 %fusion.amp_ref = f32[6,256,256]{2,1,0:T(8,128)S(1)} fusion(f32[256,256,1]{1,0,2:T(8,128)S(1)} %copy-done.12, f32[256,6,256]{2,0,1:T(8,128)S(1)} %fusion.2), kind=kOutput, calls=%fused_computation | convolution fusion | flops 1207959552 | bytes 3407872 | tf_op jit(solution)/shard_map/sac,dc->sad/dot_general | solution.py:51
  27.7 0.3 copy-done.4
  28.0 17.1 %positions.1 = (f32[2,256,512]{2,1,0:T(8,128)S(1)}, f32[2,256,512]{2,1,0:T(8,128)S(1)}, f32[2,512,256]{2,1,0:T(8,128)}, f32[1184,256]{1,0:T(8,128)S(1)}, f32[1184,256]{1,0:T(8,128)}) custom-call(s32[8,4]{1,0:T(8,128)S(1)} %copy.14.counts_ref, s32[6,2]{1,0:T(8,128)S(1)} %copy.15.spots_ref, f32[2,256,512]{2,1,0:T(8,128)S(1)} %copy-done.4, ...), custom_call_target="tpu_custom_call" | custom-call | flops 7000000000 | bytes 20000000 | tf_op jit(solution)/shard_map/positions/pallas_call | solution.py:333
  45.1 1.0 copy-done.6
  46.2 1.0 copy-done.7
  47.2 1.0 copy-done.9
  48.1 1.7 %collective-permute-start.6 = (f32[1184,256]{1,0:T(8,128)}, f32[1184,256]{1,0:T(8,128)}, u32[]{:S(2)}, u32[]{:S(2)}) collective-permute-start(f32[1184,256]{1,0:T(8,128)} %get-tuple-element.19), channel_id=1, source_target_pairs={{0,4},{1,5},{2,6},{3,7},{4,0},{5,1},{6,2},{7,3},{8,12},{9,13},{10,... | collective-permute-start | bytes 3637256 | tf_op jit(solution)/shard_map/ppermute | solution.py:30
  49.9 13.9 %collective-permute-start.10 = (f32[2,512,256]{2,1,0:T(8,128)}, f32[2,512,256]{2,1,0:T(8,128)S(1)}, u32[]{:S(2)}, u32[]{:S(2)}) collective-permute-start(f32[2,512,256]{2,1,0:T(8,128)} %get-tuple-element.21), channel_id=1, source_target_pairs={{0,1},{1,2},{2,3},{4,5},{5,6},{6,7},{8,9},{9,10},{10,11},{12,13},{... | collective-permute-start | bytes 3145736 | tf_op jit(solution)/shard_map/ppermute | solution.py:24
  63.8 1.8 %maximum_select_fusion.3 = (f32[296,256]{1,0:T(8,128)S(1)}, f32[296,256]{1,0:T(8,128)S(1)}, f32[296,256]{1,0:T(8,128)S(1)}) fusion(f32[1184,256]{1,0:T(8,128)} %collective-permute-done.6, s32[]{:T(128)S(6)} %select_n.68, f32[1184,256]{1,0:T(8,128)} %copy-done.6, pred[296]{0:T(512)(128)(4,1)S(1)} %iota_compare_fusion, s32[]{:T(128)S(6)} %select_n.74, ...), kind=kLoop, calls=%fused_computation.9 | loop fusion | flops 681984 | bytes 2728244 | tf_op jit(solution)/shard_map/jit(_where)/select_n | solution.py:245
  65.6 2.4 %collective-permute-start.7 = (f32[296,256]{1,0:T(8,128)S(1)}, f32[296,256]{1,0:T(8,128)S(1)}, u32[]{:S(2)}, u32[]{:S(2)}) collective-permute-start(f32[296,256]{1,0:T(8,128)S(1)} %get-tuple-element.28), channel_id=1, source_target_pairs={{0,8},{1,9},{2,10},{3,11},{4,12},{5,13},{6,14},{7,15},{8,0},{9,1},... | collective-permute-start | bytes 909320 | tf_op jit(solution)/shard_map/ppermute | solution.py:30
  68.0 1.5 %collective-permute-start.9 = (f32[296,256]{1,0:T(8,128)S(1)}, f32[296,256]{1,0:T(8,128)S(1)}, u32[]{:S(2)}, u32[]{:S(2)}) collective-permute-start(f32[296,256]{1,0:T(8,128)S(1)} %get-tuple-element.29), channel_id=1, source_target_pairs={{0,24},{1,25},{2,26},{3,27},{4,28},{5,29},{6,30},{7,31},{8,16},{9,... | collective-permute-start | bytes 909320 | tf_op jit(solution)/shard_map/ppermute | solution.py:30
  69.5 17.0 %collective-permute-done.10.g_left = f32[2,512,256]{2,1,0:T(8,128)S(1)} collective-permute-done((f32[2,512,256]{2,1,0:T(8,128)}, f32[2,512,256]{2,1,0:T(8,128)S(1)}, u32[]{:S(2)}, u32[]{:S(2)}) %collective-permute-start.10) | collective-permute-done | bytes 1048608 | tf_op jit(solution)/shard_map/ppermute | solution.py:24
  86.7 1.1 pad_maximum_fusion
  87.8 1.3 maximum_select_fusion
  89.1 2.3 %collective-permute-start.17 = (f32[2,256,512]{2,1,0:T(8,128)}, f32[2,256,512]{2,1,0:T(8,128)}, u32[]{:S(2)}, u32[]{:S(2)}) collective-permute-start(f32[2,256,512]{2,1,0:T(8,128)} %pad_maximum_fusion), channel_id=1, source_target_pairs={{0,4},{1,5},{2,6},{3,7},{4,8},{5,9},{6,10},{7,11},{8,12},{9,13},{1... | collective-permute-start | bytes 3145736 | tf_op jit(solution)/shard_map/ppermute | solution.py:24
  91.4 2.4 %collective-permute-start.11 = (f32[80,256]{1,0:T(8,128)S(1)}, f32[80,256]{1,0:T(8,128)S(1)}, u32[]{:S(2)}, u32[]{:S(2)}) collective-permute-start(f32[80,256]{1,0:T(8,128)S(1)} %get-tuple-element.37), channel_id=1, source_target_pairs={{0,1},{1,0},{2,3},{3,2},{4,5},{5,4},{6,7},{7,6},{8,9},{9,8},{10,11... | collective-permute-start | bytes 245768 | tf_op jit(solution)/shard_map/ppermute | solution.py:30
  93.9 1.8 %collective-permute-start.12 = (f32[80,256]{1,0:T(8,128)S(1)}, f32[80,256]{1,0:T(8,128)S(1)}, u32[]{:S(2)}, u32[]{:S(2)}) collective-permute-start(f32[80,256]{1,0:T(8,128)S(1)} %get-tuple-element.38), channel_id=1, source_target_pairs={{0,2},{1,3},{2,0},{3,1},{4,6},{5,7},{6,4},{7,5},{8,10},{9,11},{10,... | collective-permute-start | bytes 245768 | tf_op jit(solution)/shard_map/ppermute | solution.py:30
  95.6 1.1 collective-permute-start.13
  96.7 2.5 %collective-permute-done.12 = f32[80,256]{1,0:T(8,128)S(1)} collective-permute-done((f32[80,256]{1,0:T(8,128)S(1)}, f32[80,256]{1,0:T(8,128)S(1)}, u32[]{:S(2)}, u32[]{:S(2)}) %collective-permute-start.12) | collective-permute-done | bytes 81952 | tf_op jit(solution)/shard_map/ppermute | solution.py:30
  99.2 3.6 %collective-permute-done.13 = f32[80,256]{1,0:T(8,128)S(1)} collective-permute-done((f32[80,256]{1,0:T(8,128)S(1)}, f32[80,256]{1,0:T(8,128)S(1)}, u32[]{:S(2)}, u32[]{:S(2)}) %collective-permute-start.13) | collective-permute-done | bytes 81952 | tf_op jit(solution)/shard_map/ppermute | solution.py:30
  102.9 2.5 %collective-permute-start.14 = (f32[72,256]{1,0:T(8,128)S(1)}, f32[72,256]{1,0:T(8,128)S(1)}, u32[]{:S(2)}, u32[]{:S(2)}) collective-permute-start(f32[72,256]{1,0:T(8,128)S(1)} %slice.32), channel_id=1, source_target_pairs={{0,1},{1,0},{2,3},{3,2},{4,5},{5,4},{6,7},{7,6},{8,9},{9,8},{10,11... | collective-permute-start | bytes 221192 | tf_op jit(solution)/shard_map/ppermute | solution.py:30
  105.4 1.4 %collective-permute-start.15 = (f32[72,256]{1,0:T(8,128)S(1)}, f32[72,256]{1,0:T(8,128)S(1)}, u32[]{:S(2)}, u32[]{:S(2)}) collective-permute-start(f32[72,256]{1,0:T(8,128)S(1)} %slice.32), channel_id=1, source_target_pairs={{0,2},{1,3},{2,0},{3,1},{4,6},{5,7},{6,4},{7,5},{8,10},{9,11},{10,... | collective-permute-start | bytes 221192 | tf_op jit(solution)/shard_map/ppermute | solution.py:30
  106.8 1.4 %collective-permute-start.16 = (f32[72,256]{1,0:T(8,128)S(1)}, f32[72,256]{1,0:T(8,128)S(1)}, u32[]{:S(2)}, u32[]{:S(2)}) collective-permute-start(f32[72,256]{1,0:T(8,128)S(1)} %slice.32), channel_id=1, source_target_pairs={{0,3},{1,2},{2,1},{3,0},{4,7},{5,6},{6,5},{7,4},{8,11},{9,10},{10,... | collective-permute-start | bytes 221192 | tf_op jit(solution)/shard_map/ppermute | solution.py:30
  108.2 0.2 collective-permute-done.14
  108.4 2.9 %collective-permute-done.15 = f32[72,256]{1,0:T(8,128)S(1)} collective-permute-done((f32[72,256]{1,0:T(8,128)S(1)}, f32[72,256]{1,0:T(8,128)S(1)}, u32[]{:S(2)}, u32[]{:S(2)}) %collective-permute-start.15) | collective-permute-done | bytes 73760 | tf_op jit(solution)/shard_map/ppermute | solution.py:30
  111.3 2.8 %collective-permute-done.16 = f32[72,256]{1,0:T(8,128)S(1)} collective-permute-done((f32[72,256]{1,0:T(8,128)S(1)}, f32[72,256]{1,0:T(8,128)S(1)}, u32[]{:S(2)}, u32[]{:S(2)}) %collective-permute-start.16) | collective-permute-done | bytes 73760 | tf_op jit(solution)/shard_map/ppermute | solution.py:30
  114.2 2.7 %object_update.1 = f32[2,256,512]{2,1,0:T(8,128)} custom-call(f32[2,256,512]{2,1,0:T(8,128)S(1)} %copy-done.5, f32[256,512]{1,0:T(8,128)S(1)} %get-tuple-element.23.light_ref, f32[8,256]{1,0:T(8,128)S(1)} %slice.33.top_ref, f32[2,256,512]{2,1,0:T(8,128)S(1)} %copy-done.10, f32[2,512,256]{2,1,0:T(8,128)S(1)} %collective-permute-done.10.g_left, ...), custom_call_target="tpu_custom_call" | custom-call | flops 1000000 | bytes 6000000 | tf_op jit(solution)/shard_map/object_update/pallas_call | solution.py:379
  116.9 1.5 %collective-permute-start.18 = (f32[288,256]{1,0:T(8,128)S(1)}, f32[288,256]{1,0:T(8,128)S(1)}, u32[]{:S(2)}, u32[]{:S(2)}) collective-permute-start(f32[288,256]{1,0:T(8,128)S(1)} %pad_maximum_fusion.1.refs_0_), channel_id=1, source_target_pairs={{0,8},{1,9},{2,10},{3,11},{4,12},{5,13},{6,14},{7,15},{8,0},{9,1},... | collective-permute-start | bytes 884744 | tf_op jit(solution)/shard_map/ppermute | solution.py:30
  118.4 2.0 %collective-permute-start.20 = (f32[288,256]{1,0:T(8,128)S(1)}, f32[288,256]{1,0:T(8,128)S(1)}, u32[]{:S(2)}, u32[]{:S(2)}) collective-permute-start(f32[288,256]{1,0:T(8,128)S(1)} %pad_maximum_fusion.1.refs_0_), channel_id=1, source_target_pairs={{0,24},{1,25},{2,26},{3,27},{4,28},{5,29},{6,30},{7,31},{8,16},{9,... | collective-permute-start | bytes 884744 | tf_op jit(solution)/shard_map/ppermute | solution.py:30
  120.4 6.4 %collective-permute-done.18.refs_1_ = f32[288,256]{1,0:T(8,128)S(1)} collective-permute-done((f32[288,256]{1,0:T(8,128)S(1)}, f32[288,256]{1,0:T(8,128)S(1)}, u32[]{:S(2)}, u32[]{:S(2)}) %collective-permute-start.18) | collective-permute-done | bytes 294944 | tf_op jit(solution)/shard_map/ppermute | solution.py:30
  126.8 4.9 %collective-permute-done.19.refs_2_ = f32[288,256]{1,0:T(8,128)S(1)} collective-permute-done((f32[288,256]{1,0:T(8,128)S(1)}, f32[288,256]{1,0:T(8,128)S(1)}, u32[]{:S(2)}, u32[]{:S(2)}) %collective-permute-start.19) | collective-permute-done | bytes 294944 | tf_op jit(solution)/shard_map/ppermute | solution.py:30
  131.8 0.5 collective-permute-start.24
  132.3 1.1 collective-permute-done.23.refs_6_
  133.3 0.4 collective-permute-done.24.refs_7_
  133.8 1.9 %probe_update.1 = f32[2,4,256,256]{3,2,1,0:T(8,128)} custom-call(f32[2,4,256,256]{3,2,1,0:T(8,128)S(1)} %copy-done.3, f32[288,256]{1,0:T(8,128)S(1)} %pad_maximum_fusion.1.refs_0_, f32[288,256]{1,0:T(8,128)S(1)} %collective-permute-done.18.refs_1_, f32[288,256]{1,0:T(8,128)S(1)} %collective-permute-done.19.refs_2_, ...), custom_call_target="tpu_custom_call" | custom-call | flops 1000000 | bytes 6000000 | tf_op jit(solution)/shard_map/probe_update/pallas_call | solution.py:391
  (50 shorter events, 0.5 us)
Async XLA Ops:
  0.6 24.0 %copy-start = (f32[1,1,6,256,256]{4,3,2,1,0:T(8,128)S(1)}, f32[1,1,6,256,256]{4,3,2,1,0:T(8,128)}, u32[]{:S(2)}) copy-start(f32[1,1,6,256,256]{4,3,2,1,0:T(8,128)} %param.9) | copy-start | bytes 4718596
  0.6 24.0 %copy-start.12 = (f32[256,256,1]{1,0,2:T(8,128)S(1)}, f32[256,256,1]{1,0,2:T(8,128)}, u32[]{:S(2)}) copy-start(f32[256,256,1]{1,0,2:T(8,128)} %constant.45) | copy-start | bytes 786436
  1.9 21.5 %collective-permute-start.1 = (f32[2,256,256]{2,1,0:T(8,128)S(1)}, f32[2,256,256]{2,1,0:T(8,128)}, u32[]{:S(2)}, u32[]{:S(2)}) collective-permute-start(f32[2,256,256]{2,1,0:T(8,128)S(1)} %slice.24), channel_id=1, source_target_pairs={{1,0},{2,1},{3,2},{5,4},{6,5},{7,6},{9,8},{10,9},{11,10},{13,12},{... | collective-permute-start | bytes 1572872 | tf_op jit(solution)/shard_map/ppermute | solution.py:24
  3.2 24.4 %collective-permute-start = (f32[2,256,512]{2,1,0:T(8,128)}, f32[2,256,512]{2,1,0:T(8,128)}, u32[]{:S(2)}, u32[]{:S(2)}) collective-permute-start(f32[2,256,512]{2,1,0:T(8,128)} %tile_ref.3), channel_id=1, source_target_pairs={{4,0},{5,1},{6,2},{7,3},{8,4},{9,5},{10,6},{11,7},{12,8},{13,9},{1... | collective-permute-start | bytes 3145736 | tf_op jit(solution)/shard_map/ppermute | solution.py:24
  5.2 13.7 %collective-permute-start.2 = (s32[6,2]{1,0:T(8,128)S(1)}, s32[6,2]{1,0:T(8,128)S(1)}, u32[]{:S(2)}, u32[]{:S(2)}) collective-permute-start(s32[6,2]{1,0:T(8,128)S(1)} %copy.15.spots_ref), channel_id=1, source_target_pairs={{0,4},{1,5},{2,6},{3,7},{4,8},{5,9},{6,10},{7,11},{8,12},{9,13},{1... | collective-permute-start | bytes 152 | tf_op jit(solution)/shard_map/ppermute | solution.py:24
  8.3 10.7 %collective-permute-start.3 = (s32[6,2]{1,0:T(8,128)S(1)}, s32[6,2]{1,0:T(8,128)S(1)}, u32[]{:S(2)}, u32[]{:S(2)}) collective-permute-start(s32[6,2]{1,0:T(8,128)S(1)} %copy.15.spots_ref), channel_id=1, source_target_pairs={{0,1},{1,2},{2,3},{4,5},{5,6},{6,7},{8,9},{9,10},{10,11},{12,13},{... | collective-permute-start | bytes 152 | tf_op jit(solution)/shard_map/ppermute | solution.py:24
  13.8 5.7 %collective-permute-start.4 = (s32[6,2]{1,0:T(8,128)S(1)}, s32[6,2]{1,0:T(8,128)S(1)}, u32[]{:S(2)}, u32[]{:S(2)}) collective-permute-start(s32[6,2]{1,0:T(8,128)S(1)} %copy.15.spots_ref), channel_id=1, source_target_pairs={{0,5},{1,6},{2,7},{4,9},{5,10},{6,11},{8,13},{9,14},{10,15},{12,17... | collective-permute-start | bytes 152 | tf_op jit(solution)/shard_map/ppermute | solution.py:24
  19.5 1.6 %copy-start.1 = (f32[2,4,256,256]{3,2,1,0:T(8,128)S(1)}, f32[2,4,256,256]{3,2,1,0:T(8,128)}, u32[]{:S(2)}) copy-start(f32[2,4,256,256]{3,2,1,0:T(8,128)} %probe_ref.5) | copy-start | bytes 6291460
  23.4 4.2 %collective-permute-start.5 = (f32[2,256,256]{2,1,0:T(8,128)}, f32[2,256,256]{2,1,0:T(8,128)S(1)}, u32[]{:S(2)}, u32[]{:S(2)}) collective-permute-start(f32[2,256,256]{2,1,0:T(8,128)} %collective-permute-done.1.right_ref), channel_id=1, source_target_pairs={{4,0},{5,1},{6,2},{7,3},{8,4},{9,5},{10,6},{11,7},{12,8},{13,9},{1... | collective-permute-start | bytes 1572872 | tf_op jit(solution)/shard_map/ppermute | solution.py:24
  24.7 2.9 %copy-start.11 = (bf16[4,256,256]{2,1,0:T(8,128)(2,1)S(1)}, bf16[4,256,256]{2,1,0:T(8,128)(2,1)}, u32[]{:S(2)}) copy-start(bf16[4,256,256]{2,1,0:T(8,128)(2,1)} %constant.42.clone.table_ref) | copy-start | bytes 1572868
  26.1 1.6 %copy-start.2 = (f32[2,4,256,256]{3,2,1,0:T(8,128)S(1)}, f32[2,4,256,256]{3,2,1,0:T(8,128)}, u32[]{:S(2)}) copy-start(f32[2,4,256,256]{3,2,1,0:T(8,128)} %probe_ref.5) | copy-start | bytes 6291460
  26.2 1.8 %copy-start.4 = (f32[2,256,512]{2,1,0:T(8,128)S(1)}, f32[2,256,512]{2,1,0:T(8,128)}, u32[]{:S(2)}) copy-start(f32[2,256,512]{2,1,0:T(8,128)} %tile_ref.3) | copy-start | bytes 3145732
  45.1 1.0 copy-start.6
  46.2 1.0 copy-start.7
  47.2 1.0 copy-start.9
  48.1 15.7 %collective-permute-start.6 = (f32[1184,256]{1,0:T(8,128)}, f32[1184,256]{1,0:T(8,128)}, u32[]{:S(2)}, u32[]{:S(2)}) collective-permute-start(f32[1184,256]{1,0:T(8,128)} %get-tuple-element.19), channel_id=1, source_target_pairs={{0,4},{1,5},{2,6},{3,7},{4,0},{5,1},{6,2},{7,3},{8,12},{9,13},{10,... | collective-permute-start | bytes 3637256 | tf_op jit(solution)/shard_map/ppermute | solution.py:30
  49.9 36.7 %collective-permute-start.10 = (f32[2,512,256]{2,1,0:T(8,128)}, f32[2,512,256]{2,1,0:T(8,128)S(1)}, u32[]{:S(2)}, u32[]{:S(2)}) collective-permute-start(f32[2,512,256]{2,1,0:T(8,128)} %get-tuple-element.21), channel_id=1, source_target_pairs={{0,1},{1,2},{2,3},{4,5},{5,6},{6,7},{8,9},{9,10},{10,11},{12,13},{... | collective-permute-start | bytes 3145736 | tf_op jit(solution)/shard_map/ppermute | solution.py:24
  63.8 22.8 %copy-start.8 = (f32[2,256,512]{2,1,0:T(8,128)S(1)}, f32[2,256,512]{2,1,0:T(8,128)}, u32[]{:S(2)}) copy-start(f32[2,256,512]{2,1,0:T(8,128)} %copy-done.7) | copy-start | bytes 3145732
  65.6 22.2 %collective-permute-start.7 = (f32[296,256]{1,0:T(8,128)S(1)}, f32[296,256]{1,0:T(8,128)S(1)}, u32[]{:S(2)}, u32[]{:S(2)}) collective-permute-start(f32[296,256]{1,0:T(8,128)S(1)} %get-tuple-element.28), channel_id=1, source_target_pairs={{0,8},{1,9},{2,10},{3,11},{4,12},{5,13},{6,14},{7,15},{8,0},{9,1},... | collective-permute-start | bytes 909320 | tf_op jit(solution)/shard_map/ppermute | solution.py:30
  68.0 19.8 %collective-permute-start.8 = (f32[296,256]{1,0:T(8,128)S(1)}, f32[296,256]{1,0:T(8,128)S(1)}, u32[]{:S(2)}, u32[]{:S(2)}) collective-permute-start(f32[296,256]{1,0:T(8,128)S(1)} %get-tuple-element.30), channel_id=1, source_target_pairs={{0,16},{1,17},{2,18},{3,19},{4,20},{5,21},{6,22},{7,23},{8,24},{9,... | collective-permute-start | bytes 909320 | tf_op jit(solution)/shard_map/ppermute | solution.py:30
  68.0 19.8 %collective-permute-start.9 = (f32[296,256]{1,0:T(8,128)S(1)}, f32[296,256]{1,0:T(8,128)S(1)}, u32[]{:S(2)}, u32[]{:S(2)}) collective-permute-start(f32[296,256]{1,0:T(8,128)S(1)} %get-tuple-element.29), channel_id=1, source_target_pairs={{0,24},{1,25},{2,26},{3,27},{4,28},{5,29},{6,30},{7,31},{8,16},{9,... | collective-permute-start | bytes 909320 | tf_op jit(solution)/shard_map/ppermute | solution.py:30
  89.1 25.1 %collective-permute-start.17 = (f32[2,256,512]{2,1,0:T(8,128)}, f32[2,256,512]{2,1,0:T(8,128)}, u32[]{:S(2)}, u32[]{:S(2)}) collective-permute-start(f32[2,256,512]{2,1,0:T(8,128)} %pad_maximum_fusion), channel_id=1, source_target_pairs={{0,4},{1,5},{2,6},{3,7},{4,8},{5,9},{6,10},{7,11},{8,12},{9,13},{1... | collective-permute-start | bytes 3145736 | tf_op jit(solution)/shard_map/ppermute | solution.py:24
  91.4 22.8 %copy-start.5 = (f32[2,256,512]{2,1,0:T(8,128)S(1)}, f32[2,256,512]{2,1,0:T(8,128)}, u32[]{:S(2)}) copy-start(f32[2,256,512]{2,1,0:T(8,128)} %tile_ref.3) | copy-start | bytes 3145732
  91.4 22.8 %copy-start.10 = (f32[2,256,512]{2,1,0:T(8,128)S(1)}, f32[2,256,512]{2,1,0:T(8,128)}, u32[]{:S(2)}) copy-start(f32[2,256,512]{2,1,0:T(8,128)} %copy-done.9) | copy-start | bytes 3145732
  91.4 5.3 %collective-permute-start.11 = (f32[80,256]{1,0:T(8,128)S(1)}, f32[80,256]{1,0:T(8,128)S(1)}, u32[]{:S(2)}, u32[]{:S(2)}) collective-permute-start(f32[80,256]{1,0:T(8,128)S(1)} %get-tuple-element.37), channel_id=1, source_target_pairs={{0,1},{1,0},{2,3},{3,2},{4,5},{5,4},{6,7},{7,6},{8,9},{9,8},{10,11... | collective-permute-start | bytes 245768 | tf_op jit(solution)/shard_map/ppermute | solution.py:30
  93.9 5.4 %collective-permute-start.12 = (f32[80,256]{1,0:T(8,128)S(1)}, f32[80,256]{1,0:T(8,128)S(1)}, u32[]{:S(2)}, u32[]{:S(2)}) collective-permute-start(f32[80,256]{1,0:T(8,128)S(1)} %get-tuple-element.38), channel_id=1, source_target_pairs={{0,2},{1,3},{2,0},{3,1},{4,6},{5,7},{6,4},{7,5},{8,10},{9,11},{10,... | collective-permute-start | bytes 245768 | tf_op jit(solution)/shard_map/ppermute | solution.py:30
  95.6 7.2 %collective-permute-start.13 = (f32[80,256]{1,0:T(8,128)S(1)}, f32[80,256]{1,0:T(8,128)S(1)}, u32[]{:S(2)}, u32[]{:S(2)}) collective-permute-start(f32[80,256]{1,0:T(8,128)S(1)} %get-tuple-element.39), channel_id=1, source_target_pairs={{0,3},{1,2},{2,1},{3,0},{4,7},{5,6},{6,5},{7,4},{8,11},{9,10},{10,... | collective-permute-start | bytes 245768 | tf_op jit(solution)/shard_map/ppermute | solution.py:30
  102.9 5.5 %collective-permute-start.14 = (f32[72,256]{1,0:T(8,128)S(1)}, f32[72,256]{1,0:T(8,128)S(1)}, u32[]{:S(2)}, u32[]{:S(2)}) collective-permute-start(f32[72,256]{1,0:T(8,128)S(1)} %slice.32), channel_id=1, source_target_pairs={{0,1},{1,0},{2,3},{3,2},{4,5},{5,4},{6,7},{7,6},{8,9},{9,8},{10,11... | collective-permute-start | bytes 221192 | tf_op jit(solution)/shard_map/ppermute | solution.py:30
  105.4 5.9 %collective-permute-start.15 = (f32[72,256]{1,0:T(8,128)S(1)}, f32[72,256]{1,0:T(8,128)S(1)}, u32[]{:S(2)}, u32[]{:S(2)}) collective-permute-start(f32[72,256]{1,0:T(8,128)S(1)} %slice.32), channel_id=1, source_target_pairs={{0,2},{1,3},{2,0},{3,1},{4,6},{5,7},{6,4},{7,5},{8,10},{9,11},{10,... | collective-permute-start | bytes 221192 | tf_op jit(solution)/shard_map/ppermute | solution.py:30
  106.8 7.3 %collective-permute-start.16 = (f32[72,256]{1,0:T(8,128)S(1)}, f32[72,256]{1,0:T(8,128)S(1)}, u32[]{:S(2)}, u32[]{:S(2)}) collective-permute-start(f32[72,256]{1,0:T(8,128)S(1)} %slice.32), channel_id=1, source_target_pairs={{0,3},{1,2},{2,1},{3,0},{4,7},{5,6},{6,5},{7,4},{8,11},{9,10},{10,... | collective-permute-start | bytes 221192 | tf_op jit(solution)/shard_map/ppermute | solution.py:30
  114.1 19.6 %copy-start.3 = (f32[2,4,256,256]{3,2,1,0:T(8,128)S(1)}, f32[2,4,256,256]{3,2,1,0:T(8,128)}, u32[]{:S(2)}) copy-start(f32[2,4,256,256]{3,2,1,0:T(8,128)} %probe_ref.5) | copy-start | bytes 6291460
  116.9 9.9 %collective-permute-start.18 = (f32[288,256]{1,0:T(8,128)S(1)}, f32[288,256]{1,0:T(8,128)S(1)}, u32[]{:S(2)}, u32[]{:S(2)}) collective-permute-start(f32[288,256]{1,0:T(8,128)S(1)} %pad_maximum_fusion.1.refs_0_), channel_id=1, source_target_pairs={{0,8},{1,9},{2,10},{3,11},{4,12},{5,13},{6,14},{7,15},{8,0},{9,1},... | collective-permute-start | bytes 884744 | tf_op jit(solution)/shard_map/ppermute | solution.py:30
  118.4 13.4 %collective-permute-start.19 = (f32[288,256]{1,0:T(8,128)S(1)}, f32[288,256]{1,0:T(8,128)S(1)}, u32[]{:S(2)}, u32[]{:S(2)}) collective-permute-start(f32[288,256]{1,0:T(8,128)S(1)} %pad_maximum_fusion.1.refs_0_), channel_id=1, source_target_pairs={{0,16},{1,17},{2,18},{3,19},{4,20},{5,21},{6,22},{7,23},{8,24},{9,... | collective-permute-start | bytes 884744 | tf_op jit(solution)/shard_map/ppermute | solution.py:30
  118.4 13.4 %collective-permute-start.20 = (f32[288,256]{1,0:T(8,128)S(1)}, f32[288,256]{1,0:T(8,128)S(1)}, u32[]{:S(2)}, u32[]{:S(2)}) collective-permute-start(f32[288,256]{1,0:T(8,128)S(1)} %pad_maximum_fusion.1.refs_0_), channel_id=1, source_target_pairs={{0,24},{1,25},{2,26},{3,27},{4,28},{5,29},{6,30},{7,31},{8,16},{9,... | collective-permute-start | bytes 884744 | tf_op jit(solution)/shard_map/ppermute | solution.py:30
  120.4 11.9 %collective-permute-start.21 = (f32[288,256]{1,0:T(8,128)S(1)}, f32[288,256]{1,0:T(8,128)S(1)}, u32[]{:S(2)}, u32[]{:S(2)}) collective-permute-start(f32[288,256]{1,0:T(8,128)S(1)} %pad_maximum_fusion.1.refs_0_), channel_id=1, source_target_pairs={{0,4},{1,5},{2,6},{3,7},{4,0},{5,1},{6,2},{7,3},{8,12},{9,13},{10,... | collective-permute-start | bytes 884744 | tf_op jit(solution)/shard_map/ppermute | solution.py:30
  126.8 5.5 %collective-permute-start.22 = (f32[288,256]{1,0:T(8,128)S(1)}, f32[288,256]{1,0:T(8,128)S(1)}, u32[]{:S(2)}, u32[]{:S(2)}) collective-permute-start(f32[288,256]{1,0:T(8,128)S(1)} %collective-permute-done.18.refs_1_), channel_id=1, source_target_pairs={{0,4},{1,5},{2,6},{3,7},{4,0},{5,1},{6,2},{7,3},{8,12},{9,13},{10,... | collective-permute-start | bytes 884744 | tf_op jit(solution)/shard_map/ppermute | solution.py:30
  131.8 1.6 %collective-permute-start.23 = (f32[288,256]{1,0:T(8,128)S(1)}, f32[288,256]{1,0:T(8,128)S(1)}, u32[]{:S(2)}, u32[]{:S(2)}) collective-permute-start(f32[288,256]{1,0:T(8,128)S(1)} %collective-permute-done.19.refs_2_), channel_id=1, source_target_pairs={{0,4},{1,5},{2,6},{3,7},{4,0},{5,1},{6,2},{7,3},{8,12},{9,13},{10,... | collective-permute-start | bytes 884744 | tf_op jit(solution)/shard_map/ppermute | solution.py:30
  131.8 2.0 %collective-permute-start.24 = (f32[288,256]{1,0:T(8,128)S(1)}, f32[288,256]{1,0:T(8,128)S(1)}, u32[]{:S(2)}, u32[]{:S(2)}) collective-permute-start(f32[288,256]{1,0:T(8,128)S(1)} %collective-permute-done.20.refs_3_), channel_id=1, source_target_pairs={{0,4},{1,5},{2,6},{3,7},{4,0},{5,1},{6,2},{7,3},{8,12},{9,13},{10,... | collective-permute-start | bytes 884744 | tf_op jit(solution)/shard_map/ppermute | solution.py:30

commit v5 on v4

--- a/solution.py
+++ b/solution.py
@@ -94,7 +94,7 @@
 
 def main_kernel(
     counts_ref, spots_ref, tile_ref, below_ref, right_ref, corner_ref, amp_ref, probe_ref, top_ref, table_ref,
-    g_tile, g_below, g_side, mine_ref, other_ref,
+    g_tile, g_lower, g_right, mine_ref, other_ref,
     ext, gacc, stage, turned, wave, wins, sums, in_sem, out_sem,
 ):
     modes, side = probe_ref.shape[1], probe_ref.shape[2]
@@ -203,9 +203,9 @@
             at = j * (share + SUBLANES)
             stores.append((sums.at[pl.ds(base + j * share, share)], ref.at[pl.ds(at, share)]))
             stores.append((top_ref, ref.at[pl.ds(at + share, SUBLANES)]))
-    stores.append((gacc.at[:, :, pl.ds(cols, side)], g_side))
+    stores.append((gacc.at[:, pl.ds(0, rows), pl.ds(cols, side)], g_right))
     stores.append((gacc.at[:, pl.ds(0, rows), pl.ds(0, cols)], g_tile))
-    stores.append((gacc.at[:, pl.ds(rows, side), pl.ds(0, cols)], g_below))
+    stores.append((gacc.at[:, pl.ds(rows, side)], g_lower))
     stores = [pltpu.make_async_copy(a, b, out_sem.at[i]) for i, (a, b) in enumerate(stores)]
     for store in stores:
         store.start()
@@ -245,7 +245,7 @@
     return functools.reduce(lambda a, b: jnp.where(summed, a + b, jnp.maximum(a, b)), values)
 
 
-def finish_kernel(tile_ref, light_ref, top_ref, g_tile, g_left, g_up, out_ref):
+def finish_kernel(tile_ref, light_ref, top_ref, g_tile, g_left, g_up, g_diag, out_ref):
     side = g_left.shape[2]
     rows, cols = light_ref.shape
     top = top_ref[0:1, 0:1]
@@ -255,7 +255,7 @@
         for i in range(2):
             total = g_tile[i, :, part] + g_up[i, :, part]
             if at == 0:
-                total += g_left[i, :rows]
+                total += g_left[i] + g_diag[i]
             out_ref[i, :, part] = tile_ref[i, :, part] + total * scale
 
 
@@ -288,6 +288,7 @@
 VM = pl.BlockSpec(memory_space=pltpu.VMEM)
 SM = pl.BlockSpec(memory_space=pltpu.SMEM)
 ANY = pl.BlockSpec(memory_space=pl.ANY)
+HBM = pl.BlockSpec(memory_space=pltpu.HBM)
 
 
 def params(mib):
@@ -314,6 +315,8 @@
     from_left = shifted(spots, 0, 1)
     from_diag = shifted(spots, 1, 1)
     below = shifted(object_field[:, :side, :], -1, 0)
+    right, from_up, from_left, from_diag = lax.optimization_barrier((right, from_up, from_left, from_diag))
+    corner = shifted(right[:, :side, :], -1, 0)
     light, top = pl.pallas_call(
         light_kernel,
         out_shape=(f32(rows, cols), f32(SUBLANES, side)),
@@ -328,16 +331,14 @@
         name="lighting",
     )(counts, spots, from_up, from_left, from_diag, probe)
 
-    right, light = lax.optimization_barrier((right, light))
-    corner = shifted(right[:, :side, :], -1, 0)
-    g_tile, g_below, g_side, mine, other = pl.pallas_call(
+    g_tile, g_lower, g_right, mine, other = pl.pallas_call(
         main_kernel,
         out_shape=(
-            f32(2, rows, cols), f32(2, side, cols), f32(2, rows + side, side),
+            f32(2, rows, cols), f32(2, side, cols + side), f32(2, rows, side),
             f32(pairs * (share + SUBLANES), side), f32(pairs * (share + SUBLANES), side),
         ),
         in_specs=[SM] * 2 + [ANY] * 4 + [VM] * 4,
-        out_specs=(ANY,) * 5,
+        out_specs=(HBM,) * 5,
         scratch_shapes=[
             pltpu.VMEM((2, rows + side, cols + side), jnp.float32),
             pltpu.VMEM((2, rows + side, cols + side), jnp.float32),
@@ -354,8 +355,8 @@
         name="positions",
     )(counts, spots, object_field, below, right, corner, evens_first(amplitudes[0, 0]), probe, top, tables(side))
 
-    g_left = shifted(g_side, 0, 1)
     arrived = swapped(other, 1, 0)
+    g_left = shifted(g_right, 0, 1)
 
     def cut(value, start, size):
         return lax.dynamic_slice_in_dim(value, start, size, 0)
@@ -365,9 +366,8 @@
         return merge(share, [cut(mine, start, share + SUBLANES), cut(arrived, start, share + SUBLANES)])
 
     plane_sum = merge(share, [chip_sum(0)] + [swapped(chip_sum(d), 2 * d, 0) for d in range(1, pairs)])
-    lower = jnp.concatenate([g_below[:, :, :side] + g_left[:, rows:], g_below[:, :, side:]], axis=2)
-    plane_sum, lower = lax.optimization_barrier((plane_sum, lower))
-    g_up = shifted(lower, 1, 0)
+    plane_sum, g_lower, g_left = lax.optimization_barrier((plane_sum, g_lower, g_left))
+    g_up = shifted(g_lower, 1, 0)
 
     def col_part(e):
         return jnp.concatenate([cut(plane_sum, (my_col ^ e) * piece, piece), plane_sum[share:]], axis=0)
@@ -376,16 +376,17 @@
     top = own[piece:]
     own = own[:piece]
     own = jnp.concatenate([own] + [swapped(own, 0, e) for e in range(1, n_col)], axis=0)
+    own, g_up = lax.optimization_barrier((own, g_up))
+    g_diag = shifted(g_up[:, :, cols:], 0, 1)
     object_new = pl.pallas_call(
         finish_kernel,
         out_shape=f32(2, rows, cols),
-        in_specs=[VM] * 6,
+        in_specs=[VM] * 7,
         out_specs=VM,
         compiler_params=params(10),
         cost_estimate=cost(10**6, 6 * 10**6),
         name="object_update",
-    )(object_field, light, top, g_tile, g_left, g_up)
-    own, object_new = lax.optimization_barrier((own, object_new))
+    )(object_field, light, top, g_tile, g_left, g_up, g_diag)
     blocks = [own] + [swapped(own, 2 * d, 0) for d in range(1, pairs)]
     blocks = blocks + [swapped(block, 1, 0) for block in blocks]
     probe_new = pl.pallas_call(

time: 137 us -> 126 us (0.920)
  waiting for transfers between devices: 42.4 us -> 34.6 us
  Pallas kernels: 24.1 us -> 19.5 us
  local copies, waits for them, and re-layouts: 7.77 us -> 10.8 us
  starting transfers between devices: 53.2 us -> 51.2 us
    ppermute x8 -> x9, waiting for transfers between devices: 17.6 us -> 1.93 us  [shifted(): return lax.ppermute(value, ('row', 'col'), pairs)]
    ppermute x17, waiting for transfers between devices: 24.8 us -> 32.7 us  [swapped(): return lax.ppermute(value, ('row', 'col'), pairs)]
    ppermute x8 -> x9, starting transfers between devices: 33 us -> 27.1 us  [shifted(): return lax.ppermute(value, ('row', 'col'), pairs)]
    ppermute x17, starting transfers between devices: 20.2 us -> 24.1 us  [swapped(): return lax.ppermute(value, ('row', 'col'), pairs)]
    pallas_call x1, Pallas kernels: 17.1 us -> 14 us  [body(): pl.pallas_call(main_kernel, out_shape=(f32(2, rows, cols), f32(2, side, c...]
    select_n x3, other arithmetic: 3.18 us -> 4.65 us  [merge(): jnp.where(summed, a + b, jnp.maximum(a, b))]
    unnamed x27 -> x31, local copies, waits for them, and re-layouts: 5.76 us -> 6.13 us
  transfers between devices with their start and end apart: 25 -> 26, of which waited for: 11 -> 14; matrix products, arithmetic and copies ran while one was open for 6% -> 8% of each run, Pallas kernels for 2% -> 3%
where the time goes in v5:
time: 126 us
  starting transfers between devices  51.2 us (41%)
  waiting for transfers between devices  34.6 us (27%)
  Pallas kernels  19.5 us (15%)
  local copies, waits for them, and re-layouts  10.8 us (9%)
  other arithmetic  4.71 us (4%)
  matrix products  3.83 us (3%)
    ppermute x17, waiting for transfers between devices, swapped(): return lax.ppermute(value, ('row', 'col'), pairs)  32.7 us
    ppermute x9, starting transfers between devices, shifted(): return lax.ppermute(value, ('row', 'col'), pairs)  27.1 us
    ppermute x17, starting transfers between devices, swapped(): return lax.ppermute(value, ('row', 'col'), pairs)  24.1 us
    pallas_call x1, Pallas kernels, body(): pl.pallas_call(main_kernel, out_shape=(f32(2, rows, cols), f32(2, side, c...  14 us
    unnamed x31, local copies, waits for them, and re-layouts  6.13 us
    select_n x3, other arithmetic, merge(): jnp.where(summed, a + b, jnp.maximum(a, b))  4.65 us
  transfers between devices with their start and end apart: 26, of which 14 were waited for; matrix products, arithmetic and copies ran while one was open for 8% of the time, Pallas kernels for 3%

profile of v5, /device:TPU:0, one launch (start us, length us, event | category | flops | bytes accessed | tf_op | source)
XLA Modules:
  0.0 125.6 jit_solution(255462442238368224)
XLA Ops:
  0.6 2.0 %slice.18 = f32[2,256,256]{2,1,0:T(8,128)} slice(f32[2,256,512]{2,1,0:T(8,128)} %tile_ref.3), slice={[0:2], [0:256], [0:256]} | slice | bytes 1048576 | tf_op jit(solution)/shard_map/slice | solution.py:313
  2.6 1.3 %collective-permute-start = (f32[2,256,256]{2,1,0:T(8,128)}, f32[2,256,256]{2,1,0:T(8,128)S(1)}, u32[]{:S(2)}, u32[]{:S(2)}) collective-permute-start(f32[2,256,256]{2,1,0:T(8,128)} %slice.18), channel_id=1, source_target_pairs={{1,0},{2,1},{3,2},{5,4},{6,5},{7,6},{9,8},{10,9},{11,10},{13,12},{... | collective-permute-start | bytes 1572872 | tf_op jit(solution)/shard_map/ppermute | solution.py:24
  3.9 1.3 %collective-permute-start.4 = (f32[2,256,512]{2,1,0:T(8,128)}, f32[2,256,512]{2,1,0:T(8,128)S(1)}, u32[]{:S(2)}, u32[]{:S(2)}) collective-permute-start(f32[2,256,512]{2,1,0:T(8,128)} %tile_ref.3), channel_id=1, source_target_pairs={{4,0},{5,1},{6,2},{7,3},{8,4},{9,5},{10,6},{11,7},{12,8},{13,9},{1... | collective-permute-start | bytes 3145736 | tf_op jit(solution)/shard_map/ppermute | solution.py:24
  5.2 0.8 copy.13.spots_ref
  6.0 3.0 %collective-permute-start.1 = (s32[6,2]{1,0:T(8,128)S(1)}, s32[6,2]{1,0:T(8,128)S(1)}, u32[]{:S(2)}, u32[]{:S(2)}) collective-permute-start(s32[6,2]{1,0:T(8,128)S(1)} %copy.13.spots_ref), channel_id=1, source_target_pairs={{0,4},{1,5},{2,6},{3,7},{4,8},{5,9},{6,10},{7,11},{8,12},{9,13},{1... | collective-permute-start | bytes 152 | tf_op jit(solution)/shard_map/ppermute | solution.py:24
  9.0 5.6 %collective-permute-start.2 = (s32[6,2]{1,0:T(8,128)S(1)}, s32[6,2]{1,0:T(8,128)S(1)}, u32[]{:S(2)}, u32[]{:S(2)}) collective-permute-start(s32[6,2]{1,0:T(8,128)S(1)} %copy.13.spots_ref), channel_id=1, source_target_pairs={{0,1},{1,2},{2,3},{4,5},{5,6},{6,7},{8,9},{9,10},{10,11},{12,13},{... | collective-permute-start | bytes 152 | tf_op jit(solution)/shard_map/ppermute | solution.py:24
  14.6 4.4 %collective-permute-start.3 = (s32[6,2]{1,0:T(8,128)S(1)}, s32[6,2]{1,0:T(8,128)S(1)}, u32[]{:S(2)}, u32[]{:S(2)}) collective-permute-start(s32[6,2]{1,0:T(8,128)S(1)} %copy.13.spots_ref), channel_id=1, source_target_pairs={{0,5},{1,6},{2,7},{4,9},{5,10},{6,11},{8,13},{9,14},{10,15},{12,17... | collective-permute-start | bytes 152 | tf_op jit(solution)/shard_map/ppermute | solution.py:24
  18.9 0.8 copy.12.counts_ref
  19.7 0.5 collective-permute-done.3.diag_ref
  20.3 1.3 %collective-permute-start.5 = (f32[2,256,256]{2,1,0:T(8,128)S(1)}, f32[2,256,256]{2,1,0:T(8,128)S(1)}, u32[]{:S(2)}, u32[]{:S(2)}) collective-permute-start(f32[2,256,256]{2,1,0:T(8,128)S(1)} %collective-permute-done.right_ref), channel_id=1, source_target_pairs={{4,0},{5,1},{6,2},{7,3},{8,4},{9,5},{10,6},{11,7},{12,8},{13,9},{1... | collective-permute-start | bytes 1572872 | tf_op jit(solution)/shard_map/ppermute | solution.py:24
  21.6 2.4 %fusion.2 = f32[256,6,256]{2,0,1:T(8,128)S(1)} fusion(f32[256,256,1]{1,0,2:T(8,128)} %constant.45, f32[1,1,6,256,256]{4,3,2,1,0:T(8,128)S(1)} %copy-done), kind=kOutput, calls=%fused_computation.2 | convolution fusion | flops 1207959552 | bytes 3407872 | tf_op jit(solution)/shard_map/ab,sbc->sac/dot_general | solution.py:50
  24.0 1.4 %fusion.amp_ref = f32[6,256,256]{2,1,0:T(8,128)S(1)} fusion(f32[256,256,1]{1,0,2:T(8,128)S(1)} %copy-done.14, f32[256,6,256]{2,0,1:T(8,128)S(1)} %fusion.2), kind=kOutput, calls=%fused_computation | convolution fusion | flops 1207959552 | bytes 3407872 | tf_op jit(solution)/shard_map/sac,dc->sad/dot_general | solution.py:51
  25.6 2.1 %lighting.1 = (f32[256,512]{1,0:T(8,128)S(1)}, f32[8,256]{1,0:T(8,128)S(1)}) custom-call(s32[8,4]{1,0:T(8,128)S(1)} %copy.12.counts_ref, s32[6,2]{1,0:T(8,128)S(1)} %copy.13.spots_ref, s32[6,2]{1,0:T(8,128)S(1)} %collective-permute-done.1.up_ref, s32[6,2]{1,0:T(8,128)S(1)} %collective-permute-done.2.left_ref, s32[6,2]{1,0:T(8,128)S(1)} %collective-permute-done.3.diag_ref, ...), custom_call_target="tpu_custom_call" | custom-call | flops 100000000 | bytes 10000000 | tf_op jit(solution)/shard_map/lighting/pallas_call | solution.py:320
  27.7 0.8 copy-done.7
  28.4 1.0 copy-done.11
  29.4 1.2 copy-done.12
  30.7 14.0 %positions.1 = (f32[2,256,512]{2,1,0:T(8,128)S(1)}, f32[2,256,768]{2,1,0:T(8,128)}, f32[2,256,256]{2,1,0:T(8,128)}, f32[1184,256]{1,0:T(8,128)S(1)}, f32[1184,256]{1,0:T(8,128)}) custom-call(s32[8,4]{1,0:T(8,128)S(1)} %copy.12.counts_ref, s32[6,2]{1,0:T(8,128)S(1)} %copy.13.spots_ref, f32[2,256,512]{2,1,0:T(8,128)S(1)} %copy-done.3, ...), custom_call_target="tpu_custom_call" | custom-call | flops 7000000000 | bytes 20000000 | tf_op jit(solution)/shard_map/positions/pallas_call | solution.py:334
  44.7 1.0 copy-done.5
  45.7 7.6 %collective-permute-start.6 = (f32[1184,256]{1,0:T(8,128)}, f32[1184,256]{1,0:T(8,128)}, u32[]{:S(2)}, u32[]{:S(2)}) collective-permute-start(f32[1184,256]{1,0:T(8,128)} %get-tuple-element.25), channel_id=1, source_target_pairs={{0,4},{1,5},{2,6},{3,7},{4,0},{5,1},{6,2},{7,3},{8,12},{9,13},{10,... | collective-permute-start | bytes 3637256 | tf_op jit(solution)/shard_map/ppermute | solution.py:30
  53.2 2.9 %collective-permute-done.6 = f32[1184,256]{1,0:T(8,128)} collective-permute-done((f32[1184,256]{1,0:T(8,128)}, f32[1184,256]{1,0:T(8,128)}, u32[]{:S(2)}, u32[]{:S(2)}) %collective-permute-start.6) | collective-permute-done | bytes 1212448 | tf_op jit(solution)/shard_map/ppermute | solution.py:30
  56.1 2.4 %maximum_select_fusion.3 = (f32[296,256]{1,0:T(8,128)}, f32[296,256]{1,0:T(8,128)}, f32[296,256]{1,0:T(8,128)}) fusion(f32[1184,256]{1,0:T(8,128)} %collective-permute-done.6, s32[]{:T(128)S(6)} %select_n.68, f32[1184,256]{1,0:T(8,128)S(1)} %get-tuple-element.24, pred[296]{0:T(512)(128)(4,1)S(1)} %iota_compare_fusion, s32[]{:T(128)S(6)} %select_n.74, ...), kind=kLoop, calls=%fused_computation.7 | loop fusion | flops 681984 | bytes 2728244 | tf_op jit(solution)/shard_map/jit(_where)/select_n | solution.py:245
  58.5 3.7 %collective-permute-start.8 = (f32[296,256]{1,0:T(8,128)}, f32[296,256]{1,0:T(8,128)}, u32[]{:S(2)}, u32[]{:S(2)}) collective-permute-start(f32[296,256]{1,0:T(8,128)} %get-tuple-element.36), channel_id=1, source_target_pairs={{0,16},{1,17},{2,18},{3,19},{4,20},{5,21},{6,22},{7,23},{8,24},{9,... | collective-permute-start | bytes 909320 | tf_op jit(solution)/shard_map/ppermute | solution.py:30
  62.2 5.8 %collective-permute-start.10 = (f32[2,256,256]{2,1,0:T(8,128)}, f32[2,256,256]{2,1,0:T(8,128)S(1)}, u32[]{:S(2)}, u32[]{:S(2)}) collective-permute-start(f32[2,256,256]{2,1,0:T(8,128)} %get-tuple-element.27), channel_id=1, source_target_pairs={{0,1},{1,2},{2,3},{4,5},{5,6},{6,7},{8,9},{9,10},{10,11},{12,13},{... | collective-permute-start | bytes 1572872 | tf_op jit(solution)/shard_map/ppermute | solution.py:24
  68.0 1.8 %collective-permute-done.9 = f32[296,256]{1,0:T(8,128)} collective-permute-done((f32[296,256]{1,0:T(8,128)}, f32[296,256]{1,0:T(8,128)}, u32[]{:S(2)}, u32[]{:S(2)}) %collective-permute-start.9) | collective-permute-done | bytes 303136 | tf_op jit(solution)/shard_map/ppermute | solution.py:30
  69.8 5.9 %collective-permute-done.8 = f32[296,256]{1,0:T(8,128)} collective-permute-done((f32[296,256]{1,0:T(8,128)}, f32[296,256]{1,0:T(8,128)}, u32[]{:S(2)}, u32[]{:S(2)}) %collective-permute-start.8) | collective-permute-done | bytes 303136 | tf_op jit(solution)/shard_map/ppermute | solution.py:30
  75.7 2.1 %maximum_select_fusion = f32[296,256]{1,0:T(8,128)} fusion(f32[296,256]{1,0:T(8,128)} %collective-permute-done.9, f32[296,256]{1,0:T(8,128)} %collective-permute-done.8, f32[296,256]{1,0:T(8,128)} %collective-permute-done.7, f32[1184,256]{1,0:T(8,128)} %collective-permute-done.6, s32[]{:T(128)S(6)} %select_n.66, f32[1184,256]{1,0:T(8,128)S(1)} %get-tuple-element.24, ...), kind=kLoop, calls=%fused_computation.4 | loop fusion | flops 909312 | bytes 1818924 | tf_op jit(solution)/shard_map/jit(_where)/select_n | solution.py:245
  77.8 1.4 %collective-permute-done.10.g_left = f32[2,256,256]{2,1,0:T(8,128)S(1)} collective-permute-done((f32[2,256,256]{2,1,0:T(8,128)}, f32[2,256,256]{2,1,0:T(8,128)S(1)}, u32[]{:S(2)}, u32[]{:S(2)}) %collective-permute-start.10) | collective-permute-done | bytes 524320 | tf_op jit(solution)/shard_map/ppermute | solution.py:24
  79.2 0.8 copy-done.9
  80.0 1.4 %collective-permute-start.17 = (f32[2,256,768]{2,1,0:T(8,128)}, f32[2,256,768]{2,1,0:T(8,128)S(1)}, u32[]{:S(2)}, u32[]{:S(2)}) collective-permute-start(f32[2,256,768]{2,1,0:T(8,128)} %get-tuple-element.31), channel_id=1, source_target_pairs={{0,4},{1,5},{2,6},{3,7},{4,8},{5,9},{6,10},{7,11},{8,12},{9,13},{1... | collective-permute-start | bytes 4718600 | tf_op jit(solution)/shard_map/ppermute | solution.py:24
  81.4 0.7 slice.19
  82.1 1.2 constant_dynamic-slice_fusion.1
  83.3 3.2 %collective-permute-start.13 = (f32[80,256]{1,0:T(8,128)S(1)}, f32[80,256]{1,0:T(8,128)S(1)}, u32[]{:S(2)}, u32[]{:S(2)}) collective-permute-start(f32[80,256]{1,0:T(8,128)S(1)} %get-tuple-element.43), channel_id=1, source_target_pairs={{0,3},{1,2},{2,1},{3,0},{4,7},{5,6},{6,5},{7,4},{8,11},{9,10},{10,... | collective-permute-start | bytes 245768 | tf_op jit(solution)/shard_map/ppermute | solution.py:30
  86.5 1.4 %collective-permute-start.12 = (f32[80,256]{1,0:T(8,128)S(1)}, f32[80,256]{1,0:T(8,128)S(1)}, u32[]{:S(2)}, u32[]{:S(2)}) collective-permute-start(f32[80,256]{1,0:T(8,128)S(1)} %get-tuple-element.42), channel_id=1, source_target_pairs={{0,2},{1,3},{2,0},{3,1},{4,6},{5,7},{6,4},{7,5},{8,10},{9,11},{10,... | collective-permute-start | bytes 245768 | tf_op jit(solution)/shard_map/ppermute | solution.py:30
  88.1 2.0 %collective-permute-done.13 = f32[80,256]{1,0:T(8,128)S(1)} collective-permute-done((f32[80,256]{1,0:T(8,128)S(1)}, f32[80,256]{1,0:T(8,128)S(1)}, u32[]{:S(2)}, u32[]{:S(2)}) %collective-permute-start.13) | collective-permute-done | bytes 81952 | tf_op jit(solution)/shard_map/ppermute | solution.py:30
  90.0 5.7 %collective-permute-done.12 = f32[80,256]{1,0:T(8,128)S(1)} collective-permute-done((f32[80,256]{1,0:T(8,128)S(1)}, f32[80,256]{1,0:T(8,128)S(1)}, u32[]{:S(2)}, u32[]{:S(2)}) %collective-permute-start.12) | collective-permute-done | bytes 81952 | tf_op jit(solution)/shard_map/ppermute | solution.py:30
  95.9 3.2 %collective-permute-start.16 = (f32[72,256]{1,0:T(8,128)S(1)}, f32[72,256]{1,0:T(8,128)S(1)}, u32[]{:S(2)}, u32[]{:S(2)}) collective-permute-start(f32[72,256]{1,0:T(8,128)S(1)} %slice.24), channel_id=1, source_target_pairs={{0,3},{1,2},{2,1},{3,0},{4,7},{5,6},{6,5},{7,4},{8,11},{9,10},{10,... | collective-permute-start | bytes 221192 | tf_op jit(solution)/shard_map/ppermute | solution.py:30
  99.1 1.2 collective-permute-start.14
  100.3 2.5 %collective-permute-done.16 = f32[72,256]{1,0:T(8,128)S(1)} collective-permute-done((f32[72,256]{1,0:T(8,128)S(1)}, f32[72,256]{1,0:T(8,128)S(1)}, u32[]{:S(2)}, u32[]{:S(2)}) %collective-permute-start.16) | collective-permute-done | bytes 73760 | tf_op jit(solution)/shard_map/ppermute | solution.py:30
  102.9 2.4 %collective-permute-done.15 = f32[72,256]{1,0:T(8,128)S(1)} collective-permute-done((f32[72,256]{1,0:T(8,128)S(1)}, f32[72,256]{1,0:T(8,128)S(1)}, u32[]{:S(2)}, u32[]{:S(2)}) %collective-permute-start.15) | collective-permute-done | bytes 73760 | tf_op jit(solution)/shard_map/ppermute | solution.py:30
  105.4 1.1 collective-permute-start.19
  106.5 0.6 collective-permute-start.20
  107.0 1.9 %collective-permute-start.21 = (f32[288,256]{1,0:T(8,128)S(1)}, f32[288,256]{1,0:T(8,128)S(1)}, u32[]{:S(2)}, u32[]{:S(2)}) collective-permute-start(f32[288,256]{1,0:T(8,128)S(1)} %pad_maximum_fusion.refs_0_), channel_id=1, source_target_pairs={{0,24},{1,25},{2,26},{3,27},{4,28},{5,29},{6,30},{7,31},{8,16},{9,... | collective-permute-start | bytes 884744 | tf_op jit(solution)/shard_map/ppermute | solution.py:30
  109.0 3.1 %collective-permute-start.18 = (f32[2,256,256]{2,1,0:T(8,128)S(1)}, f32[2,256,256]{2,1,0:T(8,128)S(1)}, u32[]{:S(2)}, u32[]{:S(2)}) collective-permute-start(f32[2,256,256]{2,1,0:T(8,128)S(1)} %slice.22), channel_id=1, source_target_pairs={{0,1},{1,2},{2,3},{4,5},{5,6},{6,7},{8,9},{9,10},{10,11},{12,13},{... | collective-permute-start | bytes 1572872 | tf_op jit(solution)/shard_map/ppermute | solution.py:24
  112.2 3.1 %collective-permute-done.19.refs_1_ = f32[288,256]{1,0:T(8,128)S(1)} collective-permute-done((f32[288,256]{1,0:T(8,128)S(1)}, f32[288,256]{1,0:T(8,128)S(1)}, u32[]{:S(2)}, u32[]{:S(2)}) %collective-permute-start.19) | collective-permute-done | bytes 294944 | tf_op jit(solution)/shard_map/ppermute | solution.py:30
  115.3 0.7 collective-permute-done.20.refs_2_
  116.0 5.6 %collective-permute-done.21.refs_3_ = f32[288,256]{1,0:T(8,128)S(1)} collective-permute-done((f32[288,256]{1,0:T(8,128)S(1)}, f32[288,256]{1,0:T(8,128)S(1)}, u32[]{:S(2)}, u32[]{:S(2)}) %collective-permute-start.21) | collective-permute-done | bytes 294944 | tf_op jit(solution)/shard_map/ppermute | solution.py:30
  121.7 1.4 %object_update.1 = f32[2,256,512]{2,1,0:T(8,128)} custom-call(f32[2,256,512]{2,1,0:T(8,128)S(1)} %copy-done.4, f32[256,512]{1,0:T(8,128)S(1)} %copy-done.8, f32[8,256]{1,0:T(8,128)S(1)} %slice.23.top_ref, f32[2,256,512]{2,1,0:T(8,128)S(1)} %copy-done.6, f32[2,256,256]{2,1,0:T(8,128)S(1)} %copy-done.10, f32[2,256,768]{2,1,0:T(8,128)S(1)} %collective-permute-done.17.g_up, ...), custom_call_target="tpu_custom_call" | custom-call | flops 1000000 | bytes 6000000 | tf_op jit(solution)/shard_map/object_update/pallas_call | solution.py:381
  123.6 2.0 %probe_update.1 = f32[2,4,256,256]{3,2,1,0:T(8,128)} custom-call(f32[2,4,256,256]{3,2,1,0:T(8,128)S(1)} %copy-done.2, f32[288,256]{1,0:T(8,128)S(1)} %pad_maximum_fusion.refs_0_, f32[288,256]{1,0:T(8,128)S(1)} %collective-permute-done.19.refs_1_, f32[288,256]{1,0:T(8,128)S(1)} %collective-permute-done.20.refs_2_, ...), custom_call_target="tpu_custom_call" | custom-call | flops 1000000 | bytes 6000000 | tf_op jit(solution)/shard_map/probe_update/pallas_call | solution.py:392
  (55 shorter events, 1.2 us)
Async XLA Ops:
  0.6 20.9 %copy-start = (f32[1,1,6,256,256]{4,3,2,1,0:T(8,128)S(1)}, f32[1,1,6,256,256]{4,3,2,1,0:T(8,128)}, u32[]{:S(2)}) copy-start(f32[1,1,6,256,256]{4,3,2,1,0:T(8,128)} %param.9) | copy-start | bytes 4718596
  2.6 17.6 %collective-permute-start = (f32[2,256,256]{2,1,0:T(8,128)}, f32[2,256,256]{2,1,0:T(8,128)S(1)}, u32[]{:S(2)}, u32[]{:S(2)}) collective-permute-start(f32[2,256,256]{2,1,0:T(8,128)} %slice.18), channel_id=1, source_target_pairs={{1,0},{2,1},{3,2},{5,4},{6,5},{7,6},{9,8},{10,9},{11,10},{13,12},{... | collective-permute-start | bytes 1572872 | tf_op jit(solution)/shard_map/ppermute | solution.py:24
  3.9 24.5 %collective-permute-start.4 = (f32[2,256,512]{2,1,0:T(8,128)}, f32[2,256,512]{2,1,0:T(8,128)S(1)}, u32[]{:S(2)}, u32[]{:S(2)}) collective-permute-start(f32[2,256,512]{2,1,0:T(8,128)} %tile_ref.3), channel_id=1, source_target_pairs={{4,0},{5,1},{6,2},{7,3},{8,4},{9,5},{10,6},{11,7},{12,8},{13,9},{1... | collective-permute-start | bytes 3145736 | tf_op jit(solution)/shard_map/ppermute | solution.py:24
  6.0 13.7 %collective-permute-start.1 = (s32[6,2]{1,0:T(8,128)S(1)}, s32[6,2]{1,0:T(8,128)S(1)}, u32[]{:S(2)}, u32[]{:S(2)}) collective-permute-start(s32[6,2]{1,0:T(8,128)S(1)} %copy.13.spots_ref), channel_id=1, source_target_pairs={{0,4},{1,5},{2,6},{3,7},{4,8},{5,9},{6,10},{7,11},{8,12},{9,13},{1... | collective-permute-start | bytes 152 | tf_op jit(solution)/shard_map/ppermute | solution.py:24
  9.0 10.7 %collective-permute-start.2 = (s32[6,2]{1,0:T(8,128)S(1)}, s32[6,2]{1,0:T(8,128)S(1)}, u32[]{:S(2)}, u32[]{:S(2)}) collective-permute-start(s32[6,2]{1,0:T(8,128)S(1)} %copy.13.spots_ref), channel_id=1, source_target_pairs={{0,1},{1,2},{2,3},{4,5},{5,6},{6,7},{8,9},{9,10},{10,11},{12,13},{... | collective-permute-start | bytes 152 | tf_op jit(solution)/shard_map/ppermute | solution.py:24
  14.6 5.7 %collective-permute-start.3 = (s32[6,2]{1,0:T(8,128)S(1)}, s32[6,2]{1,0:T(8,128)S(1)}, u32[]{:S(2)}, u32[]{:S(2)}) collective-permute-start(s32[6,2]{1,0:T(8,128)S(1)} %copy.13.spots_ref), channel_id=1, source_target_pairs={{0,5},{1,6},{2,7},{4,9},{5,10},{6,11},{8,13},{9,14},{10,15},{12,17... | collective-permute-start | bytes 152 | tf_op jit(solution)/shard_map/ppermute | solution.py:24
  19.7 4.3 %copy-start.14 = (f32[256,256,1]{1,0,2:T(8,128)S(1)}, f32[256,256,1]{1,0,2:T(8,128)}, u32[]{:S(2)}) copy-start(f32[256,256,1]{1,0,2:T(8,128)} %constant.45) | copy-start | bytes 786436
  20.3 9.2 %collective-permute-start.5 = (f32[2,256,256]{2,1,0:T(8,128)S(1)}, f32[2,256,256]{2,1,0:T(8,128)S(1)}, u32[]{:S(2)}, u32[]{:S(2)}) collective-permute-start(f32[2,256,256]{2,1,0:T(8,128)S(1)} %collective-permute-done.right_ref), channel_id=1, source_target_pairs={{4,0},{5,1},{6,2},{7,3},{8,4},{9,5},{10,6},{11,7},{12,8},{13,9},{1... | collective-permute-start | bytes 1572872 | tf_op jit(solution)/shard_map/ppermute | solution.py:24
  24.0 1.6 %copy-start.1 = (f32[2,4,256,256]{3,2,1,0:T(8,128)S(1)}, f32[2,4,256,256]{3,2,1,0:T(8,128)}, u32[]{:S(2)}) copy-start(f32[2,4,256,256]{3,2,1,0:T(8,128)} %probe_ref.5) | copy-start | bytes 6291460
  25.6 3.9 %copy-start.3 = (f32[2,256,512]{2,1,0:T(8,128)S(1)}, f32[2,256,512]{2,1,0:T(8,128)}, u32[]{:S(2)}) copy-start(f32[2,256,512]{2,1,0:T(8,128)} %tile_ref.3) | copy-start | bytes 3145732
  25.6 3.9 %copy-start.13 = (bf16[4,256,256]{2,1,0:T(8,128)(2,1)S(1)}, bf16[4,256,256]{2,1,0:T(8,128)(2,1)}, u32[]{:S(2)}) copy-start(bf16[4,256,256]{2,1,0:T(8,128)(2,1)} %constant.42.clone.table_ref) | copy-start | bytes 1572868
  27.7 0.8 copy-start.7
  28.4 1.0 copy-start.11
  29.4 1.2 copy-start.12
  44.7 1.0 copy-start.5
  45.7 10.4 %collective-permute-start.6 = (f32[1184,256]{1,0:T(8,128)}, f32[1184,256]{1,0:T(8,128)}, u32[]{:S(2)}, u32[]{:S(2)}) collective-permute-start(f32[1184,256]{1,0:T(8,128)} %get-tuple-element.25), channel_id=1, source_target_pairs={{0,4},{1,5},{2,6},{3,7},{4,0},{5,1},{6,2},{7,3},{8,12},{9,13},{10,... | collective-permute-start | bytes 3637256 | tf_op jit(solution)/shard_map/ppermute | solution.py:30
  58.5 11.3 %collective-permute-start.9 = (f32[296,256]{1,0:T(8,128)}, f32[296,256]{1,0:T(8,128)}, u32[]{:S(2)}, u32[]{:S(2)}) collective-permute-start(f32[296,256]{1,0:T(8,128)} %get-tuple-element.35), channel_id=1, source_target_pairs={{0,24},{1,25},{2,26},{3,27},{4,28},{5,29},{6,30},{7,31},{8,16},{9,... | collective-permute-start | bytes 909320 | tf_op jit(solution)/shard_map/ppermute | solution.py:30
  58.5 17.2 %collective-permute-start.8 = (f32[296,256]{1,0:T(8,128)}, f32[296,256]{1,0:T(8,128)}, u32[]{:S(2)}, u32[]{:S(2)}) collective-permute-start(f32[296,256]{1,0:T(8,128)} %get-tuple-element.36), channel_id=1, source_target_pairs={{0,16},{1,17},{2,18},{3,19},{4,20},{5,21},{6,22},{7,23},{8,24},{9,... | collective-permute-start | bytes 909320 | tf_op jit(solution)/shard_map/ppermute | solution.py:30
  62.2 13.4 %collective-permute-start.7 = (f32[296,256]{1,0:T(8,128)}, f32[296,256]{1,0:T(8,128)}, u32[]{:S(2)}, u32[]{:S(2)}) collective-permute-start(f32[296,256]{1,0:T(8,128)} %get-tuple-element.34), channel_id=1, source_target_pairs={{0,8},{1,9},{2,10},{3,11},{4,12},{5,13},{6,14},{7,15},{8,0},{9,1},... | collective-permute-start | bytes 909320 | tf_op jit(solution)/shard_map/ppermute | solution.py:30
  62.2 17.0 %collective-permute-start.10 = (f32[2,256,256]{2,1,0:T(8,128)}, f32[2,256,256]{2,1,0:T(8,128)S(1)}, u32[]{:S(2)}, u32[]{:S(2)}) collective-permute-start(f32[2,256,256]{2,1,0:T(8,128)} %get-tuple-element.27), channel_id=1, source_target_pairs={{0,1},{1,2},{2,3},{4,5},{5,6},{6,7},{8,9},{9,10},{10,11},{12,13},{... | collective-permute-start | bytes 1572872 | tf_op jit(solution)/shard_map/ppermute | solution.py:24
  79.2 0.8 copy-start.9
  80.0 25.3 %collective-permute-start.17 = (f32[2,256,768]{2,1,0:T(8,128)}, f32[2,256,768]{2,1,0:T(8,128)S(1)}, u32[]{:S(2)}, u32[]{:S(2)}) collective-permute-start(f32[2,256,768]{2,1,0:T(8,128)} %get-tuple-element.31), channel_id=1, source_target_pairs={{0,4},{1,5},{2,6},{3,7},{4,8},{5,9},{6,10},{7,11},{8,12},{9,13},{1... | collective-permute-start | bytes 4718600 | tf_op jit(solution)/shard_map/ppermute | solution.py:24
  82.1 39.5 %copy-start.4 = (f32[2,256,512]{2,1,0:T(8,128)S(1)}, f32[2,256,512]{2,1,0:T(8,128)}, u32[]{:S(2)}) copy-start(f32[2,256,512]{2,1,0:T(8,128)} %tile_ref.3) | copy-start | bytes 3145732
  82.1 39.5 %copy-start.6 = (f32[2,256,512]{2,1,0:T(8,128)S(1)}, f32[2,256,512]{2,1,0:T(8,128)}, u32[]{:S(2)}) copy-start(f32[2,256,512]{2,1,0:T(8,128)} %copy-done.5) | copy-start | bytes 3145732
  82.1 39.5 %copy-start.8 = (f32[256,512]{1,0:T(8,128)S(1)}, f32[256,512]{1,0:T(8,128)}, u32[]{:S(2)}) copy-start(f32[256,512]{1,0:T(8,128)} %copy-done.7) | copy-start | bytes 1572868
  82.1 39.5 %copy-start.10 = (f32[2,256,256]{2,1,0:T(8,128)S(1)}, f32[2,256,256]{2,1,0:T(8,128)}, u32[]{:S(2)}) copy-start(f32[2,256,256]{2,1,0:T(8,128)} %copy-done.9) | copy-start | bytes 1572868
  83.3 6.7 %collective-permute-start.13 = (f32[80,256]{1,0:T(8,128)S(1)}, f32[80,256]{1,0:T(8,128)S(1)}, u32[]{:S(2)}, u32[]{:S(2)}) collective-permute-start(f32[80,256]{1,0:T(8,128)S(1)} %get-tuple-element.43), channel_id=1, source_target_pairs={{0,3},{1,2},{2,1},{3,0},{4,7},{5,6},{6,5},{7,4},{8,11},{9,10},{10,... | collective-permute-start | bytes 245768 | tf_op jit(solution)/shard_map/ppermute | solution.py:30
  86.5 9.2 %collective-permute-start.12 = (f32[80,256]{1,0:T(8,128)S(1)}, f32[80,256]{1,0:T(8,128)S(1)}, u32[]{:S(2)}, u32[]{:S(2)}) collective-permute-start(f32[80,256]{1,0:T(8,128)S(1)} %get-tuple-element.42), channel_id=1, source_target_pairs={{0,2},{1,3},{2,0},{3,1},{4,6},{5,7},{6,4},{7,5},{8,10},{9,11},{10,... | collective-permute-start | bytes 245768 | tf_op jit(solution)/shard_map/ppermute | solution.py:30
  87.9 7.8 %collective-permute-start.11 = (f32[80,256]{1,0:T(8,128)S(1)}, f32[80,256]{1,0:T(8,128)S(1)}, u32[]{:S(2)}, u32[]{:S(2)}) collective-permute-start(f32[80,256]{1,0:T(8,128)S(1)} %get-tuple-element.41), channel_id=1, source_target_pairs={{0,1},{1,0},{2,3},{3,2},{4,5},{5,4},{6,7},{7,6},{8,9},{9,8},{10,11... | collective-permute-start | bytes 245768 | tf_op jit(solution)/shard_map/ppermute | solution.py:30
  95.9 7.0 %collective-permute-start.16 = (f32[72,256]{1,0:T(8,128)S(1)}, f32[72,256]{1,0:T(8,128)S(1)}, u32[]{:S(2)}, u32[]{:S(2)}) collective-permute-start(f32[72,256]{1,0:T(8,128)S(1)} %slice.24), channel_id=1, source_target_pairs={{0,3},{1,2},{2,1},{3,0},{4,7},{5,6},{6,5},{7,4},{8,11},{9,10},{10,... | collective-permute-start | bytes 221192 | tf_op jit(solution)/shard_map/ppermute | solution.py:30
  99.1 6.1 %collective-permute-start.15 = (f32[72,256]{1,0:T(8,128)S(1)}, f32[72,256]{1,0:T(8,128)S(1)}, u32[]{:S(2)}, u32[]{:S(2)}) collective-permute-start(f32[72,256]{1,0:T(8,128)S(1)} %slice.24), channel_id=1, source_target_pairs={{0,2},{1,3},{2,0},{3,1},{4,6},{5,7},{6,4},{7,5},{8,10},{9,11},{10,... | collective-permute-start | bytes 221192 | tf_op jit(solution)/shard_map/ppermute | solution.py:30
  99.1 6.2 %collective-permute-start.14 = (f32[72,256]{1,0:T(8,128)S(1)}, f32[72,256]{1,0:T(8,128)S(1)}, u32[]{:S(2)}, u32[]{:S(2)}) collective-permute-start(f32[72,256]{1,0:T(8,128)S(1)} %slice.24), channel_id=1, source_target_pairs={{0,1},{1,0},{2,3},{3,2},{4,5},{5,4},{6,7},{7,6},{8,9},{9,8},{10,11... | collective-permute-start | bytes 221192 | tf_op jit(solution)/shard_map/ppermute | solution.py:30
  105.4 10.0 %collective-permute-start.19 = (f32[288,256]{1,0:T(8,128)S(1)}, f32[288,256]{1,0:T(8,128)S(1)}, u32[]{:S(2)}, u32[]{:S(2)}) collective-permute-start(f32[288,256]{1,0:T(8,128)S(1)} %pad_maximum_fusion.refs_0_), channel_id=1, source_target_pairs={{0,8},{1,9},{2,10},{3,11},{4,12},{5,13},{6,14},{7,15},{8,0},{9,1},... | collective-permute-start | bytes 884744 | tf_op jit(solution)/shard_map/ppermute | solution.py:30
  106.5 9.5 %collective-permute-start.20 = (f32[288,256]{1,0:T(8,128)S(1)}, f32[288,256]{1,0:T(8,128)S(1)}, u32[]{:S(2)}, u32[]{:S(2)}) collective-permute-start(f32[288,256]{1,0:T(8,128)S(1)} %pad_maximum_fusion.refs_0_), channel_id=1, source_target_pairs={{0,16},{1,17},{2,18},{3,19},{4,20},{5,21},{6,22},{7,23},{8,24},{9,... | collective-permute-start | bytes 884744 | tf_op jit(solution)/shard_map/ppermute | solution.py:30
  107.0 14.6 %collective-permute-start.21 = (f32[288,256]{1,0:T(8,128)S(1)}, f32[288,256]{1,0:T(8,128)S(1)}, u32[]{:S(2)}, u32[]{:S(2)}) collective-permute-start(f32[288,256]{1,0:T(8,128)S(1)} %pad_maximum_fusion.refs_0_), channel_id=1, source_target_pairs={{0,24},{1,25},{2,26},{3,27},{4,28},{5,29},{6,30},{7,31},{8,16},{9,... | collective-permute-start | bytes 884744 | tf_op jit(solution)/shard_map/ppermute | solution.py:30
  109.0 12.7 %collective-permute-start.18 = (f32[2,256,256]{2,1,0:T(8,128)S(1)}, f32[2,256,256]{2,1,0:T(8,128)S(1)}, u32[]{:S(2)}, u32[]{:S(2)}) collective-permute-start(f32[2,256,256]{2,1,0:T(8,128)S(1)} %slice.22), channel_id=1, source_target_pairs={{0,1},{1,2},{2,3},{4,5},{5,6},{6,7},{8,9},{9,10},{10,11},{12,13},{... | collective-permute-start | bytes 1572872 | tf_op jit(solution)/shard_map/ppermute | solution.py:24
  112.1 11.0 %collective-permute-start.22 = (f32[288,256]{1,0:T(8,128)S(1)}, f32[288,256]{1,0:T(8,128)S(1)}, u32[]{:S(2)}, u32[]{:S(2)}) collective-permute-start(f32[288,256]{1,0:T(8,128)S(1)} %pad_maximum_fusion.refs_0_), channel_id=1, source_target_pairs={{0,4},{1,5},{2,6},{3,7},{4,0},{5,1},{6,2},{7,3},{8,12},{9,13},{10,... | collective-permute-start | bytes 884744 | tf_op jit(solution)/shard_map/ppermute | solution.py:30
  115.3 7.8 %collective-permute-start.23 = (f32[288,256]{1,0:T(8,128)S(1)}, f32[288,256]{1,0:T(8,128)S(1)}, u32[]{:S(2)}, u32[]{:S(2)}) collective-permute-start(f32[288,256]{1,0:T(8,128)S(1)} %collective-permute-done.19.refs_1_), channel_id=1, source_target_pairs={{0,4},{1,5},{2,6},{3,7},{4,0},{5,1},{6,2},{7,3},{8,12},{9,13},{10,... | collective-permute-start | bytes 884744 | tf_op jit(solution)/shard_map/ppermute | solution.py:30
  116.0 7.1 %collective-permute-start.24 = (f32[288,256]{1,0:T(8,128)S(1)}, f32[288,256]{1,0:T(8,128)S(1)}, u32[]{:S(2)}, u32[]{:S(2)}) collective-permute-start(f32[288,256]{1,0:T(8,128)S(1)} %collective-permute-done.20.refs_2_), channel_id=1, source_target_pairs={{0,4},{1,5},{2,6},{3,7},{4,0},{5,1},{6,2},{7,3},{8,12},{9,13},{10,... | collective-permute-start | bytes 884744 | tf_op jit(solution)/shard_map/ppermute | solution.py:30
  121.6 1.6 %collective-permute-start.25 = (f32[288,256]{1,0:T(8,128)S(1)}, f32[288,256]{1,0:T(8,128)S(1)}, u32[]{:S(2)}, u32[]{:S(2)}) collective-permute-start(f32[288,256]{1,0:T(8,128)S(1)} %collective-permute-done.21.refs_3_), channel_id=1, source_target_pairs={{0,4},{1,5},{2,6},{3,7},{4,0},{5,1},{6,2},{7,3},{8,12},{9,13},{10,... | collective-permute-start | bytes 884744 | tf_op jit(solution)/shard_map/ppermute | solution.py:30
  121.7 1.9 %copy-start.2 = (f32[2,4,256,256]{3,2,1,0:T(8,128)S(1)}, f32[2,4,256,256]{3,2,1,0:T(8,128)}, u32[]{:S(2)}) copy-start(f32[2,4,256,256]{3,2,1,0:T(8,128)} %probe_ref.5) | copy-start | bytes 6291460

commit v6 on v5

--- a/solution.py
+++ b/solution.py
@@ -93,7 +93,7 @@
 
 
 def main_kernel(
-    counts_ref, spots_ref, tile_ref, below_ref, right_ref, corner_ref, amp_ref, probe_ref, top_ref, table_ref,
+    counts_ref, spots_ref, tile_ref, below_ref, right_ref, corner_ref, amp_ref, probe_ref, table_ref,
     g_tile, g_lower, g_right, mine_ref, other_ref,
     ext, gacc, stage, turned, wave, wins, sums, in_sem, out_sem,
 ):
@@ -194,15 +194,13 @@
     lax.fori_loop(0, counts_ref[my_row, my_col], step, 0)
 
     pairs = lax.axis_size("row") // 2
-    share = mine_ref.shape[0] // pairs - SUBLANES
+    share = mine_ref.shape[1]
     core = lax.rem(my_row, 2)
     stores = []
     for ref, base in ((other_ref, (1 - core) * (share * pairs)), (mine_ref, core * (share * pairs))):
         base = pl.multiple_of(base, SUBLANES)
         for j in range(pairs):
-            at = j * (share + SUBLANES)
-            stores.append((sums.at[pl.ds(base + j * share, share)], ref.at[pl.ds(at, share)]))
-            stores.append((top_ref, ref.at[pl.ds(at + share, SUBLANES)]))
+            stores.append((sums.at[pl.ds(base + j * share, share)], ref.at[j]))
     stores.append((gacc.at[:, pl.ds(0, rows), pl.ds(cols, side)], g_right))
     stores.append((gacc.at[:, pl.ds(0, rows), pl.ds(0, cols)], g_tile))
     stores.append((gacc.at[:, pl.ds(rows, side)], g_lower))
@@ -238,11 +236,6 @@
     top = jnp.max(light, axis=0, keepdims=True)
     top = jnp.max(top, axis=1, keepdims=True)
     top_ref[...] = jnp.broadcast_to(top, top_ref.shape)
-
-
-def merge(share, values):
-    summed = jnp.arange(values[0].shape[0])[:, None] < share
-    return functools.reduce(lambda a, b: jnp.where(summed, a + b, jnp.maximum(a, b)), values)
 
 
 def finish_kernel(tile_ref, light_ref, top_ref, g_tile, g_left, g_up, g_diag, out_ref):
@@ -263,7 +256,7 @@
     pairs, n_col = parts
     block_refs, out_ref, sums = refs[:-2], refs[-2], refs[-1]
     modes, side = probe_ref.shape[1], probe_ref.shape[2]
-    share = block_refs[0].shape[0]
+    share = block_refs[0].shape[0] - SUBLANES
     piece = share // n_col
     my_row, my_col = lax.axis_index("row"), lax.axis_index("col")
     core, pair = lax.rem(my_row, 2), my_row // 2
@@ -311,12 +304,41 @@
     spots = corners[0, 0]
 
     right = shifted(object_field[:, :, :side], 0, -1)
+    measured = evens_first(amplitudes[0, 0])
+    tile, measured = lax.optimization_barrier((object_field, measured))
+    below = shifted(tile[:, :side, :], -1, 0)
     from_up = shifted(spots, 1, 0)
     from_left = shifted(spots, 0, 1)
     from_diag = shifted(spots, 1, 1)
-    below = shifted(object_field[:, :side, :], -1, 0)
-    right, from_up, from_left, from_diag = lax.optimization_barrier((right, from_up, from_left, from_diag))
+    right, measured = lax.optimization_barrier((right, measured))
     corner = shifted(right[:, :side, :], -1, 0)
+    corner, from_up, from_left, from_diag = lax.optimization_barrier((corner, from_up, from_left, from_diag))
+    g_tile, g_lower, g_right, mine, other = pl.pallas_call(
+        main_kernel,
+        out_shape=(
+            f32(2, rows, cols), f32(2, side, cols + side), f32(2, rows, side),
+            f32(pairs, share, side), f32(pairs, share, side),
+        ),
+        in_specs=[SM] * 2 + [HBM] * 4 + [VM] * 3,
+        out_specs=(HBM,) * 5,
+        scratch_shapes=[
+            pltpu.VMEM((2, rows + side, cols + side), jnp.float32),
+            pltpu.VMEM((2, rows + side, cols + side), jnp.float32),
+            pltpu.VMEM((2, side, modes * side), jnp.bfloat16),
+            pltpu.VMEM((2, modes * side, side), jnp.bfloat16),
+            pltpu.VMEM((2, modes * side, side), jnp.float32),
+            pltpu.VMEM((2, side, side), jnp.float32),
+            pltpu.VMEM((total_rows, side), jnp.float32),
+            pltpu.SemaphoreType.DMA((4,)),
+            pltpu.SemaphoreType.DMA((2 * pairs + 3,)),
+        ],
+        compiler_params=params(28),
+        cost_estimate=cost(7 * 10**9, 2 * 10**7),
+        name="positions",
+    )(counts, spots, object_field, below, right, corner, measured, probe, tables(side))
+
+    arrived = swapped(other, 1, 0)
+    arrived, from_up, from_left, from_diag = lax.optimization_barrier((arrived, from_up, from_left, from_diag))
     light, top = pl.pallas_call(
         light_kernel,
         out_shape=(f32(rows, cols), f32(SUBLANES, side)),
@@ -331,53 +353,30 @@
         name="lighting",
     )(counts, spots, from_up, from_left, from_diag, probe)
 
-    g_tile, g_lower, g_right, mine, other = pl.pallas_call(
-        main_kernel,
-        out_shape=(
-            f32(2, rows, cols), f32(2, side, cols + side), f32(2, rows, side),
-            f32(pairs * (share + SUBLANES), side), f32(pairs * (share + SUBLANES), side),
-        ),
-        in_specs=[SM] * 2 + [ANY] * 4 + [VM] * 4,
-        out_specs=(HBM,) * 5,
-        scratch_shapes=[
-            pltpu.VMEM((2, rows + side, cols + side), jnp.float32),
-            pltpu.VMEM((2, rows + side, cols + side), jnp.float32),
-            pltpu.VMEM((2, side, modes * side), jnp.bfloat16),
-            pltpu.VMEM((2, modes * side, side), jnp.bfloat16),
-            pltpu.VMEM((2, modes * side, side), jnp.float32),
-            pltpu.VMEM((2, side, side), jnp.float32),
-            pltpu.VMEM((total_rows, side), jnp.float32),
-            pltpu.SemaphoreType.DMA((4,)),
-            pltpu.SemaphoreType.DMA((4 * pairs + 3,)),
-        ],
-        compiler_params=params(28),
-        cost_estimate=cost(7 * 10**9, 2 * 10**7),
-        name="positions",
-    )(counts, spots, object_field, below, right, corner, evens_first(amplitudes[0, 0]), probe, top, tables(side))
-
-    arrived = swapped(other, 1, 0)
     g_left = shifted(g_right, 0, 1)
 
-    def cut(value, start, size):
-        return lax.dynamic_slice_in_dim(value, start, size, 0)
-
     def chip_sum(d):
-        start = (pair ^ d) * (share + SUBLANES)
-        return merge(share, [cut(mine, start, share + SUBLANES), cut(arrived, start, share + SUBLANES)])
-
-    plane_sum = merge(share, [chip_sum(0)] + [swapped(chip_sum(d), 2 * d, 0) for d in range(1, pairs)])
-    plane_sum, g_lower, g_left = lax.optimization_barrier((plane_sum, g_lower, g_left))
+        return mine[pair ^ d] + arrived[pair ^ d]
+
+    plane_sum = sum([swapped(chip_sum(d), 2 * d, 0) for d in range(1, pairs)], chip_sum(0))
+    plane_sum, g_lower, g_left, top = lax.optimization_barrier((plane_sum, g_lower, g_left, top))
     g_up = shifted(g_lower, 1, 0)
 
+    plane_sum = plane_sum.reshape(n_col, piece, side)
+
     def col_part(e):
-        return jnp.concatenate([cut(plane_sum, (my_col ^ e) * piece, piece), plane_sum[share:]], axis=0)
-
-    own = merge(piece, [col_part(0)] + [swapped(col_part(e), 0, e) for e in range(1, n_col)])
-    top = own[piece:]
-    own = own[:piece]
-    own = jnp.concatenate([own] + [swapped(own, 0, e) for e in range(1, n_col)], axis=0)
-    own, g_up = lax.optimization_barrier((own, g_up))
-    g_diag = shifted(g_up[:, :, cols:], 0, 1)
+        return jnp.concatenate([plane_sum[my_col ^ e], top], axis=0)
+
+    received = [swapped(col_part(e), 0, e) for e in range(1, n_col)]
+    own = sum([value[:piece] for value in received], plane_sum[my_col])
+    top = functools.reduce(jnp.maximum, [value[piece:] for value in received], top)
+    own = jnp.concatenate([own] + [swapped(own, 0, e) for e in range(1, n_col)] + [top], axis=0)
+    own, g_up, g_corner = lax.optimization_barrier((own, g_up, g_up[:, :, cols:]))
+    g_diag = shifted(g_corner, 0, 1)
+    blocks = [own] + [swapped(own, 2 * d, 0) for d in range(1, pairs)]
+    blocks[-1], g_diag = lax.optimization_barrier((blocks[-1], g_diag))
+    blocks = blocks + [swapped(block, 1, 0) for block in blocks]
+    top = functools.reduce(jnp.maximum, [block[share:] for block in blocks])
     object_new = pl.pallas_call(
         finish_kernel,
         out_shape=f32(2, rows, cols),
@@ -387,8 +386,6 @@
         cost_estimate=cost(10**6, 6 * 10**6),
         name="object_update",
     )(object_field, light, top, g_tile, g_left, g_up, g_diag)
-    blocks = [own] + [swapped(own, 2 * d, 0) for d in range(1, pairs)]
-    blocks = blocks + [swapped(block, 1, 0) for block in blocks]
     probe_new = pl.pallas_call(
         functools.partial(probe_kernel, (pairs, n_col)),
         out_shape=f32(*probe.shape),

time: 126 us -> 139 us (1.10)
  waiting for transfers between devices: 34.6 us -> 46.5 us
  starting transfers between devices: 51.2 us -> 45.7 us
  local copies, waits for them, and re-layouts: 10.8 us -> 12.8 us
  Pallas kernels: 19.5 us -> 21.3 us
    ppermute x9, waiting for transfers between devices: 1.93 us -> 10.8 us  [shifted(): return lax.ppermute(value, ('row', 'col'), pairs)]
    unnamed x31 -> x40, local copies, waits for them, and re-layouts: 6.13 us -> 11.4 us
    select_n x3 -> x0, other arithmetic: 4.65 us -> none  [merge(): jnp.where(summed, a + b, jnp.maximum(a, b))]
    add x0 -> x2, other arithmetic: none -> 3.57 us  [the longest x1 2.24 us: chip_sum(): return mine[pair ^ d] + arrived[pair ^ d]]
    ppermute x9, starting transfers between devices: 27.1 us -> 23.6 us  [shifted(): return lax.ppermute(value, ('row', 'col'), pairs)]
    ppermute x17, waiting for transfers between devices: 32.7 us -> 35.7 us  [swapped(): return lax.ppermute(value, ('row', 'col'), pairs)]
    ppermute x17, starting transfers between devices: 24.1 us -> 22 us  [swapped(): return lax.ppermute(value, ('row', 'col'), pairs)]
    pallas_call x1, Pallas kernels: 14 us -> 15.9 us  [body(): pl.pallas_call(main_kernel, out_shape=(f32(2, rows, cols), f32(2, side, c...]
  transfers between devices with their start and end apart: 26 -> 26, of which waited for: 14 -> 14; matrix products, arithmetic and copies ran while one was open for 8% -> 6% of each run, Pallas kernels for 3% -> 2%
where the time goes in v6:
time: 139 us; the launch traced here: 138 us
  waiting for transfers between devices  46.5 us (33%)
  starting transfers between devices  45.7 us (33%)
  Pallas kernels  21.3 us (15%)
  local copies, waits for them, and re-layouts  12.8 us (9%)
  other arithmetic  5.97 us (4%)
  matrix products  4.97 us (4%)
    ppermute x17, waiting for transfers between devices, swapped(): return lax.ppermute(value, ('row', 'col'), pairs)  35.7 us
    ppermute x9, starting transfers between devices, shifted(): return lax.ppermute(value, ('row', 'col'), pairs)  23.6 us
    ppermute x17, starting transfers between devices, swapped(): return lax.ppermute(value, ('row', 'col'), pairs)  22 us
    pallas_call x1, Pallas kernels, body(): pl.pallas_call(main_kernel, out_shape=(f32(2, rows, cols), f32(2, side, c...  15.9 us
    unnamed x40, local copies, waits for them, and re-layouts  11.4 us
    ppermute x9, waiting for transfers between devices, shifted(): return lax.ppermute(value, ('row', 'col'), pairs)  10.8 us
  transfers between devices with their start and end apart: 26, of which 14 were waited for; matrix products, arithmetic and copies ran while one was open for 6% of the time, Pallas kernels for 2%

profile of v6, /device:TPU:0, one launch (start us, length us, event | category | flops | bytes accessed | tf_op | source)
XLA Modules:
  0.0 138.1 jit_solution(5359548462502151226)
XLA Ops:
  0.6 1.2 slice.48
  1.9 1.4 %collective-permute-start.1 = (f32[2,256,256]{2,1,0:T(8,128)S(1)}, f32[2,256,256]{2,1,0:T(8,128)S(1)}, u32[]{:S(2)}, u32[]{:S(2)}) collective-permute-start(f32[2,256,256]{2,1,0:T(8,128)S(1)} %slice.48), channel_id=1, source_target_pairs={{1,0},{2,1},{3,2},{5,4},{6,5},{7,6},{9,8},{10,9},{11,10},{13,12},{... | collective-permute-start | bytes 1572872 | tf_op jit(solution)/shard_map/ppermute | solution.py:24
  3.3 2.4 %fusion.2 = f32[256,6,256]{2,0,1:T(8,128)S(1)} fusion(f32[256,256,1]{1,0,2:T(8,128)} %constant.38, f32[1,1,6,256,256]{4,3,2,1,0:T(8,128)S(1)} %copy-done), kind=kOutput, calls=%fused_computation.2 | convolution fusion | flops 1207959552 | bytes 3407872 | tf_op jit(solution)/shard_map/ab,sbc->sac/dot_general | solution.py:50
  5.7 2.6 %fusion.amp_ref = f32[6,256,256]{2,1,0:T(8,128)} fusion(f32[256,256,1]{1,0,2:T(8,128)S(1)} %copy-done.15, f32[256,6,256]{2,0,1:T(8,128)S(1)} %fusion.2), kind=kOutput, calls=%fused_computation | convolution fusion | flops 1207959552 | bytes 3407872 | tf_op jit(solution)/shard_map/sac,dc->sad/dot_general | solution.py:51
  8.3 1.3 collective-permute-start
  9.6 9.2 %collective-permute-done.1.right_ref = f32[2,256,256]{2,1,0:T(8,128)S(1)} collective-permute-done((f32[2,256,256]{2,1,0:T(8,128)S(1)}, f32[2,256,256]{2,1,0:T(8,128)S(1)}, u32[]{:S(2)}, u32[]{:S(2)}) %collective-permute-start.1) | collective-permute-done | bytes 524320 | tf_op jit(solution)/shard_map/ppermute | solution.py:24
  18.8 1.3 collective-permute-start.2
  20.2 3.0 %collective-permute-start.3 = (s32[6,2]{1,0:T(8,128)S(1)}, s32[6,2]{1,0:T(8,128)S(1)}, u32[]{:S(2)}, u32[]{:S(2)}) collective-permute-start(s32[6,2]{1,0:T(8,128)S(1)} %copy.15.spots_ref), channel_id=1, source_target_pairs={{0,4},{1,5},{2,6},{3,7},{4,8},{5,9},{6,10},{7,11},{8,12},{9,13},{1... | collective-permute-start | bytes 152 | tf_op jit(solution)/shard_map/ppermute | solution.py:24
  23.3 3.6 %collective-permute-start.4 = (s32[6,2]{1,0:T(8,128)S(1)}, s32[6,2]{1,0:T(8,128)S(1)}, u32[]{:S(2)}, u32[]{:S(2)}) collective-permute-start(s32[6,2]{1,0:T(8,128)S(1)} %copy.15.spots_ref), channel_id=1, source_target_pairs={{0,1},{1,2},{2,3},{4,5},{5,6},{6,7},{8,9},{9,10},{10,11},{12,13},{... | collective-permute-start | bytes 152 | tf_op jit(solution)/shard_map/ppermute | solution.py:24
  26.9 3.9 %collective-permute-start.5 = (s32[6,2]{1,0:T(8,128)S(1)}, s32[6,2]{1,0:T(8,128)S(1)}, u32[]{:S(2)}, u32[]{:S(2)}) collective-permute-start(s32[6,2]{1,0:T(8,128)S(1)} %copy.15.spots_ref), channel_id=1, source_target_pairs={{0,5},{1,6},{2,7},{4,9},{5,10},{6,11},{8,13},{9,14},{10,15},{12,17... | collective-permute-start | bytes 152 | tf_op jit(solution)/shard_map/ppermute | solution.py:24
  30.9 1.2 collective-permute-done.5.diag_ref
  32.2 1.6 %copy-done.1 = f32[2,4,256,256]{3,2,1,0:T(8,128)S(1)} copy-done((f32[2,4,256,256]{3,2,1,0:T(8,128)S(1)}, f32[2,4,256,256]{3,2,1,0:T(8,128)}, u32[]{:S(2)}) %copy-start.1) | copy-done | bytes 2097176
  33.7 1.4 %copy-done.6 = f32[6,256,256]{2,1,0:T(8,128)S(1)} copy-done((f32[6,256,256]{2,1,0:T(8,128)S(1)}, f32[6,256,256]{2,1,0:T(8,128)}, u32[]{:S(2)}) %copy-start.6) | copy-done | bytes 1572888
  35.2 1.0 copy-done.14
  36.2 15.9 %positions.1 = (f32[2,256,512]{2,1,0:T(8,128)S(1)}, f32[2,256,768]{2,1,0:T(8,128)}, f32[2,256,256]{2,1,0:T(8,128)}, f32[4,288,256]{2,1,0:T(8,128)S(1)}, f32[4,288,256]{2,1,0:T(8,128)}) custom-call(s32[8,4]{1,0:T(8,128)S(1)} %copy.14.counts_ref, s32[6,2]{1,0:T(8,128)S(1)} %copy.15.spots_ref, f32[2,256,512]{2,1,0:T(8,128)S(1)} %copy-done.4, ...), custom_call_target="tpu_custom_call" | custom-call | flops 7000000000 | bytes 20000000 | tf_op jit(solution)/shard_map/positions/pallas_call | solution.py:316
  52.1 1.0 copy-done.7
  53.1 1.0 copy-done.8
  54.1 3.2 %collective-permute-done.6 = f32[4,288,256]{2,1,0:T(8,128)} collective-permute-done((f32[4,288,256]{2,1,0:T(8,128)}, f32[4,288,256]{2,1,0:T(8,128)}, u32[]{:S(2)}, u32[]{:S(2)}) %collective-permute-start.6) | collective-permute-done | bytes 1179680 | tf_op jit(solution)/shard_map/ppermute | solution.py:30
  57.3 2.2 %add_bitcast_fusion.2 = (f32[288,256]{1,0:T(8,128)S(1)}, f32[288,256]{1,0:T(8,128)}, f32[288,256]{1,0:T(8,128)S(1)}) fusion(f32[4,288,256]{2,1,0:T(8,128)} %collective-permute-done.6, s32[]{:T(128)S(6)} %select_n.35, f32[4,288,256]{2,1,0:T(8,128)} %copy-done.7, s32[]{:T(128)S(6)} %select_n.37, s32[]{:T(128)S(6)} %select_n.36), kind=kLoop, calls=%fused_computation.9 | loop fusion | flops 221184 | bytes 2654220 | tf_op jit(solution)/shard_map/add | solution.py:359
  59.5 3.5 %collective-permute-start.9 = (f32[288,256]{1,0:T(8,128)}, f32[288,256]{1,0:T(8,128)S(1)}, u32[]{:S(2)}, u32[]{:S(2)}) collective-permute-start(f32[288,256]{1,0:T(8,128)} %get-tuple-element.61), channel_id=1, source_target_pairs={{0,24},{1,25},{2,26},{3,27},{4,28},{5,29},{6,30},{7,31},{8,16},{9,... | collective-permute-start | bytes 884744 | tf_op jit(solution)/shard_map/ppermute | solution.py:30
  63.0 5.3 %collective-permute-start.8 = (f32[288,256]{1,0:T(8,128)S(1)}, f32[288,256]{1,0:T(8,128)}, u32[]{:S(2)}, u32[]{:S(2)}) collective-permute-start(f32[288,256]{1,0:T(8,128)S(1)} %get-tuple-element.62), channel_id=1, source_target_pairs={{0,16},{1,17},{2,18},{3,19},{4,20},{5,21},{6,22},{7,23},{8,24},{9,... | collective-permute-start | bytes 884744 | tf_op jit(solution)/shard_map/ppermute | solution.py:30
  68.9 4.4 %collective-permute-start.10 = (f32[2,256,256]{2,1,0:T(8,128)}, f32[2,256,256]{2,1,0:T(8,128)S(1)}, u32[]{:S(2)}, u32[]{:S(2)}) collective-permute-start(f32[2,256,256]{2,1,0:T(8,128)} %get-tuple-element.46), channel_id=1, source_target_pairs={{0,1},{1,2},{2,3},{4,5},{5,6},{6,7},{8,9},{9,10},{10,11},{12,13},{... | collective-permute-start | bytes 1572872 | tf_op jit(solution)/shard_map/ppermute | solution.py:24
  73.4 1.6 %copy-done.2 = f32[2,4,256,256]{3,2,1,0:T(8,128)S(1)} copy-done((f32[2,4,256,256]{3,2,1,0:T(8,128)S(1)}, f32[2,4,256,256]{3,2,1,0:T(8,128)}, u32[]{:S(2)}) %copy-start.2) | copy-done | bytes 2097176
  75.0 2.1 %lighting.1 = (f32[256,512]{1,0:T(8,128)S(1)}, f32[8,256]{1,0:T(8,128)S(1)}) custom-call(s32[8,4]{1,0:T(8,128)S(1)} %copy.14.counts_ref, s32[6,2]{1,0:T(8,128)S(1)} %copy.15.spots_ref, s32[6,2]{1,0:T(8,128)S(1)} %collective-permute-done.3.up_ref, s32[6,2]{1,0:T(8,128)S(1)} %collective-permute-done.4.left_ref, s32[6,2]{1,0:T(8,128)S(1)} %collective-permute-done.5.diag_ref, ...), custom_call_target="tpu_custom_call" | custom-call | flops 100000000 | bytes 10000000 | tf_op jit(solution)/shard_map/lighting/pallas_call | solution.py:342
  77.1 4.1 %collective-permute-done.8 = f32[288,256]{1,0:T(8,128)} collective-permute-done((f32[288,256]{1,0:T(8,128)S(1)}, f32[288,256]{1,0:T(8,128)}, u32[]{:S(2)}, u32[]{:S(2)}) %collective-permute-start.8) | collective-permute-done | bytes 294944 | tf_op jit(solution)/shard_map/ppermute | solution.py:30
  81.1 1.7 %collective-permute-done.7 = f32[288,256]{1,0:T(8,128)} collective-permute-done((f32[288,256]{1,0:T(8,128)S(1)}, f32[288,256]{1,0:T(8,128)}, u32[]{:S(2)}, u32[]{:S(2)}) %collective-permute-start.7) | collective-permute-done | bytes 294944 | tf_op jit(solution)/shard_map/ppermute | solution.py:30
  82.9 1.3 fusion.5
  84.6 0.8 copy-done.10
  85.4 1.4 collective-permute-start.17
  87.5 3.8 %collective-permute-start.12 = (f32[80,256]{1,0:T(8,128)}, f32[80,256]{1,0:T(8,128)}, u32[]{:S(2)}, u32[]{:S(2)}) collective-permute-start(f32[80,256]{1,0:T(8,128)} %get-tuple-element.67), channel_id=1, source_target_pairs={{0,2},{1,3},{2,0},{3,1},{4,6},{5,7},{6,4},{7,5},{8,10},{9,11},{10,... | collective-permute-start | bytes 245768 | tf_op jit(solution)/shard_map/ppermute | solution.py:30
  91.9 2.1 %collective-permute-done.13 = f32[80,256]{1,0:T(8,128)S(1)} collective-permute-done((f32[80,256]{1,0:T(8,128)}, f32[80,256]{1,0:T(8,128)S(1)}, u32[]{:S(2)}, u32[]{:S(2)}) %collective-permute-start.13) | collective-permute-done | bytes 81952 | tf_op jit(solution)/shard_map/ppermute | solution.py:30
  94.1 5.9 %collective-permute-done.12 = f32[80,256]{1,0:T(8,128)} collective-permute-done((f32[80,256]{1,0:T(8,128)}, f32[80,256]{1,0:T(8,128)}, u32[]{:S(2)}, u32[]{:S(2)}) %collective-permute-start.12) | collective-permute-done | bytes 81952 | tf_op jit(solution)/shard_map/ppermute | solution.py:30
  100.0 0.9 constant_dynamic-update-slice_fusion.4
  101.0 0.8 collective-permute-start.15
  101.8 3.5 %collective-permute-start.16 = (f32[72,256]{1,0:T(8,128)S(1)}, f32[72,256]{1,0:T(8,128)S(1)}, u32[]{:S(2)}, u32[]{:S(2)}) collective-permute-start(f32[72,256]{1,0:T(8,128)S(1)} %get-tuple-element.59), channel_id=1, source_target_pairs={{0,3},{1,2},{2,1},{3,0},{4,7},{5,6},{6,5},{7,4},{8,11},{9,10},{10,... | collective-permute-start | bytes 221192 | tf_op jit(solution)/shard_map/ppermute | solution.py:30
  105.4 0.9 collective-permute-done.14
  106.3 3.9 %collective-permute-done.15 = f32[72,256]{1,0:T(8,128)S(1)} collective-permute-done((f32[72,256]{1,0:T(8,128)S(1)}, f32[72,256]{1,0:T(8,128)S(1)}, u32[]{:S(2)}, u32[]{:S(2)}) %collective-permute-start.15) | collective-permute-done | bytes 73760 | tf_op jit(solution)/shard_map/ppermute | solution.py:30
  111.0 3.3 %collective-permute-start.21 = (f32[2,256,256]{2,1,0:T(8,128)S(1)}, f32[2,256,256]{2,1,0:T(8,128)S(1)}, u32[]{:S(2)}, u32[]{:S(2)}) collective-permute-start(f32[2,256,256]{2,1,0:T(8,128)S(1)} %slice.70), channel_id=1, source_target_pairs={{0,1},{1,2},{2,3},{4,5},{5,6},{6,7},{8,9},{9,10},{10,11},{12,13},{... | collective-permute-start | bytes 1572872 | tf_op jit(solution)/shard_map/ppermute | solution.py:24
  114.3 2.2 %collective-permute-start.19 = (f32[296,256]{1,0:T(8,128)S(1)}, f32[296,256]{1,0:T(8,128)S(1)}, u32[]{:S(2)}, u32[]{:S(2)}) collective-permute-start(f32[296,256]{1,0:T(8,128)S(1)} %constant_dynamic-update-slice_fusion.refs_0_), channel_id=1, source_target_pairs={{0,16},{1,17},{2,18},{3,19},{4,20},{5,21},{6,22},{7,23},{8,24},{9,... | collective-permute-start | bytes 909320 | tf_op jit(solution)/shard_map/ppermute | solution.py:30
  116.6 1.4 %collective-permute-start.20 = (f32[296,256]{1,0:T(8,128)S(1)}, f32[296,256]{1,0:T(8,128)S(1)}, u32[]{:S(2)}, u32[]{:S(2)}) collective-permute-start(f32[296,256]{1,0:T(8,128)S(1)} %constant_dynamic-update-slice_fusion.refs_0_), channel_id=1, source_target_pairs={{0,24},{1,25},{2,26},{3,27},{4,28},{5,29},{6,30},{7,31},{8,16},{9,... | collective-permute-start | bytes 909320 | tf_op jit(solution)/shard_map/ppermute | solution.py:30
  118.1 5.6 %collective-permute-done.19.refs_2_ = f32[296,256]{1,0:T(8,128)S(1)} collective-permute-done((f32[296,256]{1,0:T(8,128)S(1)}, f32[296,256]{1,0:T(8,128)S(1)}, u32[]{:S(2)}, u32[]{:S(2)}) %collective-permute-start.19) | collective-permute-done | bytes 303136 | tf_op jit(solution)/shard_map/ppermute | solution.py:30
  123.6 3.0 %collective-permute-done.18.refs_1_ = f32[296,256]{1,0:T(8,128)S(1)} collective-permute-done((f32[296,256]{1,0:T(8,128)S(1)}, f32[296,256]{1,0:T(8,128)S(1)}, u32[]{:S(2)}, u32[]{:S(2)}) %collective-permute-start.18) | collective-permute-done | bytes 303136 | tf_op jit(solution)/shard_map/ppermute | solution.py:30
  126.6 3.7 %collective-permute-done.20.refs_3_ = f32[296,256]{1,0:T(8,128)S(1)} collective-permute-done((f32[296,256]{1,0:T(8,128)S(1)}, f32[296,256]{1,0:T(8,128)S(1)}, u32[]{:S(2)}, u32[]{:S(2)}) %collective-permute-start.20) | collective-permute-done | bytes 303136 | tf_op jit(solution)/shard_map/ppermute | solution.py:30
  130.3 1.6 %collective-permute-done.25.refs_7_ = f32[296,256]{1,0:T(8,128)S(1)} collective-permute-done((f32[296,256]{1,0:T(8,128)S(1)}, f32[296,256]{1,0:T(8,128)S(1)}, u32[]{:S(2)}, u32[]{:S(2)}) %collective-permute-start.25) | collective-permute-done | bytes 303136 | tf_op jit(solution)/shard_map/ppermute | solution.py:30
  132.0 1.2 copy-done.9
  133.2 1.0 copy-done.13
  134.2 1.4 %object_update.1 = f32[2,256,512]{2,1,0:T(8,128)} custom-call(f32[2,256,512]{2,1,0:T(8,128)S(1)} %copy-done.5, f32[256,512]{1,0:T(8,128)S(1)} %copy-done.13, f32[8,256]{1,0:T(8,128)S(1)} %slice_maximum_fusion.top_ref, f32[2,256,512]{2,1,0:T(8,128)S(1)} %copy-done.9, f32[2,256,256]{2,1,0:T(8,128)S(1)} %copy-done.11, ...), custom_call_target="tpu_custom_call" | custom-call | flops 1000000 | bytes 6000000 | tf_op jit(solution)/shard_map/object_update/pallas_call | solution.py:380
  136.2 1.9 %probe_update.1 = f32[2,4,256,256]{3,2,1,0:T(8,128)} custom-call(f32[2,4,256,256]{3,2,1,0:T(8,128)S(1)} %copy-done.3, f32[296,256]{1,0:T(8,128)S(1)} %constant_dynamic-update-slice_fusion.refs_0_, f32[296,256]{1,0:T(8,128)S(1)} %collective-permute-done.18.refs_1_, f32[296,256]{1,0:T(8,128)S(1)} %collective-permute-done.19.refs_2_, ...), custom_call_target="tpu_custom_call" | custom-call | flops 1000000 | bytes 6000000 | tf_op jit(solution)/shard_map/probe_update/pallas_call | solution.py:389
  (60 shorter events, 4.1 us)
Async XLA Ops:
  0.6 2.7 %copy-start = (f32[1,1,6,256,256]{4,3,2,1,0:T(8,128)S(1)}, f32[1,1,6,256,256]{4,3,2,1,0:T(8,128)}, u32[]{:S(2)}) copy-start(f32[1,1,6,256,256]{4,3,2,1,0:T(8,128)} %param.9) | copy-start | bytes 4718596
  1.8 3.9 %copy-start.15 = (f32[256,256,1]{1,0,2:T(8,128)S(1)}, f32[256,256,1]{1,0,2:T(8,128)}, u32[]{:S(2)}) copy-start(f32[256,256,1]{1,0,2:T(8,128)} %constant.38) | copy-start | bytes 786436
  1.9 17.0 %collective-permute-start.1 = (f32[2,256,256]{2,1,0:T(8,128)S(1)}, f32[2,256,256]{2,1,0:T(8,128)S(1)}, u32[]{:S(2)}, u32[]{:S(2)}) collective-permute-start(f32[2,256,256]{2,1,0:T(8,128)S(1)} %slice.48), channel_id=1, source_target_pairs={{1,0},{2,1},{3,2},{5,4},{6,5},{7,6},{9,8},{10,9},{11,10},{13,12},{... | collective-permute-start | bytes 1572872 | tf_op jit(solution)/shard_map/ppermute | solution.py:24
  5.7 2.6 %copy-start.4 = (f32[2,256,512]{2,1,0:T(8,128)S(1)}, f32[2,256,512]{2,1,0:T(8,128)}, u32[]{:S(2)}) copy-start(f32[2,256,512]{2,1,0:T(8,128)} %tile_ref.3) | copy-start | bytes 3145732
  5.7 14.4 %copy-start.17 = (s32[1,1,6,2]{2,3,1,0:T(2,128)S(1)}, s32[1,1,6,2]{2,3,1,0:T(2,128)}, u32[]{:S(2)}) copy-start(s32[1,1,6,2]{2,3,1,0:T(2,128)} %param.10) | copy-start | bytes 148
  5.7 25.1 %copy-start.16 = (s32[8,4]{0,1:T(4,128)S(1)}, s32[8,4]{0,1:T(4,128)}, u32[]{:S(2)}) copy-start(s32[8,4]{0,1:T(4,128)} %param.11) | copy-start | bytes 388
  8.3 23.8 %collective-permute-start = (f32[2,256,512]{2,1,0:T(8,128)S(1)}, f32[2,256,512]{2,1,0:T(8,128)}, u32[]{:S(2)}, u32[]{:S(2)}) collective-permute-start(f32[2,256,512]{2,1,0:T(8,128)S(1)} %copy-done.4), channel_id=1, source_target_pairs={{4,0},{5,1},{6,2},{7,3},{8,4},{9,5},{10,6},{11,7},{12,8},{13,9},{1... | collective-permute-start | bytes 3145736 | tf_op jit(solution)/shard_map/ppermute | solution.py:24
  18.8 13.3 %collective-permute-start.2 = (f32[2,256,256]{2,1,0:T(8,128)S(1)}, f32[2,256,256]{2,1,0:T(8,128)}, u32[]{:S(2)}, u32[]{:S(2)}) collective-permute-start(f32[2,256,256]{2,1,0:T(8,128)S(1)} %collective-permute-done.1.right_ref), channel_id=1, source_target_pairs={{4,0},{5,1},{6,2},{7,3},{8,4},{9,5},{10,6},{11,7},{12,8},{13,9},{1... | collective-permute-start | bytes 1572872 | tf_op jit(solution)/shard_map/ppermute | solution.py:24
  20.2 10.7 %collective-permute-start.3 = (s32[6,2]{1,0:T(8,128)S(1)}, s32[6,2]{1,0:T(8,128)S(1)}, u32[]{:S(2)}, u32[]{:S(2)}) collective-permute-start(s32[6,2]{1,0:T(8,128)S(1)} %copy.15.spots_ref), channel_id=1, source_target_pairs={{0,4},{1,5},{2,6},{3,7},{4,8},{5,9},{6,10},{7,11},{8,12},{9,13},{1... | collective-permute-start | bytes 152 | tf_op jit(solution)/shard_map/ppermute | solution.py:24
  23.3 7.7 %collective-permute-start.4 = (s32[6,2]{1,0:T(8,128)S(1)}, s32[6,2]{1,0:T(8,128)S(1)}, u32[]{:S(2)}, u32[]{:S(2)}) collective-permute-start(s32[6,2]{1,0:T(8,128)S(1)} %copy.15.spots_ref), channel_id=1, source_target_pairs={{0,1},{1,2},{2,3},{4,5},{5,6},{6,7},{8,9},{9,10},{10,11},{12,13},{... | collective-permute-start | bytes 152 | tf_op jit(solution)/shard_map/ppermute | solution.py:24
  26.9 5.2 %collective-permute-start.5 = (s32[6,2]{1,0:T(8,128)S(1)}, s32[6,2]{1,0:T(8,128)S(1)}, u32[]{:S(2)}, u32[]{:S(2)}) collective-permute-start(s32[6,2]{1,0:T(8,128)S(1)} %copy.15.spots_ref), channel_id=1, source_target_pairs={{0,5},{1,6},{2,7},{4,9},{5,10},{6,11},{8,13},{9,14},{10,15},{12,17... | collective-permute-start | bytes 152 | tf_op jit(solution)/shard_map/ppermute | solution.py:24
  32.1 1.6 %copy-start.1 = (f32[2,4,256,256]{3,2,1,0:T(8,128)S(1)}, f32[2,4,256,256]{3,2,1,0:T(8,128)}, u32[]{:S(2)}) copy-start(f32[2,4,256,256]{3,2,1,0:T(8,128)} %probe_ref.5) | copy-start | bytes 6291460
  33.7 1.4 %copy-start.6 = (f32[6,256,256]{2,1,0:T(8,128)S(1)}, f32[6,256,256]{2,1,0:T(8,128)}, u32[]{:S(2)}) copy-start(f32[6,256,256]{2,1,0:T(8,128)} %fusion.amp_ref) | copy-start | bytes 4718596
  35.2 1.0 copy-start.14
  52.1 1.0 copy-start.7
  53.1 1.0 copy-start.8
  54.1 3.2 %collective-permute-start.6 = (f32[4,288,256]{2,1,0:T(8,128)}, f32[4,288,256]{2,1,0:T(8,128)}, u32[]{:S(2)}, u32[]{:S(2)}) collective-permute-start(f32[4,288,256]{2,1,0:T(8,128)} %get-tuple-element.35), channel_id=1, source_target_pairs={{0,4},{1,5},{2,6},{3,7},{4,0},{5,1},{6,2},{7,3},{8,12},{9,13},{10,... | collective-permute-start | bytes 3538952 | tf_op jit(solution)/shard_map/ppermute | solution.py:30
  59.5 17.5 %collective-permute-start.9 = (f32[288,256]{1,0:T(8,128)}, f32[288,256]{1,0:T(8,128)S(1)}, u32[]{:S(2)}, u32[]{:S(2)}) collective-permute-start(f32[288,256]{1,0:T(8,128)} %get-tuple-element.61), channel_id=1, source_target_pairs={{0,24},{1,25},{2,26},{3,27},{4,28},{5,29},{6,30},{7,31},{8,16},{9,... | collective-permute-start | bytes 884744 | tf_op jit(solution)/shard_map/ppermute | solution.py:30
  63.0 18.1 %collective-permute-start.8 = (f32[288,256]{1,0:T(8,128)S(1)}, f32[288,256]{1,0:T(8,128)}, u32[]{:S(2)}, u32[]{:S(2)}) collective-permute-start(f32[288,256]{1,0:T(8,128)S(1)} %get-tuple-element.62), channel_id=1, source_target_pairs={{0,16},{1,17},{2,18},{3,19},{4,20},{5,21},{6,22},{7,23},{8,24},{9,... | collective-permute-start | bytes 884744 | tf_op jit(solution)/shard_map/ppermute | solution.py:30
  68.3 14.6 %collective-permute-start.7 = (f32[288,256]{1,0:T(8,128)S(1)}, f32[288,256]{1,0:T(8,128)}, u32[]{:S(2)}, u32[]{:S(2)}) collective-permute-start(f32[288,256]{1,0:T(8,128)S(1)} %get-tuple-element.60), channel_id=1, source_target_pairs={{0,8},{1,9},{2,10},{3,11},{4,12},{5,13},{6,14},{7,15},{8,0},{9,1},... | collective-permute-start | bytes 884744 | tf_op jit(solution)/shard_map/ppermute | solution.py:30
  68.9 15.6 %collective-permute-start.10 = (f32[2,256,256]{2,1,0:T(8,128)}, f32[2,256,256]{2,1,0:T(8,128)S(1)}, u32[]{:S(2)}, u32[]{:S(2)}) collective-permute-start(f32[2,256,256]{2,1,0:T(8,128)} %get-tuple-element.46), channel_id=1, source_target_pairs={{0,1},{1,2},{2,3},{4,5},{5,6},{6,7},{8,9},{9,10},{10,11},{12,13},{... | collective-permute-start | bytes 1572872 | tf_op jit(solution)/shard_map/ppermute | solution.py:24
  73.4 1.6 %copy-start.2 = (f32[2,4,256,256]{3,2,1,0:T(8,128)S(1)}, f32[2,4,256,256]{3,2,1,0:T(8,128)}, u32[]{:S(2)}) copy-start(f32[2,4,256,256]{3,2,1,0:T(8,128)} %probe_ref.5) | copy-start | bytes 6291460
  77.0 8.3 %copy-start.12 = (f32[256,512]{1,0:T(8,128)}, f32[256,512]{1,0:T(8,128)S(1)}, u32[]{:S(2)}) copy-start(f32[256,512]{1,0:T(8,128)S(1)} %get-tuple-element.42.light_ref) | copy-start | bytes 1572868
  84.6 0.8 copy-start.10
  85.4 25.6 %collective-permute-start.17 = (f32[2,256,768]{2,1,0:T(8,128)}, f32[2,256,768]{2,1,0:T(8,128)S(1)}, u32[]{:S(2)}, u32[]{:S(2)}) collective-permute-start(f32[2,256,768]{2,1,0:T(8,128)} %get-tuple-element.50), channel_id=1, source_target_pairs={{0,4},{1,5},{2,6},{3,7},{4,8},{5,9},{6,10},{7,11},{8,12},{9,13},{1... | collective-permute-start | bytes 4718600 | tf_op jit(solution)/shard_map/ppermute | solution.py:24
  87.5 6.5 %collective-permute-start.13 = (f32[80,256]{1,0:T(8,128)}, f32[80,256]{1,0:T(8,128)S(1)}, u32[]{:S(2)}, u32[]{:S(2)}) collective-permute-start(f32[80,256]{1,0:T(8,128)} %get-tuple-element.68), channel_id=1, source_target_pairs={{0,3},{1,2},{2,1},{3,0},{4,7},{5,6},{6,5},{7,4},{8,11},{9,10},{10,... | collective-permute-start | bytes 245768 | tf_op jit(solution)/shard_map/ppermute | solution.py:30
  87.5 12.4 %collective-permute-start.12 = (f32[80,256]{1,0:T(8,128)}, f32[80,256]{1,0:T(8,128)}, u32[]{:S(2)}, u32[]{:S(2)}) collective-permute-start(f32[80,256]{1,0:T(8,128)} %get-tuple-element.67), channel_id=1, source_target_pairs={{0,2},{1,3},{2,0},{3,1},{4,6},{5,7},{6,4},{7,5},{8,10},{9,11},{10,... | collective-permute-start | bytes 245768 | tf_op jit(solution)/shard_map/ppermute | solution.py:30
  91.4 8.6 %collective-permute-start.11 = (f32[80,256]{1,0:T(8,128)}, f32[80,256]{1,0:T(8,128)}, u32[]{:S(2)}, u32[]{:S(2)}) collective-permute-start(f32[80,256]{1,0:T(8,128)} %get-tuple-element.66), channel_id=1, source_target_pairs={{0,1},{1,0},{2,3},{3,2},{4,5},{5,4},{6,7},{7,6},{8,9},{9,8},{10,11... | collective-permute-start | bytes 245768 | tf_op jit(solution)/shard_map/ppermute | solution.py:30
  91.9 40.0 %copy-start.5 = (f32[2,256,512]{2,1,0:T(8,128)S(1)}, f32[2,256,512]{2,1,0:T(8,128)}, u32[]{:S(2)}) copy-start(f32[2,256,512]{2,1,0:T(8,128)} %tile_ref.3) | copy-start | bytes 3145732
  91.9 40.0 %copy-start.11 = (f32[2,256,256]{2,1,0:T(8,128)S(1)}, f32[2,256,256]{2,1,0:T(8,128)}, u32[]{:S(2)}) copy-start(f32[2,256,256]{2,1,0:T(8,128)} %copy-done.10) | copy-start | bytes 1572868
  100.9 5.4 %collective-permute-start.14 = (f32[72,256]{1,0:T(8,128)S(1)}, f32[72,256]{1,0:T(8,128)S(1)}, u32[]{:S(2)}, u32[]{:S(2)}) collective-permute-start(f32[72,256]{1,0:T(8,128)S(1)} %get-tuple-element.59), channel_id=1, source_target_pairs={{0,1},{1,0},{2,3},{3,2},{4,5},{5,4},{6,7},{7,6},{8,9},{9,8},{10,11... | collective-permute-start | bytes 221192 | tf_op jit(solution)/shard_map/ppermute | solution.py:30
  101.0 9.2 %collective-permute-start.15 = (f32[72,256]{1,0:T(8,128)S(1)}, f32[72,256]{1,0:T(8,128)S(1)}, u32[]{:S(2)}, u32[]{:S(2)}) collective-permute-start(f32[72,256]{1,0:T(8,128)S(1)} %get-tuple-element.59), channel_id=1, source_target_pairs={{0,2},{1,3},{2,0},{3,1},{4,6},{5,7},{6,4},{7,5},{8,10},{9,11},{10,... | collective-permute-start | bytes 221192 | tf_op jit(solution)/shard_map/ppermute | solution.py:30
  101.8 8.4 %collective-permute-start.16 = (f32[72,256]{1,0:T(8,128)S(1)}, f32[72,256]{1,0:T(8,128)S(1)}, u32[]{:S(2)}, u32[]{:S(2)}) collective-permute-start(f32[72,256]{1,0:T(8,128)S(1)} %get-tuple-element.59), channel_id=1, source_target_pairs={{0,3},{1,2},{2,1},{3,0},{4,7},{5,6},{6,5},{7,4},{8,11},{9,10},{10,... | collective-permute-start | bytes 221192 | tf_op jit(solution)/shard_map/ppermute | solution.py:30
  111.0 19.3 %collective-permute-start.21 = (f32[2,256,256]{2,1,0:T(8,128)S(1)}, f32[2,256,256]{2,1,0:T(8,128)S(1)}, u32[]{:S(2)}, u32[]{:S(2)}) collective-permute-start(f32[2,256,256]{2,1,0:T(8,128)S(1)} %slice.70), channel_id=1, source_target_pairs={{0,1},{1,2},{2,3},{4,5},{5,6},{6,7},{8,9},{9,10},{10,11},{12,13},{... | collective-permute-start | bytes 1572872 | tf_op jit(solution)/shard_map/ppermute | solution.py:24
  114.3 9.4 %collective-permute-start.19 = (f32[296,256]{1,0:T(8,128)S(1)}, f32[296,256]{1,0:T(8,128)S(1)}, u32[]{:S(2)}, u32[]{:S(2)}) collective-permute-start(f32[296,256]{1,0:T(8,128)S(1)} %constant_dynamic-update-slice_fusion.refs_0_), channel_id=1, source_target_pairs={{0,16},{1,17},{2,18},{3,19},{4,20},{5,21},{6,22},{7,23},{8,24},{9,... | collective-permute-start | bytes 909320 | tf_op jit(solution)/shard_map/ppermute | solution.py:30
  116.5 10.1 %collective-permute-start.18 = (f32[296,256]{1,0:T(8,128)S(1)}, f32[296,256]{1,0:T(8,128)S(1)}, u32[]{:S(2)}, u32[]{:S(2)}) collective-permute-start(f32[296,256]{1,0:T(8,128)S(1)} %constant_dynamic-update-slice_fusion.refs_0_), channel_id=1, source_target_pairs={{0,8},{1,9},{2,10},{3,11},{4,12},{5,13},{6,14},{7,15},{8,0},{9,1},... | collective-permute-start | bytes 909320 | tf_op jit(solution)/shard_map/ppermute | solution.py:30
  116.6 13.7 %collective-permute-start.20 = (f32[296,256]{1,0:T(8,128)S(1)}, f32[296,256]{1,0:T(8,128)S(1)}, u32[]{:S(2)}, u32[]{:S(2)}) collective-permute-start(f32[296,256]{1,0:T(8,128)S(1)} %constant_dynamic-update-slice_fusion.refs_0_), channel_id=1, source_target_pairs={{0,24},{1,25},{2,26},{3,27},{4,28},{5,29},{6,30},{7,31},{8,16},{9,... | collective-permute-start | bytes 909320 | tf_op jit(solution)/shard_map/ppermute | solution.py:30
  118.0 12.3 %collective-permute-start.22 = (f32[296,256]{1,0:T(8,128)S(1)}, f32[296,256]{1,0:T(8,128)S(1)}, u32[]{:S(2)}, u32[]{:S(2)}) collective-permute-start(f32[296,256]{1,0:T(8,128)S(1)} %constant_dynamic-update-slice_fusion.refs_0_), channel_id=1, source_target_pairs={{0,4},{1,5},{2,6},{3,7},{4,0},{5,1},{6,2},{7,3},{8,12},{9,13},{10,... | collective-permute-start | bytes 909320 | tf_op jit(solution)/shard_map/ppermute | solution.py:30
  123.6 6.7 %collective-permute-start.24 = (f32[296,256]{1,0:T(8,128)S(1)}, f32[296,256]{1,0:T(8,128)S(1)}, u32[]{:S(2)}, u32[]{:S(2)}) collective-permute-start(f32[296,256]{1,0:T(8,128)S(1)} %collective-permute-done.19.refs_2_), channel_id=1, source_target_pairs={{0,4},{1,5},{2,6},{3,7},{4,0},{5,1},{6,2},{7,3},{8,12},{9,13},{10,... | collective-permute-start | bytes 909320 | tf_op jit(solution)/shard_map/ppermute | solution.py:30
  126.6 3.7 %collective-permute-start.23 = (f32[296,256]{1,0:T(8,128)S(1)}, f32[296,256]{1,0:T(8,128)S(1)}, u32[]{:S(2)}, u32[]{:S(2)}) collective-permute-start(f32[296,256]{1,0:T(8,128)S(1)} %collective-permute-done.18.refs_1_), channel_id=1, source_target_pairs={{0,4},{1,5},{2,6},{3,7},{4,0},{5,1},{6,2},{7,3},{8,12},{9,13},{10,... | collective-permute-start | bytes 909320 | tf_op jit(solution)/shard_map/ppermute | solution.py:30
  130.3 1.6 %collective-permute-start.25 = (f32[296,256]{1,0:T(8,128)S(1)}, f32[296,256]{1,0:T(8,128)S(1)}, u32[]{:S(2)}, u32[]{:S(2)}) collective-permute-start(f32[296,256]{1,0:T(8,128)S(1)} %collective-permute-done.20.refs_3_), channel_id=1, source_target_pairs={{0,4},{1,5},{2,6},{3,7},{4,0},{5,1},{6,2},{7,3},{8,12},{9,13},{10,... | collective-permute-start | bytes 909320 | tf_op jit(solution)/shard_map/ppermute | solution.py:30
  131.9 1.2 copy-start.9
  133.2 1.0 copy-start.13
  134.2 2.0 %copy-start.3 = (f32[2,4,256,256]{3,2,1,0:T(8,128)S(1)}, f32[2,4,256,256]{3,2,1,0:T(8,128)}, u32[]{:S(2)}) copy-start(f32[2,4,256,256]{3,2,1,0:T(8,128)} %probe_ref.5) | copy-start | bytes 6291460

commit v7 on v6

--- a/solution.py
+++ b/solution.py
@@ -27,6 +27,32 @@
 def swapped(value, flip_row, flip_col):
     rows, cols = lax.axis_size("row"), lax.axis_size("col")
     pairs = [(r * cols + c, (r ^ flip_row) * cols + (c ^ flip_col)) for r in range(rows) for c in range(cols)]
+    return lax.ppermute(value, ("row", "col"), pairs)
+
+
+def plane_bits():
+    return (lax.axis_size("row") // 2).bit_length() - 1
+
+
+def plane_bit(core, step):
+    return step if core == 0 else plane_bits() - 1 - step
+
+
+def plane_rank(core, pair):
+    ranks = []
+    for c in range(2):
+        rank = 0
+        for step in range(plane_bits()):
+            rank = rank * 2 + ((pair >> plane_bit(c, step)) & 1)
+        ranks.append(rank)
+    return jnp.where(core == 0, ranks[0], ranks[1])
+
+
+def flipped(value, step):
+    rows, cols = lax.axis_size("row"), lax.axis_size("col")
+    pairs = [
+        (r * cols + c, (r ^ (2 << plane_bit(r % 2, step))) * cols + c) for r in range(rows) for c in range(cols)
+    ]
     return lax.ppermute(value, ("row", "col"), pairs)
 
 
@@ -93,22 +119,26 @@
 
 
 def main_kernel(
-    counts_ref, spots_ref, tile_ref, below_ref, right_ref, corner_ref, amp_ref, probe_ref, table_ref,
+    counts_ref, spots_ref, tile_hbm, below_hbm, right_hbm, corner_hbm, amp_hbm, probe_hbm, table_hbm,
     g_tile, g_lower, g_right, mine_ref, other_ref,
-    ext, gacc, stage, turned, wave, wins, sums, in_sem, out_sem,
+    ext, gacc, stage, turned, wave, wins, sums, amp_ref, probe_ref, table_ref, in_sem, amp_sem, out_sem,
 ):
     modes, side = probe_ref.shape[1], probe_ref.shape[2]
-    rows, cols = tile_ref.shape[1], tile_ref.shape[2]
+    rows, cols = tile_hbm.shape[1], tile_hbm.shape[2]
     low = side // 2
     my_row, my_col = lax.axis_index("row"), lax.axis_index("col")
-    loads = [
-        pltpu.make_async_copy(ref, ext.at[:, pl.ds(r, ref.shape[1]), pl.ds(c, ref.shape[2])], in_sem.at[i])
-        for i, (ref, r, c) in enumerate(
-            ((tile_ref, 0, 0), (below_ref, rows, 0), (right_ref, 0, cols), (corner_ref, rows, cols))
-        )
-    ]
+    count = counts_ref[my_row, my_col]
+    loads = [(probe_hbm, probe_ref), (table_hbm, table_ref)]
+    for ref, r, c in ((tile_hbm, 0, 0), (below_hbm, rows, 0), (right_hbm, 0, cols), (corner_hbm, rows, cols)):
+        loads.append((ref, ext.at[:, pl.ds(r, ref.shape[1]), pl.ds(c, ref.shape[2])]))
+    loads = [pltpu.make_async_copy(a, b, in_sem.at[i]) for i, (a, b) in enumerate(loads)]
+
+    def amp_load(p, slot):
+        return pltpu.make_async_copy(amp_hbm.at[p], amp_ref.at[slot], amp_sem.at[slot])
+
     for load in loads:
         load.start()
+    amp_load(0, 0).start()
     gacc[...] = jnp.zeros_like(gacc)
     sums[...] = jnp.zeros_like(sums)
     for load in loads:
@@ -124,6 +154,12 @@
         return value.astype(jnp.bfloat16)
 
     def step(p, carry):
+        slot = lax.rem(p, 2)
+
+        @pl.when(p + 1 < count)
+        def _():
+            amp_load(p + 1, 1 - slot).start()
+
         row, col = spots_ref[p, 0] - my_row * rows, spots_ref[p, 1] - my_col * cols
         win_re = window_at(ext, 0, row, col, side)
         win_im = window_at(ext, 1, row, col, side)
@@ -144,12 +180,13 @@
                     turned[1, at:at + low, i * low:(i + 1) * low] = bf16(left - right)
         for parity in range(2):
             wave[parity] = dot(turned[parity], table_ref[2 + parity])
+        amp_load(p, slot).wait()
         for parity in range(2):
             model = jnp.zeros((side, low), jnp.float32)
             for k in range(modes):
                 wr, wi = wave[parity, plane(k), :low], wave[parity, plane(k), low:]
                 model += wr * wr + wi * wi
-            factor = amp_ref[p, :, parity * low:(parity + 1) * low] * lax.rsqrt(jnp.maximum(model, 1.0)) - 1.0
+            factor = amp_ref[slot, :, parity * low:(parity + 1) * low] * lax.rsqrt(jnp.maximum(model, 1.0)) - 1.0
             for k in range(modes):
                 at = k * side + parity * low
                 for i in range(2):
@@ -191,7 +228,7 @@
             add_at(gacc, i, row, col, jnp.concatenate([grads[0][i], grads[1][i]], axis=1), side)
         return carry
 
-    lax.fori_loop(0, counts_ref[my_row, my_col], step, 0)
+    lax.fori_loop(0, count, step, 0)
 
     pairs = lax.axis_size("row") // 2
     share = mine_ref.shape[1]
@@ -211,13 +248,13 @@
         store.wait()
 
 
-def light_kernel(counts_ref, spots_ref, up_ref, left_ref, diag_ref, probe_ref, light_ref, top_ref, lit, acc):
+def light_kernel(counts_ref, spots_ref, left_ref, up_ref, diag_ref, probe_ref, light_ref, top_ref, lit, acc):
     side = probe_ref.shape[2]
     rows, cols = light_ref.shape
     my_row, my_col = lax.axis_index("row"), lax.axis_index("col")
     lit[...] = jnp.sum(probe_ref[0] * probe_ref[0] + probe_ref[1] * probe_ref[1], axis=0)
     acc[...] = jnp.zeros_like(acc)
-    for ref, d_row, d_col in ((spots_ref, 0, 0), (up_ref, 1, 0), (left_ref, 0, 1), (diag_ref, 1, 1)):
+    for ref, d_row, d_col in ((spots_ref, 0, 0), (left_ref, 0, 1), (up_ref, 1, 0), (diag_ref, 1, 1)):
         inside = (my_row >= d_row) & (my_col >= d_col)
         number = counts_ref[jnp.maximum(my_row - d_row, 0), jnp.maximum(my_col - d_col, 0)]
 
@@ -262,7 +299,7 @@
     core, pair = lax.rem(my_row, 2), my_row // 2
     for i, ref in enumerate(block_refs):
         flip, d = i // pairs, i % pairs
-        base = ((core ^ flip) * pairs + (pair ^ d)) * share
+        base = ((core ^ flip) * pairs + (plane_rank(core ^ flip, pair) ^ d)) * share
         for e in range(n_col):
             to = pl.multiple_of(base + (my_col ^ e) * piece, SUBLANES)
             sums[pl.ds(to, piece)] = ref[e * piece:(e + 1) * piece]
@@ -288,6 +325,14 @@
     return pltpu.CompilerParams(vmem_limit_bytes=mib * MIB)
 
 
+def hbm(*shape):
+    return pltpu.HBM(shape, jnp.float32)
+
+
+def in_hbm(value):
+    return pltpu.with_memory_space_constraint(value, pltpu.HBM)
+
+
 def cost(flops, moved):
     return pl.CostEstimate(flops=flops, bytes_accessed=moved, transcendentals=0)
 
@@ -295,31 +340,31 @@
 def body(object_field, probe, amplitudes, corners, counts):
     rows, cols = object_field.shape[1], object_field.shape[2]
     modes, side = probe.shape[1], probe.shape[2]
+    slots = amplitudes.shape[2]
     pairs, n_col = lax.axis_size("row") // 2, lax.axis_size("col")
     step = SUBLANES * 2 * pairs * n_col
     total_rows = -(-(2 * modes + 1) * side // step) * step
     share = total_rows // (2 * pairs)
     piece = share // n_col
-    pair, my_col = lax.axis_index("row") // 2, lax.axis_index("col")
+    my_row, my_col = lax.axis_index("row"), lax.axis_index("col")
+    core, pair = my_row % 2, my_row // 2
     spots = corners[0, 0]
 
     right = shifted(object_field[:, :, :side], 0, -1)
     measured = evens_first(amplitudes[0, 0])
     tile, measured = lax.optimization_barrier((object_field, measured))
     below = shifted(tile[:, :side, :], -1, 0)
-    from_up = shifted(spots, 1, 0)
     from_left = shifted(spots, 0, 1)
-    from_diag = shifted(spots, 1, 1)
     right, measured = lax.optimization_barrier((right, measured))
     corner = shifted(right[:, :side, :], -1, 0)
-    corner, from_up, from_left, from_diag = lax.optimization_barrier((corner, from_up, from_left, from_diag))
+    corner, from_left = lax.optimization_barrier((corner, from_left))
     g_tile, g_lower, g_right, mine, other = pl.pallas_call(
         main_kernel,
         out_shape=(
-            f32(2, rows, cols), f32(2, side, cols + side), f32(2, rows, side),
-            f32(pairs, share, side), f32(pairs, share, side),
+            hbm(2, rows, cols), hbm(2, side, cols + side), hbm(2, rows, side),
+            hbm(pairs, share, side), hbm(pairs, share, side),
         ),
-        in_specs=[SM] * 2 + [HBM] * 4 + [VM] * 3,
+        in_specs=[SM] * 2 + [HBM] + [ANY] * 3 + [HBM] * 3,
         out_specs=(HBM,) * 5,
         scratch_shapes=[
             pltpu.VMEM((2, rows + side, cols + side), jnp.float32),
@@ -329,16 +374,21 @@
             pltpu.VMEM((2, modes * side, side), jnp.float32),
             pltpu.VMEM((2, side, side), jnp.float32),
             pltpu.VMEM((total_rows, side), jnp.float32),
-            pltpu.SemaphoreType.DMA((4,)),
+            pltpu.VMEM((2, side, side), jnp.float32),
+            pltpu.VMEM(probe.shape, jnp.float32),
+            pltpu.VMEM((4, side, side), jnp.bfloat16),
+            pltpu.SemaphoreType.DMA((6,)),
+            pltpu.SemaphoreType.DMA((2,)),
             pltpu.SemaphoreType.DMA((2 * pairs + 3,)),
         ],
-        compiler_params=params(28),
+        compiler_params=params(22),
         cost_estimate=cost(7 * 10**9, 2 * 10**7),
         name="positions",
-    )(counts, spots, object_field, below, right, corner, measured, probe, tables(side))
+    )(counts, spots, in_hbm(object_field), below, right, corner, *map(in_hbm, (measured, probe, tables(side))))
 
     arrived = swapped(other, 1, 0)
-    arrived, from_up, from_left, from_diag = lax.optimization_barrier((arrived, from_up, from_left, from_diag))
+    arrived, from_left = lax.optimization_barrier((arrived, from_left))
+    from_up = shifted(jnp.concatenate([spots, from_left], axis=0), 1, 0)
     light, top = pl.pallas_call(
         light_kernel,
         out_shape=(f32(rows, cols), f32(SUBLANES, side)),
@@ -351,15 +401,19 @@
         compiler_params=params(12),
         cost_estimate=cost(10**8, 10**7),
         name="lighting",
-    )(counts, spots, from_up, from_left, from_diag, probe)
+    )(counts, spots, from_left, from_up[:slots], from_up[slots:], in_hbm(probe))
 
     g_left = shifted(g_right, 0, 1)
 
-    def chip_sum(d):
-        return mine[pair ^ d] + arrived[pair ^ d]
-
-    plane_sum = sum([swapped(chip_sum(d), 2 * d, 0) for d in range(1, pairs)], chip_sum(0))
-    plane_sum, g_lower, g_left, top = lax.optimization_barrier((plane_sum, g_lower, g_left, top))
+    held = mine + arrived
+    for i in range(plane_bits()):
+        keep = (plane_rank(core, pair) >> (plane_bits() - 1 - i)) & 1
+        held = held.reshape(2, -1, share, side)
+        held = held[keep] + flipped(held[1 - keep], i)
+        if i == 0:
+            held, top = lax.optimization_barrier((held, top))
+    plane_sum = held.reshape(share, side)
+    plane_sum, g_lower, g_left = lax.optimization_barrier((plane_sum, g_lower, g_left))
     g_up = shifted(g_lower, 1, 0)
 
     plane_sum = plane_sum.reshape(n_col, piece, side)
@@ -373,7 +427,9 @@
     own = jnp.concatenate([own] + [swapped(own, 0, e) for e in range(1, n_col)] + [top], axis=0)
     own, g_up, g_corner = lax.optimization_barrier((own, g_up, g_up[:, :, cols:]))
     g_diag = shifted(g_corner, 0, 1)
-    blocks = [own] + [swapped(own, 2 * d, 0) for d in range(1, pairs)]
+    blocks = [own]
+    for i in reversed(range(plane_bits())):
+        blocks = blocks + [flipped(block, i) for block in blocks]
     blocks[-1], g_diag = lax.optimization_barrier((blocks[-1], g_diag))
     blocks = blocks + [swapped(block, 1, 0) for block in blocks]
     top = functools.reduce(jnp.maximum, [block[share:] for block in blocks])
@@ -385,7 +441,7 @@
         compiler_params=params(10),
         cost_estimate=cost(10**6, 6 * 10**6),
         name="object_update",
-    )(object_field, light, top, g_tile, g_left, g_up, g_diag)
+    )(in_hbm(object_field), light, top, in_hbm(g_tile), g_left, g_up, g_diag)
     probe_new = pl.pallas_call(
         functools.partial(probe_kernel, (pairs, n_col)),
         out_shape=f32(*probe.shape),
@@ -395,7 +451,7 @@
         compiler_params=params(14),
         cost_estimate=cost(10**6, 6 * 10**6),
         name="probe_update",
-    )(probe, *blocks)
+    )(in_hbm(probe), *blocks)
     return object_new, probe_new
 
 

time: 139 us -> 141 us (1.014)
  starting transfers between devices: 45.7 us -> 54.7 us
  local copies, waits for them, and re-layouts: 12.8 us -> 5.18 us
    ppermute x17 -> x11, waiting for transfers between devices: 35.7 us -> 17.3 us  [swapped(): return lax.ppermute(value, ('row', 'col'), pairs)]
    ppermute x9 -> x8, waiting for transfers between devices: 10.8 us -> 21.7 us  [shifted(): return lax.ppermute(value, ('row', 'col'), pairs)]
    ppermute x0 -> x5, waiting for transfers between devices: none -> 8.74 us  [flipped(): return lax.ppermute(value, ('row', 'col'), pairs)]
    unnamed x40 -> x24, local copies, waits for them, and re-layouts: 11.4 us -> 2.74 us
    ppermute x0 -> x5, starting transfers between devices: none -> 8.03 us  [flipped(): return lax.ppermute(value, ('row', 'col'), pairs)]
    ppermute x17 -> x11, starting transfers between devices: 22 us -> 30 us  [swapped(): return lax.ppermute(value, ('row', 'col'), pairs)]
    ppermute x9 -> x8, starting transfers between devices: 23.6 us -> 16.6 us  [shifted(): return lax.ppermute(value, ('row', 'col'), pairs)]
    pallas_call x1, Pallas kernels: 15.9 us -> 11.3 us  [body(): pl.pallas_call(main_kernel, out_shape=(hbm(2, rows, cols), hbm(2, side, c...]
  transfers between devices with their start and end apart: 26 -> 24, of which waited for: 14 -> 14; matrix products, arithmetic and copies ran while one was open for 6% -> 6% of each run, Pallas kernels for 2% -> 2%
where the time goes in v7:
time: 141 us; the launch traced here: 140 us
  starting transfers between devices  54.7 us (39%)
  waiting for transfers between devices  47.8 us (34%)
  Pallas kernels  20.2 us (14%)
  other arithmetic  6.38 us (5%)
  local copies, waits for them, and re-layouts  5.18 us (4%)
  matrix products  4.97 us (4%)
    ppermute x11, starting transfers between devices, swapped(): return lax.ppermute(value, ('row', 'col'), pairs)  30 us
    ppermute x8, waiting for transfers between devices, shifted(): return lax.ppermute(value, ('row', 'col'), pairs)  21.7 us
    ppermute x11, waiting for transfers between devices, swapped(): return lax.ppermute(value, ('row', 'col'), pairs)  17.3 us
    ppermute x8, starting transfers between devices, shifted(): return lax.ppermute(value, ('row', 'col'), pairs)  16.6 us
    pallas_call x1, Pallas kernels, body(): pl.pallas_call(main_kernel, out_shape=(hbm(2, rows, cols), hbm(2, side, c...  11.3 us
    ppermute x5, waiting for transfers between devices, flipped(): return lax.ppermute(value, ('row', 'col'), pairs)  8.74 us
    ppermute x5, starting transfers between devices, flipped(): return lax.ppermute(value, ('row', 'col'), pairs)  8.03 us
    pallas_call x1, Pallas kernels, body(): pl.pallas_call(functools.partial(probe_kernel, (pairs, n_col)), out_shape...  3.53 us
  transfers between devices with their start and end apart: 24, of which 14 were waited for; matrix products, arithmetic and copies ran while one was open for 6% of the time, Pallas kernels for 2%

profile of v7, /device:TPU:0, one launch (start us, length us, event | category | flops | bytes accessed | tf_op | source)
XLA Modules:
  0.0 140.1 jit_solution(7901595230499532641)
XLA Ops:
  0.6 1.2 slice.54
  1.9 1.4 %collective-permute-start.1 = (f32[2,256,256]{2,1,0:T(8,128)S(1)}, f32[2,256,256]{2,1,0:T(8,128)S(1)}, u32[]{:S(2)}, u32[]{:S(2)}) collective-permute-start(f32[2,256,256]{2,1,0:T(8,128)S(1)} %slice.54), channel_id=1, source_target_pairs={{1,0},{2,1},{3,2},{5,4},{6,5},{7,6},{9,8},{10,9},{11,10},{13,12},{... | collective-permute-start | bytes 1572872 | tf_op jit(solution)/shard_map/ppermute | solution.py:24
  3.3 2.4 %fusion.2 = f32[256,6,256]{2,0,1:T(8,128)S(1)} fusion(f32[256,256,1]{1,0,2:T(8,128)} %constant.49, f32[1,1,6,256,256]{4,3,2,1,0:T(8,128)S(1)} %copy-done), kind=kOutput, calls=%fused_computation.2 | convolution fusion | flops 1207959552 | bytes 3407872 | tf_op jit(solution)/shard_map/ab,sbc->sac/dot_general | solution.py:76
  5.7 2.6 %fusion.amp_hbm = f32[6,256,256]{2,1,0:T(8,128)} fusion(f32[256,256,1]{1,0,2:T(8,128)S(1)} %copy-done.7, f32[256,6,256]{2,0,1:T(8,128)S(1)} %fusion.2), kind=kOutput, calls=%fused_computation | convolution fusion | flops 1207959552 | bytes 3407872 | tf_op jit(solution)/shard_map/sac,dc->sad/dot_general | solution.py:77
  8.3 1.3 collective-permute-start
  9.6 9.2 %collective-permute-done.1.right_hbm = f32[2,256,256]{2,1,0:T(8,128)S(1)} collective-permute-done((f32[2,256,256]{2,1,0:T(8,128)S(1)}, f32[2,256,256]{2,1,0:T(8,128)S(1)}, u32[]{:S(2)}, u32[]{:S(2)}) %collective-permute-start.1) | collective-permute-done | bytes 524320 | tf_op jit(solution)/shard_map/ppermute | solution.py:24
  18.8 1.3 collective-permute-start.2
  20.2 3.6 %collective-permute-start.3 = (s32[6,2]{1,0:T(8,128)S(1)}, s32[6,2]{1,0:T(8,128)S(1)}, u32[]{:S(2)}, u32[]{:S(2)}) collective-permute-start(s32[6,2]{1,0:T(8,128)S(1)} %copy.21.spots_ref), channel_id=1, source_target_pairs={{0,1},{1,2},{2,3},{4,5},{5,6},{6,7},{8,9},{9,10},{10,11},{12,13},{... | collective-permute-start | bytes 152 | tf_op jit(solution)/shard_map/ppermute | solution.py:24
  24.0 1.2 collective-permute-done.3.left_ref
  25.2 11.3 %positions.1 = (f32[2,256,512]{2,1,0:T(8,128)}, f32[2,256,768]{2,1,0:T(8,128)}, f32[2,256,256]{2,1,0:T(8,128)}, f32[4,288,256]{2,1,0:T(8,128)}, f32[4,288,256]{2,1,0:T(8,128)}) custom-call(s32[8,4]{1,0:T(8,128)S(1)} %copy.20.counts_ref, s32[6,2]{1,0:T(8,128)S(1)} %copy.21.spots_ref, f32[2,256,512]{2,1,0:T(8,128)} %tile_ref.1, ...), custom_call_target="tpu_custom_call" | custom-call | flops 7000000000 | bytes 20000000 | tf_op jit(solution)/shard_map/positions/pallas_call | solution.py:361
  36.5 18.4 %collective-permute-start.4 = (f32[4,288,256]{2,1,0:T(8,128)}, f32[4,288,256]{2,1,0:T(8,128)S(1)}, u32[]{:S(2)}, u32[]{:S(2)}) collective-permute-start(f32[4,288,256]{2,1,0:T(8,128)} %get-tuple-element.32), channel_id=1, source_target_pairs={{0,4},{1,5},{2,6},{3,7},{4,0},{5,1},{6,2},{7,3},{8,12},{9,13},{10,... | collective-permute-start | bytes 3538952 | tf_op jit(solution)/shard_map/ppermute | solution.py:30
  54.9 2.7 %collective-permute-done.4 = f32[4,288,256]{2,1,0:T(8,128)S(1)} collective-permute-done((f32[4,288,256]{2,1,0:T(8,128)}, f32[4,288,256]{2,1,0:T(8,128)S(1)}, u32[]{:S(2)}, u32[]{:S(2)}) %collective-permute-start.4) | collective-permute-done | bytes 1179680 | tf_op jit(solution)/shard_map/ppermute | solution.py:30
  57.6 1.0 copy-done.6
  58.6 1.8 %add.57 = f32[4,288,256]{2,1,0:T(8,128)S(1)} add(f32[4,288,256]{2,1,0:T(8,128)} %get-tuple-element.36, f32[4,288,256]{2,1,0:T(8,128)} %copy-done.6) | non-fusion elementwise | flops 294912 | bytes 3538944 | tf_op jit(solution)/shard_map/add | solution.py:408
  60.4 0.9 dynamic-slice_bitcast_fusion
  61.3 2.3 %collective-permute-start.6 = (f32[2,288,256]{2,1,0:T(8,128)}, f32[2,288,256]{2,1,0:T(8,128)}, u32[]{:S(2)}, u32[]{:S(2)}) collective-permute-start(f32[2,288,256]{2,1,0:T(8,128)} %dynamic-slice_bitcast_fusion), channel_id=1, source_target_pairs={{0,8},{1,9},{2,10},{3,11},{4,20},{5,21},{6,22},{7,23},{8,0},{9,1},... | collective-permute-start | bytes 1769480 | tf_op jit(solution)/shard_map/ppermute | solution.py:56
  63.8 1.3 collective-permute-start.5
  65.1 0.8 collective-permute-done.5
  66.0 2.5 %lighting.1 = (f32[256,512]{1,0:T(8,128)S(1)}, f32[8,256]{1,0:T(8,128)S(1)}) custom-call(s32[8,4]{1,0:T(8,128)S(1)} %copy.20.counts_ref, s32[6,2]{1,0:T(8,128)S(1)} %copy.21.spots_ref, s32[6,2]{1,0:T(8,128)S(1)} %collective-permute-done.3.left_ref, s32[6,2]{1,0:T(8,128)S(1)} %get-tuple-element.61.up_ref, s32[6,2]{1,0:T(8,128)S(1)} %get-tuple-element.60.diag_ref, ...), custom_call_target="tpu_custom_call" | custom-call | flops 100000000 | bytes 10000000 | tf_op jit(solution)/shard_map/lighting/pallas_call | solution.py:392
  68.4 0.8 copy-done.1
  69.2 2.6 %collective-permute-done.6 = f32[2,288,256]{2,1,0:T(8,128)} collective-permute-done((f32[2,288,256]{2,1,0:T(8,128)}, f32[2,288,256]{2,1,0:T(8,128)}, u32[]{:S(2)}, u32[]{:S(2)}) %collective-permute-start.6) | collective-permute-done | bytes 589856 | tf_op jit(solution)/shard_map/ppermute | solution.py:56
  71.8 1.1 bitcast_add_fusion
  73.0 1.4 %collective-permute-start.7 = (f32[1,288,256]{2,1,0:T(8,128)S(1)}, f32[1,288,256]{2,1,0:T(8,128)S(1)}, u32[]{:S(2)}, u32[]{:S(2)}) collective-permute-start(f32[1,288,256]{2,1,0:T(8,128)S(1)} %constant_dynamic-slice_fusion), channel_id=1, source_target_pairs={{0,16},{1,17},{2,18},{3,19},{4,12},{5,13},{6,14},{7,15},{8,24},{9,... | collective-permute-start | bytes 884744 | tf_op jit(solution)/shard_map/ppermute | solution.py:56
  74.5 3.1 %collective-permute-start.8 = (f32[2,256,256]{2,1,0:T(8,128)}, f32[2,256,256]{2,1,0:T(8,128)S(1)}, u32[]{:S(2)}, u32[]{:S(2)}) collective-permute-start(f32[2,256,256]{2,1,0:T(8,128)} %get-tuple-element.41), channel_id=1, source_target_pairs={{0,1},{1,2},{2,3},{4,5},{5,6},{6,7},{8,9},{9,10},{10,11},{12,13},{... | collective-permute-start | bytes 1572872 | tf_op jit(solution)/shard_map/ppermute | solution.py:24
  77.5 2.3 %collective-permute-done.7 = f32[1,288,256]{2,1,0:T(8,128)S(1)} collective-permute-done((f32[1,288,256]{2,1,0:T(8,128)S(1)}, f32[1,288,256]{2,1,0:T(8,128)S(1)}, u32[]{:S(2)}, u32[]{:S(2)}) %collective-permute-start.7) | collective-permute-done | bytes 294944 | tf_op jit(solution)/shard_map/ppermute | solution.py:56
  79.8 1.0 add_bitcast_fusion
  80.8 6.7 %collective-permute-done.8.g_left = f32[2,256,256]{2,1,0:T(8,128)S(1)} collective-permute-done((f32[2,256,256]{2,1,0:T(8,128)}, f32[2,256,256]{2,1,0:T(8,128)S(1)}, u32[]{:S(2)}, u32[]{:S(2)}) %collective-permute-start.8) | collective-permute-done | bytes 524320 | tf_op jit(solution)/shard_map/ppermute | solution.py:24
  87.5 0.8 copy-done.3
  88.3 1.4 collective-permute-start.15
  89.7 0.7 pad_maximum_fusion.2
  90.4 5.8 %collective-permute-start.11 = (f32[80,256]{1,0:T(8,128)}, f32[80,256]{1,0:T(8,128)S(1)}, u32[]{:S(2)}, u32[]{:S(2)}) collective-permute-start(f32[80,256]{1,0:T(8,128)} %get-tuple-element.59), channel_id=1, source_target_pairs={{0,3},{1,2},{2,1},{3,0},{4,7},{5,6},{6,5},{7,4},{8,11},{9,10},{10,... | collective-permute-start | bytes 245768 | tf_op jit(solution)/shard_map/ppermute | solution.py:30
  96.5 0.6 collective-permute-start.9
  97.1 1.9 %collective-permute-done.11 = f32[80,256]{1,0:T(8,128)S(1)} collective-permute-done((f32[80,256]{1,0:T(8,128)}, f32[80,256]{1,0:T(8,128)S(1)}, u32[]{:S(2)}, u32[]{:S(2)}) %collective-permute-start.11) | collective-permute-done | bytes 81952 | tf_op jit(solution)/shard_map/ppermute | solution.py:30
  98.9 6.1 %collective-permute-done.10 = f32[80,256]{1,0:T(8,128)} collective-permute-done((f32[80,256]{1,0:T(8,128)}, f32[80,256]{1,0:T(8,128)}, u32[]{:S(2)}, u32[]{:S(2)}) %collective-permute-start.10) | collective-permute-done | bytes 81952 | tf_op jit(solution)/shard_map/ppermute | solution.py:30
  105.0 0.9 constant_dynamic-update-slice_fusion.4
  106.1 3.2 %collective-permute-start.13 = (f32[72,256]{1,0:T(8,128)S(1)}, f32[72,256]{1,0:T(8,128)S(1)}, u32[]{:S(2)}, u32[]{:S(2)}) collective-permute-start(f32[72,256]{1,0:T(8,128)S(1)} %get-tuple-element.53), channel_id=1, source_target_pairs={{0,2},{1,3},{2,0},{3,1},{4,6},{5,7},{6,4},{7,5},{8,10},{9,11},{10,... | collective-permute-start | bytes 221192 | tf_op jit(solution)/shard_map/ppermute | solution.py:30
  109.3 1.1 collective-permute-start.14
  110.4 5.1 %collective-permute-done.13 = f32[72,256]{1,0:T(8,128)S(1)} collective-permute-done((f32[72,256]{1,0:T(8,128)S(1)}, f32[72,256]{1,0:T(8,128)S(1)}, u32[]{:S(2)}, u32[]{:S(2)}) %collective-permute-start.13) | collective-permute-done | bytes 73760 | tf_op jit(solution)/shard_map/ppermute | solution.py:30
  115.6 0.7 constant_dynamic-update-slice_fusion.refs_0_
  116.3 1.7 %collective-permute-start.16 = (f32[296,256]{1,0:T(8,128)S(1)}, f32[296,256]{1,0:T(8,128)S(1)}, u32[]{:S(2)}, u32[]{:S(2)}) collective-permute-start(f32[296,256]{1,0:T(8,128)S(1)} %constant_dynamic-update-slice_fusion.refs_0_), channel_id=1, source_target_pairs={{0,16},{1,17},{2,18},{3,19},{4,12},{5,13},{6,14},{7,15},{8,24},{9,... | collective-permute-start | bytes 909320 | tf_op jit(solution)/shard_map/ppermute | solution.py:56
  118.1 3.3 %collective-permute-start.19 = (f32[2,256,256]{2,1,0:T(8,128)S(1)}, f32[2,256,256]{2,1,0:T(8,128)S(1)}, u32[]{:S(2)}, u32[]{:S(2)}) collective-permute-start(f32[2,256,256]{2,1,0:T(8,128)S(1)} %slice.80), channel_id=1, source_target_pairs={{0,1},{1,2},{2,3},{4,5},{5,6},{6,7},{8,9},{9,10},{10,11},{12,13},{... | collective-permute-start | bytes 1572872 | tf_op jit(solution)/shard_map/ppermute | solution.py:24
  121.6 2.3 %collective-permute-done.16.refs_1_ = f32[296,256]{1,0:T(8,128)S(1)} collective-permute-done((f32[296,256]{1,0:T(8,128)S(1)}, f32[296,256]{1,0:T(8,128)S(1)}, u32[]{:S(2)}, u32[]{:S(2)}) %collective-permute-start.16) | collective-permute-done | bytes 303136 | tf_op jit(solution)/shard_map/ppermute | solution.py:56
  123.8 2.4 %collective-permute-start.18 = (f32[296,256]{1,0:T(8,128)S(1)}, f32[296,256]{1,0:T(8,128)S(1)}, u32[]{:S(2)}, u32[]{:S(2)}) collective-permute-start(f32[296,256]{1,0:T(8,128)S(1)} %collective-permute-done.16.refs_1_), channel_id=1, source_target_pairs={{0,8},{1,9},{2,10},{3,11},{4,20},{5,21},{6,22},{7,23},{8,0},{9,1},... | collective-permute-start | bytes 909320 | tf_op jit(solution)/shard_map/ppermute | solution.py:56
  126.7 1.5 %collective-permute-done.17.refs_2_ = f32[296,256]{1,0:T(8,128)S(1)} collective-permute-done((f32[296,256]{1,0:T(8,128)S(1)}, f32[296,256]{1,0:T(8,128)S(1)}, u32[]{:S(2)}, u32[]{:S(2)}) %collective-permute-start.17) | collective-permute-done | bytes 303136 | tf_op jit(solution)/shard_map/ppermute | solution.py:56
  128.2 3.8 %collective-permute-done.19.g_diag = f32[2,256,256]{2,1,0:T(8,128)S(1)} collective-permute-done((f32[2,256,256]{2,1,0:T(8,128)S(1)}, f32[2,256,256]{2,1,0:T(8,128)S(1)}, u32[]{:S(2)}, u32[]{:S(2)}) %collective-permute-start.19) | collective-permute-done | bytes 524320 | tf_op jit(solution)/shard_map/ppermute | solution.py:24
  132.0 1.6 %collective-permute-done.23.refs_7_ = f32[296,256]{1,0:T(8,128)S(1)} collective-permute-done((f32[296,256]{1,0:T(8,128)S(1)}, f32[296,256]{1,0:T(8,128)S(1)}, u32[]{:S(2)}, u32[]{:S(2)}) %collective-permute-start.23) | collective-permute-done | bytes 303136 | tf_op jit(solution)/shard_map/ppermute | solution.py:30
  133.6 2.9 %object_update.1 = f32[2,256,512]{2,1,0:T(8,128)} custom-call(f32[2,256,512]{2,1,0:T(8,128)} %tile_ref.1, f32[256,512]{1,0:T(8,128)S(1)} %copy-done.2, f32[8,256]{1,0:T(8,128)S(1)} %slice_maximum_fusion.top_ref, f32[2,256,512]{2,1,0:T(8,128)} %get-tuple-element.48.g_tile, f32[2,256,256]{2,1,0:T(8,128)S(1)} %copy-done.4, ...), custom_call_target="tpu_custom_call" | custom-call | flops 1000000 | bytes 6000000 | tf_op jit(solution)/shard_map/object_update/pallas_call | solution.py:436
  136.6 3.5 %probe_update.1 = f32[2,4,256,256]{3,2,1,0:T(8,128)} custom-call(f32[2,4,256,256]{3,2,1,0:T(8,128)} %probe_ref.3, f32[296,256]{1,0:T(8,128)S(1)} %constant_dynamic-update-slice_fusion.refs_0_, f32[296,256]{1,0:T(8,128)S(1)} %collective-permute-done.16.refs_1_, f32[296,256]{1,0:T(8,128)S(1)} %collective-permute-done.17.refs_2_, ...), custom_call_target="tpu_custom_call" | custom-call | flops 1000000 | bytes 6000000 | tf_op jit(solution)/shard_map/probe_update/pallas_call | solution.py:445
  (47 shorter events, 1.7 us)
Async XLA Ops:
  0.6 2.7 %copy-start = (f32[1,1,6,256,256]{4,3,2,1,0:T(8,128)S(1)}, f32[1,1,6,256,256]{4,3,2,1,0:T(8,128)}, u32[]{:S(2)}) copy-start(f32[1,1,6,256,256]{4,3,2,1,0:T(8,128)} %param.9) | copy-start | bytes 4718596
  1.8 3.9 %copy-start.7 = (f32[256,256,1]{1,0,2:T(8,128)S(1)}, f32[256,256,1]{1,0,2:T(8,128)}, u32[]{:S(2)}) copy-start(f32[256,256,1]{1,0,2:T(8,128)} %constant.49) | copy-start | bytes 786436
  1.9 17.0 %collective-permute-start.1 = (f32[2,256,256]{2,1,0:T(8,128)S(1)}, f32[2,256,256]{2,1,0:T(8,128)S(1)}, u32[]{:S(2)}, u32[]{:S(2)}) collective-permute-start(f32[2,256,256]{2,1,0:T(8,128)S(1)} %slice.54), channel_id=1, source_target_pairs={{1,0},{2,1},{3,2},{5,4},{6,5},{7,6},{9,8},{10,9},{11,10},{13,12},{... | collective-permute-start | bytes 1572872 | tf_op jit(solution)/shard_map/ppermute | solution.py:24
  5.7 14.4 %copy-start.8 = (s32[1,1,6,2]{2,3,1,0:T(2,128)S(1)}, s32[1,1,6,2]{2,3,1,0:T(2,128)}, u32[]{:S(2)}) copy-start(s32[1,1,6,2]{2,3,1,0:T(2,128)} %param.10) | copy-start | bytes 148
  5.7 18.1 %copy-start.9 = (s32[8,4]{0,1:T(4,128)S(1)}, s32[8,4]{0,1:T(4,128)}, u32[]{:S(2)}) copy-start(s32[8,4]{0,1:T(4,128)} %param.11) | copy-start | bytes 388
  8.3 16.9 %collective-permute-start = (f32[2,256,512]{2,1,0:T(8,128)}, f32[2,256,512]{2,1,0:T(8,128)S(1)}, u32[]{:S(2)}, u32[]{:S(2)}) collective-permute-start(f32[2,256,512]{2,1,0:T(8,128)} %tile_ref.1), channel_id=1, source_target_pairs={{4,0},{5,1},{6,2},{7,3},{8,4},{9,5},{10,6},{11,7},{12,8},{13,9},{1... | collective-permute-start | bytes 3145736 | tf_op jit(solution)/shard_map/ppermute | solution.py:24
  18.8 6.3 %collective-permute-start.2 = (f32[2,256,256]{2,1,0:T(8,128)S(1)}, f32[2,256,256]{2,1,0:T(8,128)}, u32[]{:S(2)}, u32[]{:S(2)}) collective-permute-start(f32[2,256,256]{2,1,0:T(8,128)S(1)} %collective-permute-done.1.right_hbm), channel_id=1, source_target_pairs={{4,0},{5,1},{6,2},{7,3},{8,4},{9,5},{10,6},{11,7},{12,8},{13,9},{1... | collective-permute-start | bytes 1572872 | tf_op jit(solution)/shard_map/ppermute | solution.py:24
  20.2 4.9 %collective-permute-start.3 = (s32[6,2]{1,0:T(8,128)S(1)}, s32[6,2]{1,0:T(8,128)S(1)}, u32[]{:S(2)}, u32[]{:S(2)}) collective-permute-start(s32[6,2]{1,0:T(8,128)S(1)} %copy.21.spots_ref), channel_id=1, source_target_pairs={{0,1},{1,2},{2,3},{4,5},{5,6},{6,7},{8,9},{9,10},{10,11},{12,13},{... | collective-permute-start | bytes 152 | tf_op jit(solution)/shard_map/ppermute | solution.py:24
  36.5 21.1 %collective-permute-start.4 = (f32[4,288,256]{2,1,0:T(8,128)}, f32[4,288,256]{2,1,0:T(8,128)S(1)}, u32[]{:S(2)}, u32[]{:S(2)}) collective-permute-start(f32[4,288,256]{2,1,0:T(8,128)} %get-tuple-element.32), channel_id=1, source_target_pairs={{0,4},{1,5},{2,6},{3,7},{4,0},{5,1},{6,2},{7,3},{8,12},{9,13},{10,... | collective-permute-start | bytes 3538952 | tf_op jit(solution)/shard_map/ppermute | solution.py:30
  57.6 1.0 copy-start.6
  61.3 10.6 %collective-permute-start.6 = (f32[2,288,256]{2,1,0:T(8,128)}, f32[2,288,256]{2,1,0:T(8,128)}, u32[]{:S(2)}, u32[]{:S(2)}) collective-permute-start(f32[2,288,256]{2,1,0:T(8,128)} %dynamic-slice_bitcast_fusion), channel_id=1, source_target_pairs={{0,8},{1,9},{2,10},{3,11},{4,20},{5,21},{6,22},{7,23},{8,0},{9,1},... | collective-permute-start | bytes 1769480 | tf_op jit(solution)/shard_map/ppermute | solution.py:56
  63.8 2.1 %collective-permute-start.5 = (s32[12,2]{1,0:T(8,128)S(1)}, s32[12,2]{1,0:T(8,128)S(1)}, u32[]{:S(2)}, u32[]{:S(2)}) collective-permute-start(s32[12,2]{1,0:T(8,128)S(1)} %copy.19), channel_id=1, source_target_pairs={{0,4},{1,5},{2,6},{3,7},{4,8},{5,9},{6,10},{7,11},{8,12},{9,13},{1... | collective-permute-start | bytes 296 | tf_op jit(solution)/shard_map/ppermute | solution.py:24
  68.4 0.8 copy-start.1
  73.0 1.5 %copy-start.5 = (f32[2,288,256]{2,1,0:T(8,128)}, f32[2,288,256]{2,1,0:T(8,128)S(1)}, u32[]{:S(2)}) copy-start(f32[2,288,256]{2,1,0:T(8,128)S(1)} %bitcast_add_fusion) | copy-start | bytes 1769476
  73.0 6.8 %collective-permute-start.7 = (f32[1,288,256]{2,1,0:T(8,128)S(1)}, f32[1,288,256]{2,1,0:T(8,128)S(1)}, u32[]{:S(2)}, u32[]{:S(2)}) collective-permute-start(f32[1,288,256]{2,1,0:T(8,128)S(1)} %constant_dynamic-slice_fusion), channel_id=1, source_target_pairs={{0,16},{1,17},{2,18},{3,19},{4,12},{5,13},{6,14},{7,15},{8,24},{9,... | collective-permute-start | bytes 884744 | tf_op jit(solution)/shard_map/ppermute | solution.py:56
  74.5 13.0 %collective-permute-start.8 = (f32[2,256,256]{2,1,0:T(8,128)}, f32[2,256,256]{2,1,0:T(8,128)S(1)}, u32[]{:S(2)}, u32[]{:S(2)}) collective-permute-start(f32[2,256,256]{2,1,0:T(8,128)} %get-tuple-element.41), channel_id=1, source_target_pairs={{0,1},{1,2},{2,3},{4,5},{5,6},{6,7},{8,9},{9,10},{10,11},{12,13},{... | collective-permute-start | bytes 1572872 | tf_op jit(solution)/shard_map/ppermute | solution.py:24
  87.5 0.8 copy-start.3
  88.3 28.0 %collective-permute-start.15 = (f32[2,256,768]{2,1,0:T(8,128)}, f32[2,256,768]{2,1,0:T(8,128)S(1)}, u32[]{:S(2)}, u32[]{:S(2)}) collective-permute-start(f32[2,256,768]{2,1,0:T(8,128)} %get-tuple-element.44), channel_id=1, source_target_pairs={{0,4},{1,5},{2,6},{3,7},{4,8},{5,9},{6,10},{7,11},{8,12},{9,13},{1... | collective-permute-start | bytes 4718600 | tf_op jit(solution)/shard_map/ppermute | solution.py:24
  90.4 8.5 %collective-permute-start.11 = (f32[80,256]{1,0:T(8,128)}, f32[80,256]{1,0:T(8,128)S(1)}, u32[]{:S(2)}, u32[]{:S(2)}) collective-permute-start(f32[80,256]{1,0:T(8,128)} %get-tuple-element.59), channel_id=1, source_target_pairs={{0,3},{1,2},{2,1},{3,0},{4,7},{5,6},{6,5},{7,4},{8,11},{9,10},{10,... | collective-permute-start | bytes 245768 | tf_op jit(solution)/shard_map/ppermute | solution.py:30
  96.2 8.8 %collective-permute-start.10 = (f32[80,256]{1,0:T(8,128)}, f32[80,256]{1,0:T(8,128)}, u32[]{:S(2)}, u32[]{:S(2)}) collective-permute-start(f32[80,256]{1,0:T(8,128)} %get-tuple-element.58), channel_id=1, source_target_pairs={{0,2},{1,3},{2,0},{3,1},{4,6},{5,7},{6,4},{7,5},{8,10},{9,11},{10,... | collective-permute-start | bytes 245768 | tf_op jit(solution)/shard_map/ppermute | solution.py:30
  96.5 8.5 %collective-permute-start.9 = (f32[80,256]{1,0:T(8,128)}, f32[80,256]{1,0:T(8,128)}, u32[]{:S(2)}, u32[]{:S(2)}) collective-permute-start(f32[80,256]{1,0:T(8,128)} %get-tuple-element.57), channel_id=1, source_target_pairs={{0,1},{1,0},{2,3},{3,2},{4,5},{5,4},{6,7},{7,6},{8,9},{9,8},{10,11... | collective-permute-start | bytes 245768 | tf_op jit(solution)/shard_map/ppermute | solution.py:30
  97.1 36.5 %copy-start.2 = (f32[256,512]{1,0:T(8,128)S(1)}, f32[256,512]{1,0:T(8,128)}, u32[]{:S(2)}) copy-start(f32[256,512]{1,0:T(8,128)} %copy-done.1) | copy-start | bytes 1572868
  97.1 36.6 %copy-start.4 = (f32[2,256,256]{2,1,0:T(8,128)S(1)}, f32[2,256,256]{2,1,0:T(8,128)}, u32[]{:S(2)}) copy-start(f32[2,256,256]{2,1,0:T(8,128)} %copy-done.3) | copy-start | bytes 1572868
  106.0 4.5 %collective-permute-start.12 = (f32[72,256]{1,0:T(8,128)S(1)}, f32[72,256]{1,0:T(8,128)S(1)}, u32[]{:S(2)}, u32[]{:S(2)}) collective-permute-start(f32[72,256]{1,0:T(8,128)S(1)} %get-tuple-element.53), channel_id=1, source_target_pairs={{0,1},{1,0},{2,3},{3,2},{4,5},{5,4},{6,7},{7,6},{8,9},{9,8},{10,11... | collective-permute-start | bytes 221192 | tf_op jit(solution)/shard_map/ppermute | solution.py:30
  106.1 9.5 %collective-permute-start.13 = (f32[72,256]{1,0:T(8,128)S(1)}, f32[72,256]{1,0:T(8,128)S(1)}, u32[]{:S(2)}, u32[]{:S(2)}) collective-permute-start(f32[72,256]{1,0:T(8,128)S(1)} %get-tuple-element.53), channel_id=1, source_target_pairs={{0,2},{1,3},{2,0},{3,1},{4,6},{5,7},{6,4},{7,5},{8,10},{9,11},{10,... | collective-permute-start | bytes 221192 | tf_op jit(solution)/shard_map/ppermute | solution.py:30
  109.3 6.2 %collective-permute-start.14 = (f32[72,256]{1,0:T(8,128)S(1)}, f32[72,256]{1,0:T(8,128)S(1)}, u32[]{:S(2)}, u32[]{:S(2)}) collective-permute-start(f32[72,256]{1,0:T(8,128)S(1)} %get-tuple-element.53), channel_id=1, source_target_pairs={{0,3},{1,2},{2,1},{3,0},{4,7},{5,6},{6,5},{7,4},{8,11},{9,10},{10,... | collective-permute-start | bytes 221192 | tf_op jit(solution)/shard_map/ppermute | solution.py:30
  116.3 7.5 %collective-permute-start.16 = (f32[296,256]{1,0:T(8,128)S(1)}, f32[296,256]{1,0:T(8,128)S(1)}, u32[]{:S(2)}, u32[]{:S(2)}) collective-permute-start(f32[296,256]{1,0:T(8,128)S(1)} %constant_dynamic-update-slice_fusion.refs_0_), channel_id=1, source_target_pairs={{0,16},{1,17},{2,18},{3,19},{4,12},{5,13},{6,14},{7,15},{8,24},{9,... | collective-permute-start | bytes 909320 | tf_op jit(solution)/shard_map/ppermute | solution.py:56
  118.1 13.9 %collective-permute-start.19 = (f32[2,256,256]{2,1,0:T(8,128)S(1)}, f32[2,256,256]{2,1,0:T(8,128)S(1)}, u32[]{:S(2)}, u32[]{:S(2)}) collective-permute-start(f32[2,256,256]{2,1,0:T(8,128)S(1)} %slice.80), channel_id=1, source_target_pairs={{0,1},{1,2},{2,3},{4,5},{5,6},{6,7},{8,9},{9,10},{10,11},{12,13},{... | collective-permute-start | bytes 1572872 | tf_op jit(solution)/shard_map/ppermute | solution.py:24
  121.4 6.9 %collective-permute-start.17 = (f32[296,256]{1,0:T(8,128)S(1)}, f32[296,256]{1,0:T(8,128)S(1)}, u32[]{:S(2)}, u32[]{:S(2)}) collective-permute-start(f32[296,256]{1,0:T(8,128)S(1)} %constant_dynamic-update-slice_fusion.refs_0_), channel_id=1, source_target_pairs={{0,8},{1,9},{2,10},{3,11},{4,20},{5,21},{6,22},{7,23},{8,0},{9,1},... | collective-permute-start | bytes 909320 | tf_op jit(solution)/shard_map/ppermute | solution.py:56
  123.8 8.2 %collective-permute-start.18 = (f32[296,256]{1,0:T(8,128)S(1)}, f32[296,256]{1,0:T(8,128)S(1)}, u32[]{:S(2)}, u32[]{:S(2)}) collective-permute-start(f32[296,256]{1,0:T(8,128)S(1)} %collective-permute-done.16.refs_1_), channel_id=1, source_target_pairs={{0,8},{1,9},{2,10},{3,11},{4,20},{5,21},{6,22},{7,23},{8,0},{9,1},... | collective-permute-start | bytes 909320 | tf_op jit(solution)/shard_map/ppermute | solution.py:56
  126.2 5.8 %collective-permute-start.20 = (f32[296,256]{1,0:T(8,128)S(1)}, f32[296,256]{1,0:T(8,128)S(1)}, u32[]{:S(2)}, u32[]{:S(2)}) collective-permute-start(f32[296,256]{1,0:T(8,128)S(1)} %constant_dynamic-update-slice_fusion.refs_0_), channel_id=1, source_target_pairs={{0,4},{1,5},{2,6},{3,7},{4,0},{5,1},{6,2},{7,3},{8,12},{9,13},{10,... | collective-permute-start | bytes 909320 | tf_op jit(solution)/shard_map/ppermute | solution.py:30
  126.2 5.8 %collective-permute-start.21 = (f32[296,256]{1,0:T(8,128)S(1)}, f32[296,256]{1,0:T(8,128)S(1)}, u32[]{:S(2)}, u32[]{:S(2)}) collective-permute-start(f32[296,256]{1,0:T(8,128)S(1)} %collective-permute-done.16.refs_1_), channel_id=1, source_target_pairs={{0,4},{1,5},{2,6},{3,7},{4,0},{5,1},{6,2},{7,3},{8,12},{9,13},{10,... | collective-permute-start | bytes 909320 | tf_op jit(solution)/shard_map/ppermute | solution.py:30
  128.2 3.8 %collective-permute-start.22 = (f32[296,256]{1,0:T(8,128)S(1)}, f32[296,256]{1,0:T(8,128)S(1)}, u32[]{:S(2)}, u32[]{:S(2)}) collective-permute-start(f32[296,256]{1,0:T(8,128)S(1)} %collective-permute-done.17.refs_2_), channel_id=1, source_target_pairs={{0,4},{1,5},{2,6},{3,7},{4,0},{5,1},{6,2},{7,3},{8,12},{9,13},{10,... | collective-permute-start | bytes 909320 | tf_op jit(solution)/shard_map/ppermute | solution.py:30
  132.0 1.6 %collective-permute-start.23 = (f32[296,256]{1,0:T(8,128)S(1)}, f32[296,256]{1,0:T(8,128)S(1)}, u32[]{:S(2)}, u32[]{:S(2)}) collective-permute-start(f32[296,256]{1,0:T(8,128)S(1)} %collective-permute-done.18.refs_3_), channel_id=1, source_target_pairs={{0,4},{1,5},{2,6},{3,7},{4,0},{5,1},{6,2},{7,3},{8,12},{9,13},{10,... | collective-permute-start | bytes 909320 | tf_op jit(solution)/shard_map/ppermute | solution.py:30

commit v8 on v7

--- a/solution.py
+++ b/solution.py
@@ -275,7 +275,52 @@
     top_ref[...] = jnp.broadcast_to(top, top_ref.shape)
 
 
-def finish_kernel(tile_ref, light_ref, top_ref, g_tile, g_left, g_up, g_diag, out_ref):
+def fold_kernel(step, held_ref, got_ref, send_ref, keep_ref):
+    half = keep_ref.shape[0]
+    my_row = lax.axis_index("row")
+    keep = (plane_rank(lax.rem(my_row, 2), my_row // 2) >> (plane_bits() - 1 - step)) & 1
+    for ref, at in ((send_ref, (1 - keep) * half), (keep_ref, keep * half)):
+        ref[...] = held_ref[pl.ds(at, half)] + got_ref[pl.ds(at, half)]
+
+
+def fold(step, held, got):
+    count, share, side = held.shape
+    return pl.pallas_call(
+        functools.partial(fold_kernel, step),
+        out_shape=(f32(count // 2, share, side),) * 2,
+        in_specs=[VM] * 2,
+        out_specs=(VM,) * 2,
+        compiler_params=params(8),
+        cost_estimate=cost(10**6, 12 * count * share * side),
+        name="fold_plane",
+    )(held, got)
+
+
+def cut_kernel(held_ref, got_ref, top_ref, own_ref, *send_refs):
+    piece = own_ref.shape[0]
+    my_col = lax.axis_index("col")
+    for e, ref in enumerate((own_ref,) + send_refs):
+        at = pl.ds(pl.multiple_of((my_col ^ e) * piece, SUBLANES), piece)
+        ref[:piece] = held_ref[0, at] + got_ref[0, at]
+        if e:
+            ref[piece:] = top_ref[...]
+
+
+def cut(held, got, top, parts):
+    _, share, side = held.shape
+    piece = share // parts
+    return pl.pallas_call(
+        cut_kernel,
+        out_shape=(f32(piece, side),) + (f32(piece + SUBLANES, side),) * (parts - 1),
+        in_specs=[VM] * 3,
+        out_specs=(VM,) * parts,
+        compiler_params=params(4),
+        cost_estimate=cost(10**6, 12 * share * side),
+        name="cut_columns",
+    )(held, got, top)
+
+
+def finish_kernel(tile_ref, light_ref, top_ref, g_tile, g_left, g_up, out_ref):
     side = g_left.shape[2]
     rows, cols = light_ref.shape
     top = top_ref[0:1, 0:1]
@@ -285,7 +330,7 @@
         for i in range(2):
             total = g_tile[i, :, part] + g_up[i, :, part]
             if at == 0:
-                total += g_left[i] + g_diag[i]
+                total += g_left[i]
             out_ref[i, :, part] = tile_ref[i, :, part] + total * scale
 
 
@@ -355,17 +400,31 @@
     tile, measured = lax.optimization_barrier((object_field, measured))
     below = shifted(tile[:, :side, :], -1, 0)
     from_left = shifted(spots, 0, 1)
-    right, measured = lax.optimization_barrier((right, measured))
+    right, measured, from_left = lax.optimization_barrier((right, measured, from_left))
     corner = shifted(right[:, :side, :], -1, 0)
-    corner, from_left = lax.optimization_barrier((corner, from_left))
+    from_up = shifted(jnp.concatenate([spots, from_left], axis=0), 1, 0)
+    light, top = pl.pallas_call(
+        light_kernel,
+        out_shape=(f32(rows, cols), f32(SUBLANES, side)),
+        in_specs=[SM] * 5 + [VM],
+        out_specs=(VM, VM),
+        scratch_shapes=[
+            pltpu.VMEM((side, side), jnp.float32),
+            pltpu.VMEM((1, rows + 2 * side, cols + 2 * side), jnp.float32),
+        ],
+        compiler_params=params(12),
+        cost_estimate=cost(10**8, 10**7),
+        name="lighting",
+    )(counts, spots, from_left, from_up[:slots], from_up[slots:], probe)
+    corner, top = lax.optimization_barrier((corner, top))
     g_tile, g_lower, g_right, mine, other = pl.pallas_call(
         main_kernel,
         out_shape=(
             hbm(2, rows, cols), hbm(2, side, cols + side), hbm(2, rows, side),
-            hbm(pairs, share, side), hbm(pairs, share, side),
+            pltpu.VMEM((pairs, share, side), jnp.float32), hbm(pairs, share, side),
         ),
         in_specs=[SM] * 2 + [HBM] + [ANY] * 3 + [HBM] * 3,
-        out_specs=(HBM,) * 5,
+        out_specs=(HBM,) * 3 + (VM, HBM),
         scratch_shapes=[
             pltpu.VMEM((2, rows + side, cols + side), jnp.float32),
             pltpu.VMEM((2, rows + side, cols + side), jnp.float32),
@@ -387,61 +446,34 @@
     )(counts, spots, in_hbm(object_field), below, right, corner, *map(in_hbm, (measured, probe, tables(side))))
 
     arrived = swapped(other, 1, 0)
-    arrived, from_left = lax.optimization_barrier((arrived, from_left))
-    from_up = shifted(jnp.concatenate([spots, from_left], axis=0), 1, 0)
-    light, top = pl.pallas_call(
-        light_kernel,
-        out_shape=(f32(rows, cols), f32(SUBLANES, side)),
-        in_specs=[SM] * 5 + [VM],
-        out_specs=(VM, VM),
-        scratch_shapes=[
-            pltpu.VMEM((side, side), jnp.float32),
-            pltpu.VMEM((1, rows + 2 * side, cols + 2 * side), jnp.float32),
-        ],
-        compiler_params=params(12),
-        cost_estimate=cost(10**8, 10**7),
-        name="lighting",
-    )(counts, spots, from_left, from_up[:slots], from_up[slots:], in_hbm(probe))
-
-    g_left = shifted(g_right, 0, 1)
-
-    held = mine + arrived
+    held, got = mine, arrived
     for i in range(plane_bits()):
-        keep = (plane_rank(core, pair) >> (plane_bits() - 1 - i)) & 1
-        held = held.reshape(2, -1, share, side)
-        held = held[keep] + flipped(held[1 - keep], i)
-        if i == 0:
-            held, top = lax.optimization_barrier((held, top))
-    plane_sum = held.reshape(share, side)
-    plane_sum, g_lower, g_left = lax.optimization_barrier((plane_sum, g_lower, g_left))
+        send, held = fold(i, held, got)
+        got = flipped(send, i)
+    own, *sends = cut(held, got, top, n_col)
+    own, g_lower = lax.optimization_barrier((own, g_lower))
     g_up = shifted(g_lower, 1, 0)
-
-    plane_sum = plane_sum.reshape(n_col, piece, side)
-
-    def col_part(e):
-        return jnp.concatenate([plane_sum[my_col ^ e], top], axis=0)
-
-    received = [swapped(col_part(e), 0, e) for e in range(1, n_col)]
-    own = sum([value[:piece] for value in received], plane_sum[my_col])
+    received = [swapped(send, 0, e) for e, send in enumerate(sends, 1)]
+    own = sum([value[:piece] for value in received], own)
     top = functools.reduce(jnp.maximum, [value[piece:] for value in received], top)
     own = jnp.concatenate([own] + [swapped(own, 0, e) for e in range(1, n_col)] + [top], axis=0)
-    own, g_up, g_corner = lax.optimization_barrier((own, g_up, g_up[:, :, cols:]))
-    g_diag = shifted(g_corner, 0, 1)
+    own, g_up, g_right = lax.optimization_barrier((own, g_up, g_right + g_up[:, :, cols:]))
+    g_left = shifted(g_right, 0, 1)
     blocks = [own]
     for i in reversed(range(plane_bits())):
         blocks = blocks + [flipped(block, i) for block in blocks]
-    blocks[-1], g_diag = lax.optimization_barrier((blocks[-1], g_diag))
+    blocks[-1], g_left = lax.optimization_barrier((blocks[-1], g_left))
     blocks = blocks + [swapped(block, 1, 0) for block in blocks]
     top = functools.reduce(jnp.maximum, [block[share:] for block in blocks])
     object_new = pl.pallas_call(
         finish_kernel,
         out_shape=f32(2, rows, cols),
-        in_specs=[VM] * 7,
+        in_specs=[VM] * 6,
         out_specs=VM,
         compiler_params=params(10),
         cost_estimate=cost(10**6, 6 * 10**6),
         name="object_update",
-    )(in_hbm(object_field), light, top, in_hbm(g_tile), g_left, g_up, g_diag)
+    )(object_field, light, top, g_tile, g_left, g_up)
     probe_new = pl.pallas_call(
         functools.partial(probe_kernel, (pairs, n_col)),
         out_shape=f32(*probe.shape),
@@ -451,7 +483,7 @@
         compiler_params=params(14),
         cost_estimate=cost(10**6, 6 * 10**6),
         name="probe_update",
-    )(in_hbm(probe), *blocks)
+    )(probe, *blocks)
     return object_new, probe_new
 
 

time: 141 us -> 124 us (0.88)
  starting transfers between devices: 54.7 us -> 44.8 us
  other arithmetic: 6.38 us -> 0.19 us
  Pallas kernels: 20.2 us -> 22.9 us
  waiting for transfers between devices: 47.8 us -> 45.4 us
    ppermute x11, starting transfers between devices: 30 us -> 13 us  [swapped(): return lax.ppermute(value, ('row', 'col'), pairs)]
    ppermute x8 -> x7, waiting for transfers between devices: 21.7 us -> 6.94 us  [shifted(): return lax.ppermute(value, ('row', 'col'), pairs)]
    ppermute x5, waiting for transfers between devices: 8.74 us -> 20.1 us  [flipped(): return lax.ppermute(value, ('row', 'col'), pairs)]
    ppermute x5, starting transfers between devices: 8.03 us -> 16.4 us  [flipped(): return lax.ppermute(value, ('row', 'col'), pairs)]
    pallas_call x1, Pallas kernels: 11.3 us -> 17.2 us  [body(): pl.pallas_call(main_kernel, out_shape=(hbm(2, rows, cols), hbm(2, side, c...]
    add x2 -> x1, other arithmetic: 2.92 us -> 0.07 us  [body(): g_right + g_up[:, :, cols:]]
    pallas_call x1, Pallas kernels: 3.53 us -> 1.93 us  [body(): pl.pallas_call(functools.partial(probe_kernel, (pairs, n_col)), out_shape...]
    pallas_call x1, Pallas kernels: 2.91 us -> 1.36 us  [body(): pl.pallas_call(finish_kernel, out_shape=f32(2, rows, cols), in_specs=[VM]...]
  transfers between devices with their start and end apart: 24 -> 23, of which waited for: 14 -> 14; matrix products, arithmetic and copies ran while one was open for 6% -> 4% of each run, Pallas kernels for 2% -> 2%
where the time goes in v8:
time: 124 us
  waiting for transfers between devices  45.4 us (37%)
  starting transfers between devices  44.8 us (36%)
  Pallas kernels  22.9 us (18%)
  matrix products  4.97 us (4%)
  local copies, waits for them, and re-layouts  4.62 us (4%)
    ppermute x5, waiting for transfers between devices, flipped(): return lax.ppermute(value, ('row', 'col'), pairs)  20.1 us
    ppermute x11, waiting for transfers between devices, swapped(): return lax.ppermute(value, ('row', 'col'), pairs)  18.3 us
    pallas_call x1, Pallas kernels, body(): pl.pallas_call(main_kernel, out_shape=(hbm(2, rows, cols), hbm(2, side, c...  17.2 us
    ppermute x5, starting transfers between devices, flipped(): return lax.ppermute(value, ('row', 'col'), pairs)  16.4 us
    ppermute x7, starting transfers between devices, shifted(): return lax.ppermute(value, ('row', 'col'), pairs)  15.4 us
    ppermute x11, starting transfers between devices, swapped(): return lax.ppermute(value, ('row', 'col'), pairs)  13 us
    ppermute x7, waiting for transfers between devices, shifted(): return lax.ppermute(value, ('row', 'col'), pairs)  6.94 us
    dot_general x1, matrix products, evens_first(): jnp.einsum('sac,dc->sad', rows, pick, precision=lax.Precision.HIGHEST)  2.57 us
  transfers between devices with their start and end apart: 23, of which 14 were waited for; matrix products, arithmetic and copies ran while one was open for 4% of the time, Pallas kernels for 2%

profile of v8, /device:TPU:0, one launch (start us, length us, event | category | flops | bytes accessed | tf_op | source)
XLA Modules:
  0.0 123.7 jit_solution(14613270372886413830)
XLA Ops:
  0.6 2.0 %slice.54 = f32[2,256,256]{2,1,0:T(8,128)} slice(f32[2,256,512]{2,1,0:T(8,128)} %tile_ref.1), slice={[0:2], [0:256], [0:256]} | slice | bytes 1048576 | tf_op jit(solution)/shard_map/slice | solution.py:398
  2.6 1.4 %collective-permute-start = (f32[2,256,256]{2,1,0:T(8,128)}, f32[2,256,256]{2,1,0:T(8,128)S(1)}, u32[]{:S(2)}, u32[]{:S(2)}) collective-permute-start(f32[2,256,256]{2,1,0:T(8,128)} %slice.54), channel_id=1, source_target_pairs={{1,0},{2,1},{3,2},{5,4},{6,5},{7,6},{9,8},{10,9},{11,10},{13,12},{... | collective-permute-start | bytes 1572872 | tf_op jit(solution)/shard_map/ppermute | solution.py:24
  4.1 2.4 %fusion.2 = f32[256,6,256]{2,0,1:T(8,128)S(1)} fusion(f32[256,256,1]{1,0,2:T(8,128)} %constant.8, f32[1,1,6,256,256]{4,3,2,1,0:T(8,128)S(1)} %copy-done), kind=kOutput, calls=%fused_computation.2 | convolution fusion | flops 1207959552 | bytes 3407872 | tf_op jit(solution)/shard_map/ab,sbc->sac/dot_general | solution.py:76
  6.5 2.6 %fusion.amp_hbm = f32[6,256,256]{2,1,0:T(8,128)} fusion(f32[256,256,1]{1,0,2:T(8,128)S(1)} %copy-done.6, f32[256,6,256]{2,0,1:T(8,128)S(1)} %fusion.2), kind=kOutput, calls=%fused_computation | convolution fusion | flops 1207959552 | bytes 3407872 | tf_op jit(solution)/shard_map/sac,dc->sad/dot_general | solution.py:77
  9.1 1.3 %collective-permute-start.3 = (f32[2,256,512]{2,1,0:T(8,128)S(1)}, f32[2,256,512]{2,1,0:T(8,128)}, u32[]{:S(2)}, u32[]{:S(2)}) collective-permute-start(f32[2,256,512]{2,1,0:T(8,128)S(1)} %copy-done.3), channel_id=1, source_target_pairs={{4,0},{5,1},{6,2},{7,3},{8,4},{9,5},{10,6},{11,7},{12,8},{13,9},{1... | collective-permute-start | bytes 3145736 | tf_op jit(solution)/shard_map/ppermute | solution.py:24
  10.4 0.1 copy.19.spots_ref
  10.5 5.5 %collective-permute-start.1 = (s32[6,2]{1,0:T(8,128)S(1)}, s32[6,2]{1,0:T(8,128)S(1)}, u32[]{:S(2)}, u32[]{:S(2)}) collective-permute-start(s32[6,2]{1,0:T(8,128)S(1)} %copy.19.spots_ref), channel_id=1, source_target_pairs={{0,1},{1,2},{2,3},{4,5},{5,6},{6,7},{8,9},{9,10},{10,11},{12,13},{... | collective-permute-start | bytes 152 | tf_op jit(solution)/shard_map/ppermute | solution.py:24
  16.0 1.3 %collective-permute-done.1.left_ref = s32[6,2]{1,0:T(8,128)S(1)} collective-permute-done((s32[6,2]{1,0:T(8,128)S(1)}, s32[6,2]{1,0:T(8,128)S(1)}, u32[]{:S(2)}, u32[]{:S(2)}) %collective-permute-start.1) | collective-permute-done | bytes 80 | tf_op jit(solution)/shard_map/ppermute | solution.py:24
  17.3 2.5 %collective-permute-done.right_hbm = f32[2,256,256]{2,1,0:T(8,128)S(1)} collective-permute-done((f32[2,256,256]{2,1,0:T(8,128)}, f32[2,256,256]{2,1,0:T(8,128)S(1)}, u32[]{:S(2)}, u32[]{:S(2)}) %collective-permute-start) | collective-permute-done | bytes 524320 | tf_op jit(solution)/shard_map/ppermute | solution.py:24
  19.8 1.3 %collective-permute-start.4 = (f32[2,256,256]{2,1,0:T(8,128)S(1)}, f32[2,256,256]{2,1,0:T(8,128)}, u32[]{:S(2)}, u32[]{:S(2)}) collective-permute-start(f32[2,256,256]{2,1,0:T(8,128)S(1)} %collective-permute-done.right_hbm), channel_id=1, source_target_pairs={{4,0},{5,1},{6,2},{7,3},{8,4},{9,5},{10,6},{11,7},{12,8},{13,9},{1... | collective-permute-start | bytes 1572872 | tf_op jit(solution)/shard_map/ppermute | solution.py:24
  21.1 0.1 copy.16
  21.2 0.1 pad_add_fusion
  21.3 0.1 copy.17
  21.4 3.0 %collective-permute-start.2 = (s32[12,2]{1,0:T(8,128)S(1)}, s32[12,2]{1,0:T(8,128)S(1)}, u32[]{:S(2)}, u32[]{:S(2)}) collective-permute-start(s32[12,2]{1,0:T(8,128)S(1)} %copy.17), channel_id=1, source_target_pairs={{0,4},{1,5},{2,6},{3,7},{4,8},{5,9},{6,10},{7,11},{8,12},{9,13},{1... | collective-permute-start | bytes 296 | tf_op jit(solution)/shard_map/ppermute | solution.py:24
  24.4 0.1 copy.18.counts_ref
  24.5 0.7 collective-permute-done.2
  25.2 1.6 %copy-done.1 = f32[2,4,256,256]{3,2,1,0:T(8,128)S(1)} copy-done((f32[2,4,256,256]{3,2,1,0:T(8,128)S(1)}, f32[2,4,256,256]{3,2,1,0:T(8,128)}, u32[]{:S(2)}) %copy-start.1) | copy-done | bytes 2097176
  26.8 2.1 %lighting.1 = (f32[256,512]{1,0:T(8,128)S(1)}, f32[8,256]{1,0:T(8,128)S(1)}) custom-call(s32[8,4]{1,0:T(8,128)S(1)} %copy.18.counts_ref, s32[6,2]{1,0:T(8,128)S(1)} %copy.19.spots_ref, s32[6,2]{1,0:T(8,128)S(1)} %collective-permute-done.1.left_ref, s32[6,2]{1,0:T(8,128)S(1)} %get-tuple-element.63.up_ref, s32[6,2]{1,0:T(8,128)S(1)} %get-tuple-element.62.diag_ref, ...), custom_call_target="tpu_custom_call" | custom-call | flops 100000000 | bytes 10000000 | tf_op jit(solution)/shard_map/lighting/pallas_call | solution.py:406
  28.9 17.2 %positions.1 = (f32[2,256,512]{2,1,0:T(8,128)}, f32[2,256,768]{2,1,0:T(8,128)}, f32[2,256,256]{2,1,0:T(8,128)}, f32[4,288,256]{2,1,0:T(8,128)S(1)}, f32[4,288,256]{2,1,0:T(8,128)}) custom-call(s32[8,4]{1,0:T(8,128)S(1)} %copy.18.counts_ref, s32[6,2]{1,0:T(8,128)S(1)} %copy.19.spots_ref, f32[2,256,512]{2,1,0:T(8,128)} %tile_ref.1, ...), custom_call_target="tpu_custom_call" | custom-call | flops 7000000000 | bytes 20000000 | tf_op jit(solution)/shard_map/positions/pallas_call | solution.py:420
  46.1 3.5 %collective-permute-start.5 = (f32[4,288,256]{2,1,0:T(8,128)}, f32[4,288,256]{2,1,0:T(8,128)S(1)}, u32[]{:S(2)}, u32[]{:S(2)}) collective-permute-start(f32[4,288,256]{2,1,0:T(8,128)} %get-tuple-element.40), channel_id=1, source_target_pairs={{0,4},{1,5},{2,6},{3,7},{4,0},{5,1},{6,2},{7,3},{8,12},{9,13},{10,... | collective-permute-start | bytes 3538952 | tf_op jit(solution)/shard_map/ppermute | solution.py:30
  49.6 2.7 %collective-permute-done.5.got_ref = f32[4,288,256]{2,1,0:T(8,128)S(1)} collective-permute-done((f32[4,288,256]{2,1,0:T(8,128)}, f32[4,288,256]{2,1,0:T(8,128)S(1)}, u32[]{:S(2)}, u32[]{:S(2)}) %collective-permute-start.5) | collective-permute-done | bytes 1179680 | tf_op jit(solution)/shard_map/ppermute | solution.py:30
  52.3 0.2 fold_plane.2
  52.5 8.3 %collective-permute-start.6 = (f32[2,288,256]{2,1,0:T(8,128)S(1)}, f32[2,288,256]{2,1,0:T(8,128)S(1)}, u32[]{:S(2)}, u32[]{:S(2)}) collective-permute-start(f32[2,288,256]{2,1,0:T(8,128)S(1)} %get-tuple-element.42), channel_id=1, source_target_pairs={{0,8},{1,9},{2,10},{3,11},{4,20},{5,21},{6,22},{7,23},{8,0},{9,1},... | collective-permute-start | bytes 1769480 | tf_op jit(solution)/shard_map/ppermute | solution.py:56
  60.8 7.9 %collective-permute-done.6.got_ref = f32[2,288,256]{2,1,0:T(8,128)S(1)} collective-permute-done((f32[2,288,256]{2,1,0:T(8,128)S(1)}, f32[2,288,256]{2,1,0:T(8,128)S(1)}, u32[]{:S(2)}, u32[]{:S(2)}) %collective-permute-start.6) | collective-permute-done | bytes 589856 | tf_op jit(solution)/shard_map/ppermute | solution.py:56
  68.8 2.6 %collective-permute-start.7 = (f32[1,288,256]{2,1,0:T(8,128)S(1)}, f32[1,288,256]{2,1,0:T(8,128)S(1)}, u32[]{:S(2)}, u32[]{:S(2)}) collective-permute-start(f32[1,288,256]{2,1,0:T(8,128)S(1)} %get-tuple-element.44), channel_id=1, source_target_pairs={{0,16},{1,17},{2,18},{3,19},{4,12},{5,13},{6,14},{7,15},{8,24},{9,... | collective-permute-start | bytes 884744 | tf_op jit(solution)/shard_map/ppermute | solution.py:56
  71.4 4.7 %collective-permute-done.7.got_ref = f32[1,288,256]{2,1,0:T(8,128)S(1)} collective-permute-done((f32[1,288,256]{2,1,0:T(8,128)S(1)}, f32[1,288,256]{2,1,0:T(8,128)S(1)}, u32[]{:S(2)}, u32[]{:S(2)}) %collective-permute-start.7) | collective-permute-done | bytes 294944 | tf_op jit(solution)/shard_map/ppermute | solution.py:56
  76.1 1.5 %collective-permute-start.14 = (f32[2,256,768]{2,1,0:T(8,128)S(1)}, f32[2,256,768]{2,1,0:T(8,128)S(1)}, u32[]{:S(2)}, u32[]{:S(2)}) collective-permute-start(f32[2,256,768]{2,1,0:T(8,128)S(1)} %copy-done.10), channel_id=1, source_target_pairs={{0,4},{1,5},{2,6},{3,7},{4,8},{5,9},{6,10},{7,11},{8,12},{9,13},{1... | collective-permute-start | bytes 4718600 | tf_op jit(solution)/shard_map/ppermute | solution.py:24
  77.7 1.3 %collective-permute-start.8 = (f32[80,256]{1,0:T(8,128)S(1)}, f32[80,256]{1,0:T(8,128)S(1)}, u32[]{:S(2)}, u32[]{:S(2)}) collective-permute-start(f32[80,256]{1,0:T(8,128)S(1)} %get-tuple-element.49), channel_id=1, source_target_pairs={{0,1},{1,0},{2,3},{3,2},{4,5},{5,4},{6,7},{7,6},{8,9},{9,8},{10,11... | collective-permute-start | bytes 245768 | tf_op jit(solution)/shard_map/ppermute | solution.py:30
  78.9 3.3 %collective-permute-start.9 = (f32[80,256]{1,0:T(8,128)S(1)}, f32[80,256]{1,0:T(8,128)S(1)}, u32[]{:S(2)}, u32[]{:S(2)}) collective-permute-start(f32[80,256]{1,0:T(8,128)S(1)} %get-tuple-element.50), channel_id=1, source_target_pairs={{0,2},{1,3},{2,0},{3,1},{4,6},{5,7},{6,4},{7,5},{8,10},{9,11},{10,... | collective-permute-start | bytes 245768 | tf_op jit(solution)/shard_map/ppermute | solution.py:30
  82.2 3.3 %collective-permute-done.9 = f32[80,256]{1,0:T(8,128)S(1)} collective-permute-done((f32[80,256]{1,0:T(8,128)S(1)}, f32[80,256]{1,0:T(8,128)S(1)}, u32[]{:S(2)}, u32[]{:S(2)}) %collective-permute-start.9) | collective-permute-done | bytes 81952 | tf_op jit(solution)/shard_map/ppermute | solution.py:30
  85.5 2.9 %collective-permute-done.10 = f32[80,256]{1,0:T(8,128)S(1)} collective-permute-done((f32[80,256]{1,0:T(8,128)S(1)}, f32[80,256]{1,0:T(8,128)S(1)}, u32[]{:S(2)}, u32[]{:S(2)}) %collective-permute-start.10) | collective-permute-done | bytes 81952 | tf_op jit(solution)/shard_map/ppermute | solution.py:30
  88.4 2.1 %collective-permute-start.11 = (f32[72,256]{1,0:T(8,128)S(1)}, f32[72,256]{1,0:T(8,128)S(1)}, u32[]{:S(2)}, u32[]{:S(2)}) collective-permute-start(f32[72,256]{1,0:T(8,128)S(1)} %get-tuple-element.61), channel_id=1, source_target_pairs={{0,1},{1,0},{2,3},{3,2},{4,5},{5,4},{6,7},{7,6},{8,9},{9,8},{10,11... | collective-permute-start | bytes 221192 | tf_op jit(solution)/shard_map/ppermute | solution.py:30
  90.6 2.3 %collective-permute-start.13 = (f32[72,256]{1,0:T(8,128)S(1)}, f32[72,256]{1,0:T(8,128)S(1)}, u32[]{:S(2)}, u32[]{:S(2)}) collective-permute-start(f32[72,256]{1,0:T(8,128)S(1)} %get-tuple-element.61), channel_id=1, source_target_pairs={{0,3},{1,2},{2,1},{3,0},{4,7},{5,6},{6,5},{7,4},{8,11},{9,10},{10,... | collective-permute-start | bytes 221192 | tf_op jit(solution)/shard_map/ppermute | solution.py:30
  92.9 0.7 collective-permute-done.11
  93.6 7.2 %collective-permute-done.12 = f32[72,256]{1,0:T(8,128)S(1)} collective-permute-done((f32[72,256]{1,0:T(8,128)S(1)}, f32[72,256]{1,0:T(8,128)S(1)}, u32[]{:S(2)}, u32[]{:S(2)}) %collective-permute-start.12) | collective-permute-done | bytes 73760 | tf_op jit(solution)/shard_map/ppermute | solution.py:30
  100.8 0.1 slice_add_fusion
  100.9 2.8 %collective-permute-start.15 = (f32[296,256]{1,0:T(8,128)S(1)}, f32[296,256]{1,0:T(8,128)S(1)}, u32[]{:S(2)}, u32[]{:S(2)}) collective-permute-start(f32[296,256]{1,0:T(8,128)S(1)} %constant_dynamic-update-slice_fusion.refs_0_), channel_id=1, source_target_pairs={{0,16},{1,17},{2,18},{3,19},{4,12},{5,13},{6,14},{7,15},{8,24},{9,... | collective-permute-start | bytes 909320 | tf_op jit(solution)/shard_map/ppermute | solution.py:56
  103.7 1.3 %collective-permute-start.18 = (f32[2,256,256]{2,1,0:T(8,128)S(1)}, f32[2,256,256]{2,1,0:T(8,128)S(1)}, u32[]{:S(2)}, u32[]{:S(2)}) collective-permute-start(f32[2,256,256]{2,1,0:T(8,128)S(1)} %slice_add_fusion), channel_id=1, source_target_pairs={{0,1},{1,2},{2,3},{4,5},{5,6},{6,7},{8,9},{9,10},{10,11},{12,13},{... | collective-permute-start | bytes 1572872 | tf_op jit(solution)/shard_map/ppermute | solution.py:24
  105.0 0.1 collective-permute-start.16
  105.2 5.7 %collective-permute-done.15.refs_1_ = f32[296,256]{1,0:T(8,128)S(1)} collective-permute-done((f32[296,256]{1,0:T(8,128)S(1)}, f32[296,256]{1,0:T(8,128)S(1)}, u32[]{:S(2)}, u32[]{:S(2)}) %collective-permute-start.15) | collective-permute-done | bytes 303136 | tf_op jit(solution)/shard_map/ppermute | solution.py:56
  110.9 2.5 %collective-permute-start.17 = (f32[296,256]{1,0:T(8,128)S(1)}, f32[296,256]{1,0:T(8,128)S(1)}, u32[]{:S(2)}, u32[]{:S(2)}) collective-permute-start(f32[296,256]{1,0:T(8,128)S(1)} %collective-permute-done.15.refs_1_), channel_id=1, source_target_pairs={{0,8},{1,9},{2,10},{3,11},{4,20},{5,21},{6,22},{7,23},{8,0},{9,1},... | collective-permute-start | bytes 909320 | tf_op jit(solution)/shard_map/ppermute | solution.py:56
  113.4 0.5 collective-permute-start.20
  113.9 2.4 %collective-permute-done.18.g_left = f32[2,256,256]{2,1,0:T(8,128)S(1)} collective-permute-done((f32[2,256,256]{2,1,0:T(8,128)S(1)}, f32[2,256,256]{2,1,0:T(8,128)S(1)}, u32[]{:S(2)}, u32[]{:S(2)}) %collective-permute-start.18) | collective-permute-done | bytes 524320 | tf_op jit(solution)/shard_map/ppermute | solution.py:24
  116.4 1.8 %collective-permute-done.17.refs_3_ = f32[296,256]{1,0:T(8,128)S(1)} collective-permute-done((f32[296,256]{1,0:T(8,128)S(1)}, f32[296,256]{1,0:T(8,128)S(1)}, u32[]{:S(2)}, u32[]{:S(2)}) %collective-permute-start.17) | collective-permute-done | bytes 303136 | tf_op jit(solution)/shard_map/ppermute | solution.py:56
  118.2 1.6 %collective-permute-done.22.refs_7_ = f32[296,256]{1,0:T(8,128)S(1)} collective-permute-done((f32[296,256]{1,0:T(8,128)S(1)}, f32[296,256]{1,0:T(8,128)S(1)}, u32[]{:S(2)}, u32[]{:S(2)}) %collective-permute-start.22) | collective-permute-done | bytes 303136 | tf_op jit(solution)/shard_map/ppermute | solution.py:30
  119.8 1.4 %object_update.1 = f32[2,256,512]{2,1,0:T(8,128)} custom-call(f32[2,256,512]{2,1,0:T(8,128)S(1)} %copy-done.4, f32[256,512]{1,0:T(8,128)S(1)} %get-tuple-element.33.light_ref, f32[8,256]{1,0:T(8,128)S(1)} %slice_maximum_fusion.top_ref, f32[2,256,512]{2,1,0:T(8,128)S(1)} %copy-done.5, f32[2,256,256]{2,1,0:T(8,128)S(1)} %collective-permute-done.18.g_left, ...), custom_call_target="tpu_custom_call" | custom-call | flops 1000000 | bytes 6000000 | tf_op jit(solution)/shard_map/object_update/pallas_call | solution.py:468
  121.2 0.6 copy-done.2
  121.8 1.9 %probe_update.1 = f32[2,4,256,256]{3,2,1,0:T(8,128)} custom-call(f32[2,4,256,256]{3,2,1,0:T(8,128)S(1)} %copy-done.2, f32[296,256]{1,0:T(8,128)S(1)} %constant_dynamic-update-slice_fusion.refs_0_, f32[296,256]{1,0:T(8,128)S(1)} %collective-permute-done.15.refs_1_, f32[296,256]{1,0:T(8,128)S(1)} %collective-permute-done.16.refs_2_, ...), custom_call_target="tpu_custom_call" | custom-call | flops 1000000 | bytes 6000000 | tf_op jit(solution)/shard_map/probe_update/pallas_call | solution.py:477
  (43 shorter events, 0.3 us)
Async XLA Ops:
  0.6 3.4 %copy-start = (f32[1,1,6,256,256]{4,3,2,1,0:T(8,128)S(1)}, f32[1,1,6,256,256]{4,3,2,1,0:T(8,128)}, u32[]{:S(2)}) copy-start(f32[1,1,6,256,256]{4,3,2,1,0:T(8,128)} %param.9) | copy-start | bytes 4718596
  2.6 3.8 %copy-start.6 = (f32[256,256,1]{1,0,2:T(8,128)S(1)}, f32[256,256,1]{1,0,2:T(8,128)}, u32[]{:S(2)}) copy-start(f32[256,256,1]{1,0,2:T(8,128)} %constant.8) | copy-start | bytes 786436
  2.6 17.2 %collective-permute-start = (f32[2,256,256]{2,1,0:T(8,128)}, f32[2,256,256]{2,1,0:T(8,128)S(1)}, u32[]{:S(2)}, u32[]{:S(2)}) collective-permute-start(f32[2,256,256]{2,1,0:T(8,128)} %slice.54), channel_id=1, source_target_pairs={{1,0},{2,1},{3,2},{5,4},{6,5},{7,6},{9,8},{10,9},{11,10},{13,12},{... | collective-permute-start | bytes 1572872 | tf_op jit(solution)/shard_map/ppermute | solution.py:24
  6.5 2.6 %copy-start.3 = (f32[2,256,512]{2,1,0:T(8,128)S(1)}, f32[2,256,512]{2,1,0:T(8,128)}, u32[]{:S(2)}) copy-start(f32[2,256,512]{2,1,0:T(8,128)} %tile_ref.1) | copy-start | bytes 3145732
  6.5 3.9 %copy-start.8 = (s32[1,1,6,2]{2,3,1,0:T(2,128)S(1)}, s32[1,1,6,2]{2,3,1,0:T(2,128)}, u32[]{:S(2)}) copy-start(s32[1,1,6,2]{2,3,1,0:T(2,128)} %param.10) | copy-start | bytes 148
  6.5 17.9 %copy-start.9 = (s32[8,4]{0,1:T(4,128)S(1)}, s32[8,4]{0,1:T(4,128)}, u32[]{:S(2)}) copy-start(s32[8,4]{0,1:T(4,128)} %param.11) | copy-start | bytes 388
  9.1 19.8 %collective-permute-start.3 = (f32[2,256,512]{2,1,0:T(8,128)S(1)}, f32[2,256,512]{2,1,0:T(8,128)}, u32[]{:S(2)}, u32[]{:S(2)}) collective-permute-start(f32[2,256,512]{2,1,0:T(8,128)S(1)} %copy-done.3), channel_id=1, source_target_pairs={{4,0},{5,1},{6,2},{7,3},{8,4},{9,5},{10,6},{11,7},{12,8},{13,9},{1... | collective-permute-start | bytes 3145736 | tf_op jit(solution)/shard_map/ppermute | solution.py:24
  10.5 6.9 %collective-permute-start.1 = (s32[6,2]{1,0:T(8,128)S(1)}, s32[6,2]{1,0:T(8,128)S(1)}, u32[]{:S(2)}, u32[]{:S(2)}) collective-permute-start(s32[6,2]{1,0:T(8,128)S(1)} %copy.19.spots_ref), channel_id=1, source_target_pairs={{0,1},{1,2},{2,3},{4,5},{5,6},{6,7},{8,9},{9,10},{10,11},{12,13},{... | collective-permute-start | bytes 152 | tf_op jit(solution)/shard_map/ppermute | solution.py:24
  19.8 9.1 %collective-permute-start.4 = (f32[2,256,256]{2,1,0:T(8,128)S(1)}, f32[2,256,256]{2,1,0:T(8,128)}, u32[]{:S(2)}, u32[]{:S(2)}) collective-permute-start(f32[2,256,256]{2,1,0:T(8,128)S(1)} %collective-permute-done.right_hbm), channel_id=1, source_target_pairs={{4,0},{5,1},{6,2},{7,3},{8,4},{9,5},{10,6},{11,7},{12,8},{13,9},{1... | collective-permute-start | bytes 1572872 | tf_op jit(solution)/shard_map/ppermute | solution.py:24
  21.4 3.8 %collective-permute-start.2 = (s32[12,2]{1,0:T(8,128)S(1)}, s32[12,2]{1,0:T(8,128)S(1)}, u32[]{:S(2)}, u32[]{:S(2)}) collective-permute-start(s32[12,2]{1,0:T(8,128)S(1)} %copy.17), channel_id=1, source_target_pairs={{0,4},{1,5},{2,6},{3,7},{4,8},{5,9},{6,10},{7,11},{8,12},{9,13},{1... | collective-permute-start | bytes 296 | tf_op jit(solution)/shard_map/ppermute | solution.py:24
  25.2 1.6 %copy-start.1 = (f32[2,4,256,256]{3,2,1,0:T(8,128)S(1)}, f32[2,4,256,256]{3,2,1,0:T(8,128)}, u32[]{:S(2)}) copy-start(f32[2,4,256,256]{3,2,1,0:T(8,128)} %probe_ref.3) | copy-start | bytes 6291460
  46.1 6.2 %collective-permute-start.5 = (f32[4,288,256]{2,1,0:T(8,128)}, f32[4,288,256]{2,1,0:T(8,128)S(1)}, u32[]{:S(2)}, u32[]{:S(2)}) collective-permute-start(f32[4,288,256]{2,1,0:T(8,128)} %get-tuple-element.40), channel_id=1, source_target_pairs={{0,4},{1,5},{2,6},{3,7},{4,0},{5,1},{6,2},{7,3},{8,12},{9,13},{10,... | collective-permute-start | bytes 3538952 | tf_op jit(solution)/shard_map/ppermute | solution.py:30
  52.3 23.8 %copy-start.10 = (f32[2,256,768]{2,1,0:T(8,128)S(1)}, f32[2,256,768]{2,1,0:T(8,128)}, u32[]{:S(2)}) copy-start(f32[2,256,768]{2,1,0:T(8,128)} %get-tuple-element.52) | copy-start | bytes 4718596
  52.5 48.3 %copy-start.7 = (f32[2,256,256]{2,1,0:T(8,128)S(1)}, f32[2,256,256]{2,1,0:T(8,128)}, u32[]{:S(2)}) copy-start(f32[2,256,256]{2,1,0:T(8,128)} %get-tuple-element.53) | copy-start | bytes 1572868
  52.5 16.2 %collective-permute-start.6 = (f32[2,288,256]{2,1,0:T(8,128)S(1)}, f32[2,288,256]{2,1,0:T(8,128)S(1)}, u32[]{:S(2)}, u32[]{:S(2)}) collective-permute-start(f32[2,288,256]{2,1,0:T(8,128)S(1)} %get-tuple-element.42), channel_id=1, source_target_pairs={{0,8},{1,9},{2,10},{3,11},{4,20},{5,21},{6,22},{7,23},{8,0},{9,1},... | collective-permute-start | bytes 1769480 | tf_op jit(solution)/shard_map/ppermute | solution.py:56
  68.8 7.3 %collective-permute-start.7 = (f32[1,288,256]{2,1,0:T(8,128)S(1)}, f32[1,288,256]{2,1,0:T(8,128)S(1)}, u32[]{:S(2)}, u32[]{:S(2)}) collective-permute-start(f32[1,288,256]{2,1,0:T(8,128)S(1)} %get-tuple-element.44), channel_id=1, source_target_pairs={{0,16},{1,17},{2,18},{3,19},{4,12},{5,13},{6,14},{7,15},{8,24},{9,... | collective-permute-start | bytes 884744 | tf_op jit(solution)/shard_map/ppermute | solution.py:56
  76.1 43.7 %copy-start.4 = (f32[2,256,512]{2,1,0:T(8,128)S(1)}, f32[2,256,512]{2,1,0:T(8,128)}, u32[]{:S(2)}) copy-start(f32[2,256,512]{2,1,0:T(8,128)} %tile_ref.1) | copy-start | bytes 3145732
  76.1 43.8 %copy-start.5 = (f32[2,256,512]{2,1,0:T(8,128)S(1)}, f32[2,256,512]{2,1,0:T(8,128)}, u32[]{:S(2)}) copy-start(f32[2,256,512]{2,1,0:T(8,128)} %get-tuple-element.57.g_tile) | copy-start | bytes 3145732
  76.1 24.7 %collective-permute-start.14 = (f32[2,256,768]{2,1,0:T(8,128)S(1)}, f32[2,256,768]{2,1,0:T(8,128)S(1)}, u32[]{:S(2)}, u32[]{:S(2)}) collective-permute-start(f32[2,256,768]{2,1,0:T(8,128)S(1)} %copy-done.10), channel_id=1, source_target_pairs={{0,4},{1,5},{2,6},{3,7},{4,8},{5,9},{6,10},{7,11},{8,12},{9,13},{1... | collective-permute-start | bytes 4718600 | tf_op jit(solution)/shard_map/ppermute | solution.py:24
  77.7 4.5 %collective-permute-start.8 = (f32[80,256]{1,0:T(8,128)S(1)}, f32[80,256]{1,0:T(8,128)S(1)}, u32[]{:S(2)}, u32[]{:S(2)}) collective-permute-start(f32[80,256]{1,0:T(8,128)S(1)} %get-tuple-element.49), channel_id=1, source_target_pairs={{0,1},{1,0},{2,3},{3,2},{4,5},{5,4},{6,7},{7,6},{8,9},{9,8},{10,11... | collective-permute-start | bytes 245768 | tf_op jit(solution)/shard_map/ppermute | solution.py:30
  78.9 6.6 %collective-permute-start.9 = (f32[80,256]{1,0:T(8,128)S(1)}, f32[80,256]{1,0:T(8,128)S(1)}, u32[]{:S(2)}, u32[]{:S(2)}) collective-permute-start(f32[80,256]{1,0:T(8,128)S(1)} %get-tuple-element.50), channel_id=1, source_target_pairs={{0,2},{1,3},{2,0},{3,1},{4,6},{5,7},{6,4},{7,5},{8,10},{9,11},{10,... | collective-permute-start | bytes 245768 | tf_op jit(solution)/shard_map/ppermute | solution.py:30
  82.2 6.2 %collective-permute-start.10 = (f32[80,256]{1,0:T(8,128)S(1)}, f32[80,256]{1,0:T(8,128)S(1)}, u32[]{:S(2)}, u32[]{:S(2)}) collective-permute-start(f32[80,256]{1,0:T(8,128)S(1)} %get-tuple-element.51), channel_id=1, source_target_pairs={{0,3},{1,2},{2,1},{3,0},{4,7},{5,6},{6,5},{7,4},{8,11},{9,10},{10,... | collective-permute-start | bytes 245768 | tf_op jit(solution)/shard_map/ppermute | solution.py:30
  88.4 5.1 %collective-permute-start.11 = (f32[72,256]{1,0:T(8,128)S(1)}, f32[72,256]{1,0:T(8,128)S(1)}, u32[]{:S(2)}, u32[]{:S(2)}) collective-permute-start(f32[72,256]{1,0:T(8,128)S(1)} %get-tuple-element.61), channel_id=1, source_target_pairs={{0,1},{1,0},{2,3},{3,2},{4,5},{5,4},{6,7},{7,6},{8,9},{9,8},{10,11... | collective-permute-start | bytes 221192 | tf_op jit(solution)/shard_map/ppermute | solution.py:30
  90.6 10.2 %collective-permute-start.13 = (f32[72,256]{1,0:T(8,128)S(1)}, f32[72,256]{1,0:T(8,128)S(1)}, u32[]{:S(2)}, u32[]{:S(2)}) collective-permute-start(f32[72,256]{1,0:T(8,128)S(1)} %get-tuple-element.61), channel_id=1, source_target_pairs={{0,3},{1,2},{2,1},{3,0},{4,7},{5,6},{6,5},{7,4},{8,11},{9,10},{10,... | collective-permute-start | bytes 221192 | tf_op jit(solution)/shard_map/ppermute | solution.py:30
  92.9 7.9 %collective-permute-start.12 = (f32[72,256]{1,0:T(8,128)S(1)}, f32[72,256]{1,0:T(8,128)S(1)}, u32[]{:S(2)}, u32[]{:S(2)}) collective-permute-start(f32[72,256]{1,0:T(8,128)S(1)} %get-tuple-element.61), channel_id=1, source_target_pairs={{0,2},{1,3},{2,0},{3,1},{4,6},{5,7},{6,4},{7,5},{8,10},{9,11},{10,... | collective-permute-start | bytes 221192 | tf_op jit(solution)/shard_map/ppermute | solution.py:30
  100.9 10.0 %collective-permute-start.15 = (f32[296,256]{1,0:T(8,128)S(1)}, f32[296,256]{1,0:T(8,128)S(1)}, u32[]{:S(2)}, u32[]{:S(2)}) collective-permute-start(f32[296,256]{1,0:T(8,128)S(1)} %constant_dynamic-update-slice_fusion.refs_0_), channel_id=1, source_target_pairs={{0,16},{1,17},{2,18},{3,19},{4,12},{5,13},{6,14},{7,15},{8,24},{9,... | collective-permute-start | bytes 909320 | tf_op jit(solution)/shard_map/ppermute | solution.py:56
  103.7 12.6 %collective-permute-start.18 = (f32[2,256,256]{2,1,0:T(8,128)S(1)}, f32[2,256,256]{2,1,0:T(8,128)S(1)}, u32[]{:S(2)}, u32[]{:S(2)}) collective-permute-start(f32[2,256,256]{2,1,0:T(8,128)S(1)} %slice_add_fusion), channel_id=1, source_target_pairs={{0,1},{1,2},{2,3},{4,5},{5,6},{6,7},{8,9},{9,10},{10,11},{12,13},{... | collective-permute-start | bytes 1572872 | tf_op jit(solution)/shard_map/ppermute | solution.py:24
  105.0 8.9 %collective-permute-start.16 = (f32[296,256]{1,0:T(8,128)S(1)}, f32[296,256]{1,0:T(8,128)S(1)}, u32[]{:S(2)}, u32[]{:S(2)}) collective-permute-start(f32[296,256]{1,0:T(8,128)S(1)} %constant_dynamic-update-slice_fusion.refs_0_), channel_id=1, source_target_pairs={{0,8},{1,9},{2,10},{3,11},{4,20},{5,21},{6,22},{7,23},{8,0},{9,1},... | collective-permute-start | bytes 909320 | tf_op jit(solution)/shard_map/ppermute | solution.py:56
  110.9 7.3 %collective-permute-start.17 = (f32[296,256]{1,0:T(8,128)S(1)}, f32[296,256]{1,0:T(8,128)S(1)}, u32[]{:S(2)}, u32[]{:S(2)}) collective-permute-start(f32[296,256]{1,0:T(8,128)S(1)} %collective-permute-done.15.refs_1_), channel_id=1, source_target_pairs={{0,8},{1,9},{2,10},{3,11},{4,20},{5,21},{6,22},{7,23},{8,0},{9,1},... | collective-permute-start | bytes 909320 | tf_op jit(solution)/shard_map/ppermute | solution.py:56
  113.4 4.8 %collective-permute-start.19 = (f32[296,256]{1,0:T(8,128)S(1)}, f32[296,256]{1,0:T(8,128)S(1)}, u32[]{:S(2)}, u32[]{:S(2)}) collective-permute-start(f32[296,256]{1,0:T(8,128)S(1)} %constant_dynamic-update-slice_fusion.refs_0_), channel_id=1, source_target_pairs={{0,4},{1,5},{2,6},{3,7},{4,0},{5,1},{6,2},{7,3},{8,12},{9,13},{10,... | collective-permute-start | bytes 909320 | tf_op jit(solution)/shard_map/ppermute | solution.py:30
  113.4 4.8 %collective-permute-start.20 = (f32[296,256]{1,0:T(8,128)S(1)}, f32[296,256]{1,0:T(8,128)S(1)}, u32[]{:S(2)}, u32[]{:S(2)}) collective-permute-start(f32[296,256]{1,0:T(8,128)S(1)} %collective-permute-done.15.refs_1_), channel_id=1, source_target_pairs={{0,4},{1,5},{2,6},{3,7},{4,0},{5,1},{6,2},{7,3},{8,12},{9,13},{10,... | collective-permute-start | bytes 909320 | tf_op jit(solution)/shard_map/ppermute | solution.py:30
  113.9 4.3 %collective-permute-start.21 = (f32[296,256]{1,0:T(8,128)S(1)}, f32[296,256]{1,0:T(8,128)S(1)}, u32[]{:S(2)}, u32[]{:S(2)}) collective-permute-start(f32[296,256]{1,0:T(8,128)S(1)} %collective-permute-done.16.refs_2_), channel_id=1, source_target_pairs={{0,4},{1,5},{2,6},{3,7},{4,0},{5,1},{6,2},{7,3},{8,12},{9,13},{10,... | collective-permute-start | bytes 909320 | tf_op jit(solution)/shard_map/ppermute | solution.py:30
  118.2 1.6 %collective-permute-start.22 = (f32[296,256]{1,0:T(8,128)S(1)}, f32[296,256]{1,0:T(8,128)S(1)}, u32[]{:S(2)}, u32[]{:S(2)}) collective-permute-start(f32[296,256]{1,0:T(8,128)S(1)} %collective-permute-done.17.refs_3_), channel_id=1, source_target_pairs={{0,4},{1,5},{2,6},{3,7},{4,0},{5,1},{6,2},{7,3},{8,12},{9,13},{10,... | collective-permute-start | bytes 909320 | tf_op jit(solution)/shard_map/ppermute | solution.py:30
  119.8 2.0 %copy-start.2 = (f32[2,4,256,256]{3,2,1,0:T(8,128)S(1)}, f32[2,4,256,256]{3,2,1,0:T(8,128)}, u32[]{:S(2)}) copy-start(f32[2,4,256,256]{3,2,1,0:T(8,128)} %probe_ref.3) | copy-start | bytes 6291460

commit v9 on v8

--- a/solution.py
+++ b/solution.py
@@ -34,18 +34,33 @@
     return (lax.axis_size("row") // 2).bit_length() - 1
 
 
+def col_bits():
+    return lax.axis_size("col").bit_length() - 1
+
+
 def plane_bit(core, step):
     return step if core == 0 else plane_bits() - 1 - step
 
 
+def rank_by(index, bits):
+    rank = 0
+    for bit in bits:
+        rank = rank * 2 + ((index >> bit) & 1)
+    return rank
+
+
 def plane_rank(core, pair):
-    ranks = []
-    for c in range(2):
-        rank = 0
-        for step in range(plane_bits()):
-            rank = rank * 2 + ((pair >> plane_bit(c, step)) & 1)
-        ranks.append(rank)
+    ranks = [rank_by(pair, [plane_bit(c, step) for step in range(plane_bits())]) for c in range(2)]
     return jnp.where(core == 0, ranks[0], ranks[1])
+
+
+def my_plane_rank():
+    my_row = lax.axis_index("row")
+    return plane_rank(lax.rem(my_row, 2), my_row // 2)
+
+
+def my_col_rank():
+    return rank_by(lax.axis_index("col"), range(col_bits()))
 
 
 def flipped(value, step):
@@ -73,8 +88,8 @@
     side = amplitudes.shape[-1]
     order = np.concatenate([np.arange(0, side, 2), np.arange(1, side, 2)])
     pick = jnp.asarray(np.eye(side)[order], jnp.float32)
-    rows = jnp.einsum("ab,sbc->sac", pick, amplitudes, precision=lax.Precision.HIGHEST)
-    return jnp.einsum("sac,dc->sad", rows, pick, precision=lax.Precision.HIGHEST)
+    rows = jnp.einsum("ab,sbc->sac", pick, amplitudes, precision=lax.Precision.HIGH)
+    return jnp.einsum("sac,dc->sad", rows, pick, precision=lax.Precision.HIGH)
 
 
 def corner_of(row, col):
@@ -119,7 +134,7 @@
 
 
 def main_kernel(
-    counts_ref, spots_ref, tile_hbm, below_hbm, right_hbm, corner_hbm, amp_hbm, probe_hbm, table_hbm,
+    counts_ref, spots_ref, tile_hbm, below_any, right_any, corner_any, amp_hbm, probe_hbm, table_hbm,
     g_tile, g_lower, g_right, mine_ref, other_ref,
     ext, gacc, stage, turned, wave, wins, sums, amp_ref, probe_ref, table_ref, in_sem, amp_sem, out_sem,
 ):
@@ -129,7 +144,7 @@
     my_row, my_col = lax.axis_index("row"), lax.axis_index("col")
     count = counts_ref[my_row, my_col]
     loads = [(probe_hbm, probe_ref), (table_hbm, table_ref)]
-    for ref, r, c in ((tile_hbm, 0, 0), (below_hbm, rows, 0), (right_hbm, 0, cols), (corner_hbm, rows, cols)):
+    for ref, r, c in ((tile_hbm, 0, 0), (below_any, rows, 0), (right_any, 0, cols), (corner_any, rows, cols)):
         loads.append((ref, ext.at[:, pl.ds(r, ref.shape[1]), pl.ds(c, ref.shape[2])]))
     loads = [pltpu.make_async_copy(a, b, in_sem.at[i]) for i, (a, b) in enumerate(loads)]
 
@@ -230,29 +245,20 @@
 
     lax.fori_loop(0, count, step, 0)
 
-    pairs = lax.axis_size("row") // 2
-    share = mine_ref.shape[1]
+    store = pltpu.make_async_copy(gacc.at[:, pl.ds(0, rows), pl.ds(0, cols)], g_tile, out_sem.at[0])
+    store.start()
     core = lax.rem(my_row, 2)
-    stores = []
-    for ref, base in ((other_ref, (1 - core) * (share * pairs)), (mine_ref, core * (share * pairs))):
-        base = pl.multiple_of(base, SUBLANES)
-        for j in range(pairs):
-            stores.append((sums.at[pl.ds(base + j * share, share)], ref.at[j]))
-    stores.append((gacc.at[:, pl.ds(0, rows), pl.ds(cols, side)], g_right))
-    stores.append((gacc.at[:, pl.ds(0, rows), pl.ds(0, cols)], g_tile))
-    stores.append((gacc.at[:, pl.ds(rows, side)], g_lower))
-    stores = [pltpu.make_async_copy(a, b, out_sem.at[i]) for i, (a, b) in enumerate(stores)]
-    for store in stores:
-        store.start()
-    for store in stores:
-        store.wait()
-
-
-def light_kernel(counts_ref, spots_ref, left_ref, up_ref, diag_ref, probe_ref, light_ref, top_ref, lit, acc):
-    side = probe_ref.shape[2]
+    for ref, at in ((other_ref, 1 - core), (mine_ref, core)):
+        ref[...] = sums[pl.ds(pl.multiple_of(at * ref.shape[0], SUBLANES), ref.shape[0])]
+    g_lower[...] = gacc[:, rows:]
+    g_right[...] = gacc[:, :rows, cols:]
+    store.wait()
+
+
+def light_kernel(counts_ref, spots_ref, left_ref, up_ref, diag_ref, lit_ref, light_ref, top_ref, acc):
+    side = lit_ref.shape[0]
     rows, cols = light_ref.shape
     my_row, my_col = lax.axis_index("row"), lax.axis_index("col")
-    lit[...] = jnp.sum(probe_ref[0] * probe_ref[0] + probe_ref[1] * probe_ref[1], axis=0)
     acc[...] = jnp.zeros_like(acc)
     for ref, d_row, d_col in ((spots_ref, 0, 0), (left_ref, 0, 1), (up_ref, 1, 0), (diag_ref, 1, 1)):
         inside = (my_row >= d_row) & (my_col >= d_col)
@@ -263,7 +269,7 @@
 
             @pl.when((row > 0) & (col > 0))
             def _():
-                add_at(acc, 0, row, col, lit[...], side)
+                add_at(acc, 0, row, col, lit_ref[...], side)
 
             return carry
 
@@ -275,53 +281,43 @@
     top_ref[...] = jnp.broadcast_to(top, top_ref.shape)
 
 
-def fold_kernel(step, held_ref, got_ref, send_ref, keep_ref):
-    half = keep_ref.shape[0]
-    my_row = lax.axis_index("row")
-    keep = (plane_rank(lax.rem(my_row, 2), my_row // 2) >> (plane_bits() - 1 - step)) & 1
-    for ref, at in ((send_ref, (1 - keep) * half), (keep_ref, keep * half)):
-        ref[...] = held_ref[pl.ds(at, half)] + got_ref[pl.ds(at, half)]
-
-
-def fold(step, held, got):
-    count, share, side = held.shape
+def fold_kernel(rank_of, below, with_top, *refs):
+    held_ref, got_ref, top_ref = refs[:2] + ((refs[2],) if with_top else (None,))
+    send_ref, keep_ref, out_top = refs[2 + with_top:] if with_top else refs[2:] + (None,)
+    rows, half = held_ref.shape[0], keep_ref.shape[0]
+    keep = (rank_of() >> below) & 1
+    for ref, at in ((send_ref, 1 - keep), (keep_ref, keep)):
+        part = pl.ds(pl.multiple_of(at * half, SUBLANES), half)
+        ref[:half] = held_ref[part] + got_ref[part]
+    if with_top:
+        top = top_ref[...]
+        if got_ref.shape[0] > rows:
+            top = jnp.maximum(top, got_ref[rows:])
+        out_top[...] = top
+        send_ref[half:] = top
+
+
+def fold(rank_of, below, held, got, top=None):
+    rows, side = held.shape
+    half = rows // 2
+    with_top = top is not None
+    extra = SUBLANES if with_top else 0
     return pl.pallas_call(
-        functools.partial(fold_kernel, step),
-        out_shape=(f32(count // 2, share, side),) * 2,
-        in_specs=[VM] * 2,
-        out_specs=(VM,) * 2,
+        functools.partial(fold_kernel, rank_of, below, with_top),
+        out_shape=(f32(half + extra, side), f32(half, side)) + ((f32(*top.shape),) if with_top else ()),
+        in_specs=[VM] * (2 + with_top),
+        out_specs=(VM,) * (2 + with_top),
         compiler_params=params(8),
-        cost_estimate=cost(10**6, 12 * count * share * side),
-        name="fold_plane",
-    )(held, got)
-
-
-def cut_kernel(held_ref, got_ref, top_ref, own_ref, *send_refs):
-    piece = own_ref.shape[0]
-    my_col = lax.axis_index("col")
-    for e, ref in enumerate((own_ref,) + send_refs):
-        at = pl.ds(pl.multiple_of((my_col ^ e) * piece, SUBLANES), piece)
-        ref[:piece] = held_ref[0, at] + got_ref[0, at]
-        if e:
-            ref[piece:] = top_ref[...]
-
-
-def cut(held, got, top, parts):
-    _, share, side = held.shape
-    piece = share // parts
-    return pl.pallas_call(
-        cut_kernel,
-        out_shape=(f32(piece, side),) + (f32(piece + SUBLANES, side),) * (parts - 1),
-        in_specs=[VM] * 3,
-        out_specs=(VM,) * parts,
-        compiler_params=params(4),
-        cost_estimate=cost(10**6, 12 * share * side),
-        name="cut_columns",
-    )(held, got, top)
-
-
-def finish_kernel(tile_ref, light_ref, top_ref, g_tile, g_left, g_up, out_ref):
-    side = g_left.shape[2]
+        cost_estimate=cost(10**6, 12 * rows * side),
+        name="fold",
+    )(held, got, *((top,) if with_top else ()))
+
+
+def finish_kernel(parts, tile_ref, light_ref, top_ref, g_tile, g_left, g_up, probe_ref, *refs):
+    pairs, n_col = parts
+    block_refs = refs[:2 * pairs]
+    object_out, probe_out, new_object, new_probe, sums, sem = refs[2 * pairs:]
+    modes, side = probe_ref.shape[1], probe_ref.shape[2]
     rows, cols = light_ref.shape
     top = top_ref[0:1, 0:1]
     for at in range(0, cols, side):
@@ -331,29 +327,31 @@
             total = g_tile[i, :, part] + g_up[i, :, part]
             if at == 0:
                 total += g_left[i]
-            out_ref[i, :, part] = tile_ref[i, :, part] + total * scale
-
-
-def probe_kernel(parts, probe_ref, *refs):
-    pairs, n_col = parts
-    block_refs, out_ref, sums = refs[:-2], refs[-2], refs[-1]
-    modes, side = probe_ref.shape[1], probe_ref.shape[2]
+            new_object[i, :, part] = tile_ref[i, :, part] + total * scale
+    stores = [pltpu.make_async_copy(new_object, object_out, sem.at[0])]
+    stores[0].start()
+
     share = block_refs[0].shape[0] - SUBLANES
     piece = share // n_col
-    my_row, my_col = lax.axis_index("row"), lax.axis_index("col")
-    core, pair = lax.rem(my_row, 2), my_row // 2
+    my_row = lax.axis_index("row")
+    core, pair, col_rank = lax.rem(my_row, 2), my_row // 2, my_col_rank()
     for i, ref in enumerate(block_refs):
         flip, d = i // pairs, i % pairs
         base = ((core ^ flip) * pairs + (plane_rank(core ^ flip, pair) ^ d)) * share
         for e in range(n_col):
-            to = pl.multiple_of(base + (my_col ^ e) * piece, SUBLANES)
+            to = pl.multiple_of(base + (col_rank ^ e) * piece, SUBLANES)
             sums[pl.ds(to, piece)] = ref[e * piece:(e + 1) * piece]
     den = sums[2 * modes * side:(2 * modes + 1) * side]
     top = jnp.max(jnp.max(den, axis=0, keepdims=True), axis=1, keepdims=True)
     scale = 1.0 / (den + 0.1 * top)
-    for k in range(modes):
-        out_ref[0, k] = probe_ref[0, k] + sums[k * side:(k + 1) * side] * scale
-        out_ref[1, k] = probe_ref[1, k] + sums[(modes + k) * side:(modes + k + 1) * side] * scale
+    for i in range(2):
+        for k in range(modes):
+            at = (i * modes + k) * side
+            new_probe[i, k] = probe_ref[i, k] + sums[at:at + side] * scale
+        stores.append(pltpu.make_async_copy(new_probe.at[i], probe_out.at[i], sem.at[1 + i]))
+        stores[-1].start()
+    for store in stores:
+        store.wait()
 
 
 def f32(*shape):
@@ -372,6 +370,10 @@
 
 def hbm(*shape):
     return pltpu.HBM(shape, jnp.float32)
+
+
+def vmem(*shape):
+    return pltpu.VMEM(shape, jnp.float32)
 
 
 def in_hbm(value):
@@ -391,40 +393,37 @@
     total_rows = -(-(2 * modes + 1) * side // step) * step
     share = total_rows // (2 * pairs)
     piece = share // n_col
-    my_row, my_col = lax.axis_index("row"), lax.axis_index("col")
-    core, pair = my_row % 2, my_row // 2
     spots = corners[0, 0]
 
     right = shifted(object_field[:, :, :side], 0, -1)
+    below = shifted(object_field[:, :side, :], -1, 0)
+    from_left = shifted(spots, 0, 1)
+    from_up = shifted(jnp.concatenate([spots, from_left], axis=0), 1, 0)
+    lit = jnp.sum(probe[0] * probe[0] + probe[1] * probe[1], axis=0)
+    right, from_up, lit = lax.optimization_barrier((right, from_up, lit))
+    corner = shifted(right[:, :side, :], -1, 0)
     measured = evens_first(amplitudes[0, 0])
-    tile, measured = lax.optimization_barrier((object_field, measured))
-    below = shifted(tile[:, :side, :], -1, 0)
-    from_left = shifted(spots, 0, 1)
-    right, measured, from_left = lax.optimization_barrier((right, measured, from_left))
-    corner = shifted(right[:, :side, :], -1, 0)
-    from_up = shifted(jnp.concatenate([spots, from_left], axis=0), 1, 0)
     light, top = pl.pallas_call(
         light_kernel,
         out_shape=(f32(rows, cols), f32(SUBLANES, side)),
         in_specs=[SM] * 5 + [VM],
         out_specs=(VM, VM),
         scratch_shapes=[
-            pltpu.VMEM((side, side), jnp.float32),
             pltpu.VMEM((1, rows + 2 * side, cols + 2 * side), jnp.float32),
         ],
         compiler_params=params(12),
         cost_estimate=cost(10**8, 10**7),
         name="lighting",
-    )(counts, spots, from_left, from_up[:slots], from_up[slots:], probe)
-    corner, top = lax.optimization_barrier((corner, top))
+    )(counts, spots, from_left, from_up[:slots], from_up[slots:], lit)
+    corner, top, measured = lax.optimization_barrier((corner, top, measured))
     g_tile, g_lower, g_right, mine, other = pl.pallas_call(
         main_kernel,
         out_shape=(
-            hbm(2, rows, cols), hbm(2, side, cols + side), hbm(2, rows, side),
-            pltpu.VMEM((pairs, share, side), jnp.float32), hbm(pairs, share, side),
+            hbm(2, rows, cols), vmem(2, side, cols + side), vmem(2, rows, side),
+            vmem(pairs * share, side), vmem(pairs * share, side),
         ),
         in_specs=[SM] * 2 + [HBM] + [ANY] * 3 + [HBM] * 3,
-        out_specs=(HBM,) * 3 + (VM, HBM),
+        out_specs=(HBM,) + (VM,) * 4,
         scratch_shapes=[
             pltpu.VMEM((2, rows + side, cols + side), jnp.float32),
             pltpu.VMEM((2, rows + side, cols + side), jnp.float32),
@@ -438,7 +437,7 @@
             pltpu.VMEM((4, side, side), jnp.bfloat16),
             pltpu.SemaphoreType.DMA((6,)),
             pltpu.SemaphoreType.DMA((2,)),
-            pltpu.SemaphoreType.DMA((2 * pairs + 3,)),
+            pltpu.SemaphoreType.DMA((1,)),
         ],
         compiler_params=params(22),
         cost_estimate=cost(7 * 10**9, 2 * 10**7),
@@ -448,15 +447,20 @@
     arrived = swapped(other, 1, 0)
     held, got = mine, arrived
     for i in range(plane_bits()):
-        send, held = fold(i, held, got)
+        send, held = fold(my_plane_rank, plane_bits() - 1 - i, held, got)
         got = flipped(send, i)
-    own, *sends = cut(held, got, top, n_col)
-    own, g_lower = lax.optimization_barrier((own, g_lower))
+    for i in range(col_bits()):
+        send, held, top = fold(my_col_rank, col_bits() - 1 - i, held, got, top)
+        if i == 0:
+            send, g_lower = lax.optimization_barrier((send, g_lower))
+        got = swapped(send, 0, 1 << i)
     g_up = shifted(g_lower, 1, 0)
-    received = [swapped(send, 0, e) for e, send in enumerate(sends, 1)]
-    own = sum([value[:piece] for value in received], own)
-    top = functools.reduce(jnp.maximum, [value[piece:] for value in received], top)
-    own = jnp.concatenate([own] + [swapped(own, 0, e) for e in range(1, n_col)] + [top], axis=0)
+    own = held + got[:piece]
+    top = jnp.maximum(top, got[piece:])
+    pieces = [own]
+    for e in range(1, n_col):
+        pieces.append(swapped(own, 0, rank_by(e, range(col_bits()))))
+    own = jnp.concatenate(pieces + [top], axis=0)
     own, g_up, g_right = lax.optimization_barrier((own, g_up, g_right + g_up[:, :, cols:]))
     g_left = shifted(g_right, 0, 1)
     blocks = [own]
@@ -465,26 +469,21 @@
     blocks[-1], g_left = lax.optimization_barrier((blocks[-1], g_left))
     blocks = blocks + [swapped(block, 1, 0) for block in blocks]
     top = functools.reduce(jnp.maximum, [block[share:] for block in blocks])
-    object_new = pl.pallas_call(
-        finish_kernel,
-        out_shape=f32(2, rows, cols),
-        in_specs=[VM] * 6,
-        out_specs=VM,
-        compiler_params=params(10),
-        cost_estimate=cost(10**6, 6 * 10**6),
-        name="object_update",
-    )(object_field, light, top, g_tile, g_left, g_up)
-    probe_new = pl.pallas_call(
-        functools.partial(probe_kernel, (pairs, n_col)),
-        out_shape=f32(*probe.shape),
-        in_specs=[VM] * (1 + len(blocks)),
-        out_specs=VM,
-        scratch_shapes=[pltpu.VMEM((total_rows, side), jnp.float32)],
-        compiler_params=params(14),
-        cost_estimate=cost(10**6, 6 * 10**6),
-        name="probe_update",
-    )(probe, *blocks)
-    return object_new, probe_new
+    return pl.pallas_call(
+        functools.partial(finish_kernel, (pairs, n_col)),
+        out_shape=(f32(*object_field.shape), f32(*probe.shape)),
+        in_specs=[VM] * (7 + len(blocks)),
+        out_specs=(ANY, ANY),
+        scratch_shapes=[
+            pltpu.VMEM(object_field.shape, jnp.float32),
+            pltpu.VMEM(probe.shape, jnp.float32),
+            pltpu.VMEM((total_rows, side), jnp.float32),
+            pltpu.SemaphoreType.DMA((3,)),
+        ],
+        compiler_params=params(20),
+        cost_estimate=cost(10**6, 10**7),
+        name="update",
+    )(object_field, light, top, g_tile, g_left, g_up, probe, *blocks)
 
 
 def solution(mesh):

time: 124 us -> 122 us (0.984)
  starting transfers between devices: 44.8 us -> 38.3 us
  waiting for transfers between devices: 45.4 us -> 48.5 us
  local copies, waits for them, and re-layouts: 4.62 us -> 2.89 us
  other arithmetic: 0.19 us -> 1.82 us
    ppermute x5, starting transfers between devices: 16.4 us -> 9.06 us  [flipped(): return lax.ppermute(value, ('row', 'col'), pairs)]
    ppermute x7, waiting for transfers between devices: 6.94 us -> 11.7 us  [shifted(): return lax.ppermute(value, ('row', 'col'), pairs)]
    ppermute x5, waiting for transfers between devices: 20.1 us -> 17.6 us  [flipped(): return lax.ppermute(value, ('row', 'col'), pairs)]
    unnamed x26 -> x16, local copies, waits for them, and re-layouts: 2.35 us -> 0.13 us
    reduce_sum x0 -> x1, other arithmetic: none -> 1.72 us  [body(): lit = jnp.sum(probe[0] * probe[0] + probe[1] * probe[1], axis=0)]
    ppermute x11 -> x10, waiting for transfers between devices: 18.3 us -> 19.3 us  [swapped(): return lax.ppermute(value, ('row', 'col'), pairs)]
    ppermute x11 -> x10, starting transfers between devices: 13 us -> 12.8 us  [swapped(): return lax.ppermute(value, ('row', 'col'), pairs)]
  transfers between devices with their start and end apart: 23 -> 22, of which waited for: 14 -> 14; matrix products, arithmetic and copies ran while one was open for 4% -> 8% of each run, Pallas kernels for 2% -> 2%
where the time goes in v9:
time: 122 us; the launch traced here: 121 us
  waiting for transfers between devices  48.5 us (40%)
  starting transfers between devices  38.3 us (31%)
  Pallas kernels  23.2 us (19%)
  matrix products  5.42 us (4%)
  local copies, waits for them, and re-layouts  2.89 us (2%)
  other arithmetic  1.82 us (1%)
    ppermute x10, waiting for transfers between devices, swapped(): return lax.ppermute(value, ('row', 'col'), pairs)  19.3 us
    pallas_call x1, Pallas kernels, body(): pl.pallas_call(main_kernel, out_shape=(hbm(2, rows, cols), vmem(2, side,...  18.6 us
    ppermute x5, waiting for transfers between devices, flipped(): return lax.ppermute(value, ('row', 'col'), pairs)  17.6 us
    ppermute x7, starting transfers between devices, shifted(): return lax.ppermute(value, ('row', 'col'), pairs)  16.4 us
    ppermute x10, starting transfers between devices, swapped(): return lax.ppermute(value, ('row', 'col'), pairs)  12.8 us
    ppermute x7, waiting for transfers between devices, shifted(): return lax.ppermute(value, ('row', 'col'), pairs)  11.7 us
    ppermute x5, starting transfers between devices, flipped(): return lax.ppermute(value, ('row', 'col'), pairs)  9.06 us
    dot_general x1, matrix products, evens_first(): return jnp.einsum('sac,dc->sad', rows, pick, precision=lax.Precision.HIGH)  3.44 us
  transfers between devices with their start and end apart: 22, of which 14 were waited for; matrix products, arithmetic and copies ran while one was open for 8% of the time, Pallas kernels for 2%

profile of v9, /device:TPU:0, one launch (start us, length us, event | category | flops | bytes accessed | tf_op | source)
XLA Modules:
  0.0 121.0 jit_solution(3310981276498798549)
XLA Ops:
  0.6 0.0 copy-start
  0.6 0.9 copy.25.spots_ref
  1.5 5.0 %collective-permute-start = (s32[6,2]{1,0:T(8,128)S(1)}, s32[6,2]{1,0:T(8,128)S(1)}, u32[]{:S(2)}, u32[]{:S(2)}) collective-permute-start(s32[6,2]{1,0:T(8,128)S(1)} %copy.25.spots_ref), channel_id=1, source_target_pairs={{0,1},{1,2},{2,3},{4,5},{5,6},{6,7},{8,9},{9,10},{10,11},{12,13},{... | collective-permute-start | bytes 152 | tf_op jit(solution)/shard_map/ppermute | solution.py:24
  6.6 1.3 %collective-permute-start.3 = (f32[2,256,512]{2,1,0:T(8,128)}, f32[2,256,512]{2,1,0:T(8,128)S(1)}, u32[]{:S(2)}, u32[]{:S(2)}) collective-permute-start(f32[2,256,512]{2,1,0:T(8,128)} %tile_ref.1), channel_id=1, source_target_pairs={{4,0},{5,1},{6,2},{7,3},{8,4},{9,5},{10,6},{11,7},{12,8},{13,9},{1... | collective-permute-start | bytes 3145736 | tf_op jit(solution)/shard_map/ppermute | solution.py:24
  7.9 1.9 %slice.50 = f32[2,256,256]{2,1,0:T(8,128)} slice(f32[2,256,512]{2,1,0:T(8,128)} %tile_ref.1), slice={[0:2], [0:256], [0:256]} | slice | bytes 1048576 | tf_op jit(solution)/shard_map/slice | solution.py:398
  9.8 1.3 %collective-permute-start.1 = (f32[2,256,256]{2,1,0:T(8,128)}, f32[2,256,256]{2,1,0:T(8,128)S(1)}, u32[]{:S(2)}, u32[]{:S(2)}) collective-permute-start(f32[2,256,256]{2,1,0:T(8,128)} %slice.50), channel_id=1, source_target_pairs={{1,0},{2,1},{3,2},{5,4},{6,5},{7,6},{9,8},{10,9},{11,10},{13,12},{... | collective-permute-start | bytes 1572872 | tf_op jit(solution)/shard_map/ppermute | solution.py:24
  11.0 1.7 %add_reduce_fusion.lit_ref = f32[256,256]{1,0:T(8,128)S(1)} fusion(f32[2,4,256,256]{3,2,1,0:T(8,128)} %probe_ref.1), kind=kLoop, calls=%fused_computation.4 | loop fusion | flops 983040 | bytes 2359296 | tf_op jit(solution)/shard_map/reduce_sum | solution.py:402
  12.8 0.0 copy-start.5
  12.8 2.0 %fusion.2 = f32[256,6,256]{2,0,1:T(8,128)} fusion(f32[256,256,1]{1,0,2:T(8,128)S(1)} %copy-done.4, f32[1,1,6,256,256]{4,3,2,1,0:T(8,128)S(1)} %copy-done), kind=kOutput, calls=%fused_computation.2 | convolution fusion | flops 603979776 | bytes 3407872 | tf_op jit(solution)/shard_map/ab,sbc->sac/dot_general | solution.py:91
  14.8 3.0 %collective-permute-start.2 = (s32[12,2]{1,0:T(8,128)S(1)}, s32[12,2]{1,0:T(8,128)S(1)}, u32[]{:S(2)}, u32[]{:S(2)}) collective-permute-start(s32[12,2]{1,0:T(8,128)S(1)} %pad_add_fusion), channel_id=1, source_target_pairs={{0,4},{1,5},{2,6},{3,7},{4,8},{5,9},{6,10},{7,11},{8,12},{9,13},{1... | collective-permute-start | bytes 296 | tf_op jit(solution)/shard_map/ppermute | solution.py:24
  17.8 0.1 copy.24.counts_ref
  17.9 0.7 collective-permute-done.2
  18.6 7.9 %collective-permute-done.1.right_any = f32[2,256,256]{2,1,0:T(8,128)S(1)} collective-permute-done((f32[2,256,256]{2,1,0:T(8,128)}, f32[2,256,256]{2,1,0:T(8,128)S(1)}, u32[]{:S(2)}, u32[]{:S(2)}) %collective-permute-start.1) | collective-permute-done | bytes 524320 | tf_op jit(solution)/shard_map/ppermute | solution.py:24
  26.5 1.3 %collective-permute-start.4 = (f32[2,256,256]{2,1,0:T(8,128)S(1)}, f32[2,256,256]{2,1,0:T(8,128)S(1)}, u32[]{:S(2)}, u32[]{:S(2)}) collective-permute-start(f32[2,256,256]{2,1,0:T(8,128)S(1)} %collective-permute-done.1.right_any), channel_id=1, source_target_pairs={{4,0},{5,1},{6,2},{7,3},{8,4},{9,5},{10,6},{11,7},{12,8},{13,9},{1... | collective-permute-start | bytes 1572872 | tf_op jit(solution)/shard_map/ppermute | solution.py:24
  27.8 3.4 %fusion.amp_hbm = f32[6,256,256]{2,1,0:T(8,128)} fusion(f32[256,256,1]{1,0,2:T(8,128)} %constant.10, f32[256,6,256]{2,0,1:T(8,128)} %fusion.2), kind=kOutput, calls=%fused_computation | convolution fusion | flops 603979776 | bytes 3407872 | tf_op jit(solution)/shard_map/sac,dc->sad/dot_general | solution.py:92
  31.2 2.1 %lighting.1 = (f32[256,512]{1,0:T(8,128)S(1)}, f32[8,256]{1,0:T(8,128)S(1)}) custom-call(s32[8,4]{1,0:T(8,128)S(1)} %copy.24.counts_ref, s32[6,2]{1,0:T(8,128)S(1)} %copy.25.spots_ref, s32[6,2]{1,0:T(8,128)S(1)} %collective-permute-done.left_ref, s32[6,2]{1,0:T(8,128)S(1)} %get-tuple-element.65.up_ref, s32[6,2]{1,0:T(8,128)S(1)} %get-tuple-element.64.diag_ref, ...), custom_call_target="tpu_custom_call" | custom-call | flops 100000000 | bytes 10000000 | tf_op jit(solution)/shard_map/lighting/pallas_call | solution.py:406
  33.4 0.0 collective-permute-done.4.corner_any
  33.4 0.0 collective-permute-done.3.below_any
  33.4 18.6 %positions.1 = (f32[2,256,512]{2,1,0:T(8,128)}, f32[2,256,768]{2,1,0:T(8,128)S(1)}, f32[2,256,256]{2,1,0:T(8,128)S(1)}, f32[1152,256]{1,0:T(8,128)S(1)}, f32[1152,256]{1,0:T(8,128)S(1)}) custom-call(s32[8,4]{1,0:T(8,128)S(1)} %copy.24.counts_ref, s32[6,2]{1,0:T(8,128)S(1)} %copy.25.spots_ref, f32[2,256,512]{2,1,0:T(8,128)} %tile_ref.1, ...), custom_call_target="tpu_custom_call" | custom-call | flops 7000000000 | bytes 20000000 | tf_op jit(solution)/shard_map/positions/pallas_call | solution.py:419
  51.9 3.8 %collective-permute-start.5 = (f32[1152,256]{1,0:T(8,128)S(1)}, f32[1152,256]{1,0:T(8,128)S(1)}, u32[]{:S(2)}, u32[]{:S(2)}) collective-permute-start(f32[1152,256]{1,0:T(8,128)S(1)} %get-tuple-element.40), channel_id=1, source_target_pairs={{0,4},{1,5},{2,6},{3,7},{4,0},{5,1},{6,2},{7,3},{8,12},{9,13},{10,... | collective-permute-start | bytes 3538952 | tf_op jit(solution)/shard_map/ppermute | solution.py:30
  55.8 2.5 %collective-permute-done.5.refs_1_ = f32[1152,256]{1,0:T(8,128)S(1)} collective-permute-done((f32[1152,256]{1,0:T(8,128)S(1)}, f32[1152,256]{1,0:T(8,128)S(1)}, u32[]{:S(2)}, u32[]{:S(2)}) %collective-permute-start.5) | collective-permute-done | bytes 1179680 | tf_op jit(solution)/shard_map/ppermute | solution.py:30
  58.2 0.2 fold.4
  58.4 3.2 %collective-permute-start.6 = (f32[576,256]{1,0:T(8,128)S(1)}, f32[576,256]{1,0:T(8,128)S(1)}, u32[]{:S(2)}, u32[]{:S(2)}) collective-permute-start(f32[576,256]{1,0:T(8,128)S(1)} %get-tuple-element.42), channel_id=1, source_target_pairs={{0,8},{1,9},{2,10},{3,11},{4,20},{5,21},{6,22},{7,23},{8,0},{9,1},... | collective-permute-start | bytes 1769480 | tf_op jit(solution)/shard_map/ppermute | solution.py:71
  61.6 7.9 %collective-permute-done.6.refs_1_ = f32[576,256]{1,0:T(8,128)S(1)} collective-permute-done((f32[576,256]{1,0:T(8,128)S(1)}, f32[576,256]{1,0:T(8,128)S(1)}, u32[]{:S(2)}, u32[]{:S(2)}) %collective-permute-start.6) | collective-permute-done | bytes 589856 | tf_op jit(solution)/shard_map/ppermute | solution.py:71
  69.4 0.1 fold.5
  69.5 1.6 %collective-permute-start.7 = (f32[288,256]{1,0:T(8,128)S(1)}, f32[288,256]{1,0:T(8,128)S(1)}, u32[]{:S(2)}, u32[]{:S(2)}) collective-permute-start(f32[288,256]{1,0:T(8,128)S(1)} %get-tuple-element.44), channel_id=1, source_target_pairs={{0,16},{1,17},{2,18},{3,19},{4,12},{5,13},{6,14},{7,15},{8,24},{9,... | collective-permute-start | bytes 884744 | tf_op jit(solution)/shard_map/ppermute | solution.py:71
  71.1 5.2 %collective-permute-done.7.refs_1_ = f32[288,256]{1,0:T(8,128)S(1)} collective-permute-done((f32[288,256]{1,0:T(8,128)S(1)}, f32[288,256]{1,0:T(8,128)S(1)}, u32[]{:S(2)}, u32[]{:S(2)}) %collective-permute-start.7) | collective-permute-done | bytes 294944 | tf_op jit(solution)/shard_map/ppermute | solution.py:71
  76.3 1.7 %collective-permute-start.13 = (f32[2,256,768]{2,1,0:T(8,128)S(1)}, f32[2,256,768]{2,1,0:T(8,128)S(1)}, u32[]{:S(2)}, u32[]{:S(2)}) collective-permute-start(f32[2,256,768]{2,1,0:T(8,128)S(1)} %get-tuple-element.54), channel_id=1, source_target_pairs={{0,4},{1,5},{2,6},{3,7},{4,8},{5,9},{6,10},{7,11},{8,12},{9,13},{1... | collective-permute-start | bytes 4718600 | tf_op jit(solution)/shard_map/ppermute | solution.py:24
  78.0 0.1 collective-permute-start.8
  78.1 5.2 %collective-permute-done.8.refs_1_ = f32[152,256]{1,0:T(8,128)S(1)} collective-permute-done((f32[152,256]{1,0:T(8,128)S(1)}, f32[152,256]{1,0:T(8,128)S(1)}, u32[]{:S(2)}, u32[]{:S(2)}) %collective-permute-start.8) | collective-permute-done | bytes 155680 | tf_op jit(solution)/shard_map/ppermute | solution.py:30
  83.3 4.8 %collective-permute-start.9 = (f32[80,256]{1,0:T(8,128)S(1)}, f32[80,256]{1,0:T(8,128)S(1)}, u32[]{:S(2)}, u32[]{:S(2)}) collective-permute-start(f32[80,256]{1,0:T(8,128)S(1)} %get-tuple-element.52), channel_id=1, source_target_pairs={{0,2},{1,3},{2,0},{3,1},{4,6},{5,7},{6,4},{7,5},{8,10},{9,11},{10,... | collective-permute-start | bytes 245768 | tf_op jit(solution)/shard_map/ppermute | solution.py:30
  88.1 4.4 %collective-permute-done.9 = f32[80,256]{1,0:T(8,128)S(1)} collective-permute-done((f32[80,256]{1,0:T(8,128)S(1)}, f32[80,256]{1,0:T(8,128)S(1)}, u32[]{:S(2)}, u32[]{:S(2)}) %collective-permute-start.9) | collective-permute-done | bytes 81952 | tf_op jit(solution)/shard_map/ppermute | solution.py:30
  92.5 1.5 %collective-permute-start.10 = (f32[72,256]{1,0:T(8,128)S(1)}, f32[72,256]{1,0:T(8,128)S(1)}, u32[]{:S(2)}, u32[]{:S(2)}) collective-permute-start(f32[72,256]{1,0:T(8,128)S(1)} %get-tuple-element.63), channel_id=1, source_target_pairs={{0,2},{1,3},{2,0},{3,1},{4,6},{5,7},{6,4},{7,5},{8,10},{9,11},{10,... | collective-permute-start | bytes 221192 | tf_op jit(solution)/shard_map/ppermute | solution.py:30
  94.0 2.0 %collective-permute-start.11 = (f32[72,256]{1,0:T(8,128)S(1)}, f32[72,256]{1,0:T(8,128)S(1)}, u32[]{:S(2)}, u32[]{:S(2)}) collective-permute-start(f32[72,256]{1,0:T(8,128)S(1)} %get-tuple-element.63), channel_id=1, source_target_pairs={{0,1},{1,0},{2,3},{3,2},{4,5},{5,4},{6,7},{7,6},{8,9},{9,8},{10,11... | collective-permute-start | bytes 221192 | tf_op jit(solution)/shard_map/ppermute | solution.py:30
  96.1 3.6 %collective-permute-done.10 = f32[72,256]{1,0:T(8,128)S(1)} collective-permute-done((f32[72,256]{1,0:T(8,128)S(1)}, f32[72,256]{1,0:T(8,128)S(1)}, u32[]{:S(2)}, u32[]{:S(2)}) %collective-permute-start.10) | collective-permute-done | bytes 73760 | tf_op jit(solution)/shard_map/ppermute | solution.py:30
  99.7 2.0 %collective-permute-done.11 = f32[72,256]{1,0:T(8,128)S(1)} collective-permute-done((f32[72,256]{1,0:T(8,128)S(1)}, f32[72,256]{1,0:T(8,128)S(1)}, u32[]{:S(2)}, u32[]{:S(2)}) %collective-permute-start.11) | collective-permute-done | bytes 73760 | tf_op jit(solution)/shard_map/ppermute | solution.py:30
  101.7 0.1 slice_add_fusion
  101.8 2.3 %collective-permute-start.14 = (f32[296,256]{1,0:T(8,128)S(1)}, f32[296,256]{1,0:T(8,128)S(1)}, u32[]{:S(2)}, u32[]{:S(2)}) collective-permute-start(f32[296,256]{1,0:T(8,128)S(1)} %constant_dynamic-update-slice_fusion.refs_0_), channel_id=1, source_target_pairs={{0,16},{1,17},{2,18},{3,19},{4,12},{5,13},{6,14},{7,15},{8,24},{9,... | collective-permute-start | bytes 909320 | tf_op jit(solution)/shard_map/ppermute | solution.py:71
  104.1 2.9 %collective-permute-start.17 = (f32[2,256,256]{2,1,0:T(8,128)S(1)}, f32[2,256,256]{2,1,0:T(8,128)S(1)}, u32[]{:S(2)}, u32[]{:S(2)}) collective-permute-start(f32[2,256,256]{2,1,0:T(8,128)S(1)} %slice_add_fusion), channel_id=1, source_target_pairs={{0,1},{1,2},{2,3},{4,5},{5,6},{6,7},{8,9},{9,10},{10,11},{12,13},{... | collective-permute-start | bytes 1572872 | tf_op jit(solution)/shard_map/ppermute | solution.py:24
  107.0 0.1 collective-permute-start.15
  107.1 3.1 %collective-permute-done.14.refs_1_ = f32[296,256]{1,0:T(8,128)S(1)} collective-permute-done((f32[296,256]{1,0:T(8,128)S(1)}, f32[296,256]{1,0:T(8,128)S(1)}, u32[]{:S(2)}, u32[]{:S(2)}) %collective-permute-start.14) | collective-permute-done | bytes 303136 | tf_op jit(solution)/shard_map/ppermute | solution.py:71
  110.2 1.9 %collective-permute-start.16 = (f32[296,256]{1,0:T(8,128)S(1)}, f32[296,256]{1,0:T(8,128)S(1)}, u32[]{:S(2)}, u32[]{:S(2)}) collective-permute-start(f32[296,256]{1,0:T(8,128)S(1)} %collective-permute-done.14.refs_1_), channel_id=1, source_target_pairs={{0,8},{1,9},{2,10},{3,11},{4,20},{5,21},{6,22},{7,23},{8,0},{9,1},... | collective-permute-start | bytes 909320 | tf_op jit(solution)/shard_map/ppermute | solution.py:71
  112.1 0.5 collective-permute-start.19
  112.6 1.3 %collective-permute-done.15.refs_2_ = f32[296,256]{1,0:T(8,128)S(1)} collective-permute-done((f32[296,256]{1,0:T(8,128)S(1)}, f32[296,256]{1,0:T(8,128)S(1)}, u32[]{:S(2)}, u32[]{:S(2)}) %collective-permute-start.15) | collective-permute-done | bytes 303136 | tf_op jit(solution)/shard_map/ppermute | solution.py:71
  113.9 3.1 %collective-permute-done.17.g_left = f32[2,256,256]{2,1,0:T(8,128)S(1)} collective-permute-done((f32[2,256,256]{2,1,0:T(8,128)S(1)}, f32[2,256,256]{2,1,0:T(8,128)S(1)}, u32[]{:S(2)}, u32[]{:S(2)}) %collective-permute-start.17) | collective-permute-done | bytes 524320 | tf_op jit(solution)/shard_map/ppermute | solution.py:24
  117.0 0.1 collective-permute-done.16.refs_3_
  117.2 1.6 %collective-permute-done.21.refs_7_ = f32[296,256]{1,0:T(8,128)S(1)} collective-permute-done((f32[296,256]{1,0:T(8,128)S(1)}, f32[296,256]{1,0:T(8,128)S(1)}, u32[]{:S(2)}, u32[]{:S(2)}) %collective-permute-start.21) | collective-permute-done | bytes 303136 | tf_op jit(solution)/shard_map/ppermute | solution.py:30
  118.8 2.3 %update.1 = (f32[2,256,512]{2,1,0:T(8,128)}, f32[2,4,256,256]{3,2,1,0:T(8,128)}) custom-call(f32[2,256,512]{2,1,0:T(8,128)S(1)} %copy-done.2, f32[256,512]{1,0:T(8,128)S(1)} %get-tuple-element.34.light_ref, f32[8,256]{1,0:T(8,128)S(1)} %slice_maximum_fusion.top_ref, f32[2,256,512]{2,1,0:T(8,128)S(1)} %copy-done.3, ...), custom_call_target="tpu_custom_call" | custom-call | flops 1000000 | bytes 10000000 | tf_op jit(solution)/shard_map/update/pallas_call | solution.py:472
  (30 shorter events, 0.2 us)
Async XLA Ops:
  0.6 12.1 %copy-start = (f32[1,1,6,256,256]{4,3,2,1,0:T(8,128)S(1)}, f32[1,1,6,256,256]{4,3,2,1,0:T(8,128)}, u32[]{:S(2)}) copy-start(f32[1,1,6,256,256]{4,3,2,1,0:T(8,128)} %param.9) | copy-start | bytes 4718596
  1.5 11.2 %copy-start.4 = (f32[256,256,1]{1,0,2:T(8,128)S(1)}, f32[256,256,1]{1,0,2:T(8,128)}, u32[]{:S(2)}) copy-start(f32[256,256,1]{1,0,2:T(8,128)} %constant.10) | copy-start | bytes 786436
  1.5 13.2 %collective-permute-start = (s32[6,2]{1,0:T(8,128)S(1)}, s32[6,2]{1,0:T(8,128)S(1)}, u32[]{:S(2)}, u32[]{:S(2)}) collective-permute-start(s32[6,2]{1,0:T(8,128)S(1)} %copy.25.spots_ref), channel_id=1, source_target_pairs={{0,1},{1,2},{2,3},{4,5},{5,6},{6,7},{8,9},{9,10},{10,11},{12,13},{... | collective-permute-start | bytes 152 | tf_op jit(solution)/shard_map/ppermute | solution.py:24
  6.6 26.8 %collective-permute-start.3 = (f32[2,256,512]{2,1,0:T(8,128)}, f32[2,256,512]{2,1,0:T(8,128)S(1)}, u32[]{:S(2)}, u32[]{:S(2)}) collective-permute-start(f32[2,256,512]{2,1,0:T(8,128)} %tile_ref.1), channel_id=1, source_target_pairs={{4,0},{5,1},{6,2},{7,3},{8,4},{9,5},{10,6},{11,7},{12,8},{13,9},{1... | collective-permute-start | bytes 3145736 | tf_op jit(solution)/shard_map/ppermute | solution.py:24
  9.8 16.7 %collective-permute-start.1 = (f32[2,256,256]{2,1,0:T(8,128)}, f32[2,256,256]{2,1,0:T(8,128)S(1)}, u32[]{:S(2)}, u32[]{:S(2)}) collective-permute-start(f32[2,256,256]{2,1,0:T(8,128)} %slice.50), channel_id=1, source_target_pairs={{1,0},{2,1},{3,2},{5,4},{6,5},{7,6},{9,8},{10,9},{11,10},{13,12},{... | collective-permute-start | bytes 1572872 | tf_op jit(solution)/shard_map/ppermute | solution.py:24
  12.8 5.0 %copy-start.5 = (s32[8,4]{0,1:T(4,128)S(1)}, s32[8,4]{0,1:T(4,128)}, u32[]{:S(2)}) copy-start(s32[8,4]{0,1:T(4,128)} %param.11) | copy-start | bytes 388
  14.8 3.9 %collective-permute-start.2 = (s32[12,2]{1,0:T(8,128)S(1)}, s32[12,2]{1,0:T(8,128)S(1)}, u32[]{:S(2)}, u32[]{:S(2)}) collective-permute-start(s32[12,2]{1,0:T(8,128)S(1)} %pad_add_fusion), channel_id=1, source_target_pairs={{0,4},{1,5},{2,6},{3,7},{4,8},{5,9},{6,10},{7,11},{8,12},{9,13},{1... | collective-permute-start | bytes 296 | tf_op jit(solution)/shard_map/ppermute | solution.py:24
  26.5 6.9 %collective-permute-start.4 = (f32[2,256,256]{2,1,0:T(8,128)S(1)}, f32[2,256,256]{2,1,0:T(8,128)S(1)}, u32[]{:S(2)}, u32[]{:S(2)}) collective-permute-start(f32[2,256,256]{2,1,0:T(8,128)S(1)} %collective-permute-done.1.right_any), channel_id=1, source_target_pairs={{4,0},{5,1},{6,2},{7,3},{8,4},{9,5},{10,6},{11,7},{12,8},{13,9},{1... | collective-permute-start | bytes 1572872 | tf_op jit(solution)/shard_map/ppermute | solution.py:24
  51.9 6.3 %collective-permute-start.5 = (f32[1152,256]{1,0:T(8,128)S(1)}, f32[1152,256]{1,0:T(8,128)S(1)}, u32[]{:S(2)}, u32[]{:S(2)}) collective-permute-start(f32[1152,256]{1,0:T(8,128)S(1)} %get-tuple-element.40), channel_id=1, source_target_pairs={{0,4},{1,5},{2,6},{3,7},{4,0},{5,1},{6,2},{7,3},{8,12},{9,13},{10,... | collective-permute-start | bytes 3538952 | tf_op jit(solution)/shard_map/ppermute | solution.py:30
  58.4 11.0 %collective-permute-start.6 = (f32[576,256]{1,0:T(8,128)S(1)}, f32[576,256]{1,0:T(8,128)S(1)}, u32[]{:S(2)}, u32[]{:S(2)}) collective-permute-start(f32[576,256]{1,0:T(8,128)S(1)} %get-tuple-element.42), channel_id=1, source_target_pairs={{0,8},{1,9},{2,10},{3,11},{4,20},{5,21},{6,22},{7,23},{8,0},{9,1},... | collective-permute-start | bytes 1769480 | tf_op jit(solution)/shard_map/ppermute | solution.py:71
  69.4 49.3 %copy-start.3 = (f32[2,256,512]{2,1,0:T(8,128)S(1)}, f32[2,256,512]{2,1,0:T(8,128)}, u32[]{:S(2)}) copy-start(f32[2,256,512]{2,1,0:T(8,128)} %get-tuple-element.59.g_tile) | copy-start | bytes 3145732
  69.5 6.8 %collective-permute-start.7 = (f32[288,256]{1,0:T(8,128)S(1)}, f32[288,256]{1,0:T(8,128)S(1)}, u32[]{:S(2)}, u32[]{:S(2)}) collective-permute-start(f32[288,256]{1,0:T(8,128)S(1)} %get-tuple-element.44), channel_id=1, source_target_pairs={{0,16},{1,17},{2,18},{3,19},{4,12},{5,13},{6,14},{7,15},{8,24},{9,... | collective-permute-start | bytes 884744 | tf_op jit(solution)/shard_map/ppermute | solution.py:71
  76.3 42.5 %copy-start.1 = (f32[2,4,256,256]{3,2,1,0:T(8,128)S(1)}, f32[2,4,256,256]{3,2,1,0:T(8,128)}, u32[]{:S(2)}) copy-start(f32[2,4,256,256]{3,2,1,0:T(8,128)} %probe_ref.1) | copy-start | bytes 6291460
  76.3 42.5 %copy-start.2 = (f32[2,256,512]{2,1,0:T(8,128)S(1)}, f32[2,256,512]{2,1,0:T(8,128)}, u32[]{:S(2)}) copy-start(f32[2,256,512]{2,1,0:T(8,128)} %tile_ref.1) | copy-start | bytes 3145732
  76.3 25.4 %collective-permute-start.13 = (f32[2,256,768]{2,1,0:T(8,128)S(1)}, f32[2,256,768]{2,1,0:T(8,128)S(1)}, u32[]{:S(2)}, u32[]{:S(2)}) collective-permute-start(f32[2,256,768]{2,1,0:T(8,128)S(1)} %get-tuple-element.54), channel_id=1, source_target_pairs={{0,4},{1,5},{2,6},{3,7},{4,8},{5,9},{6,10},{7,11},{8,12},{9,13},{1... | collective-permute-start | bytes 4718600 | tf_op jit(solution)/shard_map/ppermute | solution.py:24
  78.0 5.3 %collective-permute-start.8 = (f32[152,256]{1,0:T(8,128)S(1)}, f32[152,256]{1,0:T(8,128)S(1)}, u32[]{:S(2)}, u32[]{:S(2)}) collective-permute-start(f32[152,256]{1,0:T(8,128)S(1)} %get-tuple-element.49), channel_id=1, source_target_pairs={{0,1},{1,0},{2,3},{3,2},{4,5},{5,4},{6,7},{7,6},{8,9},{9,8},{10,11... | collective-permute-start | bytes 466952 | tf_op jit(solution)/shard_map/ppermute | solution.py:30
  83.3 9.2 %collective-permute-start.9 = (f32[80,256]{1,0:T(8,128)S(1)}, f32[80,256]{1,0:T(8,128)S(1)}, u32[]{:S(2)}, u32[]{:S(2)}) collective-permute-start(f32[80,256]{1,0:T(8,128)S(1)} %get-tuple-element.52), channel_id=1, source_target_pairs={{0,2},{1,3},{2,0},{3,1},{4,6},{5,7},{6,4},{7,5},{8,10},{9,11},{10,... | collective-permute-start | bytes 245768 | tf_op jit(solution)/shard_map/ppermute | solution.py:30
  92.5 7.2 %collective-permute-start.10 = (f32[72,256]{1,0:T(8,128)S(1)}, f32[72,256]{1,0:T(8,128)S(1)}, u32[]{:S(2)}, u32[]{:S(2)}) collective-permute-start(f32[72,256]{1,0:T(8,128)S(1)} %get-tuple-element.63), channel_id=1, source_target_pairs={{0,2},{1,3},{2,0},{3,1},{4,6},{5,7},{6,4},{7,5},{8,10},{9,11},{10,... | collective-permute-start | bytes 221192 | tf_op jit(solution)/shard_map/ppermute | solution.py:30
  94.0 7.7 %collective-permute-start.12 = (f32[72,256]{1,0:T(8,128)S(1)}, f32[72,256]{1,0:T(8,128)S(1)}, u32[]{:S(2)}, u32[]{:S(2)}) collective-permute-start(f32[72,256]{1,0:T(8,128)S(1)} %get-tuple-element.63), channel_id=1, source_target_pairs={{0,3},{1,2},{2,1},{3,0},{4,7},{5,6},{6,5},{7,4},{8,11},{9,10},{10,... | collective-permute-start | bytes 221192 | tf_op jit(solution)/shard_map/ppermute | solution.py:30
  94.0 7.6 %collective-permute-start.11 = (f32[72,256]{1,0:T(8,128)S(1)}, f32[72,256]{1,0:T(8,128)S(1)}, u32[]{:S(2)}, u32[]{:S(2)}) collective-permute-start(f32[72,256]{1,0:T(8,128)S(1)} %get-tuple-element.63), channel_id=1, source_target_pairs={{0,1},{1,0},{2,3},{3,2},{4,5},{5,4},{6,7},{7,6},{8,9},{9,8},{10,11... | collective-permute-start | bytes 221192 | tf_op jit(solution)/shard_map/ppermute | solution.py:30
  101.8 8.4 %collective-permute-start.14 = (f32[296,256]{1,0:T(8,128)S(1)}, f32[296,256]{1,0:T(8,128)S(1)}, u32[]{:S(2)}, u32[]{:S(2)}) collective-permute-start(f32[296,256]{1,0:T(8,128)S(1)} %constant_dynamic-update-slice_fusion.refs_0_), channel_id=1, source_target_pairs={{0,16},{1,17},{2,18},{3,19},{4,12},{5,13},{6,14},{7,15},{8,24},{9,... | collective-permute-start | bytes 909320 | tf_op jit(solution)/shard_map/ppermute | solution.py:71
  104.1 12.9 %collective-permute-start.17 = (f32[2,256,256]{2,1,0:T(8,128)S(1)}, f32[2,256,256]{2,1,0:T(8,128)S(1)}, u32[]{:S(2)}, u32[]{:S(2)}) collective-permute-start(f32[2,256,256]{2,1,0:T(8,128)S(1)} %slice_add_fusion), channel_id=1, source_target_pairs={{0,1},{1,2},{2,3},{4,5},{5,6},{6,7},{8,9},{9,10},{10,11},{12,13},{... | collective-permute-start | bytes 1572872 | tf_op jit(solution)/shard_map/ppermute | solution.py:24
  107.0 6.9 %collective-permute-start.15 = (f32[296,256]{1,0:T(8,128)S(1)}, f32[296,256]{1,0:T(8,128)S(1)}, u32[]{:S(2)}, u32[]{:S(2)}) collective-permute-start(f32[296,256]{1,0:T(8,128)S(1)} %constant_dynamic-update-slice_fusion.refs_0_), channel_id=1, source_target_pairs={{0,8},{1,9},{2,10},{3,11},{4,20},{5,21},{6,22},{7,23},{8,0},{9,1},... | collective-permute-start | bytes 909320 | tf_op jit(solution)/shard_map/ppermute | solution.py:71
  110.2 6.9 %collective-permute-start.16 = (f32[296,256]{1,0:T(8,128)S(1)}, f32[296,256]{1,0:T(8,128)S(1)}, u32[]{:S(2)}, u32[]{:S(2)}) collective-permute-start(f32[296,256]{1,0:T(8,128)S(1)} %collective-permute-done.14.refs_1_), channel_id=1, source_target_pairs={{0,8},{1,9},{2,10},{3,11},{4,20},{5,21},{6,22},{7,23},{8,0},{9,1},... | collective-permute-start | bytes 909320 | tf_op jit(solution)/shard_map/ppermute | solution.py:71
  112.1 5.0 %collective-permute-start.18 = (f32[296,256]{1,0:T(8,128)S(1)}, f32[296,256]{1,0:T(8,128)S(1)}, u32[]{:S(2)}, u32[]{:S(2)}) collective-permute-start(f32[296,256]{1,0:T(8,128)S(1)} %constant_dynamic-update-slice_fusion.refs_0_), channel_id=1, source_target_pairs={{0,4},{1,5},{2,6},{3,7},{4,0},{5,1},{6,2},{7,3},{8,12},{9,13},{10,... | collective-permute-start | bytes 909320 | tf_op jit(solution)/shard_map/ppermute | solution.py:30
  112.1 5.0 %collective-permute-start.19 = (f32[296,256]{1,0:T(8,128)S(1)}, f32[296,256]{1,0:T(8,128)S(1)}, u32[]{:S(2)}, u32[]{:S(2)}) collective-permute-start(f32[296,256]{1,0:T(8,128)S(1)} %collective-permute-done.14.refs_1_), channel_id=1, source_target_pairs={{0,4},{1,5},{2,6},{3,7},{4,0},{5,1},{6,2},{7,3},{8,12},{9,13},{10,... | collective-permute-start | bytes 909320 | tf_op jit(solution)/shard_map/ppermute | solution.py:30
  113.9 3.3 %collective-permute-start.20 = (f32[296,256]{1,0:T(8,128)S(1)}, f32[296,256]{1,0:T(8,128)S(1)}, u32[]{:S(2)}, u32[]{:S(2)}) collective-permute-start(f32[296,256]{1,0:T(8,128)S(1)} %collective-permute-done.15.refs_2_), channel_id=1, source_target_pairs={{0,4},{1,5},{2,6},{3,7},{4,0},{5,1},{6,2},{7,3},{8,12},{9,13},{10,... | collective-permute-start | bytes 909320 | tf_op jit(solution)/shard_map/ppermute | solution.py:30
  117.1 1.6 %collective-permute-start.21 = (f32[296,256]{1,0:T(8,128)S(1)}, f32[296,256]{1,0:T(8,128)S(1)}, u32[]{:S(2)}, u32[]{:S(2)}) collective-permute-start(f32[296,256]{1,0:T(8,128)S(1)} %collective-permute-done.16.refs_3_), channel_id=1, source_target_pairs={{0,4},{1,5},{2,6},{3,7},{4,0},{5,1},{6,2},{7,3},{8,12},{9,13},{10,... | collective-permute-start | bytes 909320 | tf_op jit(solution)/shard_map/ppermute | solution.py:30

commit v10 on v9

--- a/solution.py
+++ b/solution.py
@@ -84,12 +84,12 @@
     return jnp.asarray(np.stack(blocks + [block.T for block in blocks]), jnp.bfloat16)
 
 
-def evens_first(amplitudes):
+def evens_first(amplitudes, rows):
     side = amplitudes.shape[-1]
     order = np.concatenate([np.arange(0, side, 2), np.arange(1, side, 2)])
     pick = jnp.asarray(np.eye(side)[order], jnp.float32)
-    rows = jnp.einsum("ab,sbc->sac", pick, amplitudes, precision=lax.Precision.HIGH)
-    return jnp.einsum("sac,dc->sad", rows, pick, precision=lax.Precision.HIGH)
+    form = "ab,sbc->sac" if rows else "cb,sab->sac"
+    return jnp.einsum(form, pick, amplitudes, precision=lax.Precision.HIGH)
 
 
 def corner_of(row, col):
@@ -135,9 +135,13 @@
 
 def main_kernel(
     counts_ref, spots_ref, tile_hbm, below_any, right_any, corner_any, amp_hbm, probe_hbm, table_hbm,
-    g_tile, g_lower, g_right, mine_ref, other_ref,
-    ext, gacc, stage, turned, wave, wins, sums, amp_ref, probe_ref, table_ref, in_sem, amp_sem, out_sem,
+    g_tile, g_lower, g_right, *rest
 ):
+    chains = (len(rest) - 13) // 2
+    mine_refs, other_refs = rest[:chains], rest[chains:2 * chains]
+    (
+        ext, gacc, stage, turned, wave, wins, sums, amp_ref, probe_ref, table_ref, in_sem, amp_sem, out_sem,
+    ) = rest[2 * chains:]
     modes, side = probe_ref.shape[1], probe_ref.shape[2]
     rows, cols = tile_hbm.shape[1], tile_hbm.shape[2]
     low = side // 2
@@ -248,8 +252,12 @@
     store = pltpu.make_async_copy(gacc.at[:, pl.ds(0, rows), pl.ds(0, cols)], g_tile, out_sem.at[0])
     store.start()
     core = lax.rem(my_row, 2)
-    for ref, at in ((other_ref, 1 - core), (mine_ref, core)):
-        ref[...] = sums[pl.ds(pl.multiple_of(at * ref.shape[0], SUBLANES), ref.shape[0])]
+    half = sums.shape[0] // 2
+    for refs, at in ((other_refs, 1 - core), (mine_refs, core)):
+        start = 0
+        for ref in refs:
+            ref[...] = sums[pl.ds(pl.multiple_of(at * half + start, SUBLANES), ref.shape[0])]
+            start += ref.shape[0]
     g_lower[...] = gacc[:, rows:]
     g_right[...] = gacc[:, :rows, cols:]
     store.wait()
@@ -314,9 +322,10 @@
 
 
 def finish_kernel(parts, tile_ref, light_ref, top_ref, g_tile, g_left, g_up, probe_ref, *refs):
-    pairs, n_col = parts
-    block_refs = refs[:2 * pairs]
-    object_out, probe_out, new_object, new_probe, sums, sem = refs[2 * pairs:]
+    pairs, n_col, pieces = parts
+    count = 2 * pairs * len(pieces)
+    block_refs = refs[:count]
+    object_out, probe_out, new_object, new_probe, sums, sem = refs[count:]
     modes, side = probe_ref.shape[1], probe_ref.shape[2]
     rows, cols = light_ref.shape
     top = top_ref[0:1, 0:1]
@@ -331,16 +340,17 @@
     stores = [pltpu.make_async_copy(new_object, object_out, sem.at[0])]
     stores[0].start()
 
-    share = block_refs[0].shape[0] - SUBLANES
-    piece = share // n_col
     my_row = lax.axis_index("row")
     core, pair, col_rank = lax.rem(my_row, 2), my_row // 2, my_col_rank()
-    for i, ref in enumerate(block_refs):
-        flip, d = i // pairs, i % pairs
-        base = ((core ^ flip) * pairs + (plane_rank(core ^ flip, pair) ^ d)) * share
-        for e in range(n_col):
-            to = pl.multiple_of(base + (col_rank ^ e) * piece, SUBLANES)
-            sums[pl.ds(to, piece)] = ref[e * piece:(e + 1) * piece]
+    half, start = sums.shape[0] // 2, 0
+    for j, piece in enumerate(pieces):
+        for i in range(2 * pairs):
+            ref, flip, d = block_refs[j * 2 * pairs + i], i // pairs, i % pairs
+            base = (core ^ flip) * half + start + (plane_rank(core ^ flip, pair) ^ d) * (n_col * piece)
+            for e in range(n_col):
+                to = pl.multiple_of(base + (col_rank ^ e) * piece, SUBLANES)
+                sums[pl.ds(to, piece)] = ref[e * piece:(e + 1) * piece]
+        start += pairs * n_col * piece
     den = sums[2 * modes * side:(2 * modes + 1) * side]
     top = jnp.max(jnp.max(den, axis=0, keepdims=True), axis=1, keepdims=True)
     scale = 1.0 / (den + 0.1 * top)
@@ -391,18 +401,21 @@
     pairs, n_col = lax.axis_size("row") // 2, lax.axis_size("col")
     step = SUBLANES * 2 * pairs * n_col
     total_rows = -(-(2 * modes + 1) * side // step) * step
-    share = total_rows // (2 * pairs)
-    piece = share // n_col
+    piece = total_rows // (2 * pairs * n_col)
+    first = -(-piece // (2 * SUBLANES)) * SUBLANES
+    pieces = [first, piece - first] if piece > first else [piece]
     spots = corners[0, 0]
 
     right = shifted(object_field[:, :, :side], 0, -1)
-    below = shifted(object_field[:, :side, :], -1, 0)
-    from_left = shifted(spots, 0, 1)
+    lit = jnp.sum(probe[0] * probe[0] + probe[1] * probe[1], axis=0)
+    measured = evens_first(amplitudes[0, 0], True)
+    tile, measured, spots_now = lax.optimization_barrier((object_field, measured, spots))
+    below = shifted(tile[:, :side, :], -1, 0)
+    from_left = shifted(spots_now, 0, 1)
+    right, from_left, lit = lax.optimization_barrier((right, from_left, lit))
+    corner = shifted(right[:, :side, :], -1, 0)
     from_up = shifted(jnp.concatenate([spots, from_left], axis=0), 1, 0)
-    lit = jnp.sum(probe[0] * probe[0] + probe[1] * probe[1], axis=0)
-    right, from_up, lit = lax.optimization_barrier((right, from_up, lit))
-    corner = shifted(right[:, :side, :], -1, 0)
-    measured = evens_first(amplitudes[0, 0])
+    measured = evens_first(measured, False)
     light, top = pl.pallas_call(
         light_kernel,
         out_shape=(f32(rows, cols), f32(SUBLANES, side)),
@@ -416,14 +429,13 @@
         name="lighting",
     )(counts, spots, from_left, from_up[:slots], from_up[slots:], lit)
     corner, top, measured = lax.optimization_barrier((corner, top, measured))
-    g_tile, g_lower, g_right, mine, other = pl.pallas_call(
+    g_tile, g_lower, g_right, *halves = pl.pallas_call(
         main_kernel,
         out_shape=(
             hbm(2, rows, cols), vmem(2, side, cols + side), vmem(2, rows, side),
-            vmem(pairs * share, side), vmem(pairs * share, side),
-        ),
+        ) + tuple(vmem(pairs * n_col * piece, side) for piece in pieces) * 2,
         in_specs=[SM] * 2 + [HBM] + [ANY] * 3 + [HBM] * 3,
-        out_specs=(HBM,) + (VM,) * 4,
+        out_specs=(HBM,) + (VM,) * (2 + 2 * len(pieces)),
         scratch_shapes=[
             pltpu.VMEM((2, rows + side, cols + side), jnp.float32),
             pltpu.VMEM((2, rows + side, cols + side), jnp.float32),
@@ -444,33 +456,41 @@
         name="positions",
     )(counts, spots, in_hbm(object_field), below, right, corner, *map(in_hbm, (measured, probe, tables(side))))
 
-    arrived = swapped(other, 1, 0)
-    held, got = mine, arrived
+    chains = []
+    for i, piece in enumerate(pieces):
+        chains.append((halves[i], swapped(halves[len(pieces) + i], 1, 0), None if i else top))
     for i in range(plane_bits()):
-        send, held = fold(my_plane_rank, plane_bits() - 1 - i, held, got)
-        got = flipped(send, i)
+        for j, (held, got, ride) in enumerate(chains):
+            send, held = fold(my_plane_rank, plane_bits() - 1 - i, held, got)
+            chains[j] = (held, flipped(send, i), ride)
     for i in range(col_bits()):
-        send, held, top = fold(my_col_rank, col_bits() - 1 - i, held, got, top)
-        if i == 0:
-            send, g_lower = lax.optimization_barrier((send, g_lower))
-        got = swapped(send, 0, 1 << i)
+        for j, (held, got, ride) in enumerate(chains):
+            send, held, *ride = fold(my_col_rank, col_bits() - 1 - i, held, got, ride)
+            if i == 0 and j == 0:
+                send, g_lower = lax.optimization_barrier((send, g_lower))
+            chains[j] = (held, swapped(send, 0, 1 << i), ride[0] if ride else None)
     g_up = shifted(g_lower, 1, 0)
-    own = held + got[:piece]
-    top = jnp.maximum(top, got[piece:])
-    pieces = [own]
-    for e in range(1, n_col):
-        pieces.append(swapped(own, 0, rank_by(e, range(col_bits()))))
-    own = jnp.concatenate(pieces + [top], axis=0)
-    own, g_up, g_right = lax.optimization_barrier((own, g_up, g_right + g_up[:, :, cols:]))
+    owns = []
+    for piece, (held, got, ride) in zip(pieces, chains):
+        own = held + got[:piece]
+        parts = [own] + [swapped(own, 0, rank_by(e, range(col_bits()))) for e in range(1, n_col)]
+        if ride is not None:
+            parts.append(jnp.maximum(ride, got[piece:]))
+        owns.append(jnp.concatenate(parts, axis=0))
+    owns[0], g_up, g_right = lax.optimization_barrier((owns[0], g_up, g_right + g_up[:, :, cols:]))
     g_left = shifted(g_right, 0, 1)
-    blocks = [own]
-    for i in reversed(range(plane_bits())):
-        blocks = blocks + [flipped(block, i) for block in blocks]
-    blocks[-1], g_left = lax.optimization_barrier((blocks[-1], g_left))
-    blocks = blocks + [swapped(block, 1, 0) for block in blocks]
-    top = functools.reduce(jnp.maximum, [block[share:] for block in blocks])
+    gathered = []
+    for j, own in enumerate(owns):
+        blocks = [own]
+        for i in reversed(range(plane_bits())):
+            blocks = blocks + [flipped(block, i) for block in blocks]
+        if j == len(owns) - 1:
+            blocks[-1], g_left = lax.optimization_barrier((blocks[-1], g_left))
+        gathered.append(blocks + [swapped(block, 1, 0) for block in blocks])
+    top = functools.reduce(jnp.maximum, [block[n_col * pieces[0]:] for block in gathered[0]])
+    blocks = sum(gathered, [])
     return pl.pallas_call(
-        functools.partial(finish_kernel, (pairs, n_col)),
+        functools.partial(finish_kernel, (pairs, n_col, pieces)),
         out_shape=(f32(*object_field.shape), f32(*probe.shape)),
         in_specs=[VM] * (7 + len(blocks)),
         out_specs=(ANY, ANY),

time: 122 us -> 150 us (1.23); the launches traced: 121 us -> 151 us
  starting transfers between devices: 38.3 us -> 72.2 us
  Pallas kernels: 23.2 us -> 11.1 us
  waiting for transfers between devices: 48.5 us -> 56.4 us
    ppermute x5 -> x10, starting transfers between devices: 9.06 us -> 29.7 us  [flipped(): return lax.ppermute(value, ('row', 'col'), pairs)]
    ppermute x10 -> x20, starting transfers between devices: 12.8 us -> 26.3 us  [swapped(): return lax.ppermute(value, ('row', 'col'), pairs)]
    ppermute x5 -> x10, waiting for transfers between devices: 17.6 us -> 30 us  [flipped(): return lax.ppermute(value, ('row', 'col'), pairs)]
    pallas_call x1, Pallas kernels: 18.6 us -> 7.12 us  [body(): pl.pallas_call(main_kernel, out_shape=(hbm(2, rows, cols), vmem(2, side,...]
    ppermute x7, waiting for transfers between devices: 11.7 us -> 4.66 us  [shifted(): return lax.ppermute(value, ('row', 'col'), pairs)]
    ppermute x10 -> x20, waiting for transfers between devices: 19.3 us -> 21.8 us  [swapped(): return lax.ppermute(value, ('row', 'col'), pairs)]
  transfers between devices with their start and end apart: 22 -> 37, of which waited for: 14 -> 19; matrix products, arithmetic and copies ran while one was open for 8% -> 6% of each run, Pallas kernels for 2% -> 1%
where the time goes in v10:
time: 150 us; the launch traced here: 151 us
  starting transfers between devices  72.2 us (48%)
  waiting for transfers between devices  56.4 us (38%)
  Pallas kernels  11.1 us (7%)
  matrix products  5.84 us (4%)
  local copies, waits for them, and re-layouts  2.5 us (2%)
  other arithmetic  2.04 us (1%)
    ppermute x10, waiting for transfers between devices, flipped(): return lax.ppermute(value, ('row', 'col'), pairs)  30 us
    ppermute x10, starting transfers between devices, flipped(): return lax.ppermute(value, ('row', 'col'), pairs)  29.7 us
    ppermute x20, starting transfers between devices, swapped(): return lax.ppermute(value, ('row', 'col'), pairs)  26.3 us
    ppermute x20, waiting for transfers between devices, swapped(): return lax.ppermute(value, ('row', 'col'), pairs)  21.8 us
    ppermute x7, starting transfers between devices, shifted(): return lax.ppermute(value, ('row', 'col'), pairs)  16.2 us
    pallas_call x1, Pallas kernels, body(): pl.pallas_call(main_kernel, out_shape=(hbm(2, rows, cols), vmem(2, side,...  7.12 us
    dot_general x2, matrix products, evens_first(): return jnp.einsum(form, pick, amplitudes, precision=lax.Precision.HIGH)  5.84 us
    ppermute x7, waiting for transfers between devices, shifted(): return lax.ppermute(value, ('row', 'col'), pairs)  4.66 us
  transfers between devices with their start and end apart: 37, of which 19 were waited for; matrix products, arithmetic and copies ran while one was open for 6% of the time, Pallas kernels for 1%

profile of v10, /device:TPU:0, one launch (start us, length us, event | category | flops | bytes accessed | tf_op | source)
XLA Modules:
  0.0 151.0 jit_solution(1598991657173777051)
XLA Ops:
  0.6 2.0 %slice.50 = f32[2,256,256]{2,1,0:T(8,128)} slice(f32[2,256,512]{2,1,0:T(8,128)} %tile_ref.1), slice={[0:2], [0:256], [0:256]} | slice | bytes 1048576 | tf_op jit(solution)/shard_map/slice | solution.py:409
  2.6 1.4 collective-permute-start
  4.1 2.9 %fusion.2 = f32[6,256,256]{2,1,0:T(8,128)} fusion(f32[256,256,1]{1,0,2:T(8,128)} %constant.10, f32[1,1,6,256,256]{4,3,2,1,0:T(8,128)S(1)} %copy-done), kind=kOutput, calls=%fused_computation.2 | convolution fusion | flops 603979776 | bytes 3407872 | tf_op jit(solution)/shard_map/ab,sbc->sac/dot_general | solution.py:92
  7.0 1.3 collective-permute-start.3
  8.4 5.5 %collective-permute-start.1 = (s32[6,2]{1,0:T(8,128)S(1)}, s32[6,2]{1,0:T(8,128)S(1)}, u32[]{:S(2)}, u32[]{:S(2)}) collective-permute-start(s32[6,2]{1,0:T(8,128)S(1)} %copy.16), channel_id=1, source_target_pairs={{0,1},{1,2},{2,3},{4,5},{5,6},{6,7},{8,9},{9,10},{10,11},{12,13},{... | collective-permute-start | bytes 152 | tf_op jit(solution)/shard_map/ppermute | solution.py:24
  14.0 1.8 %add_reduce_fusion.lit_ref = f32[256,256]{1,0:T(8,128)S(1)} fusion(f32[2,4,256,256]{3,2,1,0:T(8,128)} %probe_ref.1), kind=kLoop, calls=%fused_computation.3 | loop fusion | flops 983040 | bytes 2359296 | tf_op jit(solution)/shard_map/reduce_sum | solution.py:410
  15.9 3.9 %collective-permute-done.right_any = f32[2,256,256]{2,1,0:T(8,128)S(1)} collective-permute-done((f32[2,256,256]{2,1,0:T(8,128)}, f32[2,256,256]{2,1,0:T(8,128)S(1)}, u32[]{:S(2)}, u32[]{:S(2)}) %collective-permute-start) | collective-permute-done | bytes 524320 | tf_op jit(solution)/shard_map/ppermute | solution.py:24
  19.8 1.3 collective-permute-start.4
  21.1 2.9 %fusion.6.amp_hbm = f32[6,256,256]{2,1,0:T(8,128)} fusion(f32[6,256,256]{2,1,0:T(8,128)S(1)} %copy-done.5, f32[256,256,1]{1,0,2:T(8,128)} %constant.10), kind=kOutput, calls=%fused_computation.22 | convolution fusion | flops 603979776 | bytes 3407872 | tf_op jit(solution)/shard_map/cb,sab->sac/dot_general | solution.py:92
  24.3 3.0 %collective-permute-start.2 = (s32[12,2]{1,0:T(8,128)S(1)}, s32[12,2]{1,0:T(8,128)S(1)}, u32[]{:S(2)}, u32[]{:S(2)}) collective-permute-start(s32[12,2]{1,0:T(8,128)S(1)} %copy.18), channel_id=1, source_target_pairs={{0,4},{1,5},{2,6},{3,7},{4,8},{5,9},{6,10},{7,11},{8,12},{9,13},{1... | collective-permute-start | bytes 296 | tf_op jit(solution)/shard_map/ppermute | solution.py:24
  27.4 0.7 collective-permute-done.2
  28.1 1.4 lighting.1
  29.6 7.1 %positions.1 = (f32[2,256,512]{2,1,0:T(8,128)}, f32[2,256,768]{2,1,0:T(8,128)S(1)}, f32[2,256,256]{2,1,0:T(8,128)S(1)}, f32[640,256]{1,0:T(8,128)S(1)}, f32[512,...) custom-call(s32[8,4]{1,0:T(8,128)S(1)} %copy.19.counts_ref, s32[6,2]{1,0:T(8,128)S(1)} %copy.20.spots_ref, ...), custom_call_target="tpu_custom_call" | custom-call | flops 7000000000 | bytes 20000000 | tf_op jit(solution)/shard_map/positions/pallas_call | solution.py:432
  36.7 4.6 %collective-permute-start.5 = (f32[640,256]{1,0:T(8,128)S(1)}, f32[640,256]{1,0:T(8,128)S(1)}, u32[]{:S(2)}, u32[]{:S(2)}) collective-permute-start(f32[640,256]{1,0:T(8,128)S(1)} %get-tuple-element.56), channel_id=1, source_target_pairs={{0,4},{1,5},{2,6},{3,7},{4,0},{5,1},{6,2},{7,3},{8,12},{9,13},{10,... | collective-permute-start | bytes 1966088 | tf_op jit(solution)/shard_map/ppermute | solution.py:30
  41.3 1.7 %collective-permute-done.5.refs_1_ = f32[640,256]{1,0:T(8,128)S(1)} collective-permute-done((f32[640,256]{1,0:T(8,128)S(1)}, f32[640,256]{1,0:T(8,128)S(1)}, u32[]{:S(2)}, u32[]{:S(2)}) %collective-permute-start.5) | collective-permute-done | bytes 655392 | tf_op jit(solution)/shard_map/ppermute | solution.py:30
  43.1 9.1 %collective-permute-start.6 = (f32[320,256]{1,0:T(8,128)S(1)}, f32[320,256]{1,0:T(8,128)S(1)}, u32[]{:S(2)}, u32[]{:S(2)}) collective-permute-start(f32[320,256]{1,0:T(8,128)S(1)} %get-tuple-element.58), channel_id=1, source_target_pairs={{0,8},{1,9},{2,10},{3,11},{4,20},{5,21},{6,22},{7,23},{8,0},{9,1},... | collective-permute-start | bytes 983048 | tf_op jit(solution)/shard_map/ppermute | solution.py:71
  52.2 5.1 %collective-permute-done.6.refs_1_ = f32[320,256]{1,0:T(8,128)S(1)} collective-permute-done((f32[320,256]{1,0:T(8,128)S(1)}, f32[320,256]{1,0:T(8,128)S(1)}, u32[]{:S(2)}, u32[]{:S(2)}) %collective-permute-start.6) | collective-permute-done | bytes 327712 | tf_op jit(solution)/shard_map/ppermute | solution.py:71
  57.3 8.2 %collective-permute-start.7 = (f32[160,256]{1,0:T(8,128)S(1)}, f32[160,256]{1,0:T(8,128)S(1)}, u32[]{:S(2)}, u32[]{:S(2)}) collective-permute-start(f32[160,256]{1,0:T(8,128)S(1)} %get-tuple-element.60), channel_id=1, source_target_pairs={{0,16},{1,17},{2,18},{3,19},{4,12},{5,13},{6,14},{7,15},{8,24},{9,... | collective-permute-start | bytes 491528 | tf_op jit(solution)/shard_map/ppermute | solution.py:71
  65.5 3.3 %collective-permute-done.7.refs_1_ = f32[160,256]{1,0:T(8,128)S(1)} collective-permute-done((f32[160,256]{1,0:T(8,128)S(1)}, f32[160,256]{1,0:T(8,128)S(1)}, u32[]{:S(2)}, u32[]{:S(2)}) %collective-permute-start.7) | collective-permute-done | bytes 163872 | tf_op jit(solution)/shard_map/ppermute | solution.py:71
  68.8 1.4 collective-permute-start.13
  70.3 2.6 %collective-permute-start.22 = (f32[256,256]{1,0:T(8,128)S(1)}, f32[256,256]{1,0:T(8,128)S(1)}, u32[]{:S(2)}, u32[]{:S(2)}) collective-permute-start(f32[256,256]{1,0:T(8,128)S(1)} %get-tuple-element.77), channel_id=1, source_target_pairs={{0,8},{1,9},{2,10},{3,11},{4,20},{5,21},{6,22},{7,23},{8,0},{9,1},... | collective-permute-start | bytes 786440 | tf_op jit(solution)/shard_map/ppermute | solution.py:71
  72.9 2.2 %collective-permute-start.8 = (f32[88,256]{1,0:T(8,128)S(1)}, f32[88,256]{1,0:T(8,128)S(1)}, u32[]{:S(2)}, u32[]{:S(2)}) collective-permute-start(f32[88,256]{1,0:T(8,128)S(1)} %get-tuple-element.65), channel_id=1, source_target_pairs={{0,1},{1,0},{2,3},{3,2},{4,5},{5,4},{6,7},{7,6},{8,9},{9,8},{10,11... | collective-permute-start | bytes 270344 | tf_op jit(solution)/shard_map/ppermute | solution.py:30
  75.1 2.8 %collective-permute-done.8.refs_1_ = f32[88,256]{1,0:T(8,128)S(1)} collective-permute-done((f32[88,256]{1,0:T(8,128)S(1)}, f32[88,256]{1,0:T(8,128)S(1)}, u32[]{:S(2)}, u32[]{:S(2)}) %collective-permute-start.8) | collective-permute-done | bytes 90144 | tf_op jit(solution)/shard_map/ppermute | solution.py:30
  78.0 2.8 %collective-permute-start.9 = (f32[48,256]{1,0:T(8,128)S(1)}, f32[48,256]{1,0:T(8,128)S(1)}, u32[]{:S(2)}, u32[]{:S(2)}) collective-permute-start(f32[48,256]{1,0:T(8,128)S(1)} %get-tuple-element.68), channel_id=1, source_target_pairs={{0,2},{1,3},{2,0},{3,1},{4,6},{5,7},{6,4},{7,5},{8,10},{9,11},{10,... | collective-permute-start | bytes 147464 | tf_op jit(solution)/shard_map/ppermute | solution.py:30
  80.8 2.2 %collective-permute-start.23 = (f32[128,256]{1,0:T(8,128)S(1)}, f32[128,256]{1,0:T(8,128)S(1)}, u32[]{:S(2)}, u32[]{:S(2)}) collective-permute-start(f32[128,256]{1,0:T(8,128)S(1)} %get-tuple-element.79), channel_id=1, source_target_pairs={{0,16},{1,17},{2,18},{3,19},{4,12},{5,13},{6,14},{7,15},{8,24},{9,... | collective-permute-start | bytes 393224 | tf_op jit(solution)/shard_map/ppermute | solution.py:71
  83.0 0.8 collective-permute-done.9
  83.8 2.5 %collective-permute-start.10 = (f32[40,256]{1,0:T(8,128)S(1)}, f32[40,256]{1,0:T(8,128)S(1)}, u32[]{:S(2)}, u32[]{:S(2)}) collective-permute-start(f32[40,256]{1,0:T(8,128)S(1)} %get-tuple-element.89), channel_id=1, source_target_pairs={{0,2},{1,3},{2,0},{3,1},{4,6},{5,7},{6,4},{7,5},{8,10},{9,11},{10,... | collective-permute-start | bytes 122888 | tf_op jit(solution)/shard_map/ppermute | solution.py:30
  86.4 9.3 %collective-permute-done.23.refs_1_ = f32[128,256]{1,0:T(8,128)S(1)} collective-permute-done((f32[128,256]{1,0:T(8,128)S(1)}, f32[128,256]{1,0:T(8,128)S(1)}, u32[]{:S(2)}, u32[]{:S(2)}) %collective-permute-start.23) | collective-permute-done | bytes 131104 | tf_op jit(solution)/shard_map/ppermute | solution.py:71
  95.7 0.9 collective-permute-start.24
  96.6 4.3 %collective-permute-start.12 = (f32[40,256]{1,0:T(8,128)S(1)}, f32[40,256]{1,0:T(8,128)S(1)}, u32[]{:S(2)}, u32[]{:S(2)}) collective-permute-start(f32[40,256]{1,0:T(8,128)S(1)} %get-tuple-element.89), channel_id=1, source_target_pairs={{0,3},{1,2},{2,1},{3,0},{4,7},{5,6},{6,5},{7,4},{8,11},{9,10},{10,... | collective-permute-start | bytes 122888 | tf_op jit(solution)/shard_map/ppermute | solution.py:30
  100.9 4.4 %collective-permute-done.11 = f32[40,256]{1,0:T(8,128)S(1)} collective-permute-done((f32[40,256]{1,0:T(8,128)S(1)}, f32[40,256]{1,0:T(8,128)S(1)}, u32[]{:S(2)}, u32[]{:S(2)}) %collective-permute-start.11) | collective-permute-done | bytes 40992 | tf_op jit(solution)/shard_map/ppermute | solution.py:30
  105.5 2.2 %collective-permute-start.31 = (f32[2,256,256]{2,1,0:T(8,128)S(1)}, f32[2,256,256]{2,1,0:T(8,128)S(1)}, u32[]{:S(2)}, u32[]{:S(2)}) collective-permute-start(f32[2,256,256]{2,1,0:T(8,128)S(1)} %slice_add_fusion), channel_id=1, source_target_pairs={{0,1},{1,2},{2,3},{4,5},{5,6},{6,7},{8,9},{9,10},{10,11},{12,13},{... | collective-permute-start | bytes 1572872 | tf_op jit(solution)/shard_map/ppermute | solution.py:24
  107.8 1.9 %collective-permute-start.25 = (f32[32,256]{1,0:T(8,128)S(1)}, f32[32,256]{1,0:T(8,128)S(1)}, u32[]{:S(2)}, u32[]{:S(2)}) collective-permute-start(f32[32,256]{1,0:T(8,128)S(1)} %get-tuple-element.83), channel_id=1, source_target_pairs={{0,2},{1,3},{2,0},{3,1},{4,6},{5,7},{6,4},{7,5},{8,10},{9,11},{10,... | collective-permute-start | bytes 98312 | tf_op jit(solution)/shard_map/ppermute | solution.py:30
  109.7 9.3 %collective-permute-done.25 = f32[32,256]{1,0:T(8,128)S(1)} collective-permute-done((f32[32,256]{1,0:T(8,128)S(1)}, f32[32,256]{1,0:T(8,128)S(1)}, u32[]{:S(2)}, u32[]{:S(2)}) %collective-permute-start.25) | collective-permute-done | bytes 32800 | tf_op jit(solution)/shard_map/ppermute | solution.py:30
  119.0 4.9 %collective-permute-start.28 = (f32[32,256]{1,0:T(8,128)S(1)}, f32[32,256]{1,0:T(8,128)S(1)}, u32[]{:S(2)}, u32[]{:S(2)}) collective-permute-start(f32[32,256]{1,0:T(8,128)S(1)} %add.16), channel_id=1, source_target_pairs={{0,3},{1,2},{2,1},{3,0},{4,7},{5,6},{6,5},{7,4},{8,11},{9,10},{10,... | collective-permute-start | bytes 98312 | tf_op jit(solution)/shard_map/ppermute | solution.py:30
  123.9 0.6 collective-permute-start.26
  124.5 2.5 %collective-permute-start.14 = (f32[168,256]{1,0:T(8,128)S(1)}, f32[168,256]{1,0:T(8,128)S(1)}, u32[]{:S(2)}, u32[]{:S(2)}) collective-permute-start(f32[168,256]{1,0:T(8,128)S(1)} %constant_dynamic-update-slice_fusion.refs_0_), channel_id=1, source_target_pairs={{0,16},{1,17},{2,18},{3,19},{4,12},{5,13},{6,14},{7,15},{8,24},{9,... | collective-permute-start | bytes 516104 | tf_op jit(solution)/shard_map/ppermute | solution.py:71
  127.0 0.8 collective-permute-done.27
  127.8 0.9 collective-permute-done.26
  128.7 3.1 %collective-permute-start.29 = (f32[128,256]{1,0:T(8,128)S(1)}, f32[128,256]{1,0:T(8,128)S(1)}, u32[]{:S(2)}, u32[]{:S(2)}) collective-permute-start(f32[128,256]{1,0:T(8,128)S(1)} %pad_maximum_fusion.refs_8_), channel_id=1, source_target_pairs={{0,16},{1,17},{2,18},{3,19},{4,12},{5,13},{6,14},{7,15},{8,24},{9,... | collective-permute-start | bytes 393224 | tf_op jit(solution)/shard_map/ppermute | solution.py:71
  131.8 2.0 %collective-permute-start.16 = (f32[168,256]{1,0:T(8,128)S(1)}, f32[168,256]{1,0:T(8,128)S(1)}, u32[]{:S(2)}, u32[]{:S(2)}) collective-permute-start(f32[168,256]{1,0:T(8,128)S(1)} %collective-permute-done.14.refs_1_), channel_id=1, source_target_pairs={{0,8},{1,9},{2,10},{3,11},{4,20},{5,21},{6,22},{7,23},{8,0},{9,1},... | collective-permute-start | bytes 516104 | tf_op jit(solution)/shard_map/ppermute | solution.py:71
  133.8 2.4 %collective-permute-done.29.refs_9_ = f32[128,256]{1,0:T(8,128)S(1)} collective-permute-done((f32[128,256]{1,0:T(8,128)S(1)}, f32[128,256]{1,0:T(8,128)S(1)}, u32[]{:S(2)}, u32[]{:S(2)}) %collective-permute-start.29) | collective-permute-done | bytes 131104 | tf_op jit(solution)/shard_map/ppermute | solution.py:71
  136.2 1.0 collective-permute-done.15.refs_2_
  137.2 4.0 %collective-permute-done.30.refs_11_ = f32[128,256]{1,0:T(8,128)S(1)} collective-permute-done((f32[128,256]{1,0:T(8,128)S(1)}, f32[128,256]{1,0:T(8,128)S(1)}, u32[]{:S(2)}, u32[]{:S(2)}) %collective-permute-start.30) | collective-permute-done | bytes 131104 | tf_op jit(solution)/shard_map/ppermute | solution.py:71
  141.7 5.0 %collective-permute-done.32.refs_10_ = f32[128,256]{1,0:T(8,128)S(1)} collective-permute-done((f32[128,256]{1,0:T(8,128)S(1)}, f32[128,256]{1,0:T(8,128)S(1)}, u32[]{:S(2)}, u32[]{:S(2)}) %collective-permute-start.32) | collective-permute-done | bytes 131104 | tf_op jit(solution)/shard_map/ppermute | solution.py:71
  146.7 0.5 collective-permute-start.34
  148.0 0.5 collective-permute-done.35.refs_14_
  148.7 2.3 %update.1 = (f32[2,256,512]{2,1,0:T(8,128)}, f32[2,4,256,256]{3,2,1,0:T(8,128)}) custom-call(f32[2,256,512]{2,1,0:T(8,128)S(1)} %copy-done.3, f32[256,512]{1,0:T(8,128)S(1)} %get-tuple-element.48.light_ref, f32[8,256]{1,0:T(8,128)S(1)} %slice_maximum_fusion.top_ref, f32[2,256,512]{2,1,0:T(8,128)S(1)} %copy-done.4, ...), custom_call_target="tpu_custom_call" | custom-call | flops 1000000 | bytes 10000000 | tf_op jit(solution)/shard_map/update/pallas_call | solution.py:492
  (73 shorter events, 2.6 us)
Async XLA Ops:
  0.6 3.4 %copy-start = (f32[1,1,6,256,256]{4,3,2,1,0:T(8,128)S(1)}, f32[1,1,6,256,256]{4,3,2,1,0:T(8,128)}, u32[]{:S(2)}) copy-start(f32[1,1,6,256,256]{4,3,2,1,0:T(8,128)} %param.10) | copy-start | bytes 4718596
  2.6 4.4 %copy-start.2 = (f32[2,256,512]{2,1,0:T(8,128)S(1)}, f32[2,256,512]{2,1,0:T(8,128)}, u32[]{:S(2)}) copy-start(f32[2,256,512]{2,1,0:T(8,128)} %tile_ref.1) | copy-start | bytes 3145732
  2.6 5.6 %copy-start.6 = (s32[1,1,6,2]{2,3,1,0:T(2,128)S(1)}, s32[1,1,6,2]{2,3,1,0:T(2,128)}, u32[]{:S(2)}) copy-start(s32[1,1,6,2]{2,3,1,0:T(2,128)} %param.11) | copy-start | bytes 148
  2.6 17.2 %collective-permute-start = (f32[2,256,256]{2,1,0:T(8,128)}, f32[2,256,256]{2,1,0:T(8,128)S(1)}, u32[]{:S(2)}, u32[]{:S(2)}) collective-permute-start(f32[2,256,256]{2,1,0:T(8,128)} %slice.50), channel_id=1, source_target_pairs={{1,0},{2,1},{3,2},{5,4},{6,5},{7,6},{9,8},{10,9},{11,10},{13,12},{... | collective-permute-start | bytes 1572872 | tf_op jit(solution)/shard_map/ppermute | solution.py:24
  7.0 22.6 %collective-permute-start.3 = (f32[2,256,512]{2,1,0:T(8,128)S(1)}, f32[2,256,512]{2,1,0:T(8,128)}, u32[]{:S(2)}, u32[]{:S(2)}) collective-permute-start(f32[2,256,512]{2,1,0:T(8,128)S(1)} %copy-done.2), channel_id=1, source_target_pairs={{4,0},{5,1},{6,2},{7,3},{8,4},{9,5},{10,6},{11,7},{12,8},{13,9},{1... | collective-permute-start | bytes 3145736 | tf_op jit(solution)/shard_map/ppermute | solution.py:24
  8.4 7.5 %collective-permute-start.1 = (s32[6,2]{1,0:T(8,128)S(1)}, s32[6,2]{1,0:T(8,128)S(1)}, u32[]{:S(2)}, u32[]{:S(2)}) collective-permute-start(s32[6,2]{1,0:T(8,128)S(1)} %copy.16), channel_id=1, source_target_pairs={{0,1},{1,2},{2,3},{4,5},{5,6},{6,7},{8,9},{9,10},{10,11},{12,13},{... | collective-permute-start | bytes 152 | tf_op jit(solution)/shard_map/ppermute | solution.py:24
  14.0 7.1 %copy-start.5 = (f32[6,256,256]{2,1,0:T(8,128)S(1)}, f32[6,256,256]{2,1,0:T(8,128)}, u32[]{:S(2)}) copy-start(f32[6,256,256]{2,1,0:T(8,128)} %fusion.2) | copy-start | bytes 4718596
  15.9 11.5 %copy-start.7 = (s32[8,4]{0,1:T(4,128)S(1)}, s32[8,4]{0,1:T(4,128)}, u32[]{:S(2)}) copy-start(s32[8,4]{0,1:T(4,128)} %param.12) | copy-start | bytes 388
  19.8 9.7 %collective-permute-start.4 = (f32[2,256,256]{2,1,0:T(8,128)S(1)}, f32[2,256,256]{2,1,0:T(8,128)}, u32[]{:S(2)}, u32[]{:S(2)}) collective-permute-start(f32[2,256,256]{2,1,0:T(8,128)S(1)} %collective-permute-done.right_any), channel_id=1, source_target_pairs={{4,0},{5,1},{6,2},{7,3},{8,4},{9,5},{10,6},{11,7},{12,8},{13,9},{1... | collective-permute-start | bytes 1572872 | tf_op jit(solution)/shard_map/ppermute | solution.py:24
  24.3 3.8 %collective-permute-start.2 = (s32[12,2]{1,0:T(8,128)S(1)}, s32[12,2]{1,0:T(8,128)S(1)}, u32[]{:S(2)}, u32[]{:S(2)}) collective-permute-start(s32[12,2]{1,0:T(8,128)S(1)} %copy.18), channel_id=1, source_target_pairs={{0,4},{1,5},{2,6},{3,7},{4,8},{5,9},{6,10},{7,11},{8,12},{9,13},{1... | collective-permute-start | bytes 296 | tf_op jit(solution)/shard_map/ppermute | solution.py:24
  36.7 6.3 %collective-permute-start.5 = (f32[640,256]{1,0:T(8,128)S(1)}, f32[640,256]{1,0:T(8,128)S(1)}, u32[]{:S(2)}, u32[]{:S(2)}) collective-permute-start(f32[640,256]{1,0:T(8,128)S(1)} %get-tuple-element.56), channel_id=1, source_target_pairs={{0,4},{1,5},{2,6},{3,7},{4,0},{5,1},{6,2},{7,3},{8,12},{9,13},{10,... | collective-permute-start | bytes 1966088 | tf_op jit(solution)/shard_map/ppermute | solution.py:30
  43.1 14.1 %collective-permute-start.6 = (f32[320,256]{1,0:T(8,128)S(1)}, f32[320,256]{1,0:T(8,128)S(1)}, u32[]{:S(2)}, u32[]{:S(2)}) collective-permute-start(f32[320,256]{1,0:T(8,128)S(1)} %get-tuple-element.58), channel_id=1, source_target_pairs={{0,8},{1,9},{2,10},{3,11},{4,20},{5,21},{6,22},{7,23},{8,0},{9,1},... | collective-permute-start | bytes 983048 | tf_op jit(solution)/shard_map/ppermute | solution.py:71
  57.3 11.5 %collective-permute-start.7 = (f32[160,256]{1,0:T(8,128)S(1)}, f32[160,256]{1,0:T(8,128)S(1)}, u32[]{:S(2)}, u32[]{:S(2)}) collective-permute-start(f32[160,256]{1,0:T(8,128)S(1)} %get-tuple-element.60), channel_id=1, source_target_pairs={{0,16},{1,17},{2,18},{3,19},{4,12},{5,13},{6,14},{7,15},{8,24},{9,... | collective-permute-start | bytes 491528 | tf_op jit(solution)/shard_map/ppermute | solution.py:71
  65.5 4.7 %collective-permute-start.21 = (f32[512,256]{1,0:T(8,128)S(1)}, f32[512,256]{1,0:T(8,128)S(1)}, u32[]{:S(2)}, u32[]{:S(2)}) collective-permute-start(f32[512,256]{1,0:T(8,128)S(1)} %get-tuple-element.75), channel_id=1, source_target_pairs={{0,4},{1,5},{2,6},{3,7},{4,0},{5,1},{6,2},{7,3},{8,12},{9,13},{10,... | collective-permute-start | bytes 1572872 | tf_op jit(solution)/shard_map/ppermute | solution.py:30
  68.8 36.6 %collective-permute-start.13 = (f32[2,256,768]{2,1,0:T(8,128)S(1)}, f32[2,256,768]{2,1,0:T(8,128)S(1)}, u32[]{:S(2)}, u32[]{:S(2)}) collective-permute-start(f32[2,256,768]{2,1,0:T(8,128)S(1)} %get-tuple-element.70), channel_id=1, source_target_pairs={{0,4},{1,5},{2,6},{3,7},{4,8},{5,9},{6,10},{7,11},{8,12},{9,13},{1... | collective-permute-start | bytes 4718600 | tf_op jit(solution)/shard_map/ppermute | solution.py:24
  70.2 78.5 %copy-start.4 = (f32[2,256,512]{2,1,0:T(8,128)S(1)}, f32[2,256,512]{2,1,0:T(8,128)}, u32[]{:S(2)}) copy-start(f32[2,256,512]{2,1,0:T(8,128)} %get-tuple-element.73.g_tile) | copy-start | bytes 3145732
  70.3 10.5 %collective-permute-start.22 = (f32[256,256]{1,0:T(8,128)S(1)}, f32[256,256]{1,0:T(8,128)S(1)}, u32[]{:S(2)}, u32[]{:S(2)}) collective-permute-start(f32[256,256]{1,0:T(8,128)S(1)} %get-tuple-element.77), channel_id=1, source_target_pairs={{0,8},{1,9},{2,10},{3,11},{4,20},{5,21},{6,22},{7,23},{8,0},{9,1},... | collective-permute-start | bytes 786440 | tf_op jit(solution)/shard_map/ppermute | solution.py:71
  72.9 5.0 %collective-permute-start.8 = (f32[88,256]{1,0:T(8,128)S(1)}, f32[88,256]{1,0:T(8,128)S(1)}, u32[]{:S(2)}, u32[]{:S(2)}) collective-permute-start(f32[88,256]{1,0:T(8,128)S(1)} %get-tuple-element.65), channel_id=1, source_target_pairs={{0,1},{1,0},{2,3},{3,2},{4,5},{5,4},{6,7},{7,6},{8,9},{9,8},{10,11... | collective-permute-start | bytes 270344 | tf_op jit(solution)/shard_map/ppermute | solution.py:30
  78.0 5.8 %collective-permute-start.9 = (f32[48,256]{1,0:T(8,128)S(1)}, f32[48,256]{1,0:T(8,128)S(1)}, u32[]{:S(2)}, u32[]{:S(2)}) collective-permute-start(f32[48,256]{1,0:T(8,128)S(1)} %get-tuple-element.68), channel_id=1, source_target_pairs={{0,2},{1,3},{2,0},{3,1},{4,6},{5,7},{6,4},{7,5},{8,10},{9,11},{10,... | collective-permute-start | bytes 147464 | tf_op jit(solution)/shard_map/ppermute | solution.py:30
  80.8 67.9 %copy-start.1 = (f32[2,4,256,256]{3,2,1,0:T(8,128)S(1)}, f32[2,4,256,256]{3,2,1,0:T(8,128)}, u32[]{:S(2)}) copy-start(f32[2,4,256,256]{3,2,1,0:T(8,128)} %probe_ref.1) | copy-start | bytes 6291460
  80.8 67.9 %copy-start.3 = (f32[2,256,512]{2,1,0:T(8,128)S(1)}, f32[2,256,512]{2,1,0:T(8,128)}, u32[]{:S(2)}) copy-start(f32[2,256,512]{2,1,0:T(8,128)} %tile_ref.1) | copy-start | bytes 3145732
  80.8 14.9 %collective-permute-start.23 = (f32[128,256]{1,0:T(8,128)S(1)}, f32[128,256]{1,0:T(8,128)S(1)}, u32[]{:S(2)}, u32[]{:S(2)}) collective-permute-start(f32[128,256]{1,0:T(8,128)S(1)} %get-tuple-element.79), channel_id=1, source_target_pairs={{0,16},{1,17},{2,18},{3,19},{4,12},{5,13},{6,14},{7,15},{8,24},{9,... | collective-permute-start | bytes 393224 | tf_op jit(solution)/shard_map/ppermute | solution.py:71
  83.8 17.1 %collective-permute-start.10 = (f32[40,256]{1,0:T(8,128)S(1)}, f32[40,256]{1,0:T(8,128)S(1)}, u32[]{:S(2)}, u32[]{:S(2)}) collective-permute-start(f32[40,256]{1,0:T(8,128)S(1)} %get-tuple-element.89), channel_id=1, source_target_pairs={{0,2},{1,3},{2,0},{3,1},{4,6},{5,7},{6,4},{7,5},{8,10},{9,11},{10,... | collective-permute-start | bytes 122888 | tf_op jit(solution)/shard_map/ppermute | solution.py:30
  95.7 12.0 %collective-permute-start.24 = (f32[64,256]{1,0:T(8,128)S(1)}, f32[64,256]{1,0:T(8,128)S(1)}, u32[]{:S(2)}, u32[]{:S(2)}) collective-permute-start(f32[64,256]{1,0:T(8,128)S(1)} %get-tuple-element.81), channel_id=1, source_target_pairs={{0,1},{1,0},{2,3},{3,2},{4,5},{5,4},{6,7},{7,6},{8,9},{9,8},{10,11... | collective-permute-start | bytes 196616 | tf_op jit(solution)/shard_map/ppermute | solution.py:30
  96.6 8.8 %collective-permute-start.12 = (f32[40,256]{1,0:T(8,128)S(1)}, f32[40,256]{1,0:T(8,128)S(1)}, u32[]{:S(2)}, u32[]{:S(2)}) collective-permute-start(f32[40,256]{1,0:T(8,128)S(1)} %get-tuple-element.89), channel_id=1, source_target_pairs={{0,3},{1,2},{2,1},{3,0},{4,7},{5,6},{6,5},{7,4},{8,11},{9,10},{10,... | collective-permute-start | bytes 122888 | tf_op jit(solution)/shard_map/ppermute | solution.py:30
  100.9 4.4 %collective-permute-start.11 = (f32[40,256]{1,0:T(8,128)S(1)}, f32[40,256]{1,0:T(8,128)S(1)}, u32[]{:S(2)}, u32[]{:S(2)}) collective-permute-start(f32[40,256]{1,0:T(8,128)S(1)} %get-tuple-element.89), channel_id=1, source_target_pairs={{0,1},{1,0},{2,3},{3,2},{4,5},{5,4},{6,7},{7,6},{8,9},{9,8},{10,11... | collective-permute-start | bytes 122888 | tf_op jit(solution)/shard_map/ppermute | solution.py:30
  105.5 36.2 %collective-permute-start.31 = (f32[2,256,256]{2,1,0:T(8,128)S(1)}, f32[2,256,256]{2,1,0:T(8,128)S(1)}, u32[]{:S(2)}, u32[]{:S(2)}) collective-permute-start(f32[2,256,256]{2,1,0:T(8,128)S(1)} %slice_add_fusion), channel_id=1, source_target_pairs={{0,1},{1,2},{2,3},{4,5},{5,6},{6,7},{8,9},{9,10},{10,11},{12,13},{... | collective-permute-start | bytes 1572872 | tf_op jit(solution)/shard_map/ppermute | solution.py:24
  107.8 11.2 %collective-permute-start.25 = (f32[32,256]{1,0:T(8,128)S(1)}, f32[32,256]{1,0:T(8,128)S(1)}, u32[]{:S(2)}, u32[]{:S(2)}) collective-permute-start(f32[32,256]{1,0:T(8,128)S(1)} %get-tuple-element.83), channel_id=1, source_target_pairs={{0,2},{1,3},{2,0},{3,1},{4,6},{5,7},{6,4},{7,5},{8,10},{9,11},{10,... | collective-permute-start | bytes 98312 | tf_op jit(solution)/shard_map/ppermute | solution.py:30
  119.0 8.0 %collective-permute-start.28 = (f32[32,256]{1,0:T(8,128)S(1)}, f32[32,256]{1,0:T(8,128)S(1)}, u32[]{:S(2)}, u32[]{:S(2)}) collective-permute-start(f32[32,256]{1,0:T(8,128)S(1)} %add.16), channel_id=1, source_target_pairs={{0,3},{1,2},{2,1},{3,0},{4,7},{5,6},{6,5},{7,4},{8,11},{9,10},{10,... | collective-permute-start | bytes 98312 | tf_op jit(solution)/shard_map/ppermute | solution.py:30
  123.9 3.9 %collective-permute-start.27 = (f32[32,256]{1,0:T(8,128)S(1)}, f32[32,256]{1,0:T(8,128)S(1)}, u32[]{:S(2)}, u32[]{:S(2)}) collective-permute-start(f32[32,256]{1,0:T(8,128)S(1)} %add.16), channel_id=1, source_target_pairs={{0,1},{1,0},{2,3},{3,2},{4,5},{5,4},{6,7},{7,6},{8,9},{9,8},{10,11... | collective-permute-start | bytes 98312 | tf_op jit(solution)/shard_map/ppermute | solution.py:30
  123.9 4.8 %collective-permute-start.26 = (f32[32,256]{1,0:T(8,128)S(1)}, f32[32,256]{1,0:T(8,128)S(1)}, u32[]{:S(2)}, u32[]{:S(2)}) collective-permute-start(f32[32,256]{1,0:T(8,128)S(1)} %add.16), channel_id=1, source_target_pairs={{0,2},{1,3},{2,0},{3,1},{4,6},{5,7},{6,4},{7,5},{8,10},{9,11},{10,... | collective-permute-start | bytes 98312 | tf_op jit(solution)/shard_map/ppermute | solution.py:30
  124.5 7.3 %collective-permute-start.14 = (f32[168,256]{1,0:T(8,128)S(1)}, f32[168,256]{1,0:T(8,128)S(1)}, u32[]{:S(2)}, u32[]{:S(2)}) collective-permute-start(f32[168,256]{1,0:T(8,128)S(1)} %constant_dynamic-update-slice_fusion.refs_0_), channel_id=1, source_target_pairs={{0,16},{1,17},{2,18},{3,19},{4,12},{5,13},{6,14},{7,15},{8,24},{9,... | collective-permute-start | bytes 516104 | tf_op jit(solution)/shard_map/ppermute | solution.py:71
  128.7 7.5 %collective-permute-start.29 = (f32[128,256]{1,0:T(8,128)S(1)}, f32[128,256]{1,0:T(8,128)S(1)}, u32[]{:S(2)}, u32[]{:S(2)}) collective-permute-start(f32[128,256]{1,0:T(8,128)S(1)} %pad_maximum_fusion.refs_8_), channel_id=1, source_target_pairs={{0,16},{1,17},{2,18},{3,19},{4,12},{5,13},{6,14},{7,15},{8,24},{9,... | collective-permute-start | bytes 393224 | tf_op jit(solution)/shard_map/ppermute | solution.py:71
  131.8 5.4 %collective-permute-start.15 = (f32[168,256]{1,0:T(8,128)S(1)}, f32[168,256]{1,0:T(8,128)S(1)}, u32[]{:S(2)}, u32[]{:S(2)}) collective-permute-start(f32[168,256]{1,0:T(8,128)S(1)} %constant_dynamic-update-slice_fusion.refs_0_), channel_id=1, source_target_pairs={{0,8},{1,9},{2,10},{3,11},{4,20},{5,21},{6,22},{7,23},{8,0},{9,1},... | collective-permute-start | bytes 516104 | tf_op jit(solution)/shard_map/ppermute | solution.py:71
  131.8 9.4 %collective-permute-start.16 = (f32[168,256]{1,0:T(8,128)S(1)}, f32[168,256]{1,0:T(8,128)S(1)}, u32[]{:S(2)}, u32[]{:S(2)}) collective-permute-start(f32[168,256]{1,0:T(8,128)S(1)} %collective-permute-done.14.refs_1_), channel_id=1, source_target_pairs={{0,8},{1,9},{2,10},{3,11},{4,20},{5,21},{6,22},{7,23},{8,0},{9,1},... | collective-permute-start | bytes 516104 | tf_op jit(solution)/shard_map/ppermute | solution.py:71
  136.2 5.0 %collective-permute-start.30 = (f32[128,256]{1,0:T(8,128)S(1)}, f32[128,256]{1,0:T(8,128)S(1)}, u32[]{:S(2)}, u32[]{:S(2)}) collective-permute-start(f32[128,256]{1,0:T(8,128)S(1)} %collective-permute-done.29.refs_9_), channel_id=1, source_target_pairs={{0,8},{1,9},{2,10},{3,11},{4,20},{5,21},{6,22},{7,23},{8,0},{9,1},... | collective-permute-start | bytes 393224 | tf_op jit(solution)/shard_map/ppermute | solution.py:71
  136.2 10.5 %collective-permute-start.17 = (f32[168,256]{1,0:T(8,128)S(1)}, f32[168,256]{1,0:T(8,128)S(1)}, u32[]{:S(2)}, u32[]{:S(2)}) collective-permute-start(f32[168,256]{1,0:T(8,128)S(1)} %constant_dynamic-update-slice_fusion.refs_0_), channel_id=1, source_target_pairs={{0,4},{1,5},{2,6},{3,7},{4,0},{5,1},{6,2},{7,3},{8,12},{9,13},{10,... | collective-permute-start | bytes 516104 | tf_op jit(solution)/shard_map/ppermute | solution.py:30
  137.2 10.0 %collective-permute-start.19 = (f32[168,256]{1,0:T(8,128)S(1)}, f32[168,256]{1,0:T(8,128)S(1)}, u32[]{:S(2)}, u32[]{:S(2)}) collective-permute-start(f32[168,256]{1,0:T(8,128)S(1)} %collective-permute-done.15.refs_2_), channel_id=1, source_target_pairs={{0,4},{1,5},{2,6},{3,7},{4,0},{5,1},{6,2},{7,3},{8,12},{9,13},{10,... | collective-permute-start | bytes 516104 | tf_op jit(solution)/shard_map/ppermute | solution.py:30
  141.2 6.1 %collective-permute-start.18 = (f32[168,256]{1,0:T(8,128)S(1)}, f32[168,256]{1,0:T(8,128)S(1)}, u32[]{:S(2)}, u32[]{:S(2)}) collective-permute-start(f32[168,256]{1,0:T(8,128)S(1)} %collective-permute-done.14.refs_1_), channel_id=1, source_target_pairs={{0,4},{1,5},{2,6},{3,7},{4,0},{5,1},{6,2},{7,3},{8,12},{9,13},{10,... | collective-permute-start | bytes 516104 | tf_op jit(solution)/shard_map/ppermute | solution.py:30
  141.2 6.5 %collective-permute-start.20 = (f32[168,256]{1,0:T(8,128)S(1)}, f32[168,256]{1,0:T(8,128)S(1)}, u32[]{:S(2)}, u32[]{:S(2)}) collective-permute-start(f32[168,256]{1,0:T(8,128)S(1)} %collective-permute-done.16.refs_3_), channel_id=1, source_target_pairs={{0,4},{1,5},{2,6},{3,7},{4,0},{5,1},{6,2},{7,3},{8,12},{9,13},{10,... | collective-permute-start | bytes 516104 | tf_op jit(solution)/shard_map/ppermute | solution.py:30
  141.7 5.0 %collective-permute-start.32 = (f32[128,256]{1,0:T(8,128)S(1)}, f32[128,256]{1,0:T(8,128)S(1)}, u32[]{:S(2)}, u32[]{:S(2)}) collective-permute-start(f32[128,256]{1,0:T(8,128)S(1)} %pad_maximum_fusion.refs_8_), channel_id=1, source_target_pairs={{0,8},{1,9},{2,10},{3,11},{4,20},{5,21},{6,22},{7,23},{8,0},{9,1},... | collective-permute-start | bytes 393224 | tf_op jit(solution)/shard_map/ppermute | solution.py:71
  146.7 1.3 collective-permute-start.33
  146.7 1.9 %collective-permute-start.34 = (f32[128,256]{1,0:T(8,128)S(1)}, f32[128,256]{1,0:T(8,128)S(1)}, u32[]{:S(2)}, u32[]{:S(2)}) collective-permute-start(f32[128,256]{1,0:T(8,128)S(1)} %collective-permute-done.29.refs_9_), channel_id=1, source_target_pairs={{0,4},{1,5},{2,6},{3,7},{4,0},{5,1},{6,2},{7,3},{8,12},{9,13},{10,... | collective-permute-start | bytes 393224 | tf_op jit(solution)/shard_map/ppermute | solution.py:30
  147.2 1.3 collective-permute-start.35
  147.2 1.5 collective-permute-start.36

commit v11 on v10

--- a/solution.py
+++ b/solution.py
@@ -402,8 +402,7 @@
     step = SUBLANES * 2 * pairs * n_col
     total_rows = -(-(2 * modes + 1) * side // step) * step
     piece = total_rows // (2 * pairs * n_col)
-    first = -(-piece // (2 * SUBLANES)) * SUBLANES
-    pieces = [first, piece - first] if piece > first else [piece]
+    pieces = [piece]
     spots = corners[0, 0]
 
     right = shifted(object_field[:, :, :side], 0, -1)
@@ -412,10 +411,10 @@
     tile, measured, spots_now = lax.optimization_barrier((object_field, measured, spots))
     below = shifted(tile[:, :side, :], -1, 0)
     from_left = shifted(spots_now, 0, 1)
-    right, from_left, lit = lax.optimization_barrier((right, from_left, lit))
+    measured = evens_first(measured, False)
+    right, from_left, lit, measured = lax.optimization_barrier((right, from_left, lit, measured))
     corner = shifted(right[:, :side, :], -1, 0)
     from_up = shifted(jnp.concatenate([spots, from_left], axis=0), 1, 0)
-    measured = evens_first(measured, False)
     light, top = pl.pallas_call(
         light_kernel,
         out_shape=(f32(rows, cols), f32(SUBLANES, side)),

time: 150 us -> 118 us (0.79); the launches traced: 151 us -> 117 us
  starting transfers between devices: 72.2 us -> 35.7 us
  Pallas kernels: 11.1 us -> 23.7 us
  waiting for transfers between devices: 56.4 us -> 46.5 us
    ppermute x20 -> x10, starting transfers between devices: 26.3 us -> 4.9 us  [swapped(): return lax.ppermute(value, ('row', 'col'), pairs)]
    ppermute x10 -> x5, starting transfers between devices: 29.7 us -> 13.6 us  [flipped(): return lax.ppermute(value, ('row', 'col'), pairs)]
    pallas_call x1, Pallas kernels: 7.12 us -> 19 us  [body(): pl.pallas_call(main_kernel, out_shape=(hbm(2, rows, cols), vmem(2, side,...]
    ppermute x10 -> x5, waiting for transfers between devices: 30 us -> 20.4 us  [flipped(): return lax.ppermute(value, ('row', 'col'), pairs)]
    ppermute x20 -> x10, waiting for transfers between devices: 21.8 us -> 21.8 us  [swapped(): return lax.ppermute(value, ('row', 'col'), pairs)]
  transfers between devices with their start and end apart: 37 -> 22, of which waited for: 19 -> 14; matrix products, arithmetic and copies ran while one was open for 6% -> 7% of each run, Pallas kernels for 1% -> 2%
where the time goes in v11:
time: 118 us; the launch traced here: 117 us
  waiting for transfers between devices  46.5 us (39%)
  starting transfers between devices  35.7 us (30%)
  Pallas kernels  23.7 us (20%)
  matrix products  5.85 us (5%)
  local copies, waits for them, and re-layouts  2.51 us (2%)
  other arithmetic  1.89 us (2%)
    ppermute x10, waiting for transfers between devices, swapped(): return lax.ppermute(value, ('row', 'col'), pairs)  21.8 us
    ppermute x5, waiting for transfers between devices, flipped(): return lax.ppermute(value, ('row', 'col'), pairs)  20.4 us
    pallas_call x1, Pallas kernels, body(): pl.pallas_call(main_kernel, out_shape=(hbm(2, rows, cols), vmem(2, side,...  19 us
    ppermute x7, starting transfers between devices, shifted(): return lax.ppermute(value, ('row', 'col'), pairs)  17.2 us
    ppermute x5, starting transfers between devices, flipped(): return lax.ppermute(value, ('row', 'col'), pairs)  13.6 us
    dot_general x2, matrix products, evens_first(): return jnp.einsum(form, pick, amplitudes, precision=lax.Precision.HIGH)  5.85 us
    ppermute x10, starting transfers between devices, swapped(): return lax.ppermute(value, ('row', 'col'), pairs)  4.9 us
    ppermute x7, waiting for transfers between devices, shifted(): return lax.ppermute(value, ('row', 'col'), pairs)  4.32 us
  transfers between devices with their start and end apart: 22, of which 14 were waited for; matrix products, arithmetic and copies ran while one was open for 7% of the time, Pallas kernels for 2%

profile of v11, /device:TPU:0, one launch (start us, length us, event | category | flops | bytes accessed | tf_op | source)
XLA Modules:
  0.0 117.1 jit_solution(14848818668363709518)
XLA Ops:
  0.6 2.0 %slice.50 = f32[2,256,256]{2,1,0:T(8,128)} slice(f32[2,256,512]{2,1,0:T(8,128)} %tile_ref.1), slice={[0:2], [0:256], [0:256]} | slice | bytes 1048576 | tf_op jit(solution)/shard_map/slice | solution.py:408
  2.6 1.4 %collective-permute-start = (f32[2,256,256]{2,1,0:T(8,128)}, f32[2,256,256]{2,1,0:T(8,128)S(1)}, u32[]{:S(2)}, u32[]{:S(2)}) collective-permute-start(f32[2,256,256]{2,1,0:T(8,128)} %slice.50), channel_id=1, source_target_pairs={{1,0},{2,1},{3,2},{5,4},{6,5},{7,6},{9,8},{10,9},{11,10},{13,12},{... | collective-permute-start | bytes 1572872 | tf_op jit(solution)/shard_map/ppermute | solution.py:24
  4.1 2.9 %fusion.2 = f32[6,256,256]{2,1,0:T(8,128)} fusion(f32[256,256,1]{1,0,2:T(8,128)} %constant.10, f32[1,1,6,256,256]{4,3,2,1,0:T(8,128)S(1)} %copy-done), kind=kOutput, calls=%fused_computation.2 | convolution fusion | flops 603979776 | bytes 3407872 | tf_op jit(solution)/shard_map/ab,sbc->sac/dot_general | solution.py:92
  7.0 1.3 %collective-permute-start.3 = (f32[2,256,512]{2,1,0:T(8,128)S(1)}, f32[2,256,512]{2,1,0:T(8,128)}, u32[]{:S(2)}, u32[]{:S(2)}) collective-permute-start(f32[2,256,512]{2,1,0:T(8,128)S(1)} %copy-done.2), channel_id=1, source_target_pairs={{4,0},{5,1},{6,2},{7,3},{8,4},{9,5},{10,6},{11,7},{12,8},{13,9},{1... | collective-permute-start | bytes 3145736 | tf_op jit(solution)/shard_map/ppermute | solution.py:24
  8.3 0.1 copy.16
  8.4 5.7 %collective-permute-start.1 = (s32[6,2]{1,0:T(8,128)S(1)}, s32[6,2]{1,0:T(8,128)S(1)}, u32[]{:S(2)}, u32[]{:S(2)}) collective-permute-start(s32[6,2]{1,0:T(8,128)S(1)} %copy.16), channel_id=1, source_target_pairs={{0,1},{1,2},{2,3},{4,5},{5,6},{6,7},{8,9},{9,10},{10,11},{12,13},{... | collective-permute-start | bytes 152 | tf_op jit(solution)/shard_map/ppermute | solution.py:24
  14.1 1.7 %add_reduce_fusion.lit_ref = f32[256,256]{1,0:T(8,128)S(1)} fusion(f32[2,4,256,256]{3,2,1,0:T(8,128)} %probe_ref.1), kind=kLoop, calls=%fused_computation.3 | loop fusion | flops 983040 | bytes 2359296 | tf_op jit(solution)/shard_map/reduce_sum | solution.py:409
  15.8 2.9 %fusion.7.amp_hbm = f32[6,256,256]{2,1,0:T(8,128)} fusion(f32[6,256,256]{2,1,0:T(8,128)S(1)} %copy-done.5, f32[256,256,1]{1,0,2:T(8,128)} %constant.10), kind=kOutput, calls=%fused_computation.21 | convolution fusion | flops 603979776 | bytes 3407872 | tf_op jit(solution)/shard_map/cb,sab->sac/dot_general | solution.py:92
  18.7 1.1 collective-permute-done.right_any
  19.8 1.3 %collective-permute-start.4 = (f32[2,256,256]{2,1,0:T(8,128)S(1)}, f32[2,256,256]{2,1,0:T(8,128)}, u32[]{:S(2)}, u32[]{:S(2)}) collective-permute-start(f32[2,256,256]{2,1,0:T(8,128)S(1)} %collective-permute-done.right_any), channel_id=1, source_target_pairs={{4,0},{5,1},{6,2},{7,3},{8,4},{9,5},{10,6},{11,7},{12,8},{13,9},{1... | collective-permute-start | bytes 1572872 | tf_op jit(solution)/shard_map/ppermute | solution.py:24
  21.1 0.1 copy.20.spots_ref
  21.2 0.1 copy.17
  21.3 0.1 pad_add_fusion
  21.4 0.1 copy.18
  21.5 3.0 %collective-permute-start.2 = (s32[12,2]{1,0:T(8,128)S(1)}, s32[12,2]{1,0:T(8,128)S(1)}, u32[]{:S(2)}, u32[]{:S(2)}) collective-permute-start(s32[12,2]{1,0:T(8,128)S(1)} %copy.18), channel_id=1, source_target_pairs={{0,4},{1,5},{2,6},{3,7},{4,8},{5,9},{6,10},{7,11},{8,12},{9,13},{1... | collective-permute-start | bytes 296 | tf_op jit(solution)/shard_map/ppermute | solution.py:24
  24.5 0.1 copy.19.counts_ref
  24.6 0.7 collective-permute-done.2
  25.3 2.1 %lighting.1 = (f32[256,512]{1,0:T(8,128)S(1)}, f32[8,256]{1,0:T(8,128)S(1)}) custom-call(s32[8,4]{1,0:T(8,128)S(1)} %copy.19.counts_ref, s32[6,2]{1,0:T(8,128)S(1)} %copy.20.spots_ref, s32[6,2]{1,0:T(8,128)S(1)} %collective-permute-done.1.left_ref, s32[6,2]{1,0:T(8,128)S(1)} %get-tuple-element.73.up_ref, s32[6,2]{1,0:T(8,128)S(1)} %get-tuple-element.72.diag_ref, ...), custom_call_target="tpu_custom_call" | custom-call | flops 100000000 | bytes 10000000 | tf_op jit(solution)/shard_map/lighting/pallas_call | solution.py:418
  27.4 19.0 %positions.1 = (f32[2,256,512]{2,1,0:T(8,128)}, f32[2,256,768]{2,1,0:T(8,128)S(1)}, f32[2,256,256]{2,1,0:T(8,128)S(1)}, f32[1152,256]{1,0:T(8,128)S(1)}, f32[1152,256]{1,0:T(8,128)S(1)}) custom-call(s32[8,4]{1,0:T(8,128)S(1)} %copy.19.counts_ref, s32[6,2]{1,0:T(8,128)S(1)} %copy.20.spots_ref, f32[2,256,512]{2,1,0:T(8,128)} %tile_ref.1, ...), custom_call_target="tpu_custom_call" | custom-call | flops 7000000000 | bytes 20000000 | tf_op jit(solution)/shard_map/positions/pallas_call | solution.py:431
  46.4 0.1 collective-permute-start.5
  46.5 2.8 %collective-permute-done.5.refs_1_ = f32[1152,256]{1,0:T(8,128)S(1)} collective-permute-done((f32[1152,256]{1,0:T(8,128)S(1)}, f32[1152,256]{1,0:T(8,128)S(1)}, u32[]{:S(2)}, u32[]{:S(2)}) %collective-permute-start.5) | collective-permute-done | bytes 1179680 | tf_op jit(solution)/shard_map/ppermute | solution.py:30
  49.4 0.2 fold.4
  49.5 5.3 %collective-permute-start.6 = (f32[576,256]{1,0:T(8,128)S(1)}, f32[576,256]{1,0:T(8,128)S(1)}, u32[]{:S(2)}, u32[]{:S(2)}) collective-permute-start(f32[576,256]{1,0:T(8,128)S(1)} %get-tuple-element.50), channel_id=1, source_target_pairs={{0,8},{1,9},{2,10},{3,11},{4,20},{5,21},{6,22},{7,23},{8,0},{9,1},... | collective-permute-start | bytes 1769480 | tf_op jit(solution)/shard_map/ppermute | solution.py:71
  54.9 7.9 %collective-permute-done.6.refs_1_ = f32[576,256]{1,0:T(8,128)S(1)} collective-permute-done((f32[576,256]{1,0:T(8,128)S(1)}, f32[576,256]{1,0:T(8,128)S(1)}, u32[]{:S(2)}, u32[]{:S(2)}) %collective-permute-start.6) | collective-permute-done | bytes 589856 | tf_op jit(solution)/shard_map/ppermute | solution.py:71
  62.7 0.1 fold.5
  62.8 6.4 %collective-permute-start.7 = (f32[288,256]{1,0:T(8,128)S(1)}, f32[288,256]{1,0:T(8,128)S(1)}, u32[]{:S(2)}, u32[]{:S(2)}) collective-permute-start(f32[288,256]{1,0:T(8,128)S(1)} %get-tuple-element.52), channel_id=1, source_target_pairs={{0,16},{1,17},{2,18},{3,19},{4,12},{5,13},{6,14},{7,15},{8,24},{9,... | collective-permute-start | bytes 884744 | tf_op jit(solution)/shard_map/ppermute | solution.py:71
  69.2 4.7 %collective-permute-done.7.refs_1_ = f32[288,256]{1,0:T(8,128)S(1)} collective-permute-done((f32[288,256]{1,0:T(8,128)S(1)}, f32[288,256]{1,0:T(8,128)S(1)}, u32[]{:S(2)}, u32[]{:S(2)}) %collective-permute-start.7) | collective-permute-done | bytes 294944 | tf_op jit(solution)/shard_map/ppermute | solution.py:71
  74.0 1.7 %collective-permute-start.13 = (f32[2,256,768]{2,1,0:T(8,128)S(1)}, f32[2,256,768]{2,1,0:T(8,128)S(1)}, u32[]{:S(2)}, u32[]{:S(2)}) collective-permute-start(f32[2,256,768]{2,1,0:T(8,128)S(1)} %get-tuple-element.62), channel_id=1, source_target_pairs={{0,4},{1,5},{2,6},{3,7},{4,8},{5,9},{6,10},{7,11},{8,12},{9,13},{1... | collective-permute-start | bytes 4718600 | tf_op jit(solution)/shard_map/ppermute | solution.py:24
  75.6 0.5 collective-permute-start.8
  76.1 6.1 %collective-permute-done.8.refs_1_ = f32[152,256]{1,0:T(8,128)S(1)} collective-permute-done((f32[152,256]{1,0:T(8,128)S(1)}, f32[152,256]{1,0:T(8,128)S(1)}, u32[]{:S(2)}, u32[]{:S(2)}) %collective-permute-start.8) | collective-permute-done | bytes 155680 | tf_op jit(solution)/shard_map/ppermute | solution.py:30
  82.3 0.2 collective-permute-start.9
  82.5 6.5 %collective-permute-done.9 = f32[80,256]{1,0:T(8,128)S(1)} collective-permute-done((f32[80,256]{1,0:T(8,128)S(1)}, f32[80,256]{1,0:T(8,128)S(1)}, u32[]{:S(2)}, u32[]{:S(2)}) %collective-permute-start.9) | collective-permute-done | bytes 81952 | tf_op jit(solution)/shard_map/ppermute | solution.py:30
  89.0 0.1 collective-permute-start.10
  89.1 1.5 %collective-permute-start.12 = (f32[72,256]{1,0:T(8,128)S(1)}, f32[72,256]{1,0:T(8,128)S(1)}, u32[]{:S(2)}, u32[]{:S(2)}) collective-permute-start(f32[72,256]{1,0:T(8,128)S(1)} %get-tuple-element.71), channel_id=1, source_target_pairs={{0,3},{1,2},{2,1},{3,0},{4,7},{5,6},{6,5},{7,4},{8,11},{9,10},{10,... | collective-permute-start | bytes 221192 | tf_op jit(solution)/shard_map/ppermute | solution.py:30
  90.6 2.0 %collective-permute-start.11 = (f32[72,256]{1,0:T(8,128)S(1)}, f32[72,256]{1,0:T(8,128)S(1)}, u32[]{:S(2)}, u32[]{:S(2)}) collective-permute-start(f32[72,256]{1,0:T(8,128)S(1)} %get-tuple-element.71), channel_id=1, source_target_pairs={{0,1},{1,0},{2,3},{3,2},{4,5},{5,4},{6,7},{7,6},{8,9},{9,8},{10,11... | collective-permute-start | bytes 221192 | tf_op jit(solution)/shard_map/ppermute | solution.py:30
  92.6 4.0 %collective-permute-done.10 = f32[72,256]{1,0:T(8,128)S(1)} collective-permute-done((f32[72,256]{1,0:T(8,128)S(1)}, f32[72,256]{1,0:T(8,128)S(1)}, u32[]{:S(2)}, u32[]{:S(2)}) %collective-permute-start.10) | collective-permute-done | bytes 73760 | tf_op jit(solution)/shard_map/ppermute | solution.py:30
  96.6 0.8 collective-permute-done.11
  97.5 1.5 %collective-permute-start.14 = (f32[296,256]{1,0:T(8,128)S(1)}, f32[296,256]{1,0:T(8,128)S(1)}, u32[]{:S(2)}, u32[]{:S(2)}) collective-permute-start(f32[296,256]{1,0:T(8,128)S(1)} %constant_dynamic-update-slice_fusion.refs_0_), channel_id=1, source_target_pairs={{0,16},{1,17},{2,18},{3,19},{4,12},{5,13},{6,14},{7,15},{8,24},{9,... | collective-permute-start | bytes 909320 | tf_op jit(solution)/shard_map/ppermute | solution.py:71
  99.0 2.9 %collective-permute-start.17 = (f32[2,256,256]{2,1,0:T(8,128)S(1)}, f32[2,256,256]{2,1,0:T(8,128)S(1)}, u32[]{:S(2)}, u32[]{:S(2)}) collective-permute-start(f32[2,256,256]{2,1,0:T(8,128)S(1)} %slice_add_fusion), channel_id=1, source_target_pairs={{0,1},{1,2},{2,3},{4,5},{5,6},{6,7},{8,9},{9,10},{10,11},{12,13},{... | collective-permute-start | bytes 1572872 | tf_op jit(solution)/shard_map/ppermute | solution.py:24
  101.9 0.1 collective-permute-start.15
  102.0 4.4 %collective-permute-done.14.refs_1_ = f32[296,256]{1,0:T(8,128)S(1)} collective-permute-done((f32[296,256]{1,0:T(8,128)S(1)}, f32[296,256]{1,0:T(8,128)S(1)}, u32[]{:S(2)}, u32[]{:S(2)}) %collective-permute-start.14) | collective-permute-done | bytes 303136 | tf_op jit(solution)/shard_map/ppermute | solution.py:71
  106.4 0.3 collective-permute-start.16
  106.7 0.5 collective-permute-start.19
  107.2 1.6 %collective-permute-done.15.refs_2_ = f32[296,256]{1,0:T(8,128)S(1)} collective-permute-done((f32[296,256]{1,0:T(8,128)S(1)}, f32[296,256]{1,0:T(8,128)S(1)}, u32[]{:S(2)}, u32[]{:S(2)}) %collective-permute-start.15) | collective-permute-done | bytes 303136 | tf_op jit(solution)/shard_map/ppermute | solution.py:71
  108.8 2.5 %collective-permute-done.17.g_left = f32[2,256,256]{2,1,0:T(8,128)S(1)} collective-permute-done((f32[2,256,256]{2,1,0:T(8,128)S(1)}, f32[2,256,256]{2,1,0:T(8,128)S(1)}, u32[]{:S(2)}, u32[]{:S(2)}) %collective-permute-start.17) | collective-permute-done | bytes 524320 | tf_op jit(solution)/shard_map/ppermute | solution.py:24
  111.3 1.9 %collective-permute-done.16.refs_3_ = f32[296,256]{1,0:T(8,128)S(1)} collective-permute-done((f32[296,256]{1,0:T(8,128)S(1)}, f32[296,256]{1,0:T(8,128)S(1)}, u32[]{:S(2)}, u32[]{:S(2)}) %collective-permute-start.16) | collective-permute-done | bytes 303136 | tf_op jit(solution)/shard_map/ppermute | solution.py:71
  113.2 1.6 %collective-permute-done.21.refs_7_ = f32[296,256]{1,0:T(8,128)S(1)} collective-permute-done((f32[296,256]{1,0:T(8,128)S(1)}, f32[296,256]{1,0:T(8,128)S(1)}, u32[]{:S(2)}, u32[]{:S(2)}) %collective-permute-start.21) | collective-permute-done | bytes 303136 | tf_op jit(solution)/shard_map/ppermute | solution.py:30
  114.8 2.3 %update.1 = (f32[2,256,512]{2,1,0:T(8,128)}, f32[2,4,256,256]{3,2,1,0:T(8,128)}) custom-call(f32[2,256,512]{2,1,0:T(8,128)S(1)} %copy-done.3, f32[256,512]{1,0:T(8,128)S(1)} %get-tuple-element.40.light_ref, f32[8,256]{1,0:T(8,128)S(1)} %slice_maximum_fusion.top_ref, f32[2,256,512]{2,1,0:T(8,128)S(1)} %copy-done.4, ...), custom_call_target="tpu_custom_call" | custom-call | flops 1000000 | bytes 10000000 | tf_op jit(solution)/shard_map/update/pallas_call | solution.py:491
  (37 shorter events, 0.2 us)
Async XLA Ops:
  0.6 3.4 %copy-start = (f32[1,1,6,256,256]{4,3,2,1,0:T(8,128)S(1)}, f32[1,1,6,256,256]{4,3,2,1,0:T(8,128)}, u32[]{:S(2)}) copy-start(f32[1,1,6,256,256]{4,3,2,1,0:T(8,128)} %param.10) | copy-start | bytes 4718596
  2.6 4.4 %copy-start.2 = (f32[2,256,512]{2,1,0:T(8,128)S(1)}, f32[2,256,512]{2,1,0:T(8,128)}, u32[]{:S(2)}) copy-start(f32[2,256,512]{2,1,0:T(8,128)} %tile_ref.1) | copy-start | bytes 3145732
  2.6 5.6 %copy-start.6 = (s32[1,1,6,2]{2,3,1,0:T(2,128)S(1)}, s32[1,1,6,2]{2,3,1,0:T(2,128)}, u32[]{:S(2)}) copy-start(s32[1,1,6,2]{2,3,1,0:T(2,128)} %param.11) | copy-start | bytes 148
  2.6 17.2 %collective-permute-start = (f32[2,256,256]{2,1,0:T(8,128)}, f32[2,256,256]{2,1,0:T(8,128)S(1)}, u32[]{:S(2)}, u32[]{:S(2)}) collective-permute-start(f32[2,256,256]{2,1,0:T(8,128)} %slice.50), channel_id=1, source_target_pairs={{1,0},{2,1},{3,2},{5,4},{6,5},{7,6},{9,8},{10,9},{11,10},{13,12},{... | collective-permute-start | bytes 1572872 | tf_op jit(solution)/shard_map/ppermute | solution.py:24
  7.0 20.5 %collective-permute-start.3 = (f32[2,256,512]{2,1,0:T(8,128)S(1)}, f32[2,256,512]{2,1,0:T(8,128)}, u32[]{:S(2)}, u32[]{:S(2)}) collective-permute-start(f32[2,256,512]{2,1,0:T(8,128)S(1)} %copy-done.2), channel_id=1, source_target_pairs={{4,0},{5,1},{6,2},{7,3},{8,4},{9,5},{10,6},{11,7},{12,8},{13,9},{1... | collective-permute-start | bytes 3145736 | tf_op jit(solution)/shard_map/ppermute | solution.py:24
  8.4 7.4 %copy-start.5 = (f32[6,256,256]{2,1,0:T(8,128)S(1)}, f32[6,256,256]{2,1,0:T(8,128)}, u32[]{:S(2)}) copy-start(f32[6,256,256]{2,1,0:T(8,128)} %fusion.2) | copy-start | bytes 4718596
  8.4 10.4 %collective-permute-start.1 = (s32[6,2]{1,0:T(8,128)S(1)}, s32[6,2]{1,0:T(8,128)S(1)}, u32[]{:S(2)}, u32[]{:S(2)}) collective-permute-start(s32[6,2]{1,0:T(8,128)S(1)} %copy.16), channel_id=1, source_target_pairs={{0,1},{1,2},{2,3},{4,5},{5,6},{6,7},{8,9},{9,10},{10,11},{12,13},{... | collective-permute-start | bytes 152 | tf_op jit(solution)/shard_map/ppermute | solution.py:24
  15.8 8.7 %copy-start.7 = (s32[8,4]{0,1:T(4,128)S(1)}, s32[8,4]{0,1:T(4,128)}, u32[]{:S(2)}) copy-start(s32[8,4]{0,1:T(4,128)} %param.12) | copy-start | bytes 388
  19.8 7.6 %collective-permute-start.4 = (f32[2,256,256]{2,1,0:T(8,128)S(1)}, f32[2,256,256]{2,1,0:T(8,128)}, u32[]{:S(2)}, u32[]{:S(2)}) collective-permute-start(f32[2,256,256]{2,1,0:T(8,128)S(1)} %collective-permute-done.right_any), channel_id=1, source_target_pairs={{4,0},{5,1},{6,2},{7,3},{8,4},{9,5},{10,6},{11,7},{12,8},{13,9},{1... | collective-permute-start | bytes 1572872 | tf_op jit(solution)/shard_map/ppermute | solution.py:24
  21.5 3.8 %collective-permute-start.2 = (s32[12,2]{1,0:T(8,128)S(1)}, s32[12,2]{1,0:T(8,128)S(1)}, u32[]{:S(2)}, u32[]{:S(2)}) collective-permute-start(s32[12,2]{1,0:T(8,128)S(1)} %copy.18), channel_id=1, source_target_pairs={{0,4},{1,5},{2,6},{3,7},{4,8},{5,9},{6,10},{7,11},{8,12},{9,13},{1... | collective-permute-start | bytes 296 | tf_op jit(solution)/shard_map/ppermute | solution.py:24
  46.4 2.9 %collective-permute-start.5 = (f32[1152,256]{1,0:T(8,128)S(1)}, f32[1152,256]{1,0:T(8,128)S(1)}, u32[]{:S(2)}, u32[]{:S(2)}) collective-permute-start(f32[1152,256]{1,0:T(8,128)S(1)} %get-tuple-element.48), channel_id=1, source_target_pairs={{0,4},{1,5},{2,6},{3,7},{4,0},{5,1},{6,2},{7,3},{8,12},{9,13},{10,... | collective-permute-start | bytes 3538952 | tf_op jit(solution)/shard_map/ppermute | solution.py:30
  49.5 13.2 %collective-permute-start.6 = (f32[576,256]{1,0:T(8,128)S(1)}, f32[576,256]{1,0:T(8,128)S(1)}, u32[]{:S(2)}, u32[]{:S(2)}) collective-permute-start(f32[576,256]{1,0:T(8,128)S(1)} %get-tuple-element.50), channel_id=1, source_target_pairs={{0,8},{1,9},{2,10},{3,11},{4,20},{5,21},{6,22},{7,23},{8,0},{9,1},... | collective-permute-start | bytes 1769480 | tf_op jit(solution)/shard_map/ppermute | solution.py:71
  62.7 52.1 %copy-start.4 = (f32[2,256,512]{2,1,0:T(8,128)S(1)}, f32[2,256,512]{2,1,0:T(8,128)}, u32[]{:S(2)}) copy-start(f32[2,256,512]{2,1,0:T(8,128)} %get-tuple-element.67.g_tile) | copy-start | bytes 3145732
  62.8 11.1 %collective-permute-start.7 = (f32[288,256]{1,0:T(8,128)S(1)}, f32[288,256]{1,0:T(8,128)S(1)}, u32[]{:S(2)}, u32[]{:S(2)}) collective-permute-start(f32[288,256]{1,0:T(8,128)S(1)} %get-tuple-element.52), channel_id=1, source_target_pairs={{0,16},{1,17},{2,18},{3,19},{4,12},{5,13},{6,14},{7,15},{8,24},{9,... | collective-permute-start | bytes 884744 | tf_op jit(solution)/shard_map/ppermute | solution.py:71
  73.9 40.9 %copy-start.1 = (f32[2,4,256,256]{3,2,1,0:T(8,128)S(1)}, f32[2,4,256,256]{3,2,1,0:T(8,128)}, u32[]{:S(2)}) copy-start(f32[2,4,256,256]{3,2,1,0:T(8,128)} %probe_ref.1) | copy-start | bytes 6291460
  73.9 40.9 %copy-start.3 = (f32[2,256,512]{2,1,0:T(8,128)S(1)}, f32[2,256,512]{2,1,0:T(8,128)}, u32[]{:S(2)}) copy-start(f32[2,256,512]{2,1,0:T(8,128)} %tile_ref.1) | copy-start | bytes 3145732
  74.0 23.5 %collective-permute-start.13 = (f32[2,256,768]{2,1,0:T(8,128)S(1)}, f32[2,256,768]{2,1,0:T(8,128)S(1)}, u32[]{:S(2)}, u32[]{:S(2)}) collective-permute-start(f32[2,256,768]{2,1,0:T(8,128)S(1)} %get-tuple-element.62), channel_id=1, source_target_pairs={{0,4},{1,5},{2,6},{3,7},{4,8},{5,9},{6,10},{7,11},{8,12},{9,13},{1... | collective-permute-start | bytes 4718600 | tf_op jit(solution)/shard_map/ppermute | solution.py:24
  75.6 6.6 %collective-permute-start.8 = (f32[152,256]{1,0:T(8,128)S(1)}, f32[152,256]{1,0:T(8,128)S(1)}, u32[]{:S(2)}, u32[]{:S(2)}) collective-permute-start(f32[152,256]{1,0:T(8,128)S(1)} %get-tuple-element.57), channel_id=1, source_target_pairs={{0,1},{1,0},{2,3},{3,2},{4,5},{5,4},{6,7},{7,6},{8,9},{9,8},{10,11... | collective-permute-start | bytes 466952 | tf_op jit(solution)/shard_map/ppermute | solution.py:30
  82.3 6.7 %collective-permute-start.9 = (f32[80,256]{1,0:T(8,128)S(1)}, f32[80,256]{1,0:T(8,128)S(1)}, u32[]{:S(2)}, u32[]{:S(2)}) collective-permute-start(f32[80,256]{1,0:T(8,128)S(1)} %get-tuple-element.60), channel_id=1, source_target_pairs={{0,2},{1,3},{2,0},{3,1},{4,6},{5,7},{6,4},{7,5},{8,10},{9,11},{10,... | collective-permute-start | bytes 245768 | tf_op jit(solution)/shard_map/ppermute | solution.py:30
  89.0 7.6 %collective-permute-start.10 = (f32[72,256]{1,0:T(8,128)S(1)}, f32[72,256]{1,0:T(8,128)S(1)}, u32[]{:S(2)}, u32[]{:S(2)}) collective-permute-start(f32[72,256]{1,0:T(8,128)S(1)} %get-tuple-element.71), channel_id=1, source_target_pairs={{0,2},{1,3},{2,0},{3,1},{4,6},{5,7},{6,4},{7,5},{8,10},{9,11},{10,... | collective-permute-start | bytes 221192 | tf_op jit(solution)/shard_map/ppermute | solution.py:30
  89.1 8.3 %collective-permute-start.12 = (f32[72,256]{1,0:T(8,128)S(1)}, f32[72,256]{1,0:T(8,128)S(1)}, u32[]{:S(2)}, u32[]{:S(2)}) collective-permute-start(f32[72,256]{1,0:T(8,128)S(1)} %get-tuple-element.71), channel_id=1, source_target_pairs={{0,3},{1,2},{2,1},{3,0},{4,7},{5,6},{6,5},{7,4},{8,11},{9,10},{10,... | collective-permute-start | bytes 221192 | tf_op jit(solution)/shard_map/ppermute | solution.py:30
  90.6 6.8 %collective-permute-start.11 = (f32[72,256]{1,0:T(8,128)S(1)}, f32[72,256]{1,0:T(8,128)S(1)}, u32[]{:S(2)}, u32[]{:S(2)}) collective-permute-start(f32[72,256]{1,0:T(8,128)S(1)} %get-tuple-element.71), channel_id=1, source_target_pairs={{0,1},{1,0},{2,3},{3,2},{4,5},{5,4},{6,7},{7,6},{8,9},{9,8},{10,11... | collective-permute-start | bytes 221192 | tf_op jit(solution)/shard_map/ppermute | solution.py:30
  97.5 8.9 %collective-permute-start.14 = (f32[296,256]{1,0:T(8,128)S(1)}, f32[296,256]{1,0:T(8,128)S(1)}, u32[]{:S(2)}, u32[]{:S(2)}) collective-permute-start(f32[296,256]{1,0:T(8,128)S(1)} %constant_dynamic-update-slice_fusion.refs_0_), channel_id=1, source_target_pairs={{0,16},{1,17},{2,18},{3,19},{4,12},{5,13},{6,14},{7,15},{8,24},{9,... | collective-permute-start | bytes 909320 | tf_op jit(solution)/shard_map/ppermute | solution.py:71
  99.0 12.3 %collective-permute-start.17 = (f32[2,256,256]{2,1,0:T(8,128)S(1)}, f32[2,256,256]{2,1,0:T(8,128)S(1)}, u32[]{:S(2)}, u32[]{:S(2)}) collective-permute-start(f32[2,256,256]{2,1,0:T(8,128)S(1)} %slice_add_fusion), channel_id=1, source_target_pairs={{0,1},{1,2},{2,3},{4,5},{5,6},{6,7},{8,9},{9,10},{10,11},{12,13},{... | collective-permute-start | bytes 1572872 | tf_op jit(solution)/shard_map/ppermute | solution.py:24
  101.9 6.9 %collective-permute-start.15 = (f32[296,256]{1,0:T(8,128)S(1)}, f32[296,256]{1,0:T(8,128)S(1)}, u32[]{:S(2)}, u32[]{:S(2)}) collective-permute-start(f32[296,256]{1,0:T(8,128)S(1)} %constant_dynamic-update-slice_fusion.refs_0_), channel_id=1, source_target_pairs={{0,8},{1,9},{2,10},{3,11},{4,20},{5,21},{6,22},{7,23},{8,0},{9,1},... | collective-permute-start | bytes 909320 | tf_op jit(solution)/shard_map/ppermute | solution.py:71
  106.4 6.8 %collective-permute-start.16 = (f32[296,256]{1,0:T(8,128)S(1)}, f32[296,256]{1,0:T(8,128)S(1)}, u32[]{:S(2)}, u32[]{:S(2)}) collective-permute-start(f32[296,256]{1,0:T(8,128)S(1)} %collective-permute-done.14.refs_1_), channel_id=1, source_target_pairs={{0,8},{1,9},{2,10},{3,11},{4,20},{5,21},{6,22},{7,23},{8,0},{9,1},... | collective-permute-start | bytes 909320 | tf_op jit(solution)/shard_map/ppermute | solution.py:71
  106.7 6.5 %collective-permute-start.18 = (f32[296,256]{1,0:T(8,128)S(1)}, f32[296,256]{1,0:T(8,128)S(1)}, u32[]{:S(2)}, u32[]{:S(2)}) collective-permute-start(f32[296,256]{1,0:T(8,128)S(1)} %constant_dynamic-update-slice_fusion.refs_0_), channel_id=1, source_target_pairs={{0,4},{1,5},{2,6},{3,7},{4,0},{5,1},{6,2},{7,3},{8,12},{9,13},{10,... | collective-permute-start | bytes 909320 | tf_op jit(solution)/shard_map/ppermute | solution.py:30
  106.7 6.5 %collective-permute-start.19 = (f32[296,256]{1,0:T(8,128)S(1)}, f32[296,256]{1,0:T(8,128)S(1)}, u32[]{:S(2)}, u32[]{:S(2)}) collective-permute-start(f32[296,256]{1,0:T(8,128)S(1)} %collective-permute-done.14.refs_1_), channel_id=1, source_target_pairs={{0,4},{1,5},{2,6},{3,7},{4,0},{5,1},{6,2},{7,3},{8,12},{9,13},{10,... | collective-permute-start | bytes 909320 | tf_op jit(solution)/shard_map/ppermute | solution.py:30
  108.8 4.4 %collective-permute-start.20 = (f32[296,256]{1,0:T(8,128)S(1)}, f32[296,256]{1,0:T(8,128)S(1)}, u32[]{:S(2)}, u32[]{:S(2)}) collective-permute-start(f32[296,256]{1,0:T(8,128)S(1)} %collective-permute-done.15.refs_2_), channel_id=1, source_target_pairs={{0,4},{1,5},{2,6},{3,7},{4,0},{5,1},{6,2},{7,3},{8,12},{9,13},{10,... | collective-permute-start | bytes 909320 | tf_op jit(solution)/shard_map/ppermute | solution.py:30
  113.2 1.6 %collective-permute-start.21 = (f32[296,256]{1,0:T(8,128)S(1)}, f32[296,256]{1,0:T(8,128)S(1)}, u32[]{:S(2)}, u32[]{:S(2)}) collective-permute-start(f32[296,256]{1,0:T(8,128)S(1)} %collective-permute-done.16.refs_3_), channel_id=1, source_target_pairs={{0,4},{1,5},{2,6},{3,7},{4,0},{5,1},{6,2},{7,3},{8,12},{9,13},{10,... | collective-permute-start | bytes 909320 | tf_op jit(solution)/shard_map/ppermute | solution.py:30

commit v12 on v11

--- a/solution.py
+++ b/solution.py
@@ -197,14 +197,15 @@
                     left, right = half[i * low:(i + 1) * low, :low], half[i * low:(i + 1) * low, low:]
                     turned[0, at:at + low, i * low:(i + 1) * low] = bf16(left + right)
                     turned[1, at:at + low, i * low:(i + 1) * low] = bf16(left - right)
+        models = [jnp.zeros((side, low), jnp.float32)] * 2
         for parity in range(2):
-            wave[parity] = dot(turned[parity], table_ref[2 + parity])
+            for k in range(modes):
+                got = dot(turned[parity, plane(k)], table_ref[2 + parity])
+                wave[parity, plane(k)] = got
+                models[parity] += got[:, :low] * got[:, :low] + got[:, low:] * got[:, low:]
         amp_load(p, slot).wait()
         for parity in range(2):
-            model = jnp.zeros((side, low), jnp.float32)
-            for k in range(modes):
-                wr, wi = wave[parity, plane(k), :low], wave[parity, plane(k), low:]
-                model += wr * wr + wi * wi
+            model = models[parity]
             factor = amp_ref[slot, :, parity * low:(parity + 1) * low] * lax.rsqrt(jnp.maximum(model, 1.0)) - 1.0
             for k in range(modes):
                 at = k * side + parity * low
@@ -222,27 +223,19 @@
                         turned[parity, at:at + low, i * low:(i + 1) * low] = (
                             back[i * low:(i + 1) * low, parity * low:(parity + 1) * low]
                         )
-        for parity in range(2):
-            wave[parity] = dot(turned[parity], table_ref[parity])
-        grads = []
-        for lower in range(2):
-            part = slice(lower * low, (lower + 1) * low)
-            grad_re = jnp.zeros((side, low), jnp.float32)
-            grad_im = jnp.zeros((side, low), jnp.float32)
-            win_re, win_im = wins[0, :, part], wins[1, :, part]
-            for k in range(modes):
-                even_re, even_im = wave[0, plane(k), :low], wave[0, plane(k), low:]
-                odd_re, odd_im = wave[1, plane(k), :low], wave[1, plane(k), low:]
-                if lower:
-                    cr, ci = even_re - odd_re, even_im - odd_im
-                else:
-                    cr, ci = even_re + odd_re, even_im + odd_im
+        grads = [[jnp.zeros((side, low), jnp.float32)] * 2 for _ in range(2)]
+        for k in range(modes):
+            even = dot(turned[0, plane(k)], table_ref[0])
+            odd = dot(turned[1, plane(k)], table_ref[1])
+            for lower, chi in enumerate((even + odd, even - odd)):
+                part = slice(lower * low, (lower + 1) * low)
+                cr, ci = chi[:, :low], chi[:, low:]
                 pr, pi = probe_ref[0, k, :, part], probe_ref[1, k, :, part]
-                grad_re += pr * cr + pi * ci
-                grad_im += pr * ci - pi * cr
+                win_re, win_im = wins[0, :, part], wins[1, :, part]
+                grads[lower][0] += pr * cr + pi * ci
+                grads[lower][1] += pr * ci - pi * cr
                 sums[plane(k), part] += win_re * cr + win_im * ci
                 sums[plane(modes + k), part] += win_re * ci - win_im * cr
-            grads.append((grad_re, grad_im))
         for i in range(2):
             add_at(gacc, i, row, col, jnp.concatenate([grads[0][i], grads[1][i]], axis=1), side)
         return carry
@@ -406,15 +399,15 @@
     spots = corners[0, 0]
 
     right = shifted(object_field[:, :, :side], 0, -1)
-    lit = jnp.sum(probe[0] * probe[0] + probe[1] * probe[1], axis=0)
     measured = evens_first(amplitudes[0, 0], True)
     tile, measured, spots_now = lax.optimization_barrier((object_field, measured, spots))
     below = shifted(tile[:, :side, :], -1, 0)
     from_left = shifted(spots_now, 0, 1)
     measured = evens_first(measured, False)
-    right, from_left, lit, measured = lax.optimization_barrier((right, from_left, lit, measured))
+    right, from_left, measured, modes_now = lax.optimization_barrier((right, from_left, measured, probe))
     corner = shifted(right[:, :side, :], -1, 0)
     from_up = shifted(jnp.concatenate([spots, from_left], axis=0), 1, 0)
+    lit = jnp.sum(modes_now[0] * modes_now[0] + modes_now[1] * modes_now[1], axis=0)
     light, top = pl.pallas_call(
         light_kernel,
         out_shape=(f32(rows, cols), f32(SUBLANES, side)),

time: 118 us -> 116 us (0.983)
  Pallas kernels: 23.7 us -> 17.1 us
  starting transfers between devices: 35.7 us -> 40.9 us
    pallas_call x1, Pallas kernels: 19 us -> 12.7 us  [body(): pl.pallas_call(main_kernel, out_shape=(hbm(2, rows, cols), vmem(2, side,...]
    ppermute x10, starting transfers between devices: 4.9 us -> 8.98 us  [swapped(): return lax.ppermute(value, ('row', 'col'), pairs)]
    ppermute x10, waiting for transfers between devices: 21.8 us -> 19.7 us  [swapped(): return lax.ppermute(value, ('row', 'col'), pairs)]
    ppermute x5, starting transfers between devices: 13.6 us -> 15.4 us  [flipped(): return lax.ppermute(value, ('row', 'col'), pairs)]
    ppermute x7, waiting for transfers between devices: 4.32 us -> 5.77 us  [shifted(): return lax.ppermute(value, ('row', 'col'), pairs)]
  transfers between devices with their start and end apart: 22 -> 22, of which waited for: 14 -> 13; matrix products, arithmetic and copies ran while one was open for 7% -> 7% of each run, Pallas kernels for 2% -> 2%
where the time goes in v12:
time: 116 us; the launch traced here: 115 us
  waiting for transfers between devices  45.7 us (39%)
  starting transfers between devices  40.9 us (35%)
  Pallas kernels  17.1 us (15%)
  matrix products  6.33 us (5%)
  local copies, waits for them, and re-layouts  2.51 us (2%)
  other arithmetic  1.88 us (2%)
    ppermute x5, waiting for transfers between devices, flipped(): return lax.ppermute(value, ('row', 'col'), pairs)  20.2 us
    ppermute x10, waiting for transfers between devices, swapped(): return lax.ppermute(value, ('row', 'col'), pairs)  19.7 us
    ppermute x7, starting transfers between devices, shifted(): return lax.ppermute(value, ('row', 'col'), pairs)  16.6 us
    ppermute x5, starting transfers between devices, flipped(): return lax.ppermute(value, ('row', 'col'), pairs)  15.4 us
    pallas_call x1, Pallas kernels, body(): pl.pallas_call(main_kernel, out_shape=(hbm(2, rows, cols), vmem(2, side,...  12.7 us
    ppermute x10, starting transfers between devices, swapped(): return lax.ppermute(value, ('row', 'col'), pairs)  8.98 us
    dot_general x2, matrix products, evens_first(): return jnp.einsum(form, pick, amplitudes, precision=lax.Precision.HIGH)  6.33 us
    ppermute x7, waiting for transfers between devices, shifted(): return lax.ppermute(value, ('row', 'col'), pairs)  5.77 us
  transfers between devices with their start and end apart: 22, of which 13 were waited for; matrix products, arithmetic and copies ran while one was open for 7% of the time, Pallas kernels for 2%

profile of v12, /device:TPU:0, one launch (start us, length us, event | category | flops | bytes accessed | tf_op | source)
XLA Modules:
  0.0 115.2 jit_solution(8774357365776133197)
XLA Ops:
  0.6 0.0 copy-start
  0.6 2.0 %slice.50 = f32[2,256,256]{2,1,0:T(8,128)} slice(f32[2,256,512]{2,1,0:T(8,128)} %tile_ref.1), slice={[0:2], [0:256], [0:256]} | slice | bytes 1048576 | tf_op jit(solution)/shard_map/slice | solution.py:401
  2.6 1.4 %collective-permute-start = (f32[2,256,256]{2,1,0:T(8,128)}, f32[2,256,256]{2,1,0:T(8,128)S(1)}, u32[]{:S(2)}, u32[]{:S(2)}) collective-permute-start(f32[2,256,256]{2,1,0:T(8,128)} %slice.50), channel_id=1, source_target_pairs={{1,0},{2,1},{3,2},{5,4},{6,5},{7,6},{9,8},{10,9},{11,10},{13,12},{... | collective-permute-start | bytes 1572872 | tf_op jit(solution)/shard_map/ppermute | solution.py:24
  4.1 2.9 %fusion.2 = f32[6,256,256]{2,1,0:T(8,128)} fusion(f32[256,256,1]{1,0,2:T(8,128)} %constant.10, f32[1,1,6,256,256]{4,3,2,1,0:T(8,128)S(1)} %copy-done), kind=kOutput, calls=%fused_computation.2 | convolution fusion | flops 603979776 | bytes 3407872 | tf_op jit(solution)/shard_map/ab,sbc->sac/dot_general | solution.py:92
  7.0 1.3 %collective-permute-start.3 = (f32[2,256,512]{2,1,0:T(8,128)S(1)}, f32[2,256,512]{2,1,0:T(8,128)}, u32[]{:S(2)}, u32[]{:S(2)}) collective-permute-start(f32[2,256,512]{2,1,0:T(8,128)S(1)} %copy-done.2), channel_id=1, source_target_pairs={{4,0},{5,1},{6,2},{7,3},{8,4},{9,5},{10,6},{11,7},{12,8},{13,9},{1... | collective-permute-start | bytes 3145736 | tf_op jit(solution)/shard_map/ppermute | solution.py:24
  8.3 0.1 copy.16
  8.4 5.7 %collective-permute-start.1 = (s32[6,2]{1,0:T(8,128)S(1)}, s32[6,2]{1,0:T(8,128)S(1)}, u32[]{:S(2)}, u32[]{:S(2)}) collective-permute-start(s32[6,2]{1,0:T(8,128)S(1)} %copy.16), channel_id=1, source_target_pairs={{0,1},{1,2},{2,3},{4,5},{5,6},{6,7},{8,9},{9,10},{10,11},{12,13},{... | collective-permute-start | bytes 152 | tf_op jit(solution)/shard_map/ppermute | solution.py:24
  14.1 3.4 %fusion.7.amp_hbm = f32[6,256,256]{2,1,0:T(8,128)} fusion(f32[6,256,256]{2,1,0:T(8,128)} %fusion.2, f32[256,256,1]{1,0,2:T(8,128)S(1)} %copy-done.5), kind=kOutput, calls=%fused_computation.21 | convolution fusion | flops 603979776 | bytes 3407872 | tf_op jit(solution)/shard_map/cb,sab->sac/dot_general | solution.py:92
  17.5 2.3 %collective-permute-done.right_any = f32[2,256,256]{2,1,0:T(8,128)S(1)} collective-permute-done((f32[2,256,256]{2,1,0:T(8,128)}, f32[2,256,256]{2,1,0:T(8,128)S(1)}, u32[]{:S(2)}, u32[]{:S(2)}) %collective-permute-start) | collective-permute-done | bytes 524320 | tf_op jit(solution)/shard_map/ppermute | solution.py:24
  19.8 1.3 %collective-permute-start.4 = (f32[2,256,256]{2,1,0:T(8,128)S(1)}, f32[2,256,256]{2,1,0:T(8,128)}, u32[]{:S(2)}, u32[]{:S(2)}) collective-permute-start(f32[2,256,256]{2,1,0:T(8,128)S(1)} %collective-permute-done.right_any), channel_id=1, source_target_pairs={{4,0},{5,1},{6,2},{7,3},{8,4},{9,5},{10,6},{11,7},{12,8},{13,9},{1... | collective-permute-start | bytes 1572872 | tf_op jit(solution)/shard_map/ppermute | solution.py:24
  21.1 0.1 copy.20.spots_ref
  21.2 0.1 copy.19.counts_ref
  21.3 0.1 copy.17
  21.4 0.1 pad_add_fusion
  21.5 0.1 copy.18
  21.6 3.0 %collective-permute-start.2 = (s32[12,2]{1,0:T(8,128)S(1)}, s32[12,2]{1,0:T(8,128)S(1)}, u32[]{:S(2)}, u32[]{:S(2)}) collective-permute-start(s32[12,2]{1,0:T(8,128)S(1)} %copy.18), channel_id=1, source_target_pairs={{0,4},{1,5},{2,6},{3,7},{4,8},{5,9},{6,10},{7,11},{8,12},{9,13},{1... | collective-permute-start | bytes 296 | tf_op jit(solution)/shard_map/ppermute | solution.py:24
  24.6 1.7 %add_reduce_fusion.lit_ref = f32[256,256]{1,0:T(8,128)S(1)} fusion(f32[2,4,256,256]{3,2,1,0:T(8,128)} %probe_ref.1), kind=kLoop, calls=%fused_computation.3 | loop fusion | flops 983040 | bytes 2359296 | tf_op jit(solution)/shard_map/reduce_sum | solution.py:410
  26.3 1.8 %lighting.1 = (f32[256,512]{1,0:T(8,128)S(1)}, f32[8,256]{1,0:T(8,128)S(1)}) custom-call(s32[8,4]{1,0:T(8,128)S(1)} %copy.19.counts_ref, s32[6,2]{1,0:T(8,128)S(1)} %copy.20.spots_ref, s32[6,2]{1,0:T(8,128)S(1)} %collective-permute-done.1.left_ref, s32[6,2]{1,0:T(8,128)S(1)} %get-tuple-element.73.up_ref, s32[6,2]{1,0:T(8,128)S(1)} %get-tuple-element.72.diag_ref, ...), custom_call_target="tpu_custom_call" | custom-call | flops 100000000 | bytes 10000000 | tf_op jit(solution)/shard_map/lighting/pallas_call | solution.py:411
  28.1 12.7 %positions.1 = (f32[2,256,512]{2,1,0:T(8,128)}, f32[2,256,768]{2,1,0:T(8,128)S(1)}, f32[2,256,256]{2,1,0:T(8,128)S(1)}, f32[1152,256]{1,0:T(8,128)S(1)}, f32[1152,256]{1,0:T(8,128)S(1)}) custom-call(s32[8,4]{1,0:T(8,128)S(1)} %copy.19.counts_ref, s32[6,2]{1,0:T(8,128)S(1)} %copy.20.spots_ref, f32[2,256,512]{2,1,0:T(8,128)} %tile_ref.1, ...), custom_call_target="tpu_custom_call" | custom-call | flops 7000000000 | bytes 20000000 | tf_op jit(solution)/shard_map/positions/pallas_call | solution.py:424
  40.8 2.5 %collective-permute-start.5 = (f32[1152,256]{1,0:T(8,128)S(1)}, f32[1152,256]{1,0:T(8,128)S(1)}, u32[]{:S(2)}, u32[]{:S(2)}) collective-permute-start(f32[1152,256]{1,0:T(8,128)S(1)} %get-tuple-element.48), channel_id=1, source_target_pairs={{0,4},{1,5},{2,6},{3,7},{4,0},{5,1},{6,2},{7,3},{8,12},{9,13},{10,... | collective-permute-start | bytes 3538952 | tf_op jit(solution)/shard_map/ppermute | solution.py:30
  43.4 2.5 %collective-permute-done.5.refs_1_ = f32[1152,256]{1,0:T(8,128)S(1)} collective-permute-done((f32[1152,256]{1,0:T(8,128)S(1)}, f32[1152,256]{1,0:T(8,128)S(1)}, u32[]{:S(2)}, u32[]{:S(2)}) %collective-permute-start.5) | collective-permute-done | bytes 1179680 | tf_op jit(solution)/shard_map/ppermute | solution.py:30
  45.8 0.2 fold.4
  46.0 5.0 %collective-permute-start.6 = (f32[576,256]{1,0:T(8,128)S(1)}, f32[576,256]{1,0:T(8,128)S(1)}, u32[]{:S(2)}, u32[]{:S(2)}) collective-permute-start(f32[576,256]{1,0:T(8,128)S(1)} %get-tuple-element.50), channel_id=1, source_target_pairs={{0,8},{1,9},{2,10},{3,11},{4,20},{5,21},{6,22},{7,23},{8,0},{9,1},... | collective-permute-start | bytes 1769480 | tf_op jit(solution)/shard_map/ppermute | solution.py:71
  51.0 7.9 %collective-permute-done.6.refs_1_ = f32[576,256]{1,0:T(8,128)S(1)} collective-permute-done((f32[576,256]{1,0:T(8,128)S(1)}, f32[576,256]{1,0:T(8,128)S(1)}, u32[]{:S(2)}, u32[]{:S(2)}) %collective-permute-start.6) | collective-permute-done | bytes 589856 | tf_op jit(solution)/shard_map/ppermute | solution.py:71
  58.9 0.1 fold.5
  58.9 8.5 %collective-permute-start.7 = (f32[288,256]{1,0:T(8,128)S(1)}, f32[288,256]{1,0:T(8,128)S(1)}, u32[]{:S(2)}, u32[]{:S(2)}) collective-permute-start(f32[288,256]{1,0:T(8,128)S(1)} %get-tuple-element.52), channel_id=1, source_target_pairs={{0,16},{1,17},{2,18},{3,19},{4,12},{5,13},{6,14},{7,15},{8,24},{9,... | collective-permute-start | bytes 884744 | tf_op jit(solution)/shard_map/ppermute | solution.py:71
  67.4 4.7 %collective-permute-done.7.refs_1_ = f32[288,256]{1,0:T(8,128)S(1)} collective-permute-done((f32[288,256]{1,0:T(8,128)S(1)}, f32[288,256]{1,0:T(8,128)S(1)}, u32[]{:S(2)}, u32[]{:S(2)}) %collective-permute-start.7) | collective-permute-done | bytes 294944 | tf_op jit(solution)/shard_map/ppermute | solution.py:71
  72.2 1.7 %collective-permute-start.13 = (f32[2,256,768]{2,1,0:T(8,128)S(1)}, f32[2,256,768]{2,1,0:T(8,128)S(1)}, u32[]{:S(2)}, u32[]{:S(2)}) collective-permute-start(f32[2,256,768]{2,1,0:T(8,128)S(1)} %get-tuple-element.62), channel_id=1, source_target_pairs={{0,4},{1,5},{2,6},{3,7},{4,8},{5,9},{6,10},{7,11},{8,12},{9,13},{1... | collective-permute-start | bytes 4718600 | tf_op jit(solution)/shard_map/ppermute | solution.py:24
  73.8 0.1 collective-permute-start.8
  73.9 6.6 %collective-permute-done.8.refs_1_ = f32[152,256]{1,0:T(8,128)S(1)} collective-permute-done((f32[152,256]{1,0:T(8,128)S(1)}, f32[152,256]{1,0:T(8,128)S(1)}, u32[]{:S(2)}, u32[]{:S(2)}) %collective-permute-start.8) | collective-permute-done | bytes 155680 | tf_op jit(solution)/shard_map/ppermute | solution.py:30
  80.5 2.3 %collective-permute-start.9 = (f32[80,256]{1,0:T(8,128)S(1)}, f32[80,256]{1,0:T(8,128)S(1)}, u32[]{:S(2)}, u32[]{:S(2)}) collective-permute-start(f32[80,256]{1,0:T(8,128)S(1)} %get-tuple-element.60), channel_id=1, source_target_pairs={{0,2},{1,3},{2,0},{3,1},{4,6},{5,7},{6,4},{7,5},{8,10},{9,11},{10,... | collective-permute-start | bytes 245768 | tf_op jit(solution)/shard_map/ppermute | solution.py:30
  82.8 4.3 %collective-permute-done.9 = f32[80,256]{1,0:T(8,128)S(1)} collective-permute-done((f32[80,256]{1,0:T(8,128)S(1)}, f32[80,256]{1,0:T(8,128)S(1)}, u32[]{:S(2)}, u32[]{:S(2)}) %collective-permute-start.9) | collective-permute-done | bytes 81952 | tf_op jit(solution)/shard_map/ppermute | solution.py:30
  87.2 1.1 collective-permute-start.10
  88.2 1.5 %collective-permute-start.12 = (f32[72,256]{1,0:T(8,128)S(1)}, f32[72,256]{1,0:T(8,128)S(1)}, u32[]{:S(2)}, u32[]{:S(2)}) collective-permute-start(f32[72,256]{1,0:T(8,128)S(1)} %get-tuple-element.71), channel_id=1, source_target_pairs={{0,3},{1,2},{2,1},{3,0},{4,7},{5,6},{6,5},{7,4},{8,11},{9,10},{10,... | collective-permute-start | bytes 221192 | tf_op jit(solution)/shard_map/ppermute | solution.py:30
  89.8 0.9 collective-permute-start.11
  90.7 4.6 %collective-permute-done.10 = f32[72,256]{1,0:T(8,128)S(1)} collective-permute-done((f32[72,256]{1,0:T(8,128)S(1)}, f32[72,256]{1,0:T(8,128)S(1)}, u32[]{:S(2)}, u32[]{:S(2)}) %collective-permute-start.10) | collective-permute-done | bytes 73760 | tf_op jit(solution)/shard_map/ppermute | solution.py:30
  95.3 0.2 collective-permute-done.11
  95.5 0.1 slice_add_fusion
  95.6 1.6 %collective-permute-start.14 = (f32[296,256]{1,0:T(8,128)S(1)}, f32[296,256]{1,0:T(8,128)S(1)}, u32[]{:S(2)}, u32[]{:S(2)}) collective-permute-start(f32[296,256]{1,0:T(8,128)S(1)} %constant_dynamic-update-slice_fusion.refs_0_), channel_id=1, source_target_pairs={{0,16},{1,17},{2,18},{3,19},{4,12},{5,13},{6,14},{7,15},{8,24},{9,... | collective-permute-start | bytes 909320 | tf_op jit(solution)/shard_map/ppermute | solution.py:71
  97.2 2.2 %collective-permute-start.17 = (f32[2,256,256]{2,1,0:T(8,128)S(1)}, f32[2,256,256]{2,1,0:T(8,128)S(1)}, u32[]{:S(2)}, u32[]{:S(2)}) collective-permute-start(f32[2,256,256]{2,1,0:T(8,128)S(1)} %slice_add_fusion), channel_id=1, source_target_pairs={{0,1},{1,2},{2,3},{4,5},{5,6},{6,7},{8,9},{9,10},{10,11},{12,13},{... | collective-permute-start | bytes 1572872 | tf_op jit(solution)/shard_map/ppermute | solution.py:24
  99.4 0.3 collective-permute-start.15
  99.8 4.8 %collective-permute-done.14.refs_1_ = f32[296,256]{1,0:T(8,128)S(1)} collective-permute-done((f32[296,256]{1,0:T(8,128)S(1)}, f32[296,256]{1,0:T(8,128)S(1)}, u32[]{:S(2)}, u32[]{:S(2)}) %collective-permute-start.14) | collective-permute-done | bytes 303136 | tf_op jit(solution)/shard_map/ppermute | solution.py:71
  104.5 0.5 collective-permute-start.19
  105.0 1.3 %collective-permute-done.15.refs_2_ = f32[296,256]{1,0:T(8,128)S(1)} collective-permute-done((f32[296,256]{1,0:T(8,128)S(1)}, f32[296,256]{1,0:T(8,128)S(1)}, u32[]{:S(2)}, u32[]{:S(2)}) %collective-permute-start.15) | collective-permute-done | bytes 303136 | tf_op jit(solution)/shard_map/ppermute | solution.py:71
  106.3 3.4 %collective-permute-done.17.g_left = f32[2,256,256]{2,1,0:T(8,128)S(1)} collective-permute-done((f32[2,256,256]{2,1,0:T(8,128)S(1)}, f32[2,256,256]{2,1,0:T(8,128)S(1)}, u32[]{:S(2)}, u32[]{:S(2)}) %collective-permute-start.17) | collective-permute-done | bytes 524320 | tf_op jit(solution)/shard_map/ppermute | solution.py:24
  109.8 1.6 %collective-permute-done.16.refs_3_ = f32[296,256]{1,0:T(8,128)S(1)} collective-permute-done((f32[296,256]{1,0:T(8,128)S(1)}, f32[296,256]{1,0:T(8,128)S(1)}, u32[]{:S(2)}, u32[]{:S(2)}) %collective-permute-start.16) | collective-permute-done | bytes 303136 | tf_op jit(solution)/shard_map/ppermute | solution.py:71
  111.4 1.6 %collective-permute-done.21.refs_7_ = f32[296,256]{1,0:T(8,128)S(1)} collective-permute-done((f32[296,256]{1,0:T(8,128)S(1)}, f32[296,256]{1,0:T(8,128)S(1)}, u32[]{:S(2)}, u32[]{:S(2)}) %collective-permute-start.21) | collective-permute-done | bytes 303136 | tf_op jit(solution)/shard_map/ppermute | solution.py:30
  113.0 2.3 %update.1 = (f32[2,256,512]{2,1,0:T(8,128)}, f32[2,4,256,256]{3,2,1,0:T(8,128)}) custom-call(f32[2,256,512]{2,1,0:T(8,128)S(1)} %copy-done.3, f32[256,512]{1,0:T(8,128)S(1)} %get-tuple-element.40.light_ref, f32[8,256]{1,0:T(8,128)S(1)} %slice_maximum_fusion.top_ref, f32[2,256,512]{2,1,0:T(8,128)S(1)} %copy-done.4, ...), custom_call_target="tpu_custom_call" | custom-call | flops 1000000 | bytes 10000000 | tf_op jit(solution)/shard_map/update/pallas_call | solution.py:484
  (37 shorter events, 0.2 us)
Async XLA Ops:
  0.6 3.4 %copy-start = (f32[1,1,6,256,256]{4,3,2,1,0:T(8,128)S(1)}, f32[1,1,6,256,256]{4,3,2,1,0:T(8,128)}, u32[]{:S(2)}) copy-start(f32[1,1,6,256,256]{4,3,2,1,0:T(8,128)} %param.10) | copy-start | bytes 4718596
  2.6 4.4 %copy-start.2 = (f32[2,256,512]{2,1,0:T(8,128)S(1)}, f32[2,256,512]{2,1,0:T(8,128)}, u32[]{:S(2)}) copy-start(f32[2,256,512]{2,1,0:T(8,128)} %tile_ref.1) | copy-start | bytes 3145732
  2.6 5.6 %copy-start.6 = (s32[1,1,6,2]{2,3,1,0:T(2,128)S(1)}, s32[1,1,6,2]{2,3,1,0:T(2,128)}, u32[]{:S(2)}) copy-start(s32[1,1,6,2]{2,3,1,0:T(2,128)} %param.11) | copy-start | bytes 148
  2.6 11.4 %copy-start.5 = (f32[256,256,1]{1,0,2:T(8,128)S(1)}, f32[256,256,1]{1,0,2:T(8,128)}, u32[]{:S(2)}) copy-start(f32[256,256,1]{1,0,2:T(8,128)} %constant.10) | copy-start | bytes 786436
  2.6 17.2 %collective-permute-start = (f32[2,256,256]{2,1,0:T(8,128)}, f32[2,256,256]{2,1,0:T(8,128)S(1)}, u32[]{:S(2)}, u32[]{:S(2)}) collective-permute-start(f32[2,256,256]{2,1,0:T(8,128)} %slice.50), channel_id=1, source_target_pairs={{1,0},{2,1},{3,2},{5,4},{6,5},{7,6},{9,8},{10,9},{11,10},{13,12},{... | collective-permute-start | bytes 1572872 | tf_op jit(solution)/shard_map/ppermute | solution.py:24
  7.0 21.1 %collective-permute-start.3 = (f32[2,256,512]{2,1,0:T(8,128)S(1)}, f32[2,256,512]{2,1,0:T(8,128)}, u32[]{:S(2)}, u32[]{:S(2)}) collective-permute-start(f32[2,256,512]{2,1,0:T(8,128)S(1)} %copy-done.2), channel_id=1, source_target_pairs={{4,0},{5,1},{6,2},{7,3},{8,4},{9,5},{10,6},{11,7},{12,8},{13,9},{1... | collective-permute-start | bytes 3145736 | tf_op jit(solution)/shard_map/ppermute | solution.py:24
  8.4 12.8 %copy-start.7 = (s32[8,4]{0,1:T(4,128)S(1)}, s32[8,4]{0,1:T(4,128)}, u32[]{:S(2)}) copy-start(s32[8,4]{0,1:T(4,128)} %param.12) | copy-start | bytes 388
  8.4 9.1 %collective-permute-start.1 = (s32[6,2]{1,0:T(8,128)S(1)}, s32[6,2]{1,0:T(8,128)S(1)}, u32[]{:S(2)}, u32[]{:S(2)}) collective-permute-start(s32[6,2]{1,0:T(8,128)S(1)} %copy.16), channel_id=1, source_target_pairs={{0,1},{1,2},{2,3},{4,5},{5,6},{6,7},{8,9},{9,10},{10,11},{12,13},{... | collective-permute-start | bytes 152 | tf_op jit(solution)/shard_map/ppermute | solution.py:24
  19.8 8.3 %collective-permute-start.4 = (f32[2,256,256]{2,1,0:T(8,128)S(1)}, f32[2,256,256]{2,1,0:T(8,128)}, u32[]{:S(2)}, u32[]{:S(2)}) collective-permute-start(f32[2,256,256]{2,1,0:T(8,128)S(1)} %collective-permute-done.right_any), channel_id=1, source_target_pairs={{4,0},{5,1},{6,2},{7,3},{8,4},{9,5},{10,6},{11,7},{12,8},{13,9},{1... | collective-permute-start | bytes 1572872 | tf_op jit(solution)/shard_map/ppermute | solution.py:24
  21.6 4.7 %collective-permute-start.2 = (s32[12,2]{1,0:T(8,128)S(1)}, s32[12,2]{1,0:T(8,128)S(1)}, u32[]{:S(2)}, u32[]{:S(2)}) collective-permute-start(s32[12,2]{1,0:T(8,128)S(1)} %copy.18), channel_id=1, source_target_pairs={{0,4},{1,5},{2,6},{3,7},{4,8},{5,9},{6,10},{7,11},{8,12},{9,13},{1... | collective-permute-start | bytes 296 | tf_op jit(solution)/shard_map/ppermute | solution.py:24
  40.8 5.0 %collective-permute-start.5 = (f32[1152,256]{1,0:T(8,128)S(1)}, f32[1152,256]{1,0:T(8,128)S(1)}, u32[]{:S(2)}, u32[]{:S(2)}) collective-permute-start(f32[1152,256]{1,0:T(8,128)S(1)} %get-tuple-element.48), channel_id=1, source_target_pairs={{0,4},{1,5},{2,6},{3,7},{4,0},{5,1},{6,2},{7,3},{8,12},{9,13},{10,... | collective-permute-start | bytes 3538952 | tf_op jit(solution)/shard_map/ppermute | solution.py:30
  46.0 12.9 %collective-permute-start.6 = (f32[576,256]{1,0:T(8,128)S(1)}, f32[576,256]{1,0:T(8,128)S(1)}, u32[]{:S(2)}, u32[]{:S(2)}) collective-permute-start(f32[576,256]{1,0:T(8,128)S(1)} %get-tuple-element.50), channel_id=1, source_target_pairs={{0,8},{1,9},{2,10},{3,11},{4,20},{5,21},{6,22},{7,23},{8,0},{9,1},... | collective-permute-start | bytes 1769480 | tf_op jit(solution)/shard_map/ppermute | solution.py:71
  58.9 54.1 %copy-start.4 = (f32[2,256,512]{2,1,0:T(8,128)S(1)}, f32[2,256,512]{2,1,0:T(8,128)}, u32[]{:S(2)}) copy-start(f32[2,256,512]{2,1,0:T(8,128)} %get-tuple-element.67.g_tile) | copy-start | bytes 3145732
  58.9 13.2 %collective-permute-start.7 = (f32[288,256]{1,0:T(8,128)S(1)}, f32[288,256]{1,0:T(8,128)S(1)}, u32[]{:S(2)}, u32[]{:S(2)}) collective-permute-start(f32[288,256]{1,0:T(8,128)S(1)} %get-tuple-element.52), channel_id=1, source_target_pairs={{0,16},{1,17},{2,18},{3,19},{4,12},{5,13},{6,14},{7,15},{8,24},{9,... | collective-permute-start | bytes 884744 | tf_op jit(solution)/shard_map/ppermute | solution.py:71
  72.1 40.8 %copy-start.1 = (f32[2,4,256,256]{3,2,1,0:T(8,128)S(1)}, f32[2,4,256,256]{3,2,1,0:T(8,128)}, u32[]{:S(2)}) copy-start(f32[2,4,256,256]{3,2,1,0:T(8,128)} %probe_ref.1) | copy-start | bytes 6291460
  72.1 40.8 %copy-start.3 = (f32[2,256,512]{2,1,0:T(8,128)S(1)}, f32[2,256,512]{2,1,0:T(8,128)}, u32[]{:S(2)}) copy-start(f32[2,256,512]{2,1,0:T(8,128)} %tile_ref.1) | copy-start | bytes 3145732
  72.2 23.4 %collective-permute-start.13 = (f32[2,256,768]{2,1,0:T(8,128)S(1)}, f32[2,256,768]{2,1,0:T(8,128)S(1)}, u32[]{:S(2)}, u32[]{:S(2)}) collective-permute-start(f32[2,256,768]{2,1,0:T(8,128)S(1)} %get-tuple-element.62), channel_id=1, source_target_pairs={{0,4},{1,5},{2,6},{3,7},{4,8},{5,9},{6,10},{7,11},{8,12},{9,13},{1... | collective-permute-start | bytes 4718600 | tf_op jit(solution)/shard_map/ppermute | solution.py:24
  73.8 6.6 %collective-permute-start.8 = (f32[152,256]{1,0:T(8,128)S(1)}, f32[152,256]{1,0:T(8,128)S(1)}, u32[]{:S(2)}, u32[]{:S(2)}) collective-permute-start(f32[152,256]{1,0:T(8,128)S(1)} %get-tuple-element.57), channel_id=1, source_target_pairs={{0,1},{1,0},{2,3},{3,2},{4,5},{5,4},{6,7},{7,6},{8,9},{9,8},{10,11... | collective-permute-start | bytes 466952 | tf_op jit(solution)/shard_map/ppermute | solution.py:30
  80.5 6.7 %collective-permute-start.9 = (f32[80,256]{1,0:T(8,128)S(1)}, f32[80,256]{1,0:T(8,128)S(1)}, u32[]{:S(2)}, u32[]{:S(2)}) collective-permute-start(f32[80,256]{1,0:T(8,128)S(1)} %get-tuple-element.60), channel_id=1, source_target_pairs={{0,2},{1,3},{2,0},{3,1},{4,6},{5,7},{6,4},{7,5},{8,10},{9,11},{10,... | collective-permute-start | bytes 245768 | tf_op jit(solution)/shard_map/ppermute | solution.py:30
  87.2 8.1 %collective-permute-start.10 = (f32[72,256]{1,0:T(8,128)S(1)}, f32[72,256]{1,0:T(8,128)S(1)}, u32[]{:S(2)}, u32[]{:S(2)}) collective-permute-start(f32[72,256]{1,0:T(8,128)S(1)} %get-tuple-element.71), channel_id=1, source_target_pairs={{0,2},{1,3},{2,0},{3,1},{4,6},{5,7},{6,4},{7,5},{8,10},{9,11},{10,... | collective-permute-start | bytes 221192 | tf_op jit(solution)/shard_map/ppermute | solution.py:30
  88.2 7.3 %collective-permute-start.12 = (f32[72,256]{1,0:T(8,128)S(1)}, f32[72,256]{1,0:T(8,128)S(1)}, u32[]{:S(2)}, u32[]{:S(2)}) collective-permute-start(f32[72,256]{1,0:T(8,128)S(1)} %get-tuple-element.71), channel_id=1, source_target_pairs={{0,3},{1,2},{2,1},{3,0},{4,7},{5,6},{6,5},{7,4},{8,11},{9,10},{10,... | collective-permute-start | bytes 221192 | tf_op jit(solution)/shard_map/ppermute | solution.py:30
  89.8 5.7 %collective-permute-start.11 = (f32[72,256]{1,0:T(8,128)S(1)}, f32[72,256]{1,0:T(8,128)S(1)}, u32[]{:S(2)}, u32[]{:S(2)}) collective-permute-start(f32[72,256]{1,0:T(8,128)S(1)} %get-tuple-element.71), channel_id=1, source_target_pairs={{0,1},{1,0},{2,3},{3,2},{4,5},{5,4},{6,7},{7,6},{8,9},{9,8},{10,11... | collective-permute-start | bytes 221192 | tf_op jit(solution)/shard_map/ppermute | solution.py:30
  95.6 8.9 %collective-permute-start.14 = (f32[296,256]{1,0:T(8,128)S(1)}, f32[296,256]{1,0:T(8,128)S(1)}, u32[]{:S(2)}, u32[]{:S(2)}) collective-permute-start(f32[296,256]{1,0:T(8,128)S(1)} %constant_dynamic-update-slice_fusion.refs_0_), channel_id=1, source_target_pairs={{0,16},{1,17},{2,18},{3,19},{4,12},{5,13},{6,14},{7,15},{8,24},{9,... | collective-permute-start | bytes 909320 | tf_op jit(solution)/shard_map/ppermute | solution.py:71
  97.2 12.6 %collective-permute-start.17 = (f32[2,256,256]{2,1,0:T(8,128)S(1)}, f32[2,256,256]{2,1,0:T(8,128)S(1)}, u32[]{:S(2)}, u32[]{:S(2)}) collective-permute-start(f32[2,256,256]{2,1,0:T(8,128)S(1)} %slice_add_fusion), channel_id=1, source_target_pairs={{0,1},{1,2},{2,3},{4,5},{5,6},{6,7},{8,9},{9,10},{10,11},{12,13},{... | collective-permute-start | bytes 1572872 | tf_op jit(solution)/shard_map/ppermute | solution.py:24
  99.4 6.9 %collective-permute-start.15 = (f32[296,256]{1,0:T(8,128)S(1)}, f32[296,256]{1,0:T(8,128)S(1)}, u32[]{:S(2)}, u32[]{:S(2)}) collective-permute-start(f32[296,256]{1,0:T(8,128)S(1)} %constant_dynamic-update-slice_fusion.refs_0_), channel_id=1, source_target_pairs={{0,8},{1,9},{2,10},{3,11},{4,20},{5,21},{6,22},{7,23},{8,0},{9,1},... | collective-permute-start | bytes 909320 | tf_op jit(solution)/shard_map/ppermute | solution.py:71
  104.5 6.8 %collective-permute-start.16 = (f32[296,256]{1,0:T(8,128)S(1)}, f32[296,256]{1,0:T(8,128)S(1)}, u32[]{:S(2)}, u32[]{:S(2)}) collective-permute-start(f32[296,256]{1,0:T(8,128)S(1)} %collective-permute-done.14.refs_1_), channel_id=1, source_target_pairs={{0,8},{1,9},{2,10},{3,11},{4,20},{5,21},{6,22},{7,23},{8,0},{9,1},... | collective-permute-start | bytes 909320 | tf_op jit(solution)/shard_map/ppermute | solution.py:71
  104.5 6.8 %collective-permute-start.18 = (f32[296,256]{1,0:T(8,128)S(1)}, f32[296,256]{1,0:T(8,128)S(1)}, u32[]{:S(2)}, u32[]{:S(2)}) collective-permute-start(f32[296,256]{1,0:T(8,128)S(1)} %constant_dynamic-update-slice_fusion.refs_0_), channel_id=1, source_target_pairs={{0,4},{1,5},{2,6},{3,7},{4,0},{5,1},{6,2},{7,3},{8,12},{9,13},{10,... | collective-permute-start | bytes 909320 | tf_op jit(solution)/shard_map/ppermute | solution.py:30
  104.5 6.8 %collective-permute-start.19 = (f32[296,256]{1,0:T(8,128)S(1)}, f32[296,256]{1,0:T(8,128)S(1)}, u32[]{:S(2)}, u32[]{:S(2)}) collective-permute-start(f32[296,256]{1,0:T(8,128)S(1)} %collective-permute-done.14.refs_1_), channel_id=1, source_target_pairs={{0,4},{1,5},{2,6},{3,7},{4,0},{5,1},{6,2},{7,3},{8,12},{9,13},{10,... | collective-permute-start | bytes 909320 | tf_op jit(solution)/shard_map/ppermute | solution.py:30
  106.3 5.0 %collective-permute-start.20 = (f32[296,256]{1,0:T(8,128)S(1)}, f32[296,256]{1,0:T(8,128)S(1)}, u32[]{:S(2)}, u32[]{:S(2)}) collective-permute-start(f32[296,256]{1,0:T(8,128)S(1)} %collective-permute-done.15.refs_2_), channel_id=1, source_target_pairs={{0,4},{1,5},{2,6},{3,7},{4,0},{5,1},{6,2},{7,3},{8,12},{9,13},{10,... | collective-permute-start | bytes 909320 | tf_op jit(solution)/shard_map/ppermute | solution.py:30
  111.3 1.6 %collective-permute-start.21 = (f32[296,256]{1,0:T(8,128)S(1)}, f32[296,256]{1,0:T(8,128)S(1)}, u32[]{:S(2)}, u32[]{:S(2)}) collective-permute-start(f32[296,256]{1,0:T(8,128)S(1)} %collective-permute-done.16.refs_3_), channel_id=1, source_target_pairs={{0,4},{1,5},{2,6},{3,7},{4,0},{5,1},{6,2},{7,3},{8,12},{9,13},{10,... | collective-permute-start | bytes 909320 | tf_op jit(solution)/shard_map/ppermute | solution.py:30

commit v13 on v12

--- a/solution.py
+++ b/solution.py
@@ -84,12 +84,33 @@
     return jnp.asarray(np.stack(blocks + [block.T for block in blocks]), jnp.bfloat16)
 
 
-def evens_first(amplitudes, rows):
-    side = amplitudes.shape[-1]
+def reorder_kernel(amp_ref, pick_ref, out_ref):
+    def split(value):
+        high = value.astype(jnp.bfloat16)
+        return high, (value - high.astype(jnp.float32)).astype(jnp.bfloat16)
+
+    def dot(a, b):
+        return jnp.dot(a, b, preferred_element_type=jnp.float32)
+
+    rows = sum(dot(pick_ref[0], part) for part in split(amp_ref[0]))
+    out_ref[0] = sum(dot(part, pick_ref[1]) for part in split(rows))
+
+
+def evens_first(amplitudes):
+    slots, side, _ = amplitudes.shape
     order = np.concatenate([np.arange(0, side, 2), np.arange(1, side, 2)])
-    pick = jnp.asarray(np.eye(side)[order], jnp.float32)
-    form = "ab,sbc->sac" if rows else "cb,sab->sac"
-    return jnp.einsum(form, pick, amplitudes, precision=lax.Precision.HIGH)
+    pick = np.eye(side)[order]
+    spec = pl.BlockSpec((1, side, side), lambda p: (p, 0, 0))
+    return pl.pallas_call(
+        reorder_kernel,
+        grid=(slots,),
+        out_shape=f32(slots, side, side),
+        in_specs=[spec, pl.BlockSpec((2, side, side), lambda p: (0, 0, 0))],
+        out_specs=spec,
+        compiler_params=params(8),
+        cost_estimate=cost(slots * 8 * side**3, 8 * slots * side * side),
+        name="reorder",
+    )(amplitudes, jnp.asarray(np.stack([pick, pick.T]), jnp.bfloat16))
 
 
 def corner_of(row, col):
@@ -399,14 +420,13 @@
     spots = corners[0, 0]
 
     right = shifted(object_field[:, :, :side], 0, -1)
-    measured = evens_first(amplitudes[0, 0], True)
+    measured = evens_first(amplitudes[0, 0])
     tile, measured, spots_now = lax.optimization_barrier((object_field, measured, spots))
     below = shifted(tile[:, :side, :], -1, 0)
     from_left = shifted(spots_now, 0, 1)
-    measured = evens_first(measured, False)
-    right, from_left, measured, modes_now = lax.optimization_barrier((right, from_left, measured, probe))
+    from_up = shifted(jnp.concatenate([spots_now, from_left], axis=0), 1, 0)
+    right, from_up, measured, modes_now = lax.optimization_barrier((right, from_up, measured, probe))
     corner = shifted(right[:, :side, :], -1, 0)
-    from_up = shifted(jnp.concatenate([spots, from_left], axis=0), 1, 0)
     lit = jnp.sum(modes_now[0] * modes_now[0] + modes_now[1] * modes_now[1], axis=0)
     light, top = pl.pallas_call(
         light_kernel,

time: 116 us -> 121 us (1.043)
  Pallas kernels: 17.1 us -> 26.2 us
  matrix products: 6.33 us -> 0 us
  local copies, waits for them, and re-layouts: 2.51 us -> 5.68 us
  starting transfers between devices: 40.9 us -> 43.4 us
  waiting for transfers between devices: 45.7 us -> 43.7 us
  other arithmetic: 1.88 us -> 0.25 us
    dot_general x2 -> x0, matrix products: 6.33 us -> none  [evens_first(): return jnp.einsum(form, pick, amplitudes, precision=lax.Precision.HIGH)]
    pallas_call x1, Pallas kernels: 12.7 us -> 18.6 us  [body(): pl.pallas_call(main_kernel, out_shape=(hbm(2, rows, cols), vmem(2, side,...]
    ppermute x5, waiting for transfers between devices: 20.2 us -> 15 us  [flipped(): return lax.ppermute(value, ('row', 'col'), pairs)]
    unnamed x20 -> x24, local copies, waits for them, and re-layouts: 0.14 us -> 3.62 us
    pallas_call x0 -> x1, Pallas kernels: none -> 2.91 us  [evens_first(): pl.pallas_call(reorder_kernel, grid=(slots,), out_shape=f32(slots, side,...]
    ppermute x7, waiting for transfers between devices: 5.77 us -> 8.48 us  [shifted(): return lax.ppermute(value, ('row', 'col'), pairs)]
    ppermute x5, starting transfers between devices: 15.4 us -> 18 us  [flipped(): return lax.ppermute(value, ('row', 'col'), pairs)]
    reduce_sum x1, other arithmetic: 1.71 us -> 0.15 us  [body(): jnp.sum(modes_now[0] * modes_now[0] + modes_now[1] * modes_now[1], axis=0)]
  transfers between devices with their start and end apart: 22 -> 22, of which waited for: 13 -> 14; matrix products, arithmetic and copies ran while one was open for 7% -> 0% of each run, Pallas kernels for 2% -> 4%
where the time goes in v13:
time: 121 us; the launch traced here: 120 us
  waiting for transfers between devices  43.7 us (36%)
  starting transfers between devices  43.4 us (36%)
  Pallas kernels  26.2 us (22%)
  local copies, waits for them, and re-layouts  5.68 us (5%)
    ppermute x10, waiting for transfers between devices, swapped(): return lax.ppermute(value, ('row', 'col'), pairs)  20.2 us
    pallas_call x1, Pallas kernels, body(): pl.pallas_call(main_kernel, out_shape=(hbm(2, rows, cols), vmem(2, side,...  18.6 us
    ppermute x5, starting transfers between devices, flipped(): return lax.ppermute(value, ('row', 'col'), pairs)  18 us
    ppermute x7, starting transfers between devices, shifted(): return lax.ppermute(value, ('row', 'col'), pairs)  16.6 us
    ppermute x5, waiting for transfers between devices, flipped(): return lax.ppermute(value, ('row', 'col'), pairs)  15 us
    ppermute x10, starting transfers between devices, swapped(): return lax.ppermute(value, ('row', 'col'), pairs)  8.83 us
    ppermute x7, waiting for transfers between devices, shifted(): return lax.ppermute(value, ('row', 'col'), pairs)  8.48 us
    unnamed x24, local copies, waits for them, and re-layouts  3.62 us
  transfers between devices with their start and end apart: 22, of which 14 were waited for; matrix products, arithmetic and copies ran while one was open for 0% of the time, Pallas kernels for 4%

profile of v13, /device:TPU:0, one launch (start us, length us, event | category | flops | bytes accessed | tf_op | source)
XLA Modules:
  0.0 120.2 jit_solution(10246825888366669239)
XLA Ops:
  0.6 1.9 %slice.50 = f32[2,256,256]{2,1,0:T(8,128)} slice(f32[2,256,512]{2,1,0:T(8,128)} %tile_ref.1), slice={[0:2], [0:256], [0:256]} | slice | bytes 1048576 | tf_op jit(solution)/shard_map/slice | solution.py:422
  2.5 1.3 %collective-permute-start.1 = (f32[2,256,256]{2,1,0:T(8,128)}, f32[2,256,256]{2,1,0:T(8,128)}, u32[]{:S(2)}, u32[]{:S(2)}) collective-permute-start(f32[2,256,256]{2,1,0:T(8,128)} %slice.50), channel_id=1, source_target_pairs={{1,0},{2,1},{3,2},{5,4},{6,5},{7,6},{9,8},{10,9},{11,10},{13,12},{... | collective-permute-start | bytes 1572872 | tf_op jit(solution)/shard_map/ppermute | solution.py:24
  3.8 1.4 %copy-done.4 = f32[1,1,6,256,256]{4,3,2,1,0:T(8,128)S(1)} copy-done((f32[1,1,6,256,256]{4,3,2,1,0:T(8,128)S(1)}, f32[1,1,6,256,256]{4,3,2,1,0:T(8,128)}, u32[]{:S(2)}) %copy-start.4) | copy-done | bytes 1572888
  5.2 0.9 copy-done.7
  6.2 2.9 %reorder.1.amp_hbm = f32[6,256,256]{2,1,0:T(8,128)S(1)} custom-call(f32[6,256,256]{2,1,0:T(8,128)S(1)} %bitcast.2, bf16[2,256,256]{2,1,0:T(8,128)(2,1)S(1)} %copy-done.7), custom_call_target="tpu_custom_call" | custom-call | flops 805306368 | bytes 3145728 | tf_op jit(solution)/shard_map/reorder/pallas_call | solution.py:104
  9.1 1.1 copy-done.5
  10.2 1.3 %collective-permute-start.3 = (f32[2,256,512]{2,1,0:T(8,128)S(1)}, f32[2,256,512]{2,1,0:T(8,128)}, u32[]{:S(2)}, u32[]{:S(2)}) collective-permute-start(f32[2,256,512]{2,1,0:T(8,128)S(1)} %copy-done.2), channel_id=1, source_target_pairs={{4,0},{5,1},{6,2},{7,3},{8,4},{9,5},{10,6},{11,7},{12,8},{13,9},{1... | collective-permute-start | bytes 3145736 | tf_op jit(solution)/shard_map/ppermute | solution.py:24
  11.5 0.1 copy.22
  11.6 5.5 %collective-permute-start = (s32[6,2]{1,0:T(8,128)S(1)}, s32[6,2]{1,0:T(8,128)S(1)}, u32[]{:S(2)}, u32[]{:S(2)}) collective-permute-start(s32[6,2]{1,0:T(8,128)S(1)} %copy.22), channel_id=1, source_target_pairs={{0,1},{1,2},{2,3},{4,5},{5,6},{6,7},{8,9},{9,10},{10,11},{12,13},{... | collective-permute-start | bytes 152 | tf_op jit(solution)/shard_map/ppermute | solution.py:24
  17.2 1.3 %collective-permute-done.left_ref = s32[6,2]{1,0:T(8,128)S(1)} collective-permute-done((s32[6,2]{1,0:T(8,128)S(1)}, s32[6,2]{1,0:T(8,128)S(1)}, u32[]{:S(2)}, u32[]{:S(2)}) %collective-permute-start) | collective-permute-done | bytes 80 | tf_op jit(solution)/shard_map/ppermute | solution.py:24
  18.5 2.2 %collective-permute-start.2 = (s32[12,2]{1,0:T(8,128)S(1)}, s32[12,2]{1,0:T(8,128)S(1)}, u32[]{:S(2)}, u32[]{:S(2)}) collective-permute-start(s32[12,2]{1,0:T(8,128)S(1)} %pad_add_fusion), channel_id=1, source_target_pairs={{0,4},{1,5},{2,6},{3,7},{4,8},{5,9},{6,10},{7,11},{8,12},{9,13},{1... | collective-permute-start | bytes 296 | tf_op jit(solution)/shard_map/ppermute | solution.py:24
  20.7 0.8 collective-permute-done.2
  21.5 1.3 %collective-permute-start.4 = (f32[2,256,256]{2,1,0:T(8,128)}, f32[2,256,256]{2,1,0:T(8,128)}, u32[]{:S(2)}, u32[]{:S(2)}) collective-permute-start(f32[2,256,256]{2,1,0:T(8,128)} %collective-permute-done.1.right_any), channel_id=1, source_target_pairs={{4,0},{5,1},{6,2},{7,3},{8,4},{9,5},{10,6},{11,7},{12,8},{13,9},{1... | collective-permute-start | bytes 1572872 | tf_op jit(solution)/shard_map/ppermute | solution.py:24
  22.8 0.1 copy.25.spots_ref
  22.9 0.1 copy.24.counts_ref
  22.9 0.1 add_reduce_fusion.lit_ref
  23.1 2.1 %lighting.1 = (f32[256,512]{1,0:T(8,128)S(1)}, f32[8,256]{1,0:T(8,128)S(1)}) custom-call(s32[8,4]{1,0:T(8,128)S(1)} %copy.24.counts_ref, s32[6,2]{1,0:T(8,128)S(1)} %copy.25.spots_ref, s32[6,2]{1,0:T(8,128)S(1)} %collective-permute-done.left_ref, s32[6,2]{1,0:T(8,128)S(1)} %get-tuple-element.73.up_ref, s32[6,2]{1,0:T(8,128)S(1)} %get-tuple-element.72.diag_ref, ...), custom_call_target="tpu_custom_call" | custom-call | flops 100000000 | bytes 10000000 | tf_op jit(solution)/shard_map/lighting/pallas_call | solution.py:431
  25.2 2.2 %collective-permute-done.4.corner_any = f32[2,256,256]{2,1,0:T(8,128)} collective-permute-done((f32[2,256,256]{2,1,0:T(8,128)}, f32[2,256,256]{2,1,0:T(8,128)}, u32[]{:S(2)}, u32[]{:S(2)}) %collective-permute-start.4) | collective-permute-done | bytes 524320 | tf_op jit(solution)/shard_map/ppermute | solution.py:24
  27.5 18.6 %positions.1 = (f32[2,256,512]{2,1,0:T(8,128)}, f32[2,256,768]{2,1,0:T(8,128)S(1)}, f32[2,256,256]{2,1,0:T(8,128)S(1)}, f32[1152,256]{1,0:T(8,128)S(1)}, f32[1152,256]{1,0:T(8,128)S(1)}) custom-call(s32[8,4]{1,0:T(8,128)S(1)} %copy.24.counts_ref, s32[6,2]{1,0:T(8,128)S(1)} %copy.25.spots_ref, f32[2,256,512]{2,1,0:T(8,128)} %tile_ref.1, ...), custom_call_target="tpu_custom_call" | custom-call | flops 7000000000 | bytes 20000000 | tf_op jit(solution)/shard_map/positions/pallas_call | solution.py:444
  46.1 2.1 %collective-permute-start.5 = (f32[1152,256]{1,0:T(8,128)S(1)}, f32[1152,256]{1,0:T(8,128)S(1)}, u32[]{:S(2)}, u32[]{:S(2)}) collective-permute-start(f32[1152,256]{1,0:T(8,128)S(1)} %get-tuple-element.48), channel_id=1, source_target_pairs={{0,4},{1,5},{2,6},{3,7},{4,0},{5,1},{6,2},{7,3},{8,12},{9,13},{10,... | collective-permute-start | bytes 3538952 | tf_op jit(solution)/shard_map/ppermute | solution.py:30
  48.2 2.5 %collective-permute-done.5.refs_1_ = f32[1152,256]{1,0:T(8,128)S(1)} collective-permute-done((f32[1152,256]{1,0:T(8,128)S(1)}, f32[1152,256]{1,0:T(8,128)S(1)}, u32[]{:S(2)}, u32[]{:S(2)}) %collective-permute-start.5) | collective-permute-done | bytes 1179680 | tf_op jit(solution)/shard_map/ppermute | solution.py:30
  50.7 0.2 fold.4
  50.8 6.0 %collective-permute-start.6 = (f32[576,256]{1,0:T(8,128)S(1)}, f32[576,256]{1,0:T(8,128)S(1)}, u32[]{:S(2)}, u32[]{:S(2)}) collective-permute-start(f32[576,256]{1,0:T(8,128)S(1)} %get-tuple-element.50), channel_id=1, source_target_pairs={{0,8},{1,9},{2,10},{3,11},{4,20},{5,21},{6,22},{7,23},{8,0},{9,1},... | collective-permute-start | bytes 1769480 | tf_op jit(solution)/shard_map/ppermute | solution.py:71
  56.9 7.9 %collective-permute-done.6.refs_1_ = f32[576,256]{1,0:T(8,128)S(1)} collective-permute-done((f32[576,256]{1,0:T(8,128)S(1)}, f32[576,256]{1,0:T(8,128)S(1)}, u32[]{:S(2)}, u32[]{:S(2)}) %collective-permute-start.6) | collective-permute-done | bytes 589856 | tf_op jit(solution)/shard_map/ppermute | solution.py:71
  64.7 0.1 fold.5
  64.8 6.5 %collective-permute-start.7 = (f32[288,256]{1,0:T(8,128)S(1)}, f32[288,256]{1,0:T(8,128)S(1)}, u32[]{:S(2)}, u32[]{:S(2)}) collective-permute-start(f32[288,256]{1,0:T(8,128)S(1)} %get-tuple-element.52), channel_id=1, source_target_pairs={{0,16},{1,17},{2,18},{3,19},{4,12},{5,13},{6,14},{7,15},{8,24},{9,... | collective-permute-start | bytes 884744 | tf_op jit(solution)/shard_map/ppermute | solution.py:71
  71.2 4.7 %collective-permute-done.7.refs_1_ = f32[288,256]{1,0:T(8,128)S(1)} collective-permute-done((f32[288,256]{1,0:T(8,128)S(1)}, f32[288,256]{1,0:T(8,128)S(1)}, u32[]{:S(2)}, u32[]{:S(2)}) %collective-permute-start.7) | collective-permute-done | bytes 294944 | tf_op jit(solution)/shard_map/ppermute | solution.py:71
  76.0 1.7 %collective-permute-start.13 = (f32[2,256,768]{2,1,0:T(8,128)S(1)}, f32[2,256,768]{2,1,0:T(8,128)S(1)}, u32[]{:S(2)}, u32[]{:S(2)}) collective-permute-start(f32[2,256,768]{2,1,0:T(8,128)S(1)} %get-tuple-element.62), channel_id=1, source_target_pairs={{0,4},{1,5},{2,6},{3,7},{4,8},{5,9},{6,10},{7,11},{8,12},{9,13},{1... | collective-permute-start | bytes 4718600 | tf_op jit(solution)/shard_map/ppermute | solution.py:24
  77.7 2.6 %collective-permute-start.8 = (f32[152,256]{1,0:T(8,128)S(1)}, f32[152,256]{1,0:T(8,128)S(1)}, u32[]{:S(2)}, u32[]{:S(2)}) collective-permute-start(f32[152,256]{1,0:T(8,128)S(1)} %get-tuple-element.57), channel_id=1, source_target_pairs={{0,1},{1,0},{2,3},{3,2},{4,5},{5,4},{6,7},{7,6},{8,9},{9,8},{10,11... | collective-permute-start | bytes 466952 | tf_op jit(solution)/shard_map/ppermute | solution.py:30
  80.3 4.8 %collective-permute-done.8.refs_1_ = f32[152,256]{1,0:T(8,128)S(1)} collective-permute-done((f32[152,256]{1,0:T(8,128)S(1)}, f32[152,256]{1,0:T(8,128)S(1)}, u32[]{:S(2)}, u32[]{:S(2)}) %collective-permute-start.8) | collective-permute-done | bytes 155680 | tf_op jit(solution)/shard_map/ppermute | solution.py:30
  85.1 0.1 collective-permute-start.9
  85.2 7.1 %collective-permute-done.9 = f32[80,256]{1,0:T(8,128)S(1)} collective-permute-done((f32[80,256]{1,0:T(8,128)S(1)}, f32[80,256]{1,0:T(8,128)S(1)}, u32[]{:S(2)}, u32[]{:S(2)}) %collective-permute-start.9) | collective-permute-done | bytes 81952 | tf_op jit(solution)/shard_map/ppermute | solution.py:30
  92.3 0.1 collective-permute-start.10
  92.4 2.3 %collective-permute-start.12 = (f32[72,256]{1,0:T(8,128)S(1)}, f32[72,256]{1,0:T(8,128)S(1)}, u32[]{:S(2)}, u32[]{:S(2)}) collective-permute-start(f32[72,256]{1,0:T(8,128)S(1)} %get-tuple-element.71), channel_id=1, source_target_pairs={{0,3},{1,2},{2,1},{3,0},{4,7},{5,6},{6,5},{7,4},{8,11},{9,10},{10,... | collective-permute-start | bytes 221192 | tf_op jit(solution)/shard_map/ppermute | solution.py:30
  94.7 1.1 collective-permute-start.11
  95.8 4.0 %collective-permute-done.10 = f32[72,256]{1,0:T(8,128)S(1)} collective-permute-done((f32[72,256]{1,0:T(8,128)S(1)}, f32[72,256]{1,0:T(8,128)S(1)}, u32[]{:S(2)}, u32[]{:S(2)}) %collective-permute-start.10) | collective-permute-done | bytes 73760 | tf_op jit(solution)/shard_map/ppermute | solution.py:30
  99.8 0.3 collective-permute-done.11
  100.2 0.1 slice_add_fusion
  100.2 1.6 %collective-permute-start.14 = (f32[296,256]{1,0:T(8,128)S(1)}, f32[296,256]{1,0:T(8,128)S(1)}, u32[]{:S(2)}, u32[]{:S(2)}) collective-permute-start(f32[296,256]{1,0:T(8,128)S(1)} %constant_dynamic-update-slice_fusion.refs_0_), channel_id=1, source_target_pairs={{0,16},{1,17},{2,18},{3,19},{4,12},{5,13},{6,14},{7,15},{8,24},{9,... | collective-permute-start | bytes 909320 | tf_op jit(solution)/shard_map/ppermute | solution.py:71
  101.9 3.4 %collective-permute-start.17 = (f32[2,256,256]{2,1,0:T(8,128)S(1)}, f32[2,256,256]{2,1,0:T(8,128)S(1)}, u32[]{:S(2)}, u32[]{:S(2)}) collective-permute-start(f32[2,256,256]{2,1,0:T(8,128)S(1)} %slice_add_fusion), channel_id=1, source_target_pairs={{0,1},{1,2},{2,3},{4,5},{5,6},{6,7},{8,9},{9,10},{10,11},{12,13},{... | collective-permute-start | bytes 1572872 | tf_op jit(solution)/shard_map/ppermute | solution.py:24
  105.3 0.1 collective-permute-start.15
  105.3 1.8 %collective-permute-done.14.refs_1_ = f32[296,256]{1,0:T(8,128)S(1)} collective-permute-done((f32[296,256]{1,0:T(8,128)S(1)}, f32[296,256]{1,0:T(8,128)S(1)}, u32[]{:S(2)}, u32[]{:S(2)}) %collective-permute-start.14) | collective-permute-done | bytes 303136 | tf_op jit(solution)/shard_map/ppermute | solution.py:71
  107.2 3.8 %collective-permute-start.16 = (f32[296,256]{1,0:T(8,128)S(1)}, f32[296,256]{1,0:T(8,128)S(1)}, u32[]{:S(2)}, u32[]{:S(2)}) collective-permute-start(f32[296,256]{1,0:T(8,128)S(1)} %collective-permute-done.14.refs_1_), channel_id=1, source_target_pairs={{0,8},{1,9},{2,10},{3,11},{4,20},{5,21},{6,22},{7,23},{8,0},{9,1},... | collective-permute-start | bytes 909320 | tf_op jit(solution)/shard_map/ppermute | solution.py:71
  111.0 0.5 collective-permute-start.19
  111.5 0.6 collective-permute-done.15.refs_2_
  112.1 4.1 %collective-permute-done.17.g_left = f32[2,256,256]{2,1,0:T(8,128)S(1)} collective-permute-done((f32[2,256,256]{2,1,0:T(8,128)S(1)}, f32[2,256,256]{2,1,0:T(8,128)S(1)}, u32[]{:S(2)}, u32[]{:S(2)}) %collective-permute-start.17) | collective-permute-done | bytes 524320 | tf_op jit(solution)/shard_map/ppermute | solution.py:24
  116.3 1.6 %collective-permute-done.21.refs_7_ = f32[296,256]{1,0:T(8,128)S(1)} collective-permute-done((f32[296,256]{1,0:T(8,128)S(1)}, f32[296,256]{1,0:T(8,128)S(1)}, u32[]{:S(2)}, u32[]{:S(2)}) %collective-permute-start.21) | collective-permute-done | bytes 303136 | tf_op jit(solution)/shard_map/ppermute | solution.py:30
  117.9 2.3 %update.1 = (f32[2,256,512]{2,1,0:T(8,128)}, f32[2,4,256,256]{3,2,1,0:T(8,128)}) custom-call(f32[2,256,512]{2,1,0:T(8,128)S(1)} %copy-done.3, f32[256,512]{1,0:T(8,128)S(1)} %get-tuple-element.40.light_ref, f32[8,256]{1,0:T(8,128)S(1)} %slice_maximum_fusion.top_ref, f32[2,256,512]{2,1,0:T(8,128)S(1)} %copy-done.6, ...), custom_call_target="tpu_custom_call" | custom-call | flops 1000000 | bytes 10000000 | tf_op jit(solution)/shard_map/update/pallas_call | solution.py:504
  (38 shorter events, 0.2 us)
Async XLA Ops:
  2.5 19.0 %collective-permute-start.1 = (f32[2,256,256]{2,1,0:T(8,128)}, f32[2,256,256]{2,1,0:T(8,128)}, u32[]{:S(2)}, u32[]{:S(2)}) collective-permute-start(f32[2,256,256]{2,1,0:T(8,128)} %slice.50), channel_id=1, source_target_pairs={{1,0},{2,1},{3,2},{5,4},{6,5},{7,6},{9,8},{10,9},{11,10},{13,12},{... | collective-permute-start | bytes 1572872 | tf_op jit(solution)/shard_map/ppermute | solution.py:24
  3.8 1.4 %copy-start.4 = (f32[1,1,6,256,256]{4,3,2,1,0:T(8,128)S(1)}, f32[1,1,6,256,256]{4,3,2,1,0:T(8,128)}, u32[]{:S(2)}) copy-start(f32[1,1,6,256,256]{4,3,2,1,0:T(8,128)} %param.9) | copy-start | bytes 4718596
  5.2 0.9 copy-start.7
  6.1 4.1 %copy-start.2 = (f32[2,256,512]{2,1,0:T(8,128)S(1)}, f32[2,256,512]{2,1,0:T(8,128)}, u32[]{:S(2)}) copy-start(f32[2,256,512]{2,1,0:T(8,128)} %tile_ref.1) | copy-start | bytes 3145732
  6.2 5.4 %copy-start.8 = (s32[1,1,6,2]{2,3,1,0:T(2,128)S(1)}, s32[1,1,6,2]{2,3,1,0:T(2,128)}, u32[]{:S(2)}) copy-start(s32[1,1,6,2]{2,3,1,0:T(2,128)} %param.10) | copy-start | bytes 148
  6.2 16.7 %copy-start.9 = (s32[8,4]{0,1:T(4,128)S(1)}, s32[8,4]{0,1:T(4,128)}, u32[]{:S(2)}) copy-start(s32[8,4]{0,1:T(4,128)} %param.11) | copy-start | bytes 388
  6.2 16.8 %copy-start = (f32[2,4,256,256]{3,2,1,0:T(8,128)S(1)}, f32[2,4,256,256]{3,2,1,0:T(8,128)}, u32[]{:S(2)}) copy-start(f32[2,4,256,256]{3,2,1,0:T(8,128)} %probe_ref.1) | copy-start | bytes 6291460
  9.1 1.1 copy-start.5
  10.2 17.3 %collective-permute-start.3 = (f32[2,256,512]{2,1,0:T(8,128)S(1)}, f32[2,256,512]{2,1,0:T(8,128)}, u32[]{:S(2)}, u32[]{:S(2)}) collective-permute-start(f32[2,256,512]{2,1,0:T(8,128)S(1)} %copy-done.2), channel_id=1, source_target_pairs={{4,0},{5,1},{6,2},{7,3},{8,4},{9,5},{10,6},{11,7},{12,8},{13,9},{1... | collective-permute-start | bytes 3145736 | tf_op jit(solution)/shard_map/ppermute | solution.py:24
  11.6 6.9 %collective-permute-start = (s32[6,2]{1,0:T(8,128)S(1)}, s32[6,2]{1,0:T(8,128)S(1)}, u32[]{:S(2)}, u32[]{:S(2)}) collective-permute-start(s32[6,2]{1,0:T(8,128)S(1)} %copy.22), channel_id=1, source_target_pairs={{0,1},{1,2},{2,3},{4,5},{5,6},{6,7},{8,9},{9,10},{10,11},{12,13},{... | collective-permute-start | bytes 152 | tf_op jit(solution)/shard_map/ppermute | solution.py:24
  18.5 3.0 %collective-permute-start.2 = (s32[12,2]{1,0:T(8,128)S(1)}, s32[12,2]{1,0:T(8,128)S(1)}, u32[]{:S(2)}, u32[]{:S(2)}) collective-permute-start(s32[12,2]{1,0:T(8,128)S(1)} %pad_add_fusion), channel_id=1, source_target_pairs={{0,4},{1,5},{2,6},{3,7},{4,8},{5,9},{6,10},{7,11},{8,12},{9,13},{1... | collective-permute-start | bytes 296 | tf_op jit(solution)/shard_map/ppermute | solution.py:24
  21.5 6.0 %collective-permute-start.4 = (f32[2,256,256]{2,1,0:T(8,128)}, f32[2,256,256]{2,1,0:T(8,128)}, u32[]{:S(2)}, u32[]{:S(2)}) collective-permute-start(f32[2,256,256]{2,1,0:T(8,128)} %collective-permute-done.1.right_any), channel_id=1, source_target_pairs={{4,0},{5,1},{6,2},{7,3},{8,4},{9,5},{10,6},{11,7},{12,8},{13,9},{1... | collective-permute-start | bytes 1572872 | tf_op jit(solution)/shard_map/ppermute | solution.py:24
  46.1 4.6 %collective-permute-start.5 = (f32[1152,256]{1,0:T(8,128)S(1)}, f32[1152,256]{1,0:T(8,128)S(1)}, u32[]{:S(2)}, u32[]{:S(2)}) collective-permute-start(f32[1152,256]{1,0:T(8,128)S(1)} %get-tuple-element.48), channel_id=1, source_target_pairs={{0,4},{1,5},{2,6},{3,7},{4,0},{5,1},{6,2},{7,3},{8,12},{9,13},{10,... | collective-permute-start | bytes 3538952 | tf_op jit(solution)/shard_map/ppermute | solution.py:30
  50.8 13.9 %collective-permute-start.6 = (f32[576,256]{1,0:T(8,128)S(1)}, f32[576,256]{1,0:T(8,128)S(1)}, u32[]{:S(2)}, u32[]{:S(2)}) collective-permute-start(f32[576,256]{1,0:T(8,128)S(1)} %get-tuple-element.50), channel_id=1, source_target_pairs={{0,8},{1,9},{2,10},{3,11},{4,20},{5,21},{6,22},{7,23},{8,0},{9,1},... | collective-permute-start | bytes 1769480 | tf_op jit(solution)/shard_map/ppermute | solution.py:71
  64.7 53.1 %copy-start.6 = (f32[2,256,512]{2,1,0:T(8,128)S(1)}, f32[2,256,512]{2,1,0:T(8,128)}, u32[]{:S(2)}) copy-start(f32[2,256,512]{2,1,0:T(8,128)} %get-tuple-element.67.g_tile) | copy-start | bytes 3145732
  64.8 11.2 %collective-permute-start.7 = (f32[288,256]{1,0:T(8,128)S(1)}, f32[288,256]{1,0:T(8,128)S(1)}, u32[]{:S(2)}, u32[]{:S(2)}) collective-permute-start(f32[288,256]{1,0:T(8,128)S(1)} %get-tuple-element.52), channel_id=1, source_target_pairs={{0,16},{1,17},{2,18},{3,19},{4,12},{5,13},{6,14},{7,15},{8,24},{9,... | collective-permute-start | bytes 884744 | tf_op jit(solution)/shard_map/ppermute | solution.py:71
  76.0 41.9 %copy-start.1 = (f32[2,4,256,256]{3,2,1,0:T(8,128)S(1)}, f32[2,4,256,256]{3,2,1,0:T(8,128)}, u32[]{:S(2)}) copy-start(f32[2,4,256,256]{3,2,1,0:T(8,128)} %probe_ref.1) | copy-start | bytes 6291460
  76.0 41.9 %copy-start.3 = (f32[2,256,512]{2,1,0:T(8,128)S(1)}, f32[2,256,512]{2,1,0:T(8,128)}, u32[]{:S(2)}) copy-start(f32[2,256,512]{2,1,0:T(8,128)} %tile_ref.1) | copy-start | bytes 3145732
  76.0 24.2 %collective-permute-start.13 = (f32[2,256,768]{2,1,0:T(8,128)S(1)}, f32[2,256,768]{2,1,0:T(8,128)S(1)}, u32[]{:S(2)}, u32[]{:S(2)}) collective-permute-start(f32[2,256,768]{2,1,0:T(8,128)S(1)} %get-tuple-element.62), channel_id=1, source_target_pairs={{0,4},{1,5},{2,6},{3,7},{4,8},{5,9},{6,10},{7,11},{8,12},{9,13},{1... | collective-permute-start | bytes 4718600 | tf_op jit(solution)/shard_map/ppermute | solution.py:24
  77.7 7.4 %collective-permute-start.8 = (f32[152,256]{1,0:T(8,128)S(1)}, f32[152,256]{1,0:T(8,128)S(1)}, u32[]{:S(2)}, u32[]{:S(2)}) collective-permute-start(f32[152,256]{1,0:T(8,128)S(1)} %get-tuple-element.57), channel_id=1, source_target_pairs={{0,1},{1,0},{2,3},{3,2},{4,5},{5,4},{6,7},{7,6},{8,9},{9,8},{10,11... | collective-permute-start | bytes 466952 | tf_op jit(solution)/shard_map/ppermute | solution.py:30
  85.1 7.1 %collective-permute-start.9 = (f32[80,256]{1,0:T(8,128)S(1)}, f32[80,256]{1,0:T(8,128)S(1)}, u32[]{:S(2)}, u32[]{:S(2)}) collective-permute-start(f32[80,256]{1,0:T(8,128)S(1)} %get-tuple-element.60), channel_id=1, source_target_pairs={{0,2},{1,3},{2,0},{3,1},{4,6},{5,7},{6,4},{7,5},{8,10},{9,11},{10,... | collective-permute-start | bytes 245768 | tf_op jit(solution)/shard_map/ppermute | solution.py:30
  92.3 7.5 %collective-permute-start.10 = (f32[72,256]{1,0:T(8,128)S(1)}, f32[72,256]{1,0:T(8,128)S(1)}, u32[]{:S(2)}, u32[]{:S(2)}) collective-permute-start(f32[72,256]{1,0:T(8,128)S(1)} %get-tuple-element.71), channel_id=1, source_target_pairs={{0,2},{1,3},{2,0},{3,1},{4,6},{5,7},{6,4},{7,5},{8,10},{9,11},{10,... | collective-permute-start | bytes 221192 | tf_op jit(solution)/shard_map/ppermute | solution.py:30
  92.4 7.8 %collective-permute-start.12 = (f32[72,256]{1,0:T(8,128)S(1)}, f32[72,256]{1,0:T(8,128)S(1)}, u32[]{:S(2)}, u32[]{:S(2)}) collective-permute-start(f32[72,256]{1,0:T(8,128)S(1)} %get-tuple-element.71), channel_id=1, source_target_pairs={{0,3},{1,2},{2,1},{3,0},{4,7},{5,6},{6,5},{7,4},{8,11},{9,10},{10,... | collective-permute-start | bytes 221192 | tf_op jit(solution)/shard_map/ppermute | solution.py:30
  94.7 5.4 %collective-permute-start.11 = (f32[72,256]{1,0:T(8,128)S(1)}, f32[72,256]{1,0:T(8,128)S(1)}, u32[]{:S(2)}, u32[]{:S(2)}) collective-permute-start(f32[72,256]{1,0:T(8,128)S(1)} %get-tuple-element.71), channel_id=1, source_target_pairs={{0,1},{1,0},{2,3},{3,2},{4,5},{5,4},{6,7},{7,6},{8,9},{9,8},{10,11... | collective-permute-start | bytes 221192 | tf_op jit(solution)/shard_map/ppermute | solution.py:30
  100.2 6.9 %collective-permute-start.14 = (f32[296,256]{1,0:T(8,128)S(1)}, f32[296,256]{1,0:T(8,128)S(1)}, u32[]{:S(2)}, u32[]{:S(2)}) collective-permute-start(f32[296,256]{1,0:T(8,128)S(1)} %constant_dynamic-update-slice_fusion.refs_0_), channel_id=1, source_target_pairs={{0,16},{1,17},{2,18},{3,19},{4,12},{5,13},{6,14},{7,15},{8,24},{9,... | collective-permute-start | bytes 909320 | tf_op jit(solution)/shard_map/ppermute | solution.py:71
  101.9 14.4 %collective-permute-start.17 = (f32[2,256,256]{2,1,0:T(8,128)S(1)}, f32[2,256,256]{2,1,0:T(8,128)S(1)}, u32[]{:S(2)}, u32[]{:S(2)}) collective-permute-start(f32[2,256,256]{2,1,0:T(8,128)S(1)} %slice_add_fusion), channel_id=1, source_target_pairs={{0,1},{1,2},{2,3},{4,5},{5,6},{6,7},{8,9},{9,10},{10,11},{12,13},{... | collective-permute-start | bytes 1572872 | tf_op jit(solution)/shard_map/ppermute | solution.py:24
  105.3 6.9 %collective-permute-start.15 = (f32[296,256]{1,0:T(8,128)S(1)}, f32[296,256]{1,0:T(8,128)S(1)}, u32[]{:S(2)}, u32[]{:S(2)}) collective-permute-start(f32[296,256]{1,0:T(8,128)S(1)} %constant_dynamic-update-slice_fusion.refs_0_), channel_id=1, source_target_pairs={{0,8},{1,9},{2,10},{3,11},{4,20},{5,21},{6,22},{7,23},{8,0},{9,1},... | collective-permute-start | bytes 909320 | tf_op jit(solution)/shard_map/ppermute | solution.py:71
  107.2 9.1 %collective-permute-start.16 = (f32[296,256]{1,0:T(8,128)S(1)}, f32[296,256]{1,0:T(8,128)S(1)}, u32[]{:S(2)}, u32[]{:S(2)}) collective-permute-start(f32[296,256]{1,0:T(8,128)S(1)} %collective-permute-done.14.refs_1_), channel_id=1, source_target_pairs={{0,8},{1,9},{2,10},{3,11},{4,20},{5,21},{6,22},{7,23},{8,0},{9,1},... | collective-permute-start | bytes 909320 | tf_op jit(solution)/shard_map/ppermute | solution.py:71
  111.0 5.3 %collective-permute-start.18 = (f32[296,256]{1,0:T(8,128)S(1)}, f32[296,256]{1,0:T(8,128)S(1)}, u32[]{:S(2)}, u32[]{:S(2)}) collective-permute-start(f32[296,256]{1,0:T(8,128)S(1)} %constant_dynamic-update-slice_fusion.refs_0_), channel_id=1, source_target_pairs={{0,4},{1,5},{2,6},{3,7},{4,0},{5,1},{6,2},{7,3},{8,12},{9,13},{10,... | collective-permute-start | bytes 909320 | tf_op jit(solution)/shard_map/ppermute | solution.py:30
  111.0 5.3 %collective-permute-start.19 = (f32[296,256]{1,0:T(8,128)S(1)}, f32[296,256]{1,0:T(8,128)S(1)}, u32[]{:S(2)}, u32[]{:S(2)}) collective-permute-start(f32[296,256]{1,0:T(8,128)S(1)} %collective-permute-done.14.refs_1_), channel_id=1, source_target_pairs={{0,4},{1,5},{2,6},{3,7},{4,0},{5,1},{6,2},{7,3},{8,12},{9,13},{10,... | collective-permute-start | bytes 909320 | tf_op jit(solution)/shard_map/ppermute | solution.py:30
  112.1 4.1 %collective-permute-start.20 = (f32[296,256]{1,0:T(8,128)S(1)}, f32[296,256]{1,0:T(8,128)S(1)}, u32[]{:S(2)}, u32[]{:S(2)}) collective-permute-start(f32[296,256]{1,0:T(8,128)S(1)} %collective-permute-done.15.refs_2_), channel_id=1, source_target_pairs={{0,4},{1,5},{2,6},{3,7},{4,0},{5,1},{6,2},{7,3},{8,12},{9,13},{10,... | collective-permute-start | bytes 909320 | tf_op jit(solution)/shard_map/ppermute | solution.py:30
  116.3 1.6 %collective-permute-start.21 = (f32[296,256]{1,0:T(8,128)S(1)}, f32[296,256]{1,0:T(8,128)S(1)}, u32[]{:S(2)}, u32[]{:S(2)}) collective-permute-start(f32[296,256]{1,0:T(8,128)S(1)} %collective-permute-done.16.refs_3_), channel_id=1, source_target_pairs={{0,4},{1,5},{2,6},{3,7},{4,0},{5,1},{6,2},{7,3},{8,12},{9,13},{10,... | collective-permute-start | bytes 909320 | tf_op jit(solution)/shard_map/ppermute | solution.py:30

commit v14 on v12

--- a/solution.py
+++ b/solution.py
@@ -256,12 +256,14 @@
     store.wait()
 
 
-def light_kernel(counts_ref, spots_ref, left_ref, up_ref, diag_ref, lit_ref, light_ref, top_ref, acc):
+def light_kernel(sides, last, counts_ref, *refs):
+    spot_refs, (lit_ref, *rest) = refs[:len(sides)], refs[len(sides):]
+    light_ref, acc = rest[1 if last else 0], rest[-1]
     side = lit_ref.shape[0]
     rows, cols = light_ref.shape
     my_row, my_col = lax.axis_index("row"), lax.axis_index("col")
     acc[...] = jnp.zeros_like(acc)
-    for ref, d_row, d_col in ((spots_ref, 0, 0), (left_ref, 0, 1), (up_ref, 1, 0), (diag_ref, 1, 1)):
+    for ref, (d_row, d_col) in zip(spot_refs, sides):
         inside = (my_row >= d_row) & (my_col >= d_col)
         number = counts_ref[jnp.maximum(my_row - d_row, 0), jnp.maximum(my_col - d_col, 0)]
 
@@ -276,10 +278,28 @@
 
         lax.fori_loop(0, jnp.where(inside, number, 0), step, 0)
     light = acc[0, side:side + rows, side:side + cols]
+    if last:
+        light += rest[0][...]
+        top_ref = rest[2]
+        top = jnp.max(light, axis=0, keepdims=True)
+        top = jnp.max(top, axis=1, keepdims=True)
+        top_ref[...] = jnp.broadcast_to(top, top_ref.shape)
     light_ref[...] = light
-    top = jnp.max(light, axis=0, keepdims=True)
-    top = jnp.max(top, axis=1, keepdims=True)
-    top_ref[...] = jnp.broadcast_to(top, top_ref.shape)
+
+
+def add_light(sides, counts, spots, lit, shape, before=None):
+    last = before is not None
+    (rows, cols), side = shape, lit.shape[0]
+    return pl.pallas_call(
+        functools.partial(light_kernel, sides, last),
+        out_shape=(f32(rows, cols), f32(SUBLANES, side)) if last else f32(rows, cols),
+        in_specs=[SM] * (1 + len(sides)) + [VM] * (1 + last),
+        out_specs=(VM, VM) if last else VM,
+        scratch_shapes=[pltpu.VMEM((1, rows + 2 * side, cols + 2 * side), jnp.float32)],
+        compiler_params=params(12),
+        cost_estimate=cost(10**8, 6 * 10**6),
+        name="lighting_end" if last else "lighting_start",
+    )(counts, *spots, lit, *((before,) if last else ()))
 
 
 def fold_kernel(rank_of, below, with_top, *refs):
@@ -408,18 +428,10 @@
     corner = shifted(right[:, :side, :], -1, 0)
     from_up = shifted(jnp.concatenate([spots, from_left], axis=0), 1, 0)
     lit = jnp.sum(modes_now[0] * modes_now[0] + modes_now[1] * modes_now[1], axis=0)
-    light, top = pl.pallas_call(
-        light_kernel,
-        out_shape=(f32(rows, cols), f32(SUBLANES, side)),
-        in_specs=[SM] * 5 + [VM],
-        out_specs=(VM, VM),
-        scratch_shapes=[
-            pltpu.VMEM((1, rows + 2 * side, cols + 2 * side), jnp.float32),
-        ],
-        compiler_params=params(12),
-        cost_estimate=cost(10**8, 10**7),
-        name="lighting",
-    )(counts, spots, from_left, from_up[:slots], from_up[slots:], lit)
+    light = add_light(((0, 0), (0, 1)), counts, (spots, from_left), lit, (rows, cols))
+    light, top = add_light(
+        ((1, 0), (1, 1)), counts, (from_up[:slots], from_up[slots:]), lit, (rows, cols), light
+    )
     corner, top, measured = lax.optimization_barrier((corner, top, measured))
     g_tile, g_lower, g_right, *halves = pl.pallas_call(
         main_kernel,

time: 116 us -> 118 us (1.017)
  Pallas kernels: 17.1 us -> 27 us
  waiting for transfers between devices: 45.7 us -> 36.9 us
    pallas_call x1, Pallas kernels: 12.7 us -> 21.3 us  [body(): pl.pallas_call(main_kernel, out_shape=(hbm(2, rows, cols), vmem(2, side,...]
    ppermute x10, starting transfers between devices: 8.98 us -> 13.9 us  [swapped(): return lax.ppermute(value, ('row', 'col'), pairs)]
    ppermute x10, waiting for transfers between devices: 19.7 us -> 15.1 us  [swapped(): return lax.ppermute(value, ('row', 'col'), pairs)]
    ppermute x5, starting transfers between devices: 15.4 us -> 10.9 us  [flipped(): return lax.ppermute(value, ('row', 'col'), pairs)]
    ppermute x5, waiting for transfers between devices: 20.2 us -> 16 us  [flipped(): return lax.ppermute(value, ('row', 'col'), pairs)]
    pallas_call x1 -> x2, Pallas kernels: 1.77 us -> 3.15 us  [add_light(): pl.pallas_call(functools.partial(light_kernel, sides, last), out_shape=(f...]
  transfers between devices with their start and end apart: 22 -> 22, of which waited for: 13 -> 11; matrix products, arithmetic and copies ran while one was open for 7% -> 7% of each run, Pallas kernels for 2% -> 3%
where the time goes in v14:
time: 118 us; the launch traced here: 117 us
  starting transfers between devices  41.9 us (36%)
  waiting for transfers between devices  36.9 us (31%)
  Pallas kernels  27 us (23%)
  matrix products  6.34 us (5%)
  local copies, waits for them, and re-layouts  2.51 us (2%)
  other arithmetic  1.91 us (2%)
    pallas_call x1, Pallas kernels, body(): pl.pallas_call(main_kernel, out_shape=(hbm(2, rows, cols), vmem(2, side,...  21.3 us
    ppermute x7, starting transfers between devices, shifted(): return lax.ppermute(value, ('row', 'col'), pairs)  17.1 us
    ppermute x5, waiting for transfers between devices, flipped(): return lax.ppermute(value, ('row', 'col'), pairs)  16 us
    ppermute x10, waiting for transfers between devices, swapped(): return lax.ppermute(value, ('row', 'col'), pairs)  15.1 us
    ppermute x10, starting transfers between devices, swapped(): return lax.ppermute(value, ('row', 'col'), pairs)  13.9 us
    ppermute x5, starting transfers between devices, flipped(): return lax.ppermute(value, ('row', 'col'), pairs)  10.9 us
    dot_general x2, matrix products, evens_first(): return jnp.einsum(form, pick, amplitudes, precision=lax.Precision.HIGH)  6.34 us
    ppermute x7, waiting for transfers between devices, shifted(): return lax.ppermute(value, ('row', 'col'), pairs)  5.72 us
  transfers between devices with their start and end apart: 22, of which 11 were waited for; matrix products, arithmetic and copies ran while one was open for 7% of the time, Pallas kernels for 3%

profile of v14, /device:TPU:0, one launch (start us, length us, event | category | flops | bytes accessed | tf_op | source)
XLA Modules:
  0.0 117.3 jit_solution(14163299403677463694)
XLA Ops:
  0.6 0.0 copy-start
  0.6 2.0 %slice.50 = f32[2,256,256]{2,1,0:T(8,128)} slice(f32[2,256,512]{2,1,0:T(8,128)} %tile_ref.1), slice={[0:2], [0:256], [0:256]} | slice | bytes 1048576 | tf_op jit(solution)/shard_map/slice | solution.py:421
  2.6 1.4 %collective-permute-start = (f32[2,256,256]{2,1,0:T(8,128)}, f32[2,256,256]{2,1,0:T(8,128)S(1)}, u32[]{:S(2)}, u32[]{:S(2)}) collective-permute-start(f32[2,256,256]{2,1,0:T(8,128)} %slice.50), channel_id=1, source_target_pairs={{1,0},{2,1},{3,2},{5,4},{6,5},{7,6},{9,8},{10,9},{11,10},{13,12},{... | collective-permute-start | bytes 1572872 | tf_op jit(solution)/shard_map/ppermute | solution.py:24
  4.1 2.9 %fusion.2 = f32[6,256,256]{2,1,0:T(8,128)} fusion(f32[256,256,1]{1,0,2:T(8,128)} %constant.10, f32[1,1,6,256,256]{4,3,2,1,0:T(8,128)S(1)} %copy-done), kind=kOutput, calls=%fused_computation.2 | convolution fusion | flops 603979776 | bytes 3407872 | tf_op jit(solution)/shard_map/ab,sbc->sac/dot_general | solution.py:92
  7.0 1.3 %collective-permute-start.3 = (f32[2,256,512]{2,1,0:T(8,128)S(1)}, f32[2,256,512]{2,1,0:T(8,128)}, u32[]{:S(2)}, u32[]{:S(2)}) collective-permute-start(f32[2,256,512]{2,1,0:T(8,128)S(1)} %copy-done.2), channel_id=1, source_target_pairs={{4,0},{5,1},{6,2},{7,3},{8,4},{9,5},{10,6},{11,7},{12,8},{13,9},{1... | collective-permute-start | bytes 3145736 | tf_op jit(solution)/shard_map/ppermute | solution.py:24
  8.3 0.1 copy.17
  8.4 5.5 %collective-permute-start.1 = (s32[6,2]{1,0:T(8,128)S(1)}, s32[6,2]{1,0:T(8,128)S(1)}, u32[]{:S(2)}, u32[]{:S(2)}) collective-permute-start(s32[6,2]{1,0:T(8,128)S(1)} %copy.17), channel_id=1, source_target_pairs={{0,1},{1,2},{2,3},{4,5},{5,6},{6,7},{8,9},{9,10},{10,11},{12,13},{... | collective-permute-start | bytes 152 | tf_op jit(solution)/shard_map/ppermute | solution.py:24
  14.0 0.1 copy.21.refs_0_.spots_ref
  14.1 0.1 copy.22.counts_ref
  14.1 3.4 %fusion.7.amp_hbm = f32[6,256,256]{2,1,0:T(8,128)} fusion(f32[6,256,256]{2,1,0:T(8,128)} %fusion.2, f32[256,256,1]{1,0,2:T(8,128)S(1)} %copy-done.5), kind=kOutput, calls=%fused_computation.21 | convolution fusion | flops 603979776 | bytes 3407872 | tf_op jit(solution)/shard_map/cb,sab->sac/dot_general | solution.py:92
  17.6 2.3 %collective-permute-done.right_any = f32[2,256,256]{2,1,0:T(8,128)S(1)} collective-permute-done((f32[2,256,256]{2,1,0:T(8,128)}, f32[2,256,256]{2,1,0:T(8,128)S(1)}, u32[]{:S(2)}, u32[]{:S(2)}) %collective-permute-start) | collective-permute-done | bytes 524320 | tf_op jit(solution)/shard_map/ppermute | solution.py:24
  19.8 0.1 copy.18
  19.9 1.3 %collective-permute-start.4 = (f32[2,256,256]{2,1,0:T(8,128)S(1)}, f32[2,256,256]{2,1,0:T(8,128)}, u32[]{:S(2)}, u32[]{:S(2)}) collective-permute-start(f32[2,256,256]{2,1,0:T(8,128)S(1)} %collective-permute-done.right_any), channel_id=1, source_target_pairs={{4,0},{5,1},{6,2},{7,3},{8,4},{9,5},{10,6},{11,7},{12,8},{13,9},{1... | collective-permute-start | bytes 1572872 | tf_op jit(solution)/shard_map/ppermute | solution.py:24
  21.2 0.1 pad_add_fusion
  21.3 0.1 copy.19
  21.4 3.0 %collective-permute-start.2 = (s32[12,2]{1,0:T(8,128)S(1)}, s32[12,2]{1,0:T(8,128)S(1)}, u32[]{:S(2)}, u32[]{:S(2)}) collective-permute-start(s32[12,2]{1,0:T(8,128)S(1)} %copy.19), channel_id=1, source_target_pairs={{0,4},{1,5},{2,6},{3,7},{4,8},{5,9},{6,10},{7,11},{8,12},{9,13},{1... | collective-permute-start | bytes 296 | tf_op jit(solution)/shard_map/ppermute | solution.py:24
  24.4 1.7 %add_reduce_fusion.refs_2_ = f32[256,256]{1,0:T(8,128)S(1)} fusion(f32[2,4,256,256]{3,2,1,0:T(8,128)} %probe_ref.1), kind=kLoop, calls=%fused_computation.3 | loop fusion | flops 983040 | bytes 2359296 | tf_op jit(solution)/shard_map/reduce_sum | solution.py:430
  26.1 2.1 %lighting_start.1.refs_3_ = f32[256,512]{1,0:T(8,128)S(1)} custom-call(s32[8,4]{1,0:T(8,128)S(1)} %copy.22.counts_ref, s32[6,2]{1,0:T(8,128)S(1)} %copy.21.refs_0_.spots_ref, s32[6,2]{1,0:T(8,128)S(1)} %collective-permute-done.1.refs_1_, f32[256,256]{1,0:T(8,128)S(1)} %add_reduce_fusion.refs_2_), custom_call_target="tpu_custom_call" | custom-call | flops 100000000 | bytes 6000000 | tf_op jit(solution)/shard_map/lighting_start/pallas_call | solution.py:293
  28.2 1.1 lighting_end.1
  29.3 21.3 %positions.1 = (f32[2,256,512]{2,1,0:T(8,128)}, f32[2,256,768]{2,1,0:T(8,128)S(1)}, f32[2,256,256]{2,1,0:T(8,128)S(1)}, f32[1152,256]{1,0:T(8,128)S(1)}, f32[1152,256]{1,0:T(8,128)S(1)}) custom-call(s32[8,4]{1,0:T(8,128)S(1)} %copy.22.counts_ref, s32[6,2]{1,0:T(8,128)S(1)} %copy.21.refs_0_.spots_ref, f32[2,256,512]{2,1,0:T(8,128)} %tile_ref.1, ...), custom_call_target="tpu_custom_call" | custom-call | flops 7000000000 | bytes 20000000 | tf_op jit(solution)/shard_map/positions/pallas_call | solution.py:436
  50.7 0.1 collective-permute-start.5
  50.7 2.8 %collective-permute-done.5.refs_1_ = f32[1152,256]{1,0:T(8,128)S(1)} collective-permute-done((f32[1152,256]{1,0:T(8,128)S(1)}, f32[1152,256]{1,0:T(8,128)S(1)}, u32[]{:S(2)}, u32[]{:S(2)}) %collective-permute-start.5) | collective-permute-done | bytes 1179680 | tf_op jit(solution)/shard_map/ppermute | solution.py:30
  53.6 0.1 fold.4
  53.7 2.3 %collective-permute-start.6 = (f32[576,256]{1,0:T(8,128)S(1)}, f32[576,256]{1,0:T(8,128)S(1)}, u32[]{:S(2)}, u32[]{:S(2)}) collective-permute-start(f32[576,256]{1,0:T(8,128)S(1)} %get-tuple-element.50), channel_id=1, source_target_pairs={{0,8},{1,9},{2,10},{3,11},{4,20},{5,21},{6,22},{7,23},{8,0},{9,1},... | collective-permute-start | bytes 1769480 | tf_op jit(solution)/shard_map/ppermute | solution.py:71
  56.0 7.9 %collective-permute-done.6.refs_1_ = f32[576,256]{1,0:T(8,128)S(1)} collective-permute-done((f32[576,256]{1,0:T(8,128)S(1)}, f32[576,256]{1,0:T(8,128)S(1)}, u32[]{:S(2)}, u32[]{:S(2)}) %collective-permute-start.6) | collective-permute-done | bytes 589856 | tf_op jit(solution)/shard_map/ppermute | solution.py:71
  63.8 0.1 fold.5
  63.9 0.1 collective-permute-start.7
  64.0 6.7 %collective-permute-done.7.refs_1_ = f32[288,256]{1,0:T(8,128)S(1)} collective-permute-done((f32[288,256]{1,0:T(8,128)S(1)}, f32[288,256]{1,0:T(8,128)S(1)}, u32[]{:S(2)}, u32[]{:S(2)}) %collective-permute-start.7) | collective-permute-done | bytes 294944 | tf_op jit(solution)/shard_map/ppermute | solution.py:71
  70.7 1.7 %collective-permute-start.13 = (f32[2,256,768]{2,1,0:T(8,128)S(1)}, f32[2,256,768]{2,1,0:T(8,128)S(1)}, u32[]{:S(2)}, u32[]{:S(2)}) collective-permute-start(f32[2,256,768]{2,1,0:T(8,128)S(1)} %get-tuple-element.62), channel_id=1, source_target_pairs={{0,4},{1,5},{2,6},{3,7},{4,8},{5,9},{6,10},{7,11},{8,12},{9,13},{1... | collective-permute-start | bytes 4718600 | tf_op jit(solution)/shard_map/ppermute | solution.py:24
  72.4 3.2 %collective-permute-start.8 = (f32[152,256]{1,0:T(8,128)S(1)}, f32[152,256]{1,0:T(8,128)S(1)}, u32[]{:S(2)}, u32[]{:S(2)}) collective-permute-start(f32[152,256]{1,0:T(8,128)S(1)} %get-tuple-element.57), channel_id=1, source_target_pairs={{0,1},{1,0},{2,3},{3,2},{4,5},{5,4},{6,7},{7,6},{8,9},{9,8},{10,11... | collective-permute-start | bytes 466952 | tf_op jit(solution)/shard_map/ppermute | solution.py:30
  75.6 3.2 %collective-permute-done.8.refs_1_ = f32[152,256]{1,0:T(8,128)S(1)} collective-permute-done((f32[152,256]{1,0:T(8,128)S(1)}, f32[152,256]{1,0:T(8,128)S(1)}, u32[]{:S(2)}, u32[]{:S(2)}) %collective-permute-start.8) | collective-permute-done | bytes 155680 | tf_op jit(solution)/shard_map/ppermute | solution.py:30
  78.8 3.3 %collective-permute-start.9 = (f32[80,256]{1,0:T(8,128)S(1)}, f32[80,256]{1,0:T(8,128)S(1)}, u32[]{:S(2)}, u32[]{:S(2)}) collective-permute-start(f32[80,256]{1,0:T(8,128)S(1)} %get-tuple-element.60), channel_id=1, source_target_pairs={{0,2},{1,3},{2,0},{3,1},{4,6},{5,7},{6,4},{7,5},{8,10},{9,11},{10,... | collective-permute-start | bytes 245768 | tf_op jit(solution)/shard_map/ppermute | solution.py:30
  82.2 2.8 %collective-permute-done.9 = f32[80,256]{1,0:T(8,128)S(1)} collective-permute-done((f32[80,256]{1,0:T(8,128)S(1)}, f32[80,256]{1,0:T(8,128)S(1)}, u32[]{:S(2)}, u32[]{:S(2)}) %collective-permute-start.9) | collective-permute-done | bytes 81952 | tf_op jit(solution)/shard_map/ppermute | solution.py:30
  85.0 3.3 %collective-permute-start.10 = (f32[72,256]{1,0:T(8,128)S(1)}, f32[72,256]{1,0:T(8,128)S(1)}, u32[]{:S(2)}, u32[]{:S(2)}) collective-permute-start(f32[72,256]{1,0:T(8,128)S(1)} %get-tuple-element.71), channel_id=1, source_target_pairs={{0,2},{1,3},{2,0},{3,1},{4,6},{5,7},{6,4},{7,5},{8,10},{9,11},{10,... | collective-permute-start | bytes 221192 | tf_op jit(solution)/shard_map/ppermute | solution.py:30
  88.3 2.9 %collective-permute-start.12 = (f32[72,256]{1,0:T(8,128)S(1)}, f32[72,256]{1,0:T(8,128)S(1)}, u32[]{:S(2)}, u32[]{:S(2)}) collective-permute-start(f32[72,256]{1,0:T(8,128)S(1)} %get-tuple-element.71), channel_id=1, source_target_pairs={{0,3},{1,2},{2,1},{3,0},{4,7},{5,6},{6,5},{7,4},{8,11},{9,10},{10,... | collective-permute-start | bytes 221192 | tf_op jit(solution)/shard_map/ppermute | solution.py:30
  91.2 0.5 collective-permute-start.11
  91.7 4.8 %collective-permute-done.11 = f32[72,256]{1,0:T(8,128)S(1)} collective-permute-done((f32[72,256]{1,0:T(8,128)S(1)}, f32[72,256]{1,0:T(8,128)S(1)}, u32[]{:S(2)}, u32[]{:S(2)}) %collective-permute-start.11) | collective-permute-done | bytes 73760 | tf_op jit(solution)/shard_map/ppermute | solution.py:30
  96.5 0.1 slice_add_fusion
  96.6 1.5 %collective-permute-start.14 = (f32[296,256]{1,0:T(8,128)S(1)}, f32[296,256]{1,0:T(8,128)S(1)}, u32[]{:S(2)}, u32[]{:S(2)}) collective-permute-start(f32[296,256]{1,0:T(8,128)S(1)} %constant_dynamic-update-slice_fusion.refs_0_), channel_id=1, source_target_pairs={{0,16},{1,17},{2,18},{3,19},{4,12},{5,13},{6,14},{7,15},{8,24},{9,... | collective-permute-start | bytes 909320 | tf_op jit(solution)/shard_map/ppermute | solution.py:71
  98.1 2.9 %collective-permute-start.17 = (f32[2,256,256]{2,1,0:T(8,128)S(1)}, f32[2,256,256]{2,1,0:T(8,128)S(1)}, u32[]{:S(2)}, u32[]{:S(2)}) collective-permute-start(f32[2,256,256]{2,1,0:T(8,128)S(1)} %slice_add_fusion), channel_id=1, source_target_pairs={{0,1},{1,2},{2,3},{4,5},{5,6},{6,7},{8,9},{9,10},{10,11},{12,13},{... | collective-permute-start | bytes 1572872 | tf_op jit(solution)/shard_map/ppermute | solution.py:24
  100.9 2.0 %collective-permute-start.15 = (f32[296,256]{1,0:T(8,128)S(1)}, f32[296,256]{1,0:T(8,128)S(1)}, u32[]{:S(2)}, u32[]{:S(2)}) collective-permute-start(f32[296,256]{1,0:T(8,128)S(1)} %constant_dynamic-update-slice_fusion.refs_0_), channel_id=1, source_target_pairs={{0,8},{1,9},{2,10},{3,11},{4,20},{5,21},{6,22},{7,23},{8,0},{9,1},... | collective-permute-start | bytes 909320 | tf_op jit(solution)/shard_map/ppermute | solution.py:71
  102.9 0.6 collective-permute-done.14.refs_1_
  103.5 5.1 %collective-permute-start.16 = (f32[296,256]{1,0:T(8,128)S(1)}, f32[296,256]{1,0:T(8,128)S(1)}, u32[]{:S(2)}, u32[]{:S(2)}) collective-permute-start(f32[296,256]{1,0:T(8,128)S(1)} %collective-permute-done.14.refs_1_), channel_id=1, source_target_pairs={{0,8},{1,9},{2,10},{3,11},{4,20},{5,21},{6,22},{7,23},{8,0},{9,1},... | collective-permute-start | bytes 909320 | tf_op jit(solution)/shard_map/ppermute | solution.py:71
  108.6 0.5 collective-permute-start.19
  109.1 3.4 %collective-permute-done.17.g_left = f32[2,256,256]{2,1,0:T(8,128)S(1)} collective-permute-done((f32[2,256,256]{2,1,0:T(8,128)S(1)}, f32[2,256,256]{2,1,0:T(8,128)S(1)}, u32[]{:S(2)}, u32[]{:S(2)}) %collective-permute-start.17) | collective-permute-done | bytes 524320 | tf_op jit(solution)/shard_map/ppermute | solution.py:24
  112.6 0.8 collective-permute-done.16.refs_3_
  113.4 1.6 %collective-permute-done.21.refs_7_ = f32[296,256]{1,0:T(8,128)S(1)} collective-permute-done((f32[296,256]{1,0:T(8,128)S(1)}, f32[296,256]{1,0:T(8,128)S(1)}, u32[]{:S(2)}, u32[]{:S(2)}) %collective-permute-start.21) | collective-permute-done | bytes 303136 | tf_op jit(solution)/shard_map/ppermute | solution.py:30
  115.0 2.3 %update.1 = (f32[2,256,512]{2,1,0:T(8,128)}, f32[2,4,256,256]{3,2,1,0:T(8,128)}) custom-call(f32[2,256,512]{2,1,0:T(8,128)S(1)} %copy-done.3, f32[256,512]{1,0:T(8,128)S(1)} %get-tuple-element.40.light_ref, f32[8,256]{1,0:T(8,128)S(1)} %slice_maximum_fusion.top_ref, f32[2,256,512]{2,1,0:T(8,128)S(1)} %copy-done.4, ...), custom_call_target="tpu_custom_call" | custom-call | flops 1000000 | bytes 10000000 | tf_op jit(solution)/shard_map/update/pallas_call | solution.py:496
  (38 shorter events, 0.2 us)
Async XLA Ops:
  0.6 3.4 %copy-start = (f32[1,1,6,256,256]{4,3,2,1,0:T(8,128)S(1)}, f32[1,1,6,256,256]{4,3,2,1,0:T(8,128)}, u32[]{:S(2)}) copy-start(f32[1,1,6,256,256]{4,3,2,1,0:T(8,128)} %param.10) | copy-start | bytes 4718596
  2.6 4.4 %copy-start.2 = (f32[2,256,512]{2,1,0:T(8,128)S(1)}, f32[2,256,512]{2,1,0:T(8,128)}, u32[]{:S(2)}) copy-start(f32[2,256,512]{2,1,0:T(8,128)} %tile_ref.1) | copy-start | bytes 3145732
  2.6 5.7 %copy-start.6 = (s32[1,1,6,2]{2,3,1,0:T(2,128)S(1)}, s32[1,1,6,2]{2,3,1,0:T(2,128)}, u32[]{:S(2)}) copy-start(s32[1,1,6,2]{2,3,1,0:T(2,128)} %param.11) | copy-start | bytes 148
  2.6 11.4 %copy-start.7 = (s32[8,4]{0,1:T(4,128)S(1)}, s32[8,4]{0,1:T(4,128)}, u32[]{:S(2)}) copy-start(s32[8,4]{0,1:T(4,128)} %param.12) | copy-start | bytes 388
  2.6 11.5 %copy-start.5 = (f32[256,256,1]{1,0,2:T(8,128)S(1)}, f32[256,256,1]{1,0,2:T(8,128)}, u32[]{:S(2)}) copy-start(f32[256,256,1]{1,0,2:T(8,128)} %constant.10) | copy-start | bytes 786436
  2.6 17.2 %collective-permute-start = (f32[2,256,256]{2,1,0:T(8,128)}, f32[2,256,256]{2,1,0:T(8,128)S(1)}, u32[]{:S(2)}, u32[]{:S(2)}) collective-permute-start(f32[2,256,256]{2,1,0:T(8,128)} %slice.50), channel_id=1, source_target_pairs={{1,0},{2,1},{3,2},{5,4},{6,5},{7,6},{9,8},{10,9},{11,10},{13,12},{... | collective-permute-start | bytes 1572872 | tf_op jit(solution)/shard_map/ppermute | solution.py:24
  7.0 22.3 %collective-permute-start.3 = (f32[2,256,512]{2,1,0:T(8,128)S(1)}, f32[2,256,512]{2,1,0:T(8,128)}, u32[]{:S(2)}, u32[]{:S(2)}) collective-permute-start(f32[2,256,512]{2,1,0:T(8,128)S(1)} %copy-done.2), channel_id=1, source_target_pairs={{4,0},{5,1},{6,2},{7,3},{8,4},{9,5},{10,6},{11,7},{12,8},{13,9},{1... | collective-permute-start | bytes 3145736 | tf_op jit(solution)/shard_map/ppermute | solution.py:24
  8.4 9.1 %collective-permute-start.1 = (s32[6,2]{1,0:T(8,128)S(1)}, s32[6,2]{1,0:T(8,128)S(1)}, u32[]{:S(2)}, u32[]{:S(2)}) collective-permute-start(s32[6,2]{1,0:T(8,128)S(1)} %copy.17), channel_id=1, source_target_pairs={{0,1},{1,2},{2,3},{4,5},{5,6},{6,7},{8,9},{9,10},{10,11},{12,13},{... | collective-permute-start | bytes 152 | tf_op jit(solution)/shard_map/ppermute | solution.py:24
  19.9 9.4 %collective-permute-start.4 = (f32[2,256,256]{2,1,0:T(8,128)S(1)}, f32[2,256,256]{2,1,0:T(8,128)}, u32[]{:S(2)}, u32[]{:S(2)}) collective-permute-start(f32[2,256,256]{2,1,0:T(8,128)S(1)} %collective-permute-done.right_any), channel_id=1, source_target_pairs={{4,0},{5,1},{6,2},{7,3},{8,4},{9,5},{10,6},{11,7},{12,8},{13,9},{1... | collective-permute-start | bytes 1572872 | tf_op jit(solution)/shard_map/ppermute | solution.py:24
  21.4 6.8 %collective-permute-start.2 = (s32[12,2]{1,0:T(8,128)S(1)}, s32[12,2]{1,0:T(8,128)S(1)}, u32[]{:S(2)}, u32[]{:S(2)}) collective-permute-start(s32[12,2]{1,0:T(8,128)S(1)} %copy.19), channel_id=1, source_target_pairs={{0,4},{1,5},{2,6},{3,7},{4,8},{5,9},{6,10},{7,11},{8,12},{9,13},{1... | collective-permute-start | bytes 296 | tf_op jit(solution)/shard_map/ppermute | solution.py:24
  50.7 2.9 %collective-permute-start.5 = (f32[1152,256]{1,0:T(8,128)S(1)}, f32[1152,256]{1,0:T(8,128)S(1)}, u32[]{:S(2)}, u32[]{:S(2)}) collective-permute-start(f32[1152,256]{1,0:T(8,128)S(1)} %get-tuple-element.48), channel_id=1, source_target_pairs={{0,4},{1,5},{2,6},{3,7},{4,0},{5,1},{6,2},{7,3},{8,12},{9,13},{10,... | collective-permute-start | bytes 3538952 | tf_op jit(solution)/shard_map/ppermute | solution.py:30
  53.7 10.1 %collective-permute-start.6 = (f32[576,256]{1,0:T(8,128)S(1)}, f32[576,256]{1,0:T(8,128)S(1)}, u32[]{:S(2)}, u32[]{:S(2)}) collective-permute-start(f32[576,256]{1,0:T(8,128)S(1)} %get-tuple-element.50), channel_id=1, source_target_pairs={{0,8},{1,9},{2,10},{3,11},{4,20},{5,21},{6,22},{7,23},{8,0},{9,1},... | collective-permute-start | bytes 1769480 | tf_op jit(solution)/shard_map/ppermute | solution.py:71
  63.8 51.2 %copy-start.4 = (f32[2,256,512]{2,1,0:T(8,128)S(1)}, f32[2,256,512]{2,1,0:T(8,128)}, u32[]{:S(2)}) copy-start(f32[2,256,512]{2,1,0:T(8,128)} %get-tuple-element.67.g_tile) | copy-start | bytes 3145732
  63.9 6.8 %collective-permute-start.7 = (f32[288,256]{1,0:T(8,128)S(1)}, f32[288,256]{1,0:T(8,128)S(1)}, u32[]{:S(2)}, u32[]{:S(2)}) collective-permute-start(f32[288,256]{1,0:T(8,128)S(1)} %get-tuple-element.52), channel_id=1, source_target_pairs={{0,16},{1,17},{2,18},{3,19},{4,12},{5,13},{6,14},{7,15},{8,24},{9,... | collective-permute-start | bytes 884744 | tf_op jit(solution)/shard_map/ppermute | solution.py:71
  70.7 44.4 %copy-start.1 = (f32[2,4,256,256]{3,2,1,0:T(8,128)S(1)}, f32[2,4,256,256]{3,2,1,0:T(8,128)}, u32[]{:S(2)}) copy-start(f32[2,4,256,256]{3,2,1,0:T(8,128)} %probe_ref.1) | copy-start | bytes 6291460
  70.7 44.4 %copy-start.3 = (f32[2,256,512]{2,1,0:T(8,128)S(1)}, f32[2,256,512]{2,1,0:T(8,128)}, u32[]{:S(2)}) copy-start(f32[2,256,512]{2,1,0:T(8,128)} %tile_ref.1) | copy-start | bytes 3145732
  70.7 25.8 %collective-permute-start.13 = (f32[2,256,768]{2,1,0:T(8,128)S(1)}, f32[2,256,768]{2,1,0:T(8,128)S(1)}, u32[]{:S(2)}, u32[]{:S(2)}) collective-permute-start(f32[2,256,768]{2,1,0:T(8,128)S(1)} %get-tuple-element.62), channel_id=1, source_target_pairs={{0,4},{1,5},{2,6},{3,7},{4,8},{5,9},{6,10},{7,11},{8,12},{9,13},{1... | collective-permute-start | bytes 4718600 | tf_op jit(solution)/shard_map/ppermute | solution.py:24
  72.4 6.4 %collective-permute-start.8 = (f32[152,256]{1,0:T(8,128)S(1)}, f32[152,256]{1,0:T(8,128)S(1)}, u32[]{:S(2)}, u32[]{:S(2)}) collective-permute-start(f32[152,256]{1,0:T(8,128)S(1)} %get-tuple-element.57), channel_id=1, source_target_pairs={{0,1},{1,0},{2,3},{3,2},{4,5},{5,4},{6,7},{7,6},{8,9},{9,8},{10,11... | collective-permute-start | bytes 466952 | tf_op jit(solution)/shard_map/ppermute | solution.py:30
  78.8 6.1 %collective-permute-start.9 = (f32[80,256]{1,0:T(8,128)S(1)}, f32[80,256]{1,0:T(8,128)S(1)}, u32[]{:S(2)}, u32[]{:S(2)}) collective-permute-start(f32[80,256]{1,0:T(8,128)S(1)} %get-tuple-element.60), channel_id=1, source_target_pairs={{0,2},{1,3},{2,0},{3,1},{4,6},{5,7},{6,4},{7,5},{8,10},{9,11},{10,... | collective-permute-start | bytes 245768 | tf_op jit(solution)/shard_map/ppermute | solution.py:30
  85.0 6.7 %collective-permute-start.10 = (f32[72,256]{1,0:T(8,128)S(1)}, f32[72,256]{1,0:T(8,128)S(1)}, u32[]{:S(2)}, u32[]{:S(2)}) collective-permute-start(f32[72,256]{1,0:T(8,128)S(1)} %get-tuple-element.71), channel_id=1, source_target_pairs={{0,2},{1,3},{2,0},{3,1},{4,6},{5,7},{6,4},{7,5},{8,10},{9,11},{10,... | collective-permute-start | bytes 221192 | tf_op jit(solution)/shard_map/ppermute | solution.py:30
  88.3 8.2 %collective-permute-start.12 = (f32[72,256]{1,0:T(8,128)S(1)}, f32[72,256]{1,0:T(8,128)S(1)}, u32[]{:S(2)}, u32[]{:S(2)}) collective-permute-start(f32[72,256]{1,0:T(8,128)S(1)} %get-tuple-element.71), channel_id=1, source_target_pairs={{0,3},{1,2},{2,1},{3,0},{4,7},{5,6},{6,5},{7,4},{8,11},{9,10},{10,... | collective-permute-start | bytes 221192 | tf_op jit(solution)/shard_map/ppermute | solution.py:30
  91.2 5.3 %collective-permute-start.11 = (f32[72,256]{1,0:T(8,128)S(1)}, f32[72,256]{1,0:T(8,128)S(1)}, u32[]{:S(2)}, u32[]{:S(2)}) collective-permute-start(f32[72,256]{1,0:T(8,128)S(1)} %get-tuple-element.71), channel_id=1, source_target_pairs={{0,1},{1,0},{2,3},{3,2},{4,5},{5,4},{6,7},{7,6},{8,9},{9,8},{10,11... | collective-permute-start | bytes 221192 | tf_op jit(solution)/shard_map/ppermute | solution.py:30
  96.6 6.9 %collective-permute-start.14 = (f32[296,256]{1,0:T(8,128)S(1)}, f32[296,256]{1,0:T(8,128)S(1)}, u32[]{:S(2)}, u32[]{:S(2)}) collective-permute-start(f32[296,256]{1,0:T(8,128)S(1)} %constant_dynamic-update-slice_fusion.refs_0_), channel_id=1, source_target_pairs={{0,16},{1,17},{2,18},{3,19},{4,12},{5,13},{6,14},{7,15},{8,24},{9,... | collective-permute-start | bytes 909320 | tf_op jit(solution)/shard_map/ppermute | solution.py:71
  98.1 14.5 %collective-permute-start.17 = (f32[2,256,256]{2,1,0:T(8,128)S(1)}, f32[2,256,256]{2,1,0:T(8,128)S(1)}, u32[]{:S(2)}, u32[]{:S(2)}) collective-permute-start(f32[2,256,256]{2,1,0:T(8,128)S(1)} %slice_add_fusion), channel_id=1, source_target_pairs={{0,1},{1,2},{2,3},{4,5},{5,6},{6,7},{8,9},{9,10},{10,11},{12,13},{... | collective-permute-start | bytes 1572872 | tf_op jit(solution)/shard_map/ppermute | solution.py:24
  100.9 8.2 %collective-permute-start.15 = (f32[296,256]{1,0:T(8,128)S(1)}, f32[296,256]{1,0:T(8,128)S(1)}, u32[]{:S(2)}, u32[]{:S(2)}) collective-permute-start(f32[296,256]{1,0:T(8,128)S(1)} %constant_dynamic-update-slice_fusion.refs_0_), channel_id=1, source_target_pairs={{0,8},{1,9},{2,10},{3,11},{4,20},{5,21},{6,22},{7,23},{8,0},{9,1},... | collective-permute-start | bytes 909320 | tf_op jit(solution)/shard_map/ppermute | solution.py:71
  103.5 9.9 %collective-permute-start.16 = (f32[296,256]{1,0:T(8,128)S(1)}, f32[296,256]{1,0:T(8,128)S(1)}, u32[]{:S(2)}, u32[]{:S(2)}) collective-permute-start(f32[296,256]{1,0:T(8,128)S(1)} %collective-permute-done.14.refs_1_), channel_id=1, source_target_pairs={{0,8},{1,9},{2,10},{3,11},{4,20},{5,21},{6,22},{7,23},{8,0},{9,1},... | collective-permute-start | bytes 909320 | tf_op jit(solution)/shard_map/ppermute | solution.py:71
  108.6 4.8 %collective-permute-start.18 = (f32[296,256]{1,0:T(8,128)S(1)}, f32[296,256]{1,0:T(8,128)S(1)}, u32[]{:S(2)}, u32[]{:S(2)}) collective-permute-start(f32[296,256]{1,0:T(8,128)S(1)} %constant_dynamic-update-slice_fusion.refs_0_), channel_id=1, source_target_pairs={{0,4},{1,5},{2,6},{3,7},{4,0},{5,1},{6,2},{7,3},{8,12},{9,13},{10,... | collective-permute-start | bytes 909320 | tf_op jit(solution)/shard_map/ppermute | solution.py:30
  108.6 4.8 %collective-permute-start.19 = (f32[296,256]{1,0:T(8,128)S(1)}, f32[296,256]{1,0:T(8,128)S(1)}, u32[]{:S(2)}, u32[]{:S(2)}) collective-permute-start(f32[296,256]{1,0:T(8,128)S(1)} %collective-permute-done.14.refs_1_), channel_id=1, source_target_pairs={{0,4},{1,5},{2,6},{3,7},{4,0},{5,1},{6,2},{7,3},{8,12},{9,13},{10,... | collective-permute-start | bytes 909320 | tf_op jit(solution)/shard_map/ppermute | solution.py:30
  109.1 4.3 %collective-permute-start.20 = (f32[296,256]{1,0:T(8,128)S(1)}, f32[296,256]{1,0:T(8,128)S(1)}, u32[]{:S(2)}, u32[]{:S(2)}) collective-permute-start(f32[296,256]{1,0:T(8,128)S(1)} %collective-permute-done.15.refs_2_), channel_id=1, source_target_pairs={{0,4},{1,5},{2,6},{3,7},{4,0},{5,1},{6,2},{7,3},{8,12},{9,13},{10,... | collective-permute-start | bytes 909320 | tf_op jit(solution)/shard_map/ppermute | solution.py:30
  113.4 1.6 %collective-permute-start.21 = (f32[296,256]{1,0:T(8,128)S(1)}, f32[296,256]{1,0:T(8,128)S(1)}, u32[]{:S(2)}, u32[]{:S(2)}) collective-permute-start(f32[296,256]{1,0:T(8,128)S(1)} %collective-permute-done.16.refs_3_), channel_id=1, source_target_pairs={{0,4},{1,5},{2,6},{3,7},{4,0},{5,1},{6,2},{7,3},{8,12},{9,13},{10,... | collective-permute-start | bytes 909320 | tf_op jit(solution)/shard_map/ppermute | solution.py:30

commit v15 on v14

--- a/solution.py
+++ b/solution.py
@@ -466,12 +466,12 @@
     for i in range(plane_bits()):
         for j, (held, got, ride) in enumerate(chains):
             send, held = fold(my_plane_rank, plane_bits() - 1 - i, held, got)
+            if i == plane_bits() - 1 and j == 0:
+                send, g_lower = lax.optimization_barrier((send, g_lower))
             chains[j] = (held, flipped(send, i), ride)
     for i in range(col_bits()):
         for j, (held, got, ride) in enumerate(chains):
             send, held, *ride = fold(my_col_rank, col_bits() - 1 - i, held, got, ride)
-            if i == 0 and j == 0:
-                send, g_lower = lax.optimization_barrier((send, g_lower))
             chains[j] = (held, swapped(send, 0, 1 << i), ride[0] if ride else None)
     g_up = shifted(g_lower, 1, 0)
     owns = []

time: 118 us -> 133 us (1.13)
  waiting for transfers between devices: 36.9 us -> 64.8 us
  starting transfers between devices: 41.9 us -> 29.1 us
    ppermute x5, waiting for transfers between devices: 16 us -> 40.5 us  [flipped(): return lax.ppermute(value, ('row', 'col'), pairs)]
    ppermute x5, starting transfers between devices: 10.9 us -> 2.06 us  [flipped(): return lax.ppermute(value, ('row', 'col'), pairs)]
    ppermute x10, waiting for transfers between devices: 15.1 us -> 20.6 us  [swapped(): return lax.ppermute(value, ('row', 'col'), pairs)]
    ppermute x10, starting transfers between devices: 13.9 us -> 10.1 us  [swapped(): return lax.ppermute(value, ('row', 'col'), pairs)]
    ppermute x7, waiting for transfers between devices: 5.72 us -> 3.78 us  [shifted(): return lax.ppermute(value, ('row', 'col'), pairs)]
  transfers between devices with their start and end apart: 22 -> 22, of which waited for: 11 -> 13; matrix products, arithmetic and copies ran while one was open for 7% -> 7% of each run, Pallas kernels for 3% -> 2%
where the time goes in v15:
time: 133 us
  waiting for transfers between devices  64.8 us (49%)
  starting transfers between devices  29.1 us (22%)
  Pallas kernels  27 us (20%)
  matrix products  6.34 us (5%)
  local copies, waits for them, and re-layouts  2.51 us (2%)
  other arithmetic  1.91 us (1%)
    ppermute x5, waiting for transfers between devices, flipped(): return lax.ppermute(value, ('row', 'col'), pairs)  40.5 us
    pallas_call x1, Pallas kernels, body(): pl.pallas_call(main_kernel, out_shape=(hbm(2, rows, cols), vmem(2, side,...  21.3 us
    ppermute x10, waiting for transfers between devices, swapped(): return lax.ppermute(value, ('row', 'col'), pairs)  20.6 us
    ppermute x7, starting transfers between devices, shifted(): return lax.ppermute(value, ('row', 'col'), pairs)  17 us
    ppermute x10, starting transfers between devices, swapped(): return lax.ppermute(value, ('row', 'col'), pairs)  10.1 us
    dot_general x2, matrix products, evens_first(): return jnp.einsum(form, pick, amplitudes, precision=lax.Precision.HIGH)  6.34 us
    ppermute x7, waiting for transfers between devices, shifted(): return lax.ppermute(value, ('row', 'col'), pairs)  3.78 us
    pallas_call x2, Pallas kernels, add_light(): pl.pallas_call(functools.partial(light_kernel, sides, last), out_shape=(f...  3.15 us
  transfers between devices with their start and end apart: 22, of which 13 were waited for; matrix products, arithmetic and copies ran while one was open for 7% of the time, Pallas kernels for 2%

profile of v15, /device:TPU:0, one launch (start us, length us, event | category | flops | bytes accessed | tf_op | source)
XLA Modules:
  0.0 132.6 jit_solution(13047803412401424601)
XLA Ops:
  0.6 2.0 %slice.50 = f32[2,256,256]{2,1,0:T(8,128)} slice(f32[2,256,512]{2,1,0:T(8,128)} %tile_ref.1), slice={[0:2], [0:256], [0:256]} | slice | bytes 1048576 | tf_op jit(solution)/shard_map/slice | solution.py:421
  2.6 1.4 %collective-permute-start = (f32[2,256,256]{2,1,0:T(8,128)}, f32[2,256,256]{2,1,0:T(8,128)S(1)}, u32[]{:S(2)}, u32[]{:S(2)}) collective-permute-start(f32[2,256,256]{2,1,0:T(8,128)} %slice.50), channel_id=1, source_target_pairs={{1,0},{2,1},{3,2},{5,4},{6,5},{7,6},{9,8},{10,9},{11,10},{13,12},{... | collective-permute-start | bytes 1572872 | tf_op jit(solution)/shard_map/ppermute | solution.py:24
  4.1 2.9 %fusion.2 = f32[6,256,256]{2,1,0:T(8,128)} fusion(f32[256,256,1]{1,0,2:T(8,128)} %constant.10, f32[1,1,6,256,256]{4,3,2,1,0:T(8,128)S(1)} %copy-done), kind=kOutput, calls=%fused_computation.2 | convolution fusion | flops 603979776 | bytes 3407872 | tf_op jit(solution)/shard_map/ab,sbc->sac/dot_general | solution.py:92
  7.0 1.3 collective-permute-start.3
  8.3 0.1 copy.17
  8.4 5.5 %collective-permute-start.1 = (s32[6,2]{1,0:T(8,128)S(1)}, s32[6,2]{1,0:T(8,128)S(1)}, u32[]{:S(2)}, u32[]{:S(2)}) collective-permute-start(s32[6,2]{1,0:T(8,128)S(1)} %copy.17), channel_id=1, source_target_pairs={{0,1},{1,2},{2,3},{4,5},{5,6},{6,7},{8,9},{9,10},{10,11},{12,13},{... | collective-permute-start | bytes 152 | tf_op jit(solution)/shard_map/ppermute | solution.py:24
  14.0 0.1 copy.21.refs_0_.spots_ref
  14.1 0.1 copy.22.counts_ref
  14.1 3.4 %fusion.7.amp_hbm = f32[6,256,256]{2,1,0:T(8,128)} fusion(f32[6,256,256]{2,1,0:T(8,128)} %fusion.2, f32[256,256,1]{1,0,2:T(8,128)S(1)} %copy-done.5), kind=kOutput, calls=%fused_computation.21 | convolution fusion | flops 603979776 | bytes 3407872 | tf_op jit(solution)/shard_map/cb,sab->sac/dot_general | solution.py:92
  17.6 2.3 %collective-permute-done.right_any = f32[2,256,256]{2,1,0:T(8,128)S(1)} collective-permute-done((f32[2,256,256]{2,1,0:T(8,128)}, f32[2,256,256]{2,1,0:T(8,128)S(1)}, u32[]{:S(2)}, u32[]{:S(2)}) %collective-permute-start) | collective-permute-done | bytes 524320 | tf_op jit(solution)/shard_map/ppermute | solution.py:24
  19.8 0.1 copy.18
  19.9 1.3 collective-permute-start.4
  21.2 0.1 pad_add_fusion
  21.3 0.1 copy.19
  21.4 3.0 %collective-permute-start.2 = (s32[12,2]{1,0:T(8,128)S(1)}, s32[12,2]{1,0:T(8,128)S(1)}, u32[]{:S(2)}, u32[]{:S(2)}) collective-permute-start(s32[12,2]{1,0:T(8,128)S(1)} %copy.19), channel_id=1, source_target_pairs={{0,4},{1,5},{2,6},{3,7},{4,8},{5,9},{6,10},{7,11},{8,12},{9,13},{1... | collective-permute-start | bytes 296 | tf_op jit(solution)/shard_map/ppermute | solution.py:24
  24.4 1.7 %add_reduce_fusion.refs_2_ = f32[256,256]{1,0:T(8,128)S(1)} fusion(f32[2,4,256,256]{3,2,1,0:T(8,128)} %probe_ref.1), kind=kLoop, calls=%fused_computation.3 | loop fusion | flops 983040 | bytes 2359296 | tf_op jit(solution)/shard_map/reduce_sum | solution.py:430
  26.1 2.1 %lighting_start.1.refs_3_ = f32[256,512]{1,0:T(8,128)S(1)} custom-call(s32[8,4]{1,0:T(8,128)S(1)} %copy.22.counts_ref, s32[6,2]{1,0:T(8,128)S(1)} %copy.21.refs_0_.spots_ref, s32[6,2]{1,0:T(8,128)S(1)} %collective-permute-done.1.refs_1_, f32[256,256]{1,0:T(8,128)S(1)} %add_reduce_fusion.refs_2_), custom_call_target="tpu_custom_call" | custom-call | flops 100000000 | bytes 6000000 | tf_op jit(solution)/shard_map/lighting_start/pallas_call | solution.py:293
  28.2 1.1 lighting_end.1
  29.3 21.3 %positions.1 = (f32[2,256,512]{2,1,0:T(8,128)}, f32[2,256,768]{2,1,0:T(8,128)S(1)}, f32[2,256,256]{2,1,0:T(8,128)S(1)}, f32[1152,256]{1,0:T(8,128)S(1)}, f32[1152,256]{1,0:T(8,128)S(1)}) custom-call(s32[8,4]{1,0:T(8,128)S(1)} %copy.22.counts_ref, s32[6,2]{1,0:T(8,128)S(1)} %copy.21.refs_0_.spots_ref, f32[2,256,512]{2,1,0:T(8,128)} %tile_ref.1, ...), custom_call_target="tpu_custom_call" | custom-call | flops 7000000000 | bytes 20000000 | tf_op jit(solution)/shard_map/positions/pallas_call | solution.py:436
  50.7 0.1 collective-permute-start.5
  50.7 2.8 %collective-permute-done.5.refs_1_ = f32[1152,256]{1,0:T(8,128)S(1)} collective-permute-done((f32[1152,256]{1,0:T(8,128)S(1)}, f32[1152,256]{1,0:T(8,128)S(1)}, u32[]{:S(2)}, u32[]{:S(2)}) %collective-permute-start.5) | collective-permute-done | bytes 1179680 | tf_op jit(solution)/shard_map/ppermute | solution.py:30
  53.6 0.1 fold.4
  53.7 0.1 collective-permute-start.6
  53.8 9.9 %collective-permute-done.6.refs_1_ = f32[576,256]{1,0:T(8,128)S(1)} collective-permute-done((f32[576,256]{1,0:T(8,128)S(1)}, f32[576,256]{1,0:T(8,128)S(1)}, u32[]{:S(2)}, u32[]{:S(2)}) %collective-permute-start.6) | collective-permute-done | bytes 589856 | tf_op jit(solution)/shard_map/ppermute | solution.py:71
  63.7 0.1 fold.5
  63.7 1.5 %collective-permute-start.13 = (f32[2,256,768]{2,1,0:T(8,128)S(1)}, f32[2,256,768]{2,1,0:T(8,128)S(1)}, u32[]{:S(2)}, u32[]{:S(2)}) collective-permute-start(f32[2,256,768]{2,1,0:T(8,128)S(1)} %get-tuple-element.62), channel_id=1, source_target_pairs={{0,4},{1,5},{2,6},{3,7},{4,8},{5,9},{6,10},{7,11},{8,12},{9,13},{1... | collective-permute-start | bytes 4718600 | tf_op jit(solution)/shard_map/ppermute | solution.py:24
  65.3 0.1 collective-permute-start.7
  65.3 21.1 %collective-permute-done.7.refs_1_ = f32[288,256]{1,0:T(8,128)S(1)} collective-permute-done((f32[288,256]{1,0:T(8,128)S(1)}, f32[288,256]{1,0:T(8,128)S(1)}, u32[]{:S(2)}, u32[]{:S(2)}) %collective-permute-start.7) | collective-permute-done | bytes 294944 | tf_op jit(solution)/shard_map/ppermute | solution.py:71
  86.5 5.9 %collective-permute-start.8 = (f32[152,256]{1,0:T(8,128)S(1)}, f32[152,256]{1,0:T(8,128)S(1)}, u32[]{:S(2)}, u32[]{:S(2)}) collective-permute-start(f32[152,256]{1,0:T(8,128)S(1)} %get-tuple-element.57), channel_id=1, source_target_pairs={{0,1},{1,0},{2,3},{3,2},{4,5},{5,4},{6,7},{7,6},{8,9},{9,8},{10,11... | collective-permute-start | bytes 466952 | tf_op jit(solution)/shard_map/ppermute | solution.py:30
  92.3 4.5 %collective-permute-done.8.refs_1_ = f32[152,256]{1,0:T(8,128)S(1)} collective-permute-done((f32[152,256]{1,0:T(8,128)S(1)}, f32[152,256]{1,0:T(8,128)S(1)}, u32[]{:S(2)}, u32[]{:S(2)}) %collective-permute-start.8) | collective-permute-done | bytes 155680 | tf_op jit(solution)/shard_map/ppermute | solution.py:30
  96.9 0.1 collective-permute-start.9
  97.0 7.2 %collective-permute-done.9 = f32[80,256]{1,0:T(8,128)S(1)} collective-permute-done((f32[80,256]{1,0:T(8,128)S(1)}, f32[80,256]{1,0:T(8,128)S(1)}, u32[]{:S(2)}, u32[]{:S(2)}) %collective-permute-start.9) | collective-permute-done | bytes 81952 | tf_op jit(solution)/shard_map/ppermute | solution.py:30
  104.1 0.1 collective-permute-start.10
  104.2 2.9 %collective-permute-start.12 = (f32[72,256]{1,0:T(8,128)S(1)}, f32[72,256]{1,0:T(8,128)S(1)}, u32[]{:S(2)}, u32[]{:S(2)}) collective-permute-start(f32[72,256]{1,0:T(8,128)S(1)} %get-tuple-element.71), channel_id=1, source_target_pairs={{0,3},{1,2},{2,1},{3,0},{4,7},{5,6},{6,5},{7,4},{8,11},{9,10},{10,... | collective-permute-start | bytes 221192 | tf_op jit(solution)/shard_map/ppermute | solution.py:30
  107.1 0.6 collective-permute-start.11
  107.7 3.9 %collective-permute-done.10 = f32[72,256]{1,0:T(8,128)S(1)} collective-permute-done((f32[72,256]{1,0:T(8,128)S(1)}, f32[72,256]{1,0:T(8,128)S(1)}, u32[]{:S(2)}, u32[]{:S(2)}) %collective-permute-start.10) | collective-permute-done | bytes 73760 | tf_op jit(solution)/shard_map/ppermute | solution.py:30
  111.6 0.6 collective-permute-done.11
  112.2 0.1 slice_add_fusion
  112.3 1.8 %collective-permute-start.14 = (f32[296,256]{1,0:T(8,128)S(1)}, f32[296,256]{1,0:T(8,128)S(1)}, u32[]{:S(2)}, u32[]{:S(2)}) collective-permute-start(f32[296,256]{1,0:T(8,128)S(1)} %constant_dynamic-update-slice_fusion.refs_0_), channel_id=1, source_target_pairs={{0,16},{1,17},{2,18},{3,19},{4,12},{5,13},{6,14},{7,15},{8,24},{9,... | collective-permute-start | bytes 909320 | tf_op jit(solution)/shard_map/ppermute | solution.py:71
  114.2 2.9 %collective-permute-start.17 = (f32[2,256,256]{2,1,0:T(8,128)S(1)}, f32[2,256,256]{2,1,0:T(8,128)S(1)}, u32[]{:S(2)}, u32[]{:S(2)}) collective-permute-start(f32[2,256,256]{2,1,0:T(8,128)S(1)} %slice_add_fusion), channel_id=1, source_target_pairs={{0,1},{1,2},{2,3},{4,5},{5,6},{6,7},{8,9},{9,10},{10,11},{12,13},{... | collective-permute-start | bytes 1572872 | tf_op jit(solution)/shard_map/ppermute | solution.py:24
  117.1 0.1 collective-permute-start.15
  117.2 4.7 %collective-permute-done.14.refs_1_ = f32[296,256]{1,0:T(8,128)S(1)} collective-permute-done((f32[296,256]{1,0:T(8,128)S(1)}, f32[296,256]{1,0:T(8,128)S(1)}, u32[]{:S(2)}, u32[]{:S(2)}) %collective-permute-start.14) | collective-permute-done | bytes 303136 | tf_op jit(solution)/shard_map/ppermute | solution.py:71
  121.9 0.5 collective-permute-start.19
  122.4 1.6 %collective-permute-done.15.refs_2_ = f32[296,256]{1,0:T(8,128)S(1)} collective-permute-done((f32[296,256]{1,0:T(8,128)S(1)}, f32[296,256]{1,0:T(8,128)S(1)}, u32[]{:S(2)}, u32[]{:S(2)}) %collective-permute-start.15) | collective-permute-done | bytes 303136 | tf_op jit(solution)/shard_map/ppermute | solution.py:71
  124.0 1.5 %collective-permute-done.17.g_left = f32[2,256,256]{2,1,0:T(8,128)S(1)} collective-permute-done((f32[2,256,256]{2,1,0:T(8,128)S(1)}, f32[2,256,256]{2,1,0:T(8,128)S(1)}, u32[]{:S(2)}, u32[]{:S(2)}) %collective-permute-start.17) | collective-permute-done | bytes 524320 | tf_op jit(solution)/shard_map/ppermute | solution.py:24
  125.5 3.2 %collective-permute-done.16.refs_3_ = f32[296,256]{1,0:T(8,128)S(1)} collective-permute-done((f32[296,256]{1,0:T(8,128)S(1)}, f32[296,256]{1,0:T(8,128)S(1)}, u32[]{:S(2)}, u32[]{:S(2)}) %collective-permute-start.16) | collective-permute-done | bytes 303136 | tf_op jit(solution)/shard_map/ppermute | solution.py:71
  128.7 1.6 %collective-permute-done.21.refs_7_ = f32[296,256]{1,0:T(8,128)S(1)} collective-permute-done((f32[296,256]{1,0:T(8,128)S(1)}, f32[296,256]{1,0:T(8,128)S(1)}, u32[]{:S(2)}, u32[]{:S(2)}) %collective-permute-start.21) | collective-permute-done | bytes 303136 | tf_op jit(solution)/shard_map/ppermute | solution.py:30
  130.3 2.3 %update.1 = (f32[2,256,512]{2,1,0:T(8,128)}, f32[2,4,256,256]{3,2,1,0:T(8,128)}) custom-call(f32[2,256,512]{2,1,0:T(8,128)S(1)} %copy-done.3, f32[256,512]{1,0:T(8,128)S(1)} %get-tuple-element.40.light_ref, f32[8,256]{1,0:T(8,128)S(1)} %slice_maximum_fusion.top_ref, f32[2,256,512]{2,1,0:T(8,128)S(1)} %copy-done.4, ...), custom_call_target="tpu_custom_call" | custom-call | flops 1000000 | bytes 10000000 | tf_op jit(solution)/shard_map/update/pallas_call | solution.py:496
  (38 shorter events, 0.2 us)
Async XLA Ops:
  0.6 3.4 %copy-start = (f32[1,1,6,256,256]{4,3,2,1,0:T(8,128)S(1)}, f32[1,1,6,256,256]{4,3,2,1,0:T(8,128)}, u32[]{:S(2)}) copy-start(f32[1,1,6,256,256]{4,3,2,1,0:T(8,128)} %param.10) | copy-start | bytes 4718596
  2.6 4.4 %copy-start.2 = (f32[2,256,512]{2,1,0:T(8,128)S(1)}, f32[2,256,512]{2,1,0:T(8,128)}, u32[]{:S(2)}) copy-start(f32[2,256,512]{2,1,0:T(8,128)} %tile_ref.1) | copy-start | bytes 3145732
  2.6 5.7 %copy-start.6 = (s32[1,1,6,2]{2,3,1,0:T(2,128)S(1)}, s32[1,1,6,2]{2,3,1,0:T(2,128)}, u32[]{:S(2)}) copy-start(s32[1,1,6,2]{2,3,1,0:T(2,128)} %param.11) | copy-start | bytes 148
  2.6 11.4 %copy-start.7 = (s32[8,4]{0,1:T(4,128)S(1)}, s32[8,4]{0,1:T(4,128)}, u32[]{:S(2)}) copy-start(s32[8,4]{0,1:T(4,128)} %param.12) | copy-start | bytes 388
  2.6 11.5 %copy-start.5 = (f32[256,256,1]{1,0,2:T(8,128)S(1)}, f32[256,256,1]{1,0,2:T(8,128)}, u32[]{:S(2)}) copy-start(f32[256,256,1]{1,0,2:T(8,128)} %constant.10) | copy-start | bytes 786436
  2.6 17.2 %collective-permute-start = (f32[2,256,256]{2,1,0:T(8,128)}, f32[2,256,256]{2,1,0:T(8,128)S(1)}, u32[]{:S(2)}, u32[]{:S(2)}) collective-permute-start(f32[2,256,256]{2,1,0:T(8,128)} %slice.50), channel_id=1, source_target_pairs={{1,0},{2,1},{3,2},{5,4},{6,5},{7,6},{9,8},{10,9},{11,10},{13,12},{... | collective-permute-start | bytes 1572872 | tf_op jit(solution)/shard_map/ppermute | solution.py:24
  7.0 22.3 %collective-permute-start.3 = (f32[2,256,512]{2,1,0:T(8,128)S(1)}, f32[2,256,512]{2,1,0:T(8,128)}, u32[]{:S(2)}, u32[]{:S(2)}) collective-permute-start(f32[2,256,512]{2,1,0:T(8,128)S(1)} %copy-done.2), channel_id=1, source_target_pairs={{4,0},{5,1},{6,2},{7,3},{8,4},{9,5},{10,6},{11,7},{12,8},{13,9},{1... | collective-permute-start | bytes 3145736 | tf_op jit(solution)/shard_map/ppermute | solution.py:24
  8.4 9.1 %collective-permute-start.1 = (s32[6,2]{1,0:T(8,128)S(1)}, s32[6,2]{1,0:T(8,128)S(1)}, u32[]{:S(2)}, u32[]{:S(2)}) collective-permute-start(s32[6,2]{1,0:T(8,128)S(1)} %copy.17), channel_id=1, source_target_pairs={{0,1},{1,2},{2,3},{4,5},{5,6},{6,7},{8,9},{9,10},{10,11},{12,13},{... | collective-permute-start | bytes 152 | tf_op jit(solution)/shard_map/ppermute | solution.py:24
  19.9 9.4 %collective-permute-start.4 = (f32[2,256,256]{2,1,0:T(8,128)S(1)}, f32[2,256,256]{2,1,0:T(8,128)}, u32[]{:S(2)}, u32[]{:S(2)}) collective-permute-start(f32[2,256,256]{2,1,0:T(8,128)S(1)} %collective-permute-done.right_any), channel_id=1, source_target_pairs={{4,0},{5,1},{6,2},{7,3},{8,4},{9,5},{10,6},{11,7},{12,8},{13,9},{1... | collective-permute-start | bytes 1572872 | tf_op jit(solution)/shard_map/ppermute | solution.py:24
  21.4 6.8 %collective-permute-start.2 = (s32[12,2]{1,0:T(8,128)S(1)}, s32[12,2]{1,0:T(8,128)S(1)}, u32[]{:S(2)}, u32[]{:S(2)}) collective-permute-start(s32[12,2]{1,0:T(8,128)S(1)} %copy.19), channel_id=1, source_target_pairs={{0,4},{1,5},{2,6},{3,7},{4,8},{5,9},{6,10},{7,11},{8,12},{9,13},{1... | collective-permute-start | bytes 296 | tf_op jit(solution)/shard_map/ppermute | solution.py:24
  50.7 2.9 %collective-permute-start.5 = (f32[1152,256]{1,0:T(8,128)S(1)}, f32[1152,256]{1,0:T(8,128)S(1)}, u32[]{:S(2)}, u32[]{:S(2)}) collective-permute-start(f32[1152,256]{1,0:T(8,128)S(1)} %get-tuple-element.48), channel_id=1, source_target_pairs={{0,4},{1,5},{2,6},{3,7},{4,0},{5,1},{6,2},{7,3},{8,12},{9,13},{10,... | collective-permute-start | bytes 3538952 | tf_op jit(solution)/shard_map/ppermute | solution.py:30
  53.7 9.9 %collective-permute-start.6 = (f32[576,256]{1,0:T(8,128)S(1)}, f32[576,256]{1,0:T(8,128)S(1)}, u32[]{:S(2)}, u32[]{:S(2)}) collective-permute-start(f32[576,256]{1,0:T(8,128)S(1)} %get-tuple-element.50), channel_id=1, source_target_pairs={{0,8},{1,9},{2,10},{3,11},{4,20},{5,21},{6,22},{7,23},{8,0},{9,1},... | collective-permute-start | bytes 1769480 | tf_op jit(solution)/shard_map/ppermute | solution.py:71
  63.7 66.7 %copy-start.4 = (f32[2,256,512]{2,1,0:T(8,128)S(1)}, f32[2,256,512]{2,1,0:T(8,128)}, u32[]{:S(2)}) copy-start(f32[2,256,512]{2,1,0:T(8,128)} %get-tuple-element.67.g_tile) | copy-start | bytes 3145732
  63.7 48.5 %collective-permute-start.13 = (f32[2,256,768]{2,1,0:T(8,128)S(1)}, f32[2,256,768]{2,1,0:T(8,128)S(1)}, u32[]{:S(2)}, u32[]{:S(2)}) collective-permute-start(f32[2,256,768]{2,1,0:T(8,128)S(1)} %get-tuple-element.62), channel_id=1, source_target_pairs={{0,4},{1,5},{2,6},{3,7},{4,8},{5,9},{6,10},{7,11},{8,12},{9,13},{1... | collective-permute-start | bytes 4718600 | tf_op jit(solution)/shard_map/ppermute | solution.py:24
  65.3 21.2 %collective-permute-start.7 = (f32[288,256]{1,0:T(8,128)S(1)}, f32[288,256]{1,0:T(8,128)S(1)}, u32[]{:S(2)}, u32[]{:S(2)}) collective-permute-start(f32[288,256]{1,0:T(8,128)S(1)} %get-tuple-element.54), channel_id=1, source_target_pairs={{0,16},{1,17},{2,18},{3,19},{4,12},{5,13},{6,14},{7,15},{8,24},{9,... | collective-permute-start | bytes 884744 | tf_op jit(solution)/shard_map/ppermute | solution.py:71
  86.4 43.9 %copy-start.1 = (f32[2,4,256,256]{3,2,1,0:T(8,128)S(1)}, f32[2,4,256,256]{3,2,1,0:T(8,128)}, u32[]{:S(2)}) copy-start(f32[2,4,256,256]{3,2,1,0:T(8,128)} %probe_ref.1) | copy-start | bytes 6291460
  86.4 43.9 %copy-start.3 = (f32[2,256,512]{2,1,0:T(8,128)S(1)}, f32[2,256,512]{2,1,0:T(8,128)}, u32[]{:S(2)}) copy-start(f32[2,256,512]{2,1,0:T(8,128)} %tile_ref.1) | copy-start | bytes 3145732
  86.5 10.4 %collective-permute-start.8 = (f32[152,256]{1,0:T(8,128)S(1)}, f32[152,256]{1,0:T(8,128)S(1)}, u32[]{:S(2)}, u32[]{:S(2)}) collective-permute-start(f32[152,256]{1,0:T(8,128)S(1)} %get-tuple-element.57), channel_id=1, source_target_pairs={{0,1},{1,0},{2,3},{3,2},{4,5},{5,4},{6,7},{7,6},{8,9},{9,8},{10,11... | collective-permute-start | bytes 466952 | tf_op jit(solution)/shard_map/ppermute | solution.py:30
  96.9 7.2 %collective-permute-start.9 = (f32[80,256]{1,0:T(8,128)S(1)}, f32[80,256]{1,0:T(8,128)S(1)}, u32[]{:S(2)}, u32[]{:S(2)}) collective-permute-start(f32[80,256]{1,0:T(8,128)S(1)} %get-tuple-element.60), channel_id=1, source_target_pairs={{0,2},{1,3},{2,0},{3,1},{4,6},{5,7},{6,4},{7,5},{8,10},{9,11},{10,... | collective-permute-start | bytes 245768 | tf_op jit(solution)/shard_map/ppermute | solution.py:30
  104.1 7.5 %collective-permute-start.10 = (f32[72,256]{1,0:T(8,128)S(1)}, f32[72,256]{1,0:T(8,128)S(1)}, u32[]{:S(2)}, u32[]{:S(2)}) collective-permute-start(f32[72,256]{1,0:T(8,128)S(1)} %get-tuple-element.71), channel_id=1, source_target_pairs={{0,2},{1,3},{2,0},{3,1},{4,6},{5,7},{6,4},{7,5},{8,10},{9,11},{10,... | collective-permute-start | bytes 221192 | tf_op jit(solution)/shard_map/ppermute | solution.py:30
  104.2 8.0 %collective-permute-start.12 = (f32[72,256]{1,0:T(8,128)S(1)}, f32[72,256]{1,0:T(8,128)S(1)}, u32[]{:S(2)}, u32[]{:S(2)}) collective-permute-start(f32[72,256]{1,0:T(8,128)S(1)} %get-tuple-element.71), channel_id=1, source_target_pairs={{0,3},{1,2},{2,1},{3,0},{4,7},{5,6},{6,5},{7,4},{8,11},{9,10},{10,... | collective-permute-start | bytes 221192 | tf_op jit(solution)/shard_map/ppermute | solution.py:30
  107.1 5.1 %collective-permute-start.11 = (f32[72,256]{1,0:T(8,128)S(1)}, f32[72,256]{1,0:T(8,128)S(1)}, u32[]{:S(2)}, u32[]{:S(2)}) collective-permute-start(f32[72,256]{1,0:T(8,128)S(1)} %get-tuple-element.71), channel_id=1, source_target_pairs={{0,1},{1,0},{2,3},{3,2},{4,5},{5,4},{6,7},{7,6},{8,9},{9,8},{10,11... | collective-permute-start | bytes 221192 | tf_op jit(solution)/shard_map/ppermute | solution.py:30
  112.3 9.6 %collective-permute-start.14 = (f32[296,256]{1,0:T(8,128)S(1)}, f32[296,256]{1,0:T(8,128)S(1)}, u32[]{:S(2)}, u32[]{:S(2)}) collective-permute-start(f32[296,256]{1,0:T(8,128)S(1)} %constant_dynamic-update-slice_fusion.refs_0_), channel_id=1, source_target_pairs={{0,16},{1,17},{2,18},{3,19},{4,12},{5,13},{6,14},{7,15},{8,24},{9,... | collective-permute-start | bytes 909320 | tf_op jit(solution)/shard_map/ppermute | solution.py:71
  114.2 11.3 %collective-permute-start.17 = (f32[2,256,256]{2,1,0:T(8,128)S(1)}, f32[2,256,256]{2,1,0:T(8,128)S(1)}, u32[]{:S(2)}, u32[]{:S(2)}) collective-permute-start(f32[2,256,256]{2,1,0:T(8,128)S(1)} %slice_add_fusion), channel_id=1, source_target_pairs={{0,1},{1,2},{2,3},{4,5},{5,6},{6,7},{8,9},{9,10},{10,11},{12,13},{... | collective-permute-start | bytes 1572872 | tf_op jit(solution)/shard_map/ppermute | solution.py:24
  117.1 6.9 %collective-permute-start.15 = (f32[296,256]{1,0:T(8,128)S(1)}, f32[296,256]{1,0:T(8,128)S(1)}, u32[]{:S(2)}, u32[]{:S(2)}) collective-permute-start(f32[296,256]{1,0:T(8,128)S(1)} %constant_dynamic-update-slice_fusion.refs_0_), channel_id=1, source_target_pairs={{0,8},{1,9},{2,10},{3,11},{4,20},{5,21},{6,22},{7,23},{8,0},{9,1},... | collective-permute-start | bytes 909320 | tf_op jit(solution)/shard_map/ppermute | solution.py:71
  121.9 6.8 %collective-permute-start.16 = (f32[296,256]{1,0:T(8,128)S(1)}, f32[296,256]{1,0:T(8,128)S(1)}, u32[]{:S(2)}, u32[]{:S(2)}) collective-permute-start(f32[296,256]{1,0:T(8,128)S(1)} %collective-permute-done.14.refs_1_), channel_id=1, source_target_pairs={{0,8},{1,9},{2,10},{3,11},{4,20},{5,21},{6,22},{7,23},{8,0},{9,1},... | collective-permute-start | bytes 909320 | tf_op jit(solution)/shard_map/ppermute | solution.py:71
  121.9 6.8 %collective-permute-start.18 = (f32[296,256]{1,0:T(8,128)S(1)}, f32[296,256]{1,0:T(8,128)S(1)}, u32[]{:S(2)}, u32[]{:S(2)}) collective-permute-start(f32[296,256]{1,0:T(8,128)S(1)} %constant_dynamic-update-slice_fusion.refs_0_), channel_id=1, source_target_pairs={{0,4},{1,5},{2,6},{3,7},{4,0},{5,1},{6,2},{7,3},{8,12},{9,13},{10,... | collective-permute-start | bytes 909320 | tf_op jit(solution)/shard_map/ppermute | solution.py:30
  121.9 6.8 %collective-permute-start.19 = (f32[296,256]{1,0:T(8,128)S(1)}, f32[296,256]{1,0:T(8,128)S(1)}, u32[]{:S(2)}, u32[]{:S(2)}) collective-permute-start(f32[296,256]{1,0:T(8,128)S(1)} %collective-permute-done.14.refs_1_), channel_id=1, source_target_pairs={{0,4},{1,5},{2,6},{3,7},{4,0},{5,1},{6,2},{7,3},{8,12},{9,13},{10,... | collective-permute-start | bytes 909320 | tf_op jit(solution)/shard_map/ppermute | solution.py:30
  124.0 4.7 %collective-permute-start.20 = (f32[296,256]{1,0:T(8,128)S(1)}, f32[296,256]{1,0:T(8,128)S(1)}, u32[]{:S(2)}, u32[]{:S(2)}) collective-permute-start(f32[296,256]{1,0:T(8,128)S(1)} %collective-permute-done.15.refs_2_), channel_id=1, source_target_pairs={{0,4},{1,5},{2,6},{3,7},{4,0},{5,1},{6,2},{7,3},{8,12},{9,13},{10,... | collective-permute-start | bytes 909320 | tf_op jit(solution)/shard_map/ppermute | solution.py:30
  128.7 1.6 %collective-permute-start.21 = (f32[296,256]{1,0:T(8,128)S(1)}, f32[296,256]{1,0:T(8,128)S(1)}, u32[]{:S(2)}, u32[]{:S(2)}) collective-permute-start(f32[296,256]{1,0:T(8,128)S(1)} %collective-permute-done.16.refs_3_), channel_id=1, source_target_pairs={{0,4},{1,5},{2,6},{3,7},{4,0},{5,1},{6,2},{7,3},{8,12},{9,13},{10,... | collective-permute-start | bytes 909320 | tf_op jit(solution)/shard_map/ppermute | solution.py:30

commit v16 on v14

--- a/solution.py
+++ b/solution.py
@@ -419,15 +419,15 @@
     spots = corners[0, 0]
 
     right = shifted(object_field[:, :, :side], 0, -1)
-    measured = evens_first(amplitudes[0, 0], True)
-    tile, measured, spots_now = lax.optimization_barrier((object_field, measured, spots))
+    lit = jnp.sum(probe[0] * probe[0] + probe[1] * probe[1], axis=0)
+    tile, lit, spots_now, patterns = lax.optimization_barrier((object_field, lit, spots, amplitudes[0, 0]))
+    measured = evens_first(patterns, True)
     below = shifted(tile[:, :side, :], -1, 0)
     from_left = shifted(spots_now, 0, 1)
     measured = evens_first(measured, False)
-    right, from_left, measured, modes_now = lax.optimization_barrier((right, from_left, measured, probe))
+    right, from_left, measured = lax.optimization_barrier((right, from_left, measured))
     corner = shifted(right[:, :side, :], -1, 0)
     from_up = shifted(jnp.concatenate([spots, from_left], axis=0), 1, 0)
-    lit = jnp.sum(modes_now[0] * modes_now[0] + modes_now[1] * modes_now[1], axis=0)
     light = add_light(((0, 0), (0, 1)), counts, (spots, from_left), lit, (rows, cols))
     light, top = add_light(
         ((1, 0), (1, 1)), counts, (from_up[:slots], from_up[slots:]), lit, (rows, cols), light

time: 118 us -> 119 us (level)
  waiting for transfers between devices: 36.9 us -> 51.1 us
  starting transfers between devices: 41.9 us -> 35.4 us
  Pallas kernels: 27 us -> 24 us
  matrix products: 6.34 us -> 3.73 us
  local copies, waits for them, and re-layouts: 2.51 us -> 0.72 us
    ppermute x7, waiting for transfers between devices: 5.72 us -> 12.6 us  [shifted(): return lax.ppermute(value, ('row', 'col'), pairs)]
    ppermute x10, starting transfers between devices: 13.9 us -> 8.29 us  [swapped(): return lax.ppermute(value, ('row', 'col'), pairs)]
    ppermute x10, waiting for transfers between devices: 15.1 us -> 19.3 us  [swapped(): return lax.ppermute(value, ('row', 'col'), pairs)]
    ppermute x5, waiting for transfers between devices: 16 us -> 19.2 us  [flipped(): return lax.ppermute(value, ('row', 'col'), pairs)]
    pallas_call x1, Pallas kernels: 21.3 us -> 18.5 us  [body(): pl.pallas_call(main_kernel, out_shape=(hbm(2, rows, cols), vmem(2, side,...]
    dot_general x2, matrix products: 6.34 us -> 3.73 us  [evens_first(): return jnp.einsum(form, pick, amplitudes, precision=lax.Precision.HIGH)]
    slice x1, local copies, waits for them, and re-layouts: 1.99 us -> 0.04 us  [body(): right = shifted(object_field[:, :, :side], 0, -1)]
  transfers between devices with their start and end apart: 22 -> 22, of which waited for: 11 -> 12; matrix products, arithmetic and copies ran while one was open for 7% -> 4% of each run, Pallas kernels for 3% -> 3%
where the time goes in v16:
time: 119 us; the launch traced here: 118 us
  waiting for transfers between devices  51.1 us (43%)
  starting transfers between devices  35.4 us (30%)
  Pallas kernels  24 us (20%)
  matrix products  3.73 us (3%)
  other arithmetic  2.03 us (2%)
    ppermute x10, waiting for transfers between devices, swapped(): return lax.ppermute(value, ('row', 'col'), pairs)  19.3 us
    ppermute x5, waiting for transfers between devices, flipped(): return lax.ppermute(value, ('row', 'col'), pairs)  19.2 us
    pallas_call x1, Pallas kernels, body(): pl.pallas_call(main_kernel, out_shape=(hbm(2, rows, cols), vmem(2, side,...  18.5 us
    ppermute x7, starting transfers between devices, shifted(): return lax.ppermute(value, ('row', 'col'), pairs)  16.4 us
    ppermute x7, waiting for transfers between devices, shifted(): return lax.ppermute(value, ('row', 'col'), pairs)  12.6 us
    ppermute x5, starting transfers between devices, flipped(): return lax.ppermute(value, ('row', 'col'), pairs)  10.7 us
    ppermute x10, starting transfers between devices, swapped(): return lax.ppermute(value, ('row', 'col'), pairs)  8.29 us
    dot_general x2, matrix products, evens_first(): return jnp.einsum(form, pick, amplitudes, precision=lax.Precision.HIGH)  3.73 us
  transfers between devices with their start and end apart: 22, of which 12 were waited for; matrix products, arithmetic and copies ran while one was open for 4% of the time, Pallas kernels for 3%

profile of v16, /device:TPU:0, one launch (start us, length us, event | category | flops | bytes accessed | tf_op | source)
XLA Modules:
  0.0 118.0 jit_solution(1765580265581918312)
XLA Ops:
  0.7 1.9 %add_reduce_fusion.refs_2_ = f32[256,256]{1,0:T(8,128)S(1)} fusion(f32[2,4,256,256]{3,2,1,0:T(8,128)} %probe_ref.1), kind=kLoop, calls=%fused_computation.2 | loop fusion | flops 983040 | bytes 2359296 | tf_op jit(solution)/shard_map/reduce_sum | solution.py:422
  2.5 0.2 copy-done
  2.7 0.1 copy.17
  2.8 4.9 %collective-permute-start.1 = (s32[6,2]{1,0:T(8,128)S(1)}, s32[6,2]{1,0:T(8,128)S(1)}, u32[]{:S(2)}, u32[]{:S(2)}) collective-permute-start(s32[6,2]{1,0:T(8,128)S(1)} %copy.17), channel_id=1, source_target_pairs={{0,1},{1,2},{2,3},{4,5},{5,6},{6,7},{8,9},{9,10},{10,11},{12,13},{... | collective-permute-start | bytes 152 | tf_op jit(solution)/shard_map/ppermute | solution.py:24
  7.8 1.4 %collective-permute-start = (f32[2,256,256]{2,1,0:T(8,128)S(1)}, f32[2,256,256]{2,1,0:T(8,128)S(1)}, u32[]{:S(2)}, u32[]{:S(2)}) collective-permute-start(f32[2,256,256]{2,1,0:T(8,128)S(1)} %slice.50), channel_id=1, source_target_pairs={{1,0},{2,1},{3,2},{5,4},{6,5},{7,6},{9,8},{10,9},{11,10},{13,12},{... | collective-permute-start | bytes 1572872 | tf_op jit(solution)/shard_map/ppermute | solution.py:24
  9.2 1.3 %collective-permute-start.3 = (f32[2,256,512]{2,1,0:T(8,128)S(1)}, f32[2,256,512]{2,1,0:T(8,128)}, u32[]{:S(2)}, u32[]{:S(2)}) collective-permute-start(f32[2,256,512]{2,1,0:T(8,128)S(1)} %copy-done.2), channel_id=1, source_target_pairs={{4,0},{5,1},{6,2},{7,3},{8,4},{9,5},{10,6},{11,7},{12,8},{13,9},{1... | collective-permute-start | bytes 3145736 | tf_op jit(solution)/shard_map/ppermute | solution.py:24
  10.5 1.8 %fusion.4 = f32[6,256,256]{1,2,0:T(8,128)S(1)} fusion(f32[6,256,256]{2,1,0:T(8,128)S(1)} %bitcast.9, f32[256,256,1]{1,0,2:T(8,128)} %constant.10), kind=kOutput, calls=%fused_computation.20 | convolution fusion | flops 603979776 | bytes 3407872 | tf_op jit(solution)/shard_map/ab,sbc->sac/dot_general | solution.py:92
  12.3 2.0 %fusion.amp_hbm = f32[6,256,256]{2,1,0:T(8,128)} fusion(f32[256,256,1]{1,0,2:T(8,128)S(1)} %copy-done.5, f32[6,256,256]{1,2,0:T(8,128)S(1)} %fusion.4), kind=kOutput, calls=%fused_computation | convolution fusion | flops 603979776 | bytes 3407872 | tf_op jit(solution)/shard_map/cb,sab->sac/dot_general | solution.py:92
  14.3 8.9 %collective-permute-done.right_any = f32[2,256,256]{2,1,0:T(8,128)S(1)} collective-permute-done((f32[2,256,256]{2,1,0:T(8,128)S(1)}, f32[2,256,256]{2,1,0:T(8,128)S(1)}, u32[]{:S(2)}, u32[]{:S(2)}) %collective-permute-start) | collective-permute-done | bytes 524320 | tf_op jit(solution)/shard_map/ppermute | solution.py:24
  23.2 1.3 %collective-permute-start.4 = (f32[2,256,256]{2,1,0:T(8,128)S(1)}, f32[2,256,256]{2,1,0:T(8,128)}, u32[]{:S(2)}, u32[]{:S(2)}) collective-permute-start(f32[2,256,256]{2,1,0:T(8,128)S(1)} %collective-permute-done.right_any), channel_id=1, source_target_pairs={{4,0},{5,1},{6,2},{7,3},{8,4},{9,5},{10,6},{11,7},{12,8},{13,9},{1... | collective-permute-start | bytes 1572872 | tf_op jit(solution)/shard_map/ppermute | solution.py:24
  24.5 0.1 copy.21.refs_0_.spots_ref
  24.6 0.1 copy.22.counts_ref
  24.7 0.1 copy.18
  24.7 0.1 pad_add_fusion
  24.8 0.1 copy.19
  24.9 3.0 %collective-permute-start.2 = (s32[12,2]{1,0:T(8,128)S(1)}, s32[12,2]{1,0:T(8,128)S(1)}, u32[]{:S(2)}, u32[]{:S(2)}) collective-permute-start(s32[12,2]{1,0:T(8,128)S(1)} %copy.19), channel_id=1, source_target_pairs={{0,4},{1,5},{2,6},{3,7},{4,8},{5,9},{6,10},{7,11},{8,12},{9,13},{1... | collective-permute-start | bytes 296 | tf_op jit(solution)/shard_map/ppermute | solution.py:24
  27.9 1.9 %lighting_start.1.refs_3_ = f32[256,512]{1,0:T(8,128)S(1)} custom-call(s32[8,4]{1,0:T(8,128)S(1)} %copy.22.counts_ref, s32[6,2]{1,0:T(8,128)S(1)} %copy.21.refs_0_.spots_ref, s32[6,2]{1,0:T(8,128)S(1)} %collective-permute-done.1.refs_1_, f32[256,256]{1,0:T(8,128)S(1)} %add_reduce_fusion.refs_2_), custom_call_target="tpu_custom_call" | custom-call | flops 100000000 | bytes 6000000 | tf_op jit(solution)/shard_map/lighting_start/pallas_call | solution.py:293
  29.9 1.1 lighting_end.1
  31.0 18.5 %positions.1 = (f32[2,256,512]{2,1,0:T(8,128)}, f32[2,256,768]{2,1,0:T(8,128)S(1)}, f32[2,256,256]{2,1,0:T(8,128)S(1)}, f32[1152,256]{1,0:T(8,128)S(1)}, f32[1152,256]{1,0:T(8,128)S(1)}) custom-call(s32[8,4]{1,0:T(8,128)S(1)} %copy.22.counts_ref, s32[6,2]{1,0:T(8,128)S(1)} %copy.21.refs_0_.spots_ref, f32[2,256,512]{2,1,0:T(8,128)} %tile_ref.1, ...), custom_call_target="tpu_custom_call" | custom-call | flops 7000000000 | bytes 20000000 | tf_op jit(solution)/shard_map/positions/pallas_call | solution.py:436
  49.4 0.1 collective-permute-start.5
  49.5 2.8 %collective-permute-done.5.refs_1_ = f32[1152,256]{1,0:T(8,128)S(1)} collective-permute-done((f32[1152,256]{1,0:T(8,128)S(1)}, f32[1152,256]{1,0:T(8,128)S(1)}, u32[]{:S(2)}, u32[]{:S(2)}) %collective-permute-start.5) | collective-permute-done | bytes 1179680 | tf_op jit(solution)/shard_map/ppermute | solution.py:30
  52.3 0.2 fold.4
  52.5 6.8 %collective-permute-start.6 = (f32[576,256]{1,0:T(8,128)S(1)}, f32[576,256]{1,0:T(8,128)S(1)}, u32[]{:S(2)}, u32[]{:S(2)}) collective-permute-start(f32[576,256]{1,0:T(8,128)S(1)} %get-tuple-element.50), channel_id=1, source_target_pairs={{0,8},{1,9},{2,10},{3,11},{4,20},{5,21},{6,22},{7,23},{8,0},{9,1},... | collective-permute-start | bytes 1769480 | tf_op jit(solution)/shard_map/ppermute | solution.py:71
  59.3 7.9 %collective-permute-done.6.refs_1_ = f32[576,256]{1,0:T(8,128)S(1)} collective-permute-done((f32[576,256]{1,0:T(8,128)S(1)}, f32[576,256]{1,0:T(8,128)S(1)}, u32[]{:S(2)}, u32[]{:S(2)}) %collective-permute-start.6) | collective-permute-done | bytes 589856 | tf_op jit(solution)/shard_map/ppermute | solution.py:71
  67.2 0.1 fold.5
  67.3 0.1 collective-permute-start.7
  67.3 6.7 %collective-permute-done.7.refs_1_ = f32[288,256]{1,0:T(8,128)S(1)} collective-permute-done((f32[288,256]{1,0:T(8,128)S(1)}, f32[288,256]{1,0:T(8,128)S(1)}, u32[]{:S(2)}, u32[]{:S(2)}) %collective-permute-start.7) | collective-permute-done | bytes 294944 | tf_op jit(solution)/shard_map/ppermute | solution.py:71
  74.1 1.7 %collective-permute-start.13 = (f32[2,256,768]{2,1,0:T(8,128)S(1)}, f32[2,256,768]{2,1,0:T(8,128)S(1)}, u32[]{:S(2)}, u32[]{:S(2)}) collective-permute-start(f32[2,256,768]{2,1,0:T(8,128)S(1)} %get-tuple-element.62), channel_id=1, source_target_pairs={{0,4},{1,5},{2,6},{3,7},{4,8},{5,9},{6,10},{7,11},{8,12},{9,13},{1... | collective-permute-start | bytes 4718600 | tf_op jit(solution)/shard_map/ppermute | solution.py:24
  75.8 0.2 collective-permute-start.8
  76.0 5.1 %collective-permute-done.8.refs_1_ = f32[152,256]{1,0:T(8,128)S(1)} collective-permute-done((f32[152,256]{1,0:T(8,128)S(1)}, f32[152,256]{1,0:T(8,128)S(1)}, u32[]{:S(2)}, u32[]{:S(2)}) %collective-permute-start.8) | collective-permute-done | bytes 155680 | tf_op jit(solution)/shard_map/ppermute | solution.py:30
  81.1 4.0 %collective-permute-start.9 = (f32[80,256]{1,0:T(8,128)S(1)}, f32[80,256]{1,0:T(8,128)S(1)}, u32[]{:S(2)}, u32[]{:S(2)}) collective-permute-start(f32[80,256]{1,0:T(8,128)S(1)} %get-tuple-element.60), channel_id=1, source_target_pairs={{0,2},{1,3},{2,0},{3,1},{4,6},{5,7},{6,4},{7,5},{8,10},{9,11},{10,... | collective-permute-start | bytes 245768 | tf_op jit(solution)/shard_map/ppermute | solution.py:30
  85.0 4.0 %collective-permute-done.9 = f32[80,256]{1,0:T(8,128)S(1)} collective-permute-done((f32[80,256]{1,0:T(8,128)S(1)}, f32[80,256]{1,0:T(8,128)S(1)}, u32[]{:S(2)}, u32[]{:S(2)}) %collective-permute-start.9) | collective-permute-done | bytes 81952 | tf_op jit(solution)/shard_map/ppermute | solution.py:30
  89.1 1.4 %collective-permute-start.10 = (f32[72,256]{1,0:T(8,128)S(1)}, f32[72,256]{1,0:T(8,128)S(1)}, u32[]{:S(2)}, u32[]{:S(2)}) collective-permute-start(f32[72,256]{1,0:T(8,128)S(1)} %get-tuple-element.71), channel_id=1, source_target_pairs={{0,2},{1,3},{2,0},{3,1},{4,6},{5,7},{6,4},{7,5},{8,10},{9,11},{10,... | collective-permute-start | bytes 221192 | tf_op jit(solution)/shard_map/ppermute | solution.py:30
  90.5 1.3 %collective-permute-start.12 = (f32[72,256]{1,0:T(8,128)S(1)}, f32[72,256]{1,0:T(8,128)S(1)}, u32[]{:S(2)}, u32[]{:S(2)}) collective-permute-start(f32[72,256]{1,0:T(8,128)S(1)} %get-tuple-element.71), channel_id=1, source_target_pairs={{0,3},{1,2},{2,1},{3,0},{4,7},{5,6},{6,5},{7,4},{8,11},{9,10},{10,... | collective-permute-start | bytes 221192 | tf_op jit(solution)/shard_map/ppermute | solution.py:30
  91.8 0.8 collective-permute-start.11
  92.6 4.6 %collective-permute-done.10 = f32[72,256]{1,0:T(8,128)S(1)} collective-permute-done((f32[72,256]{1,0:T(8,128)S(1)}, f32[72,256]{1,0:T(8,128)S(1)}, u32[]{:S(2)}, u32[]{:S(2)}) %collective-permute-start.10) | collective-permute-done | bytes 73760 | tf_op jit(solution)/shard_map/ppermute | solution.py:30
  97.3 1.2 collective-permute-done.11
  98.5 0.1 slice_add_fusion
  98.6 2.1 %collective-permute-start.14 = (f32[296,256]{1,0:T(8,128)S(1)}, f32[296,256]{1,0:T(8,128)S(1)}, u32[]{:S(2)}, u32[]{:S(2)}) collective-permute-start(f32[296,256]{1,0:T(8,128)S(1)} %constant_dynamic-update-slice_fusion.refs_0_), channel_id=1, source_target_pairs={{0,16},{1,17},{2,18},{3,19},{4,12},{5,13},{6,14},{7,15},{8,24},{9,... | collective-permute-start | bytes 909320 | tf_op jit(solution)/shard_map/ppermute | solution.py:71
  100.7 2.8 %collective-permute-start.17 = (f32[2,256,256]{2,1,0:T(8,128)S(1)}, f32[2,256,256]{2,1,0:T(8,128)S(1)}, u32[]{:S(2)}, u32[]{:S(2)}) collective-permute-start(f32[2,256,256]{2,1,0:T(8,128)S(1)} %slice_add_fusion), channel_id=1, source_target_pairs={{0,1},{1,2},{2,3},{4,5},{5,6},{6,7},{8,9},{9,10},{10,11},{12,13},{... | collective-permute-start | bytes 1572872 | tf_op jit(solution)/shard_map/ppermute | solution.py:24
  103.5 0.1 collective-permute-start.15
  103.6 3.5 %collective-permute-done.14.refs_1_ = f32[296,256]{1,0:T(8,128)S(1)} collective-permute-done((f32[296,256]{1,0:T(8,128)S(1)}, f32[296,256]{1,0:T(8,128)S(1)}, u32[]{:S(2)}, u32[]{:S(2)}) %collective-permute-start.14) | collective-permute-done | bytes 303136 | tf_op jit(solution)/shard_map/ppermute | solution.py:71
  107.1 1.6 %collective-permute-start.16 = (f32[296,256]{1,0:T(8,128)S(1)}, f32[296,256]{1,0:T(8,128)S(1)}, u32[]{:S(2)}, u32[]{:S(2)}) collective-permute-start(f32[296,256]{1,0:T(8,128)S(1)} %collective-permute-done.14.refs_1_), channel_id=1, source_target_pairs={{0,8},{1,9},{2,10},{3,11},{4,20},{5,21},{6,22},{7,23},{8,0},{9,1},... | collective-permute-start | bytes 909320 | tf_op jit(solution)/shard_map/ppermute | solution.py:71
  108.7 0.5 collective-permute-start.19
  109.3 1.1 collective-permute-done.15.refs_2_
  110.4 3.7 %collective-permute-done.17.g_left = f32[2,256,256]{2,1,0:T(8,128)S(1)} collective-permute-done((f32[2,256,256]{2,1,0:T(8,128)S(1)}, f32[2,256,256]{2,1,0:T(8,128)S(1)}, u32[]{:S(2)}, u32[]{:S(2)}) %collective-permute-start.17) | collective-permute-done | bytes 524320 | tf_op jit(solution)/shard_map/ppermute | solution.py:24
  114.1 1.6 %collective-permute-done.21.refs_7_ = f32[296,256]{1,0:T(8,128)S(1)} collective-permute-done((f32[296,256]{1,0:T(8,128)S(1)}, f32[296,256]{1,0:T(8,128)S(1)}, u32[]{:S(2)}, u32[]{:S(2)}) %collective-permute-start.21) | collective-permute-done | bytes 303136 | tf_op jit(solution)/shard_map/ppermute | solution.py:30
  115.7 2.3 %update.1 = (f32[2,256,512]{2,1,0:T(8,128)}, f32[2,4,256,256]{3,2,1,0:T(8,128)}) custom-call(f32[2,256,512]{2,1,0:T(8,128)S(1)} %copy-done.3, f32[256,512]{1,0:T(8,128)S(1)} %get-tuple-element.40.light_ref, f32[8,256]{1,0:T(8,128)S(1)} %slice_maximum_fusion.top_ref, f32[2,256,512]{2,1,0:T(8,128)S(1)} %copy-done.4, ...), custom_call_target="tpu_custom_call" | custom-call | flops 1000000 | bytes 10000000 | tf_op jit(solution)/shard_map/update/pallas_call | solution.py:496
  (38 shorter events, 0.2 us)
Async XLA Ops:
  0.6 2.1 %copy-start = (f32[1,1,6,256,256]{4,3,2,1,0:T(8,128)S(1)}, f32[1,1,6,256,256]{4,3,2,1,0:T(8,128)}, u32[]{:S(2)}) copy-start(f32[1,1,6,256,256]{4,3,2,1,0:T(8,128)} %param.10) | copy-start | bytes 4718596
  0.6 7.1 %copy-start.2 = (f32[2,256,512]{2,1,0:T(8,128)S(1)}, f32[2,256,512]{2,1,0:T(8,128)}, u32[]{:S(2)}) copy-start(f32[2,256,512]{2,1,0:T(8,128)} %tile_ref.1) | copy-start | bytes 3145732
  0.7 2.0 %copy-start.6 = (s32[1,1,6,2]{2,3,1,0:T(2,128)S(1)}, s32[1,1,6,2]{2,3,1,0:T(2,128)}, u32[]{:S(2)}) copy-start(s32[1,1,6,2]{2,3,1,0:T(2,128)} %param.11) | copy-start | bytes 148
  2.8 11.5 %collective-permute-start.1 = (s32[6,2]{1,0:T(8,128)S(1)}, s32[6,2]{1,0:T(8,128)S(1)}, u32[]{:S(2)}, u32[]{:S(2)}) collective-permute-start(s32[6,2]{1,0:T(8,128)S(1)} %copy.17), channel_id=1, source_target_pairs={{0,1},{1,2},{2,3},{4,5},{5,6},{6,7},{8,9},{9,10},{10,11},{12,13},{... | collective-permute-start | bytes 152 | tf_op jit(solution)/shard_map/ppermute | solution.py:24
  7.8 4.5 %copy-start.5 = (f32[256,256,1]{1,0,2:T(8,128)S(1)}, f32[256,256,1]{1,0,2:T(8,128)}, u32[]{:S(2)}) copy-start(f32[256,256,1]{1,0,2:T(8,128)} %constant.10) | copy-start | bytes 786436
  7.8 15.4 %collective-permute-start = (f32[2,256,256]{2,1,0:T(8,128)S(1)}, f32[2,256,256]{2,1,0:T(8,128)S(1)}, u32[]{:S(2)}, u32[]{:S(2)}) collective-permute-start(f32[2,256,256]{2,1,0:T(8,128)S(1)} %slice.50), channel_id=1, source_target_pairs={{1,0},{2,1},{3,2},{5,4},{6,5},{7,6},{9,8},{10,9},{11,10},{13,12},{... | collective-permute-start | bytes 1572872 | tf_op jit(solution)/shard_map/ppermute | solution.py:24
  9.2 21.8 %collective-permute-start.3 = (f32[2,256,512]{2,1,0:T(8,128)S(1)}, f32[2,256,512]{2,1,0:T(8,128)}, u32[]{:S(2)}, u32[]{:S(2)}) collective-permute-start(f32[2,256,512]{2,1,0:T(8,128)S(1)} %copy-done.2), channel_id=1, source_target_pairs={{4,0},{5,1},{6,2},{7,3},{8,4},{9,5},{10,6},{11,7},{12,8},{13,9},{1... | collective-permute-start | bytes 3145736 | tf_op jit(solution)/shard_map/ppermute | solution.py:24
  12.3 12.3 %copy-start.7 = (s32[8,4]{0,1:T(4,128)S(1)}, s32[8,4]{0,1:T(4,128)}, u32[]{:S(2)}) copy-start(s32[8,4]{0,1:T(4,128)} %param.12) | copy-start | bytes 388
  23.2 7.8 %collective-permute-start.4 = (f32[2,256,256]{2,1,0:T(8,128)S(1)}, f32[2,256,256]{2,1,0:T(8,128)}, u32[]{:S(2)}, u32[]{:S(2)}) collective-permute-start(f32[2,256,256]{2,1,0:T(8,128)S(1)} %collective-permute-done.right_any), channel_id=1, source_target_pairs={{4,0},{5,1},{6,2},{7,3},{8,4},{9,5},{10,6},{11,7},{12,8},{13,9},{1... | collective-permute-start | bytes 1572872 | tf_op jit(solution)/shard_map/ppermute | solution.py:24
  24.9 4.9 %collective-permute-start.2 = (s32[12,2]{1,0:T(8,128)S(1)}, s32[12,2]{1,0:T(8,128)S(1)}, u32[]{:S(2)}, u32[]{:S(2)}) collective-permute-start(s32[12,2]{1,0:T(8,128)S(1)} %copy.19), channel_id=1, source_target_pairs={{0,4},{1,5},{2,6},{3,7},{4,8},{5,9},{6,10},{7,11},{8,12},{9,13},{1... | collective-permute-start | bytes 296 | tf_op jit(solution)/shard_map/ppermute | solution.py:24
  49.4 2.9 %collective-permute-start.5 = (f32[1152,256]{1,0:T(8,128)S(1)}, f32[1152,256]{1,0:T(8,128)S(1)}, u32[]{:S(2)}, u32[]{:S(2)}) collective-permute-start(f32[1152,256]{1,0:T(8,128)S(1)} %get-tuple-element.48), channel_id=1, source_target_pairs={{0,4},{1,5},{2,6},{3,7},{4,0},{5,1},{6,2},{7,3},{8,12},{9,13},{10,... | collective-permute-start | bytes 3538952 | tf_op jit(solution)/shard_map/ppermute | solution.py:30
  52.5 14.7 %collective-permute-start.6 = (f32[576,256]{1,0:T(8,128)S(1)}, f32[576,256]{1,0:T(8,128)S(1)}, u32[]{:S(2)}, u32[]{:S(2)}) collective-permute-start(f32[576,256]{1,0:T(8,128)S(1)} %get-tuple-element.50), channel_id=1, source_target_pairs={{0,8},{1,9},{2,10},{3,11},{4,20},{5,21},{6,22},{7,23},{8,0},{9,1},... | collective-permute-start | bytes 1769480 | tf_op jit(solution)/shard_map/ppermute | solution.py:71
  67.2 48.4 %copy-start.4 = (f32[2,256,512]{2,1,0:T(8,128)S(1)}, f32[2,256,512]{2,1,0:T(8,128)}, u32[]{:S(2)}) copy-start(f32[2,256,512]{2,1,0:T(8,128)} %get-tuple-element.67.g_tile) | copy-start | bytes 3145732
  67.3 6.8 %collective-permute-start.7 = (f32[288,256]{1,0:T(8,128)S(1)}, f32[288,256]{1,0:T(8,128)S(1)}, u32[]{:S(2)}, u32[]{:S(2)}) collective-permute-start(f32[288,256]{1,0:T(8,128)S(1)} %get-tuple-element.52), channel_id=1, source_target_pairs={{0,16},{1,17},{2,18},{3,19},{4,12},{5,13},{6,14},{7,15},{8,24},{9,... | collective-permute-start | bytes 884744 | tf_op jit(solution)/shard_map/ppermute | solution.py:71
  74.1 41.6 %copy-start.1 = (f32[2,4,256,256]{3,2,1,0:T(8,128)S(1)}, f32[2,4,256,256]{3,2,1,0:T(8,128)}, u32[]{:S(2)}) copy-start(f32[2,4,256,256]{3,2,1,0:T(8,128)} %probe_ref.1) | copy-start | bytes 6291460
  74.1 41.6 %copy-start.3 = (f32[2,256,512]{2,1,0:T(8,128)S(1)}, f32[2,256,512]{2,1,0:T(8,128)}, u32[]{:S(2)}) copy-start(f32[2,256,512]{2,1,0:T(8,128)} %tile_ref.1) | copy-start | bytes 3145732
  74.1 24.4 %collective-permute-start.13 = (f32[2,256,768]{2,1,0:T(8,128)S(1)}, f32[2,256,768]{2,1,0:T(8,128)S(1)}, u32[]{:S(2)}, u32[]{:S(2)}) collective-permute-start(f32[2,256,768]{2,1,0:T(8,128)S(1)} %get-tuple-element.62), channel_id=1, source_target_pairs={{0,4},{1,5},{2,6},{3,7},{4,8},{5,9},{6,10},{7,11},{8,12},{9,13},{1... | collective-permute-start | bytes 4718600 | tf_op jit(solution)/shard_map/ppermute | solution.py:24
  75.8 5.3 %collective-permute-start.8 = (f32[152,256]{1,0:T(8,128)S(1)}, f32[152,256]{1,0:T(8,128)S(1)}, u32[]{:S(2)}, u32[]{:S(2)}) collective-permute-start(f32[152,256]{1,0:T(8,128)S(1)} %get-tuple-element.57), channel_id=1, source_target_pairs={{0,1},{1,0},{2,3},{3,2},{4,5},{5,4},{6,7},{7,6},{8,9},{9,8},{10,11... | collective-permute-start | bytes 466952 | tf_op jit(solution)/shard_map/ppermute | solution.py:30
  81.1 8.0 %collective-permute-start.9 = (f32[80,256]{1,0:T(8,128)S(1)}, f32[80,256]{1,0:T(8,128)S(1)}, u32[]{:S(2)}, u32[]{:S(2)}) collective-permute-start(f32[80,256]{1,0:T(8,128)S(1)} %get-tuple-element.60), channel_id=1, source_target_pairs={{0,2},{1,3},{2,0},{3,1},{4,6},{5,7},{6,4},{7,5},{8,10},{9,11},{10,... | collective-permute-start | bytes 245768 | tf_op jit(solution)/shard_map/ppermute | solution.py:30
  89.1 8.2 %collective-permute-start.10 = (f32[72,256]{1,0:T(8,128)S(1)}, f32[72,256]{1,0:T(8,128)S(1)}, u32[]{:S(2)}, u32[]{:S(2)}) collective-permute-start(f32[72,256]{1,0:T(8,128)S(1)} %get-tuple-element.71), channel_id=1, source_target_pairs={{0,2},{1,3},{2,0},{3,1},{4,6},{5,7},{6,4},{7,5},{8,10},{9,11},{10,... | collective-permute-start | bytes 221192 | tf_op jit(solution)/shard_map/ppermute | solution.py:30
  90.5 8.0 %collective-permute-start.12 = (f32[72,256]{1,0:T(8,128)S(1)}, f32[72,256]{1,0:T(8,128)S(1)}, u32[]{:S(2)}, u32[]{:S(2)}) collective-permute-start(f32[72,256]{1,0:T(8,128)S(1)} %get-tuple-element.71), channel_id=1, source_target_pairs={{0,3},{1,2},{2,1},{3,0},{4,7},{5,6},{6,5},{7,4},{8,11},{9,10},{10,... | collective-permute-start | bytes 221192 | tf_op jit(solution)/shard_map/ppermute | solution.py:30
  91.8 6.7 %collective-permute-start.11 = (f32[72,256]{1,0:T(8,128)S(1)}, f32[72,256]{1,0:T(8,128)S(1)}, u32[]{:S(2)}, u32[]{:S(2)}) collective-permute-start(f32[72,256]{1,0:T(8,128)S(1)} %get-tuple-element.71), channel_id=1, source_target_pairs={{0,1},{1,0},{2,3},{3,2},{4,5},{5,4},{6,7},{7,6},{8,9},{9,8},{10,11... | collective-permute-start | bytes 221192 | tf_op jit(solution)/shard_map/ppermute | solution.py:30
  98.6 8.5 %collective-permute-start.14 = (f32[296,256]{1,0:T(8,128)S(1)}, f32[296,256]{1,0:T(8,128)S(1)}, u32[]{:S(2)}, u32[]{:S(2)}) collective-permute-start(f32[296,256]{1,0:T(8,128)S(1)} %constant_dynamic-update-slice_fusion.refs_0_), channel_id=1, source_target_pairs={{0,16},{1,17},{2,18},{3,19},{4,12},{5,13},{6,14},{7,15},{8,24},{9,... | collective-permute-start | bytes 909320 | tf_op jit(solution)/shard_map/ppermute | solution.py:71
  100.7 13.3 %collective-permute-start.17 = (f32[2,256,256]{2,1,0:T(8,128)S(1)}, f32[2,256,256]{2,1,0:T(8,128)S(1)}, u32[]{:S(2)}, u32[]{:S(2)}) collective-permute-start(f32[2,256,256]{2,1,0:T(8,128)S(1)} %slice_add_fusion), channel_id=1, source_target_pairs={{0,1},{1,2},{2,3},{4,5},{5,6},{6,7},{8,9},{9,10},{10,11},{12,13},{... | collective-permute-start | bytes 1572872 | tf_op jit(solution)/shard_map/ppermute | solution.py:24
  103.5 6.9 %collective-permute-start.15 = (f32[296,256]{1,0:T(8,128)S(1)}, f32[296,256]{1,0:T(8,128)S(1)}, u32[]{:S(2)}, u32[]{:S(2)}) collective-permute-start(f32[296,256]{1,0:T(8,128)S(1)} %constant_dynamic-update-slice_fusion.refs_0_), channel_id=1, source_target_pairs={{0,8},{1,9},{2,10},{3,11},{4,20},{5,21},{6,22},{7,23},{8,0},{9,1},... | collective-permute-start | bytes 909320 | tf_op jit(solution)/shard_map/ppermute | solution.py:71
  107.1 6.9 %collective-permute-start.16 = (f32[296,256]{1,0:T(8,128)S(1)}, f32[296,256]{1,0:T(8,128)S(1)}, u32[]{:S(2)}, u32[]{:S(2)}) collective-permute-start(f32[296,256]{1,0:T(8,128)S(1)} %collective-permute-done.14.refs_1_), channel_id=1, source_target_pairs={{0,8},{1,9},{2,10},{3,11},{4,20},{5,21},{6,22},{7,23},{8,0},{9,1},... | collective-permute-start | bytes 909320 | tf_op jit(solution)/shard_map/ppermute | solution.py:71
  108.7 5.3 %collective-permute-start.18 = (f32[296,256]{1,0:T(8,128)S(1)}, f32[296,256]{1,0:T(8,128)S(1)}, u32[]{:S(2)}, u32[]{:S(2)}) collective-permute-start(f32[296,256]{1,0:T(8,128)S(1)} %constant_dynamic-update-slice_fusion.refs_0_), channel_id=1, source_target_pairs={{0,4},{1,5},{2,6},{3,7},{4,0},{5,1},{6,2},{7,3},{8,12},{9,13},{10,... | collective-permute-start | bytes 909320 | tf_op jit(solution)/shard_map/ppermute | solution.py:30
  108.7 5.3 %collective-permute-start.19 = (f32[296,256]{1,0:T(8,128)S(1)}, f32[296,256]{1,0:T(8,128)S(1)}, u32[]{:S(2)}, u32[]{:S(2)}) collective-permute-start(f32[296,256]{1,0:T(8,128)S(1)} %collective-permute-done.14.refs_1_), channel_id=1, source_target_pairs={{0,4},{1,5},{2,6},{3,7},{4,0},{5,1},{6,2},{7,3},{8,12},{9,13},{10,... | collective-permute-start | bytes 909320 | tf_op jit(solution)/shard_map/ppermute | solution.py:30
  110.3 3.7 %collective-permute-start.20 = (f32[296,256]{1,0:T(8,128)S(1)}, f32[296,256]{1,0:T(8,128)S(1)}, u32[]{:S(2)}, u32[]{:S(2)}) collective-permute-start(f32[296,256]{1,0:T(8,128)S(1)} %collective-permute-done.15.refs_2_), channel_id=1, source_target_pairs={{0,4},{1,5},{2,6},{3,7},{4,0},{5,1},{6,2},{7,3},{8,12},{9,13},{10,... | collective-permute-start | bytes 909320 | tf_op jit(solution)/shard_map/ppermute | solution.py:30
  114.0 1.6 %collective-permute-start.21 = (f32[296,256]{1,0:T(8,128)S(1)}, f32[296,256]{1,0:T(8,128)S(1)}, u32[]{:S(2)}, u32[]{:S(2)}) collective-permute-start(f32[296,256]{1,0:T(8,128)S(1)} %collective-permute-done.16.refs_3_), channel_id=1, source_target_pairs={{0,4},{1,5},{2,6},{3,7},{4,0},{5,1},{6,2},{7,3},{8,12},{9,13},{10,... | collective-permute-start | bytes 909320 | tf_op jit(solution)/shard_map/ppermute | solution.py:30
